TPU v7x, 32 devices: a whole 2x2x4 slice. The times are simulated.
32 devices in a mesh: rep: 4 (over y, core), fsdp: 8 (over z, x).
Axes of the slice: x: 2, y: 2, z: 4, core: 2. Of those that a mesh axis runs over, the one named last changes fastest.
Arguments:
- latents: bfloat16 [32, 1024, 1024], P(('rep', 'fsdp')), may hold values from -6 to 6
- conditions: bfloat16 [32, 1024], P('rep'), may hold values from -6 to 6
- modulator: bfloat16 [1024, 6144], P('fsdp'), may hold values from -0.1875 to 0.1875
- modulbias: bfloat16 [6144], P('fsdp'), may hold values from -4 to 4
- projector: bfloat16 [1024, 3072], P('fsdp'), may hold values from -0.1875 to 0.1875
- querybias: bfloat16 [1024], P('fsdp'), may hold values from -6 to 6
- valuebias: bfloat16 [1024], P('fsdp'), may hold values from -0.4375 to 0.4375
- outweight: bfloat16 [1024, 1024], P('fsdp'), may hold values from -3 to 3
- outbiases: bfloat16 [1024], P('fsdp'), may hold values from -4 to 4
- expander: bfloat16 [1024, 4096], P('fsdp'), may hold values from -0.1875 to 0.1875
- expandbias: bfloat16 [4096], P('fsdp'), may hold values from -4 to 4
- shrinker: bfloat16 [4096, 1024], P('fsdp'), may hold values from -0.09375 to 0.09375
- shrinkbias: bfloat16 [1024], P('fsdp'), may hold values from -4 to 4
- upstream: bfloat16 [32, 1024, 1024], P(('rep', 'fsdp')), may hold values from -6 to 6
Outputs:
- layer_out: float32 [32, 1024, 1024], P(('rep', 'fsdp'))
- latents_grad: float32 [32, 1024, 1024], P(('rep', 'fsdp'))
- conditions_grad: float32 [32, 1024], P('rep', 'fsdp')
- modulator_grad: float32 [1024, 6144], P('fsdp')
- modulbias_grad: float32 [6144], P('fsdp')
- projector_grad: float32 [1024, 3072], P('fsdp')
- querybias_grad: float32 [1024], P('fsdp')
- valuebias_grad: float32 [1024], P('fsdp')
- outweight_grad: float32 [1024, 1024], P('fsdp')
- outbiases_grad: float32 [1024], P('fsdp')
- expander_grad: float32 [1024, 4096], P('fsdp')
- expandbias_grad: float32 [4096], P('fsdp')
- shrinker_grad: float32 [4096, 1024], P('fsdp')
- shrinkbias_grad: float32 [1024], P('fsdp')
All inputs are finite; a program needn't handle non-finite values.
Results may differ from a plain program's by a relative error of at most 0.015.
The roundings to bfloat16 on the way count: a program that leaves them out, or rounds other values in their place, can miss the bound.
Values may be sent and summed in bfloat16 or wider, within the bound.
No kernel may reach another device: no remote copies, remote signals or barrier semaphores. Data moves between devices by JAX's collectives and lax.ppermute only.
A program may use at most 256 MiB of HBM per device.

v0:
```python
from functools import partial

import jax
import jax.numpy as jnp
from jax import lax
from jax.sharding import PartitionSpec as P

HEADS = 16
HEAD_DIM = 64


EPS_NORM = 1e-06


def normalize(values):
    average = jnp.mean(values, axis=-1, keepdims=True)
    centred = values - average
    variance = jnp.mean(centred * centred, axis=-1, keepdims=True)
    return centred * lax.rsqrt(variance + EPS_NORM)


def modulate(values, shifts, scales):
    return normalize(values) * (1.0 + scales[:, None, :]) + shifts[:, None, :]


def split_pairs(stacked):
    blocks, length, feature = stacked.shape
    grouped = stacked.reshape(blocks, length, HEADS // 2, 2 * HEAD_DIM).transpose(0, 2, 1, 3)
    return grouped.reshape(blocks * (HEADS // 2), length, 2 * HEAD_DIM)


def join_pairs(paired, blocks):
    length = paired.shape[1]
    grouped = paired.reshape(blocks, HEADS // 2, length, 2 * HEAD_DIM).transpose(0, 2, 1, 3)
    return grouped.reshape(blocks, length, HEADS * HEAD_DIM)


def pair_scores(query_pair, key_pair):
    length = query_pair.shape[0]
    query_heads = query_pair.reshape(length, 2, HEAD_DIM)
    key_heads = key_pair.reshape(length, 2, HEAD_DIM)
    scores = jnp.einsum("qhd,khd->hqk", query_heads, key_heads, preferred_element_type=jnp.float32)
    return (scores * HEAD_DIM ** (-0.5), query_heads, key_heads)


def pair_forward(operands):
    query_pair, key_pair, value_pair = operands
    length = query_pair.shape[0]
    scores, _, _ = pair_scores(query_pair, key_pair)
    value_heads = value_pair.reshape(length, 2, HEAD_DIM)
    top_score = jnp.max(scores, axis=-1, keepdims=True)
    exp_terms = jnp.exp(scores - top_score)
    denominator = jnp.sum(exp_terms, axis=-1, keepdims=True)
    attn_probs = (exp_terms / denominator).astype(jnp.bfloat16)
    attended = jnp.einsum(
        "hqk,khd->qhd", attn_probs, value_heads, preferred_element_type=jnp.float32
    )
    log_total = (top_score + jnp.log(denominator))[:, :, 0]
    return (attended.reshape(length, 2 * HEAD_DIM).astype(jnp.bfloat16), log_total)


def pair_backward(operands):
    query_pair, key_pair, value_pair, grad_pair, log_total = operands
    length = query_pair.shape[0]
    scores, query_heads, key_heads = pair_scores(query_pair, key_pair)
    value_heads = value_pair.reshape(length, 2, HEAD_DIM)
    grad_heads = grad_pair.reshape(length, 2, HEAD_DIM)
    probs_full = jnp.exp(scores - log_total[:, :, None])
    probs_low = probs_full.astype(jnp.bfloat16)
    d_value = jnp.einsum("hqk,qhd->khd", probs_low, grad_heads, preferred_element_type=jnp.float32)
    d_probs = jnp.einsum(
        "qhd,khd->hqk", grad_heads, value_heads, preferred_element_type=jnp.float32
    )
    row_sum = jnp.sum(probs_full * d_probs, axis=-1, keepdims=True)
    d_scores = (probs_full * (d_probs - row_sum)).astype(jnp.bfloat16)
    d_query = jnp.einsum(
        "hqk,khd->qhd", d_scores, key_heads, preferred_element_type=jnp.float32
    ) * HEAD_DIM ** (-0.5)
    d_key = jnp.einsum(
        "hqk,qhd->khd", d_scores, query_heads, preferred_element_type=jnp.float32
    ) * HEAD_DIM ** (-0.5)
    return (
        d_query.reshape(length, 2 * HEAD_DIM).astype(jnp.bfloat16),
        d_key.reshape(length, 2 * HEAD_DIM).astype(jnp.bfloat16),
        d_value.reshape(length, 2 * HEAD_DIM).astype(jnp.bfloat16),
    )


def on_device(
    latents,
    conditions,
    modulator,
    modulbias,
    projector,
    querybias,
    valuebias,
    outweight,
    outbiases,
    expander,
    expandbias,
    shrinker,
    shrinkbias,
    upstream,
):
    seqs_dev, seq_len, feature = latents.shape
    token_count = seqs_dev * seq_len
    shard_id = lax.axis_index("fsdp")
    own_rows = modulator.shape[0]
    own_bias = modulbias.shape[0]
    cond_full = conditions.astype(jnp.float32)
    cond_slice = lax.dynamic_slice_in_dim(cond_full, shard_id * own_rows, own_rows, 1)
    cond_act = jax.nn.silu(cond_slice).astype(jnp.bfloat16)
    mod_term = jnp.dot(cond_act, modulator, preferred_element_type=jnp.float32)
    bias_row = lax.dynamic_update_slice_in_dim(
        jnp.zeros((6 * feature,), jnp.float32),
        modulbias.astype(jnp.float32),
        shard_id * own_bias,
        0,
    )
    modvals = lax.psum_scatter(
        mod_term + bias_row[None, :], "fsdp", scatter_dimension=0, tiled=True
    ).reshape(seqs_dev, 6, feature)
    shift_a, scale_a, gate_a = (modvals[:, 0], modvals[:, 1], modvals[:, 2])
    shift_m, scale_m, gate_m = (modvals[:, 3], modvals[:, 4], modvals[:, 5])
    w_proj, b_query, b_value, w_out, b_out = (
        lax.all_gather(projector, "fsdp", axis=0, tiled=True),
        lax.all_gather(querybias, "fsdp", axis=0, tiled=True),
        lax.all_gather(valuebias, "fsdp", axis=0, tiled=True),
        lax.all_gather(outweight, "fsdp", axis=0, tiled=True),
        lax.all_gather(outbiases, "fsdp", axis=0, tiled=True),
    )
    resid_in = latents.astype(jnp.float32)
    norm_a = modulate(resid_in, shift_a, scale_a).astype(jnp.bfloat16).reshape(token_count, feature)
    projected = jnp.dot(norm_a, w_proj, preferred_element_type=jnp.float32)
    queries = (
        (projected[:, :feature] + b_query.astype(jnp.float32))
        .astype(jnp.bfloat16)
        .reshape(seqs_dev, seq_len, feature)
    )
    key_rows = (
        projected[:, feature : 2 * feature].astype(jnp.bfloat16).reshape(seqs_dev, seq_len, feature)
    )
    values = (
        (projected[:, 2 * feature :] + b_value.astype(jnp.float32))
        .astype(jnp.bfloat16)
        .reshape(seqs_dev, seq_len, feature)
    )
    paired_query = split_pairs(queries)
    paired_key = split_pairs(key_rows)
    paired_value = split_pairs(values)
    attended_pairs, log_totals = lax.map(pair_forward, (paired_query, paired_key, paired_value))
    attended = join_pairs(attended_pairs, seqs_dev).reshape(token_count, feature)
    branch_a = (
        jnp.dot(attended, w_out, preferred_element_type=jnp.float32) + b_out.astype(jnp.float32)
    ).reshape(seqs_dev, seq_len, feature)
    middle = resid_in + gate_a[:, None, :] * branch_a
    w_expand, b_expand, w_shrink, b_shrink = (
        lax.all_gather(expander, "fsdp", axis=0, tiled=True),
        lax.all_gather(expandbias, "fsdp", axis=0, tiled=True),
        lax.all_gather(shrinker, "fsdp", axis=0, tiled=True),
        lax.all_gather(shrinkbias, "fsdp", axis=0, tiled=True),
    )
    norm_m = modulate(middle, shift_m, scale_m).astype(jnp.bfloat16).reshape(token_count, feature)
    pre_act = jnp.dot(norm_m, w_expand, preferred_element_type=jnp.float32) + b_expand.astype(
        jnp.float32
    )
    gelu_fn = partial(jax.nn.gelu, approximate=True)
    hidden = gelu_fn(pre_act).astype(jnp.bfloat16)
    branch_m = (
        jnp.dot(hidden, w_shrink, preferred_element_type=jnp.float32) + b_shrink.astype(jnp.float32)
    ).reshape(seqs_dev, seq_len, feature)
    layer_out = middle + gate_m[:, None, :] * branch_m
    back_proj, back_out, back_expand, back_shrink = (
        lax.all_gather(projector, "fsdp", axis=0, tiled=True),
        lax.all_gather(outweight, "fsdp", axis=0, tiled=True),
        lax.all_gather(expander, "fsdp", axis=0, tiled=True),
        lax.all_gather(shrinker, "fsdp", axis=0, tiled=True),
    )
    grad_out = upstream.astype(jnp.float32)
    d_branch_m = (gate_m[:, None, :] * grad_out).astype(jnp.bfloat16).reshape(token_count, feature)
    d_gate_m = jnp.sum(grad_out * branch_m, axis=1)
    g_shrinkbias = jnp.sum(d_branch_m, axis=0, dtype=jnp.float32)
    g_shrinker = jnp.einsum("nf,nd->fd", hidden, d_branch_m, preferred_element_type=jnp.float32)
    d_hidden = jnp.einsum("nd,fd->nf", d_branch_m, back_shrink, preferred_element_type=jnp.float32)
    _, gelu_pull = jax.vjp(gelu_fn, pre_act)
    d_pre = gelu_pull(d_hidden)[0].astype(jnp.bfloat16)
    g_expandbias = jnp.sum(d_pre, axis=0, dtype=jnp.float32)
    g_expander = jnp.einsum("nd,nf->df", norm_m, d_pre, preferred_element_type=jnp.float32)
    d_norm_m = jnp.einsum(
        "nf,df->nd", d_pre, back_expand, preferred_element_type=jnp.float32
    ).reshape(seqs_dev, seq_len, feature)
    _, norm_pull_m = jax.vjp(modulate, middle, shift_m, scale_m)
    d_mid_norm, d_shift_m, d_scale_m = norm_pull_m(d_norm_m)
    d_middle = grad_out + d_mid_norm
    d_branch_a = (gate_a[:, None, :] * d_middle).astype(jnp.bfloat16).reshape(token_count, feature)
    d_gate_a = jnp.sum(d_middle * branch_a, axis=1)
    g_outbiases = jnp.sum(d_branch_a, axis=0, dtype=jnp.float32)
    g_outweight = jnp.einsum("nd,ne->de", attended, d_branch_a, preferred_element_type=jnp.float32)
    d_attended = (
        jnp.einsum("ne,de->nd", d_branch_a, back_out, preferred_element_type=jnp.float32)
        .astype(jnp.bfloat16)
        .reshape(seqs_dev, seq_len, feature)
    )
    pair_query, pair_key, pair_value = lax.map(
        pair_backward, (paired_query, paired_key, paired_value, split_pairs(d_attended), log_totals)
    )
    d_projected = jnp.concatenate(
        [
            join_pairs(pair_query, seqs_dev).reshape(token_count, feature),
            join_pairs(pair_key, seqs_dev).reshape(token_count, feature),
            join_pairs(pair_value, seqs_dev).reshape(token_count, feature),
        ],
        axis=1,
    )
    g_querybias = jnp.sum(d_projected[:, :feature], axis=0, dtype=jnp.float32)
    g_valuebias = jnp.sum(d_projected[:, 2 * feature :], axis=0, dtype=jnp.float32)
    g_projector = jnp.einsum("nd,ne->de", norm_a, d_projected, preferred_element_type=jnp.float32)
    d_norm_a = jnp.einsum(
        "ne,de->nd", d_projected, back_proj, preferred_element_type=jnp.float32
    ).reshape(seqs_dev, seq_len, feature)
    _, norm_pull_a = jax.vjp(modulate, resid_in, shift_a, scale_a)
    d_in_norm, d_shift_a, d_scale_a = norm_pull_a(d_norm_a)
    latents_grad = d_middle + d_in_norm
    mod_partial = jnp.stack(
        [d_shift_a, d_scale_a, d_gate_a, d_shift_m, d_scale_m, d_gate_m], axis=1
    ).reshape(seqs_dev, 6 * feature)
    d_mod = lax.all_gather(mod_partial.astype(jnp.bfloat16), "fsdp", axis=0, tiled=True)
    g_modbias = jnp.sum(
        lax.dynamic_slice_in_dim(d_mod, shard_id * own_bias, own_bias, 1), axis=0, dtype=jnp.float32
    )
    g_modulator = jnp.einsum("sr,sc->rc", cond_act, d_mod, preferred_element_type=jnp.float32)
    d_cond_act = jnp.einsum("sc,rc->sr", d_mod, modulator, preferred_element_type=jnp.float32)
    _, silu_pull = jax.vjp(jax.nn.silu, cond_slice)
    conditions_grad = silu_pull(d_cond_act)[0]
    owned = (
        lax.psum_scatter(g_projector, "fsdp", scatter_dimension=0, tiled=True),
        lax.psum_scatter(g_querybias, "fsdp", scatter_dimension=0, tiled=True),
        lax.psum_scatter(g_valuebias, "fsdp", scatter_dimension=0, tiled=True),
        lax.psum_scatter(g_outweight, "fsdp", scatter_dimension=0, tiled=True),
        lax.psum_scatter(g_outbiases, "fsdp", scatter_dimension=0, tiled=True),
        lax.psum_scatter(g_expander, "fsdp", scatter_dimension=0, tiled=True),
        lax.psum_scatter(g_expandbias, "fsdp", scatter_dimension=0, tiled=True),
        lax.psum_scatter(g_shrinker, "fsdp", scatter_dimension=0, tiled=True),
        lax.psum_scatter(g_shrinkbias, "fsdp", scatter_dimension=0, tiled=True),
    )
    summed = (
        lax.psum(owned[0].astype(jnp.bfloat16), "rep").astype(jnp.float32),
        lax.psum(owned[1].astype(jnp.bfloat16), "rep").astype(jnp.float32),
        lax.psum(owned[2].astype(jnp.bfloat16), "rep").astype(jnp.float32),
        lax.psum(owned[3].astype(jnp.bfloat16), "rep").astype(jnp.float32),
        lax.psum(owned[4].astype(jnp.bfloat16), "rep").astype(jnp.float32),
        lax.psum(owned[5].astype(jnp.bfloat16), "rep").astype(jnp.float32),
        lax.psum(owned[6].astype(jnp.bfloat16), "rep").astype(jnp.float32),
        lax.psum(owned[7].astype(jnp.bfloat16), "rep").astype(jnp.float32),
        lax.psum(owned[8].astype(jnp.bfloat16), "rep").astype(jnp.float32),
        lax.psum(g_modulator.astype(jnp.bfloat16), "rep").astype(jnp.float32),
        lax.psum(g_modbias.astype(jnp.bfloat16), "rep").astype(jnp.float32),
    )
    final_grads = summed[:9]
    ada_sums = summed[9:]
    return (
        layer_out,
        latents_grad,
        conditions_grad,
        ada_sums[0],
        ada_sums[1],
        final_grads[0],
        final_grads[1],
        final_grads[2],
        final_grads[3],
        final_grads[4],
        final_grads[5],
        final_grads[6],
        final_grads[7],
        final_grads[8],
    )


def solution(mesh):
    return jax.shard_map(
        on_device,
        mesh=mesh,
        in_specs=(
            P(("rep", "fsdp"), None, None),
            P("rep", None),
            P("fsdp", None),
            P("fsdp"),
            P("fsdp", None),
            P("fsdp"),
            P("fsdp"),
            P("fsdp", None),
            P("fsdp"),
            P("fsdp", None),
            P("fsdp"),
            P("fsdp", None),
            P("fsdp"),
            P(("rep", "fsdp"), None, None),
        ),
        out_specs=(
            P(("rep", "fsdp"), None, None),
            P(("rep", "fsdp"), None, None),
            P("rep", "fsdp"),
            P("fsdp", None),
            P("fsdp"),
            P("fsdp", None),
            P("fsdp"),
            P("fsdp"),
            P("fsdp", None),
            P("fsdp"),
            P("fsdp", None),
            P("fsdp"),
            P("fsdp", None),
            P("fsdp"),
        ),
        check_vma=False,
    )
```

profile of v0, /device:TPU:0, one launch (start us, length us, event | category | flops | bytes accessed | tf_op | source)
XLA Modules:
  0.0 1593.7 jit_solution(6538860000452444665)
XLA Ops:
  21.3 22.1 %all-gather = bf16[8,1,128]{2,1,0:T(2,128)(2,1)S(1)} all-gather(bf16[1,1,128]{2,1,0:T(2,128)(2,1)S(1)} %bitcast.275), channel_id=1, replica_groups=mesh['rep'=4,'fsdp'=8] {'fsdp'}, dimensions={0}, use_global_device_ids=true | all-gather | bytes 2304 | tf_op jit(solution)/shard_map/all_gather | solution.py:128
  43.4 16.2 %all-gather.1 = bf16[8,1,128]{2,1,0:T(2,128)(2,1)S(1)} all-gather(bf16[1,1,128]{2,1,0:T(2,128)(2,1)S(1)} %bitcast.276), channel_id=1, replica_groups=mesh['rep'=4,'fsdp'=8] {'fsdp'}, dimensions={0}, use_global_device_ids=true | all-gather | bytes 2304 | tf_op jit(solution)/shard_map/all_gather | solution.py:127
  59.6 18.2 %all-gather.2 = bf16[8,1,128]{2,1,0:T(2,128)(2,1)S(1)} all-gather(bf16[1,1,128]{2,1,0:T(2,128)(2,1)S(1)} %bitcast.277), channel_id=1, replica_groups=mesh['rep'=4,'fsdp'=8] {'fsdp'}, dimensions={0}, use_global_device_ids=true | all-gather | bytes 2304 | tf_op jit(solution)/shard_map/all_gather | solution.py:130
  77.8 26.4 %all-gather.3 = bf16[8,1,512]{2,1,0:T(2,128)(2,1)S(1)} all-gather(bf16[1,1,512]{2,1,0:T(2,128)(2,1)S(1)} %reshape.386), channel_id=1, replica_groups=mesh['rep'=4,'fsdp'=8] {'fsdp'}, dimensions={0}, use_global_device_ids=true | all-gather | bytes 9216 | tf_op jit(solution)/shard_map/all_gather | solution.py:159
  110.5 74.7 %all-gather.11.cloned.1.call-done = bf16[1024,3072]{1,0:T(8,128)(2,1)} async-done(((bf16[128,3072]{1,0:T(8,128)(2,1)}), bf16[1024,3072]{1,0:T(8,128)(2,1)}) %all-gather.11.cloned.1.call-update) | async-done | bytes 6291472 | tf_op jit(solution)/shard_map/all_gather | solution.py:126
  185.3 9.9 fusion.71
  213.6 58.4 %while.26 = (s32[]{:T(128)}, bf16[8,1024,128]{1,2,0:T(8,128)(2,1)}, f32[8,2,1024]{2,1,0:T(2,128)S(1)}, bf16[8,1024,128]{1,2,0:T(8,128)(2,1)}, bf16[8,1024,128]{1...) while((s32[]{:T(128)}, bf16[8,1024,128]{1,2,0:T(8,128)(2,1)}, f32[8,2,1024]{2,1,0:T(2,128)S(1)}, ...), condition=%wide.region_6.7_spmd, body=%wide.region_3.6_spmd.sunk | while | flops 555874304 | bytes 28377688 | solution.py:151
  272.1 7.9 fusion.79
  282.5 78.5 %all-gather.15.cloned.1.call-done = bf16[1024,4096]{1,0:T(8,128)(2,1)} async-done(((bf16[128,4096]{1,0:T(8,128)(2,1)}), bf16[1024,4096]{1,0:T(8,128)(2,1)}) %all-gather.15.cloned.1.call-update) | async-done | bytes 8388624 | tf_op jit(solution)/shard_map/all_gather | solution.py:158
  361.0 22.2 %multiply_convert_fusion.1 = (bf16[1024,4096]{1,0:T(8,128)(2,1)}, f32[1024,4096]{1,0:T(8,128)}) fusion(f32[4096]{0:T(1024)S(1)} %bitcast.264, bf16[1024,4096]{1,0:T(8,128)(2,1)} %all-gather.15.cloned.1.call-done, f32[1,1024,1024]{1,2,0:T(8,128)} %copy-done.2, f32[1024]{0:T(1024)S(1)} %bitcast.268, f32[1024]{0:T(1024)S(1)} %bitcast.247, ...), kind=kOutput, calls=%fused_computation.41 | convolution fusion | flops 8637120512 | bytes 37781504 | tf_op jit(solution)/shard_map/dot_general | solution.py:164
  383.2 103.2 %all-gather.17.cloned.1.call-done = bf16[4096,1024]{1,0:T(8,128)(2,1)} async-done(((bf16[512,1024]{1,0:T(8,128)(2,1)}), bf16[4096,1024]{1,0:T(8,128)(2,1)}) %all-gather.17.cloned.1.call-update) | async-done | bytes 8388624 | tf_op jit(solution)/shard_map/all_gather | solution.py:160
  486.4 27.5 %convert_reduce_fusion = (f32[4096]{0:T(1024)}, bf16[1024,4096]{1,0:T(8,128)(2,1)}) fusion(f32[1024,4096]{1,0:T(8,128)} %get-tuple-element.222, f32[4096]{0:T(1024)S(1)} %bitcast.265, bf16[4096,1024]{1,0:T(8,128)(2,1)} %all-gather.17.cloned.1.call-done, bf16[1,1024,1024]{1,2,0:T(8,128)(2,1)} %copy.69, f32[1024]{0:T(1024)S(1)} %bitcast.256), kind=kOutput, calls=%fused_computation.40 | convolution fusion | flops 8689545216 | bytes 35688448 | tf_op jit(solution)/shard_map/nd,fd->nf/dot_general | solution.py:184
  513.9 15.9 fusion.82
  535.1 5.4 fusion.35
  546.6 6.0 fusion.84
  552.7 5.9 convolution_convert_fusion.1
  563.4 121.5 %while.27 = (s32[]{:T(128)}, bf16[8,1024,128]{1,2,0:T(8,128)(2,1)}, bf16[8,1024,128]{1,2,0:T(8,128)(2,1)}, bf16[8,1024,128]{1,2,0:T(8,128)(2,1)}, bf16[8,1024,12...) while((s32[]{:T(128)}, bf16[8,1024,128]{1,2,0:T(8,128)(2,1)}, ...), condition=%wide.region_13.14_spmd, body=%wide.region_11.13_spmd.sunk | while | flops 1367996416 | bytes 69264504 | solution.py:204
  684.9 14.8 fusion.38
  700.4 17.0 %fusion.73 = f32[1024,4096]{1,0:T(8,128)} fusion(bf16[1024,4096]{1,0:T(8,128)(2,1)} %get-tuple-element.228, f32[1,1024,1024]{1,2,0:T(8,128)} %copy-done.2, f32[1024]{0:T(1024)S(1)} %bitcast.269, f32[1024]{0:T(1024)S(1)} %bitcast.250, f32[1024]{0:T(1024)S(1)} %fusion.59, f32[1024]{0:T(1024)S(1)} %broadcast_multiply_fusion), kind=kOutput, calls=%fused_computation.134 | convolution fusion | flops 8595177472 | bytes 29376512 | tf_op jit(solution)/shard_map/nd,nf->df/dot_general | solution.py:188
  718.0 16.7 %fusion.64 = f32[4096,1024]{1,0:T(8,128)} fusion(bf16[1024,4096]{1,0:T(8,128)(2,1)} %get-tuple-element.221, bf16[1,1024,1024]{1,2,0:T(8,128)(2,1)} %copy.69, f32[1024]{0:T(1024)S(1)} %bitcast.258), kind=kOutput, calls=%fused_computation.131 | convolution fusion | flops 8593080320 | bytes 27267072 | tf_op jit(solution)/shard_map/nf,nd->fd/dot_general | solution.py:183
  735.4 18.4 %all-gather.4 = bf16[8,1,128]{2,1,0:T(2,128)(2,1)S(1)} all-gather(bf16[1,1,128]{2,1,0:T(2,128)(2,1)S(1)} %bitcast.278), channel_id=1, replica_groups=mesh['rep'=4,'fsdp'=8] {'fsdp'}, dimensions={0}, use_global_device_ids=true | all-gather | bytes 2304 | tf_op jit(solution)/shard_map/all_gather | solution.py:161
  753.8 12.6 fusion.81
  778.7 22.2 %fusion.32 = (bf16[1024]{0:T(1024)(128)(2,1)S(1)}, bf16[1024]{0:T(1024)(128)(2,1)S(1)}, f32[1,1024,1024]{1,2,0:T(8,128)}, f32[1,1024,1024]{1,2,0:T(8,128)}) fusion(bf16[1,1024,1024]{1,2,0:T(8,128)(2,1)} %copy.69, f32[1024]{0:T(1024)S(1)} %bitcast.274, f32[1024,1024]{0,1:T(8,128)} %get-tuple-element.220, f32[1024]{0:T(1024)S(1)} %bitcast.273, ...), kind=kOutput, calls=%fused_computation.65 | convolution fusion | flops 8610904064 | bytes 46178304 | tf_op jit(solution)/shard_map/dot_general | solution.py:170
  801.1 31.6 %all-gather.5 = bf16[8,1,6144]{2,1,0:T(2,128)(2,1)S(1)} all-gather(bf16[1,1,6144]{2,1,0:T(2,128)(2,1)S(1)} %reshape.390), channel_id=1, replica_groups=mesh['rep'=4,'fsdp'=8] {'fsdp'}, dimensions={0}, use_global_device_ids=true | all-gather | bytes 110592 | tf_op jit(solution)/shard_map/all_gather | solution.py:227
  836.9 72.1 %reduce-scatter.5.cloned.1.call-done = f32[128,3072]{1,0:T(8,128)} async-done(((f32[1024,3072]{1,0:T(8,128)}), f32[128,3072]{1,0:T(8,128)}) %reduce-scatter.5.cloned.1.call-update) | async-done | bytes 1572880 | tf_op jit(solution)/shard_map/reduce_scatter | solution.py:236
  911.4 282.6 %reduce-scatter.9.cloned.1.call-done = f32[128,4096]{1,0:T(8,128)} async-done(((f32[1024,4096]{1,0:T(8,128)}), f32[128,4096]{1,0:T(8,128)}) %reduce-scatter.9.cloned.1.call-update) | async-done | bytes 2097168 | tf_op jit(solution)/shard_map/reduce_scatter | solution.py:241
  1196.7 283.3 %reduce-scatter.11.cloned.1.call-done = f32[512,1024]{1,0:T(8,128)} async-done(((f32[4096,1024]{1,0:T(8,128)}), f32[512,1024]{1,0:T(8,128)}) %reduce-scatter.11.cloned.1.call-update) | async-done | bytes 2097168 | tf_op jit(solution)/shard_map/reduce_scatter | solution.py:243
  1487.0 35.2 %all-reduce.6 = (bf16[1024]{0:T(1024)(128)(2,1)S(1)}, bf16[1024]{0:T(1024)(128)(2,1)S(1)}, bf16[1024]{0:T(1024)(128)(2,1)S(1)}, bf16[4096]{0:T(1024)(128)(2,1)S(1)}, bf16[1024]{0:T(1024)(128)(2,1)S(1)}) all-reduce(f32[1024]{0:T(1024)S(1)} %bitcast.267, f32[1024]{0:T(1024)S(1)} %bitcast.266, ...), channel_id=4, replica_groups=mesh['rep'=4,'fsdp'=8] {'fsdp'}, use_global_device_ids=true, to_apply=%region_28.29.clone | all-reduce | flops 8192 | bytes 49152
  1522.6 6.5 all-reduce.7
  1532.3 5.4 copy.74
  1537.8 5.6 copy.75
  1545.1 32.7 %all-reduce.14.cloned.1.call-done = (bf16[128,6144]{1,0:T(8,128)(2,1)}, bf16[128,3072]{1,0:T(8,128)(2,1)}, bf16[128,1024]{1,0:T(8,128)(2,1)}, bf16[128,4096]{1,0:T(8,128)(2,1)}, bf16[512,1024]{1,0:T(8,128)(2,1)}) async-done(((bf16[128,6144]{1,0:T(8,128)(2,1)}, bf16[128,3072]{1,0:T(8,128)(2,1)}, bf16[128,1024]{1,0:T(8,128)(2,1)}, bf16[128,4096]{1,0:T(8,128)(2,1)}, bf16[512,1024]{1,0:T(8,128)(2,1)}), ...) | async-done | bytes 4718608 | tf_op jit(solution)/shard_map/psum | solution.py:256
  (341 shorter events, 279.7 us)
Async XLA Ops:
  7.2 101.6 %all-reduce.12.cloned.1.call-start = ((), (), s32[]{:S(2)}) async-start(), calls=%async_computation.12 | async-start | bytes 393216
  10.3 174.9 %all-gather.11.cloned.1.call-start = ((), (), s32[]{:S(2)}) async-start(), calls=%async_computation.4 | async-start | bytes 7077888 | tf_op jit(solution)/shard_map/all_gather | solution.py:126
  11.1 261.0 %all-gather.13.cloned.1.call-start = ((), (), s32[]{:S(2)}) async-start(), calls=%async_computation.5 | async-start | bytes 2359296 | tf_op jit(solution)/shard_map/all_gather | solution.py:129
  11.8 349.2 %all-gather.15.cloned.1.call-start = ((), (), s32[]{:S(2)}) async-start(), calls=%async_computation.6 | async-start | bytes 9437184 | tf_op jit(solution)/shard_map/all_gather | solution.py:158
  12.4 474.0 %all-gather.17.cloned.1.call-start = ((), (), s32[]{:S(2)}) async-start(), calls=%async_computation.7 | async-start | bytes 9437184 | tf_op jit(solution)/shard_map/all_gather | solution.py:160
  13.0 822.2 %reduce-scatter.7.cloned.1.call-start = ((), (), s32[]{:S(2)}) async-start(), calls=%async_computation.9 | async-start | bytes 4718592 | tf_op jit(solution)/shard_map/reduce_scatter | solution.py:239
  13.0 8.3 copy-start.37
  13.0 30.3 %copy-start.38 = (bf16[128]{0:T(256)(128)(2,1)S(1)}, bf16[128]{0:T(256)(128)(2,1)}, u32[]{:S(2)}) copy-start(bf16[128]{0:T(256)(128)(2,1)} %param.23) | copy-start | bytes 772
  13.1 46.5 %copy-start.39 = (bf16[128]{0:T(256)(128)(2,1)S(1)}, bf16[128]{0:T(256)(128)(2,1)}, u32[]{:S(2)}) copy-start(bf16[128]{0:T(256)(128)(2,1)} %param.26) | copy-start | bytes 772
  13.1 64.7 %copy-start.36 = (bf16[512]{0:T(512)(128)(2,1)S(1)}, bf16[512]{0:T(512)(128)(2,1)}, u32[]{:S(2)}) copy-start(bf16[512]{0:T(512)(128)(2,1)} %param.28) | copy-start | bytes 3076
  17.0 91.2 %copy-start.41 = (u32[32]{0:T(128)S(1)}, u32[32]{0:T(128)}, u32[]{:S(2)}) copy-start(u32[32]{0:T(128)} %constant.97) | copy-start | bytes 388
  19.0 176.2 %copy-start.13 = (f32[1024]{0:T(1024)}, f32[1024]{0:T(1024)S(1)}, u32[]{:S(2)}) copy-start(f32[1024]{0:T(1024)S(1)} %broadcast_multiply_fusion.1) | copy-start | bytes 12292
  21.3 56.5 %copy-start.17 = (f32[1024]{0:T(1024)}, f32[1024]{0:T(1024)S(1)}, u32[]{:S(2)}) copy-start(f32[1024]{0:T(1024)S(1)} %fusion.29) | copy-start | bytes 12292
  21.3 173.9 %copy-start.15 = (f32[1024]{0:T(1024)}, f32[1024]{0:T(1024)S(1)}, u32[]{:S(2)}) copy-start(f32[1024]{0:T(1024)S(1)} %fusion.58) | copy-start | bytes 12292
  77.8 194.3 %copy-start.33 = (f32[8,1,128]{2,1,0:T(1,128)}, f32[8,1,128]{2,1,0:T(1,128)S(1)}, u32[]{:S(2)}) copy-start(f32[8,1,128]{2,1,0:T(1,128)S(1)} %convert_element_type.273) | copy-start | bytes 12292
  110.5 84.7 %copy-start.19 = (f32[1,1,1024]{2,1,0:T(1,128)}, f32[1,1,1024]{2,1,0:T(1,128)S(1)}, u32[]{:S(2)}) copy-start(f32[1,1,1024]{2,1,0:T(1,128)S(1)} %get-tuple-element.218) | copy-start | bytes 12292
  110.5 84.7 %copy-start.31 = (f32[1,1,1024]{2,1,0:T(1,128)}, f32[1,1,1024]{2,1,0:T(1,128)S(1)}, u32[]{:S(2)}) copy-start(f32[1,1,1024]{2,1,0:T(1,128)S(1)} %get-tuple-element.217) | copy-start | bytes 12292
  110.5 250.5 %copy-start.29 = (f32[1,1,1024]{2,1,0:T(1,128)}, f32[1,1,1024]{2,1,0:T(1,128)S(1)}, u32[]{:S(2)}) copy-start(f32[1,1,1024]{2,1,0:T(1,128)S(1)} %get-tuple-element.215) | copy-start | bytes 12292
  110.5 431.6 %copy-start.21 = (f32[1,1,1024]{2,1,0:T(1,128)}, f32[1,1,1024]{2,1,0:T(1,128)S(1)}, u32[]{:S(2)}) copy-start(f32[1,1,1024]{2,1,0:T(1,128)S(1)} %get-tuple-element.214) | copy-start | bytes 12292
  535.1 5.4 copy-start.3
  535.1 5.9 copy-start.4
  552.6 356.4 %reduce-scatter.5.cloned.1.call-start = ((), (), s32[]{:S(2)}) async-start(), calls=%async_computation.8 | async-start | bytes 14155776 | tf_op jit(solution)/shard_map/reduce_scatter | solution.py:236
  563.4 121.5 %copy-start.14 = (f32[1024]{0:T(1024)S(1)}, f32[1024]{0:T(1024)}, u32[]{:S(2)}) copy-start(f32[1024]{0:T(1024)} %copy-done.13) | copy-start | bytes 12292
  563.4 121.5 %copy-start.16 = (f32[1024]{0:T(1024)S(1)}, f32[1024]{0:T(1024)}, u32[]{:S(2)}) copy-start(f32[1024]{0:T(1024)} %copy-done.15) | copy-start | bytes 12292
  563.4 121.5 %copy-start.20 = (f32[1,1,1024]{2,1,0:T(1,128)S(1)}, f32[1,1,1024]{2,1,0:T(1,128)}, u32[]{:S(2)}) copy-start(f32[1,1,1024]{2,1,0:T(1,128)} %copy-done.19) | copy-start | bytes 12292
  563.4 121.5 %copy-start.32 = (f32[1,1,1024]{2,1,0:T(1,128)S(1)}, f32[1,1,1024]{2,1,0:T(1,128)}, u32[]{:S(2)}) copy-start(f32[1,1,1024]{2,1,0:T(1,128)} %copy-done.31) | copy-start | bytes 12292
  699.7 494.3 %reduce-scatter.9.cloned.1.call-start = ((), (), s32[]{:S(2)}) async-start(), calls=%async_computation.10 | async-start | bytes 18874368 | tf_op jit(solution)/shard_map/reduce_scatter | solution.py:241
  717.4 762.6 %reduce-scatter.11.cloned.1.call-start = ((), (), s32[]{:S(2)}) async-start(), calls=%async_computation.11 | async-start | bytes 18874368 | tf_op jit(solution)/shard_map/reduce_scatter | solution.py:243
  734.7 843.1 %all-reduce.14.cloned.1.call-start = ((), (), s32[]{:S(2)}) async-start(), calls=%async_computation.13 | async-start | bytes 9437184 | tf_op jit(solution)/shard_map/psum | solution.py:256
  778.7 22.3 %copy-start.28 = (bf16[1024]{0:T(1024)(128)(2,1)S(1)}, bf16[1024]{0:T(1024)(128)(2,1)}, u32[]{:S(2)}) copy-start(bf16[1024]{0:T(1024)(128)(2,1)} %get-tuple-element.143) | copy-start | bytes 6148
  778.7 22.3 %copy-start.35 = (bf16[1024]{0:T(1024)(128)(2,1)S(1)}, bf16[1024]{0:T(1024)(128)(2,1)}, u32[]{:S(2)}) copy-start(bf16[1024]{0:T(1024)(128)(2,1)} %get-tuple-element.225) | copy-start | bytes 6148
  1577.8 5.1 copy-start.9
  (20 other events, 56.9 us)
Sparse Core Ops, SparseCore 0:
  11.9 72.7 all-reduce.11
  87.1 98.0 all-gather.10
  187.6 47.6 all-gather.12
  237.5 123.4 all-gather.14
  363.2 123.1 all-gather.16
  552.7 86.2 reduce-scatter.6
  699.8 209.0 reduce-scatter.4
  912.7 281.2 reduce-scatter.8
  1198.3 281.7 reduce-scatter.10
  1483.7 94.0 all-reduce.13
where the time goes:
time: 1600 us; the launch traced here: 1590 us
  waiting for transfers between devices  930 us (58%)
  matrix products  266 us (17%)
  blocking collectives  175 us (11%)
  local copies, waits for them, and re-layouts  126 us (8%)
  other arithmetic  79.7 us (5%)
  between operations  16.2 us (1%)
    reduce_scatter x1, waiting for transfers between devices, on_device(): lax.psum_scatter(g_shrinker, 'fsdp', scatter_dimension=0, tiled=True)  283 us
    reduce_scatter x1, waiting for transfers between devices, on_device(): lax.psum_scatter(g_expander, 'fsdp', scatter_dimension=0, tiled=True)  283 us
    all_gather x1, waiting for transfers between devices, on_device(): lax.all_gather(shrinker, 'fsdp', axis=0, tiled=True)  103 us
    all_gather x1, waiting for transfers between devices, on_device(): lax.all_gather(expander, 'fsdp', axis=0, tiled=True)  78.5 us
    all_gather x1, waiting for transfers between devices, on_device(): lax.all_gather(projector, 'fsdp', axis=0, tiled=True)  74.7 us
    reduce_scatter x1, waiting for transfers between devices, on_device(): lax.psum_scatter(g_projector, 'fsdp', scatter_dimension=0, tiled=True)  72.1 us
    dynamic_slice x48, local copies, waits for them, and re-layouts, on_device(): lax.map(pair_forward, (paired_query, paired_key, paired_value))  47.6 us
    unnamed x1, blocking collectives  35.2 us
  transfers between devices with their start and end apart: 10, of which 7 were waited for; matrix products, arithmetic and copies ran while one was open for 24% of the time, Pallas kernels for 0%

commit v1 on v0

v1 whole, which is shorter than its diff:
```python
from functools import partial

import jax
import jax.numpy as jnp
from jax import lax
from jax.sharding import PartitionSpec as P

HEADS = 16
HEAD_DIM = 64


EPS_NORM = 1e-06


def normalize(values):
    average = jnp.mean(values, axis=-1, keepdims=True)
    centred = values - average
    variance = jnp.mean(centred * centred, axis=-1, keepdims=True)
    return centred * lax.rsqrt(variance + EPS_NORM)


def modulate(values, shifts, scales):
    return normalize(values) * (1.0 + scales[:, None, :]) + shifts[:, None, :]


def split_pairs(stacked):
    blocks, length, feature = stacked.shape
    grouped = stacked.reshape(blocks, length, HEADS // 2, 2 * HEAD_DIM).transpose(0, 2, 1, 3)
    return grouped.reshape(blocks * (HEADS // 2), length, 2 * HEAD_DIM)


def join_pairs(paired, blocks):
    length = paired.shape[1]
    grouped = paired.reshape(blocks, HEADS // 2, length, 2 * HEAD_DIM).transpose(0, 2, 1, 3)
    return grouped.reshape(blocks, length, HEADS * HEAD_DIM)


def pair_scores(query_pair, key_pair):
    length = query_pair.shape[0]
    query_heads = query_pair.reshape(length, 2, HEAD_DIM)
    key_heads = key_pair.reshape(length, 2, HEAD_DIM)
    scores = jnp.einsum("qhd,khd->hqk", query_heads, key_heads, preferred_element_type=jnp.float32)
    return (scores * HEAD_DIM ** (-0.5), query_heads, key_heads)


def pair_forward(operands):
    query_pair, key_pair, value_pair = operands
    length = query_pair.shape[0]
    scores, _, _ = pair_scores(query_pair, key_pair)
    value_heads = value_pair.reshape(length, 2, HEAD_DIM)
    top_score = jnp.max(scores, axis=-1, keepdims=True)
    exp_terms = jnp.exp(scores - top_score)
    denominator = jnp.sum(exp_terms, axis=-1, keepdims=True)
    attn_probs = (exp_terms / denominator).astype(jnp.bfloat16)
    attended = jnp.einsum(
        "hqk,khd->qhd", attn_probs, value_heads, preferred_element_type=jnp.float32
    )
    log_total = (top_score + jnp.log(denominator))[:, :, 0]
    return (attended.reshape(length, 2 * HEAD_DIM).astype(jnp.bfloat16), log_total)


def pair_backward(operands):
    query_pair, key_pair, value_pair, grad_pair, log_total = operands
    length = query_pair.shape[0]
    scores, query_heads, key_heads = pair_scores(query_pair, key_pair)
    value_heads = value_pair.reshape(length, 2, HEAD_DIM)
    grad_heads = grad_pair.reshape(length, 2, HEAD_DIM)
    probs_full = jnp.exp(scores - log_total[:, :, None])
    probs_low = probs_full.astype(jnp.bfloat16)
    d_value = jnp.einsum("hqk,qhd->khd", probs_low, grad_heads, preferred_element_type=jnp.float32)
    d_probs = jnp.einsum(
        "qhd,khd->hqk", grad_heads, value_heads, preferred_element_type=jnp.float32
    )
    row_sum = jnp.sum(probs_full * d_probs, axis=-1, keepdims=True)
    d_scores = (probs_full * (d_probs - row_sum)).astype(jnp.bfloat16)
    d_query = jnp.einsum(
        "hqk,khd->qhd", d_scores, key_heads, preferred_element_type=jnp.float32
    ) * HEAD_DIM ** (-0.5)
    d_key = jnp.einsum(
        "hqk,qhd->khd", d_scores, query_heads, preferred_element_type=jnp.float32
    ) * HEAD_DIM ** (-0.5)
    return (
        d_query.reshape(length, 2 * HEAD_DIM).astype(jnp.bfloat16),
        d_key.reshape(length, 2 * HEAD_DIM).astype(jnp.bfloat16),
        d_value.reshape(length, 2 * HEAD_DIM).astype(jnp.bfloat16),
    )


def gather_rows(weight):
    part = weight.shape[0] // lax.axis_size("rep")
    own = lax.dynamic_slice_in_dim(weight, lax.axis_index("rep") * part, part, 0)
    return lax.all_gather(own, ("fsdp", "rep"), axis=0, tiled=True)


def scatter_rows(grad):
    own = lax.psum_scatter(
        grad.astype(jnp.bfloat16), ("fsdp", "rep"), scatter_dimension=0, tiled=True
    )
    return lax.all_gather(own, "rep", axis=0, tiled=True).astype(jnp.float32)


def on_device(
    latents,
    conditions,
    modulator,
    modulbias,
    projector,
    querybias,
    valuebias,
    outweight,
    outbiases,
    expander,
    expandbias,
    shrinker,
    shrinkbias,
    upstream,
):
    seqs_dev, seq_len, feature = latents.shape
    token_count = seqs_dev * seq_len
    shard_id = lax.axis_index("fsdp")
    shards = lax.axis_size("fsdp")
    own_rows = modulator.shape[0]
    own_bias = modulbias.shape[0]
    cond_full = conditions.astype(jnp.float32)
    cond_slice = lax.dynamic_slice_in_dim(cond_full, shard_id * own_rows, own_rows, 1)
    cond_act = jax.nn.silu(cond_slice).astype(jnp.bfloat16)
    mod_term = jnp.dot(cond_act, modulator, preferred_element_type=jnp.float32)
    bias_parts = (modulbias, querybias, valuebias, outbiases, expandbias, shrinkbias)
    own_biases = jnp.concatenate([part.astype(jnp.float32) for part in bias_parts])
    mod_width = seqs_dev * 6 * feature
    sent = jnp.concatenate(
        [
            mod_term.reshape(shards, mod_width),
            jnp.broadcast_to(own_biases[None, :], (shards, own_biases.shape[0])),
        ],
        axis=1,
    )
    got = lax.all_to_all(sent, "fsdp", split_axis=0, concat_axis=0, tiled=True)
    full_biases = []
    start = mod_width
    for part in bias_parts:
        full_biases.append(got[:, start : start + part.shape[0]].reshape(-1))
        start += part.shape[0]
    full_modbias, b_query, b_value, b_out, b_expand, b_shrink = full_biases
    modvals = jnp.sum(got[:, :mod_width], axis=0).reshape(seqs_dev, 6, feature) + full_modbias.reshape(
        1, 6, feature
    )
    shift_a, scale_a, gate_a = (modvals[:, 0], modvals[:, 1], modvals[:, 2])
    shift_m, scale_m, gate_m = (modvals[:, 3], modvals[:, 4], modvals[:, 5])
    w_proj = gather_rows(projector)
    w_out = gather_rows(outweight)
    w_expand = gather_rows(expander)
    w_shrink = gather_rows(shrinker)
    resid_in = latents.astype(jnp.float32)
    norm_a = modulate(resid_in, shift_a, scale_a).astype(jnp.bfloat16).reshape(token_count, feature)
    projected = jnp.dot(norm_a, w_proj, preferred_element_type=jnp.float32)
    queries = (
        (projected[:, :feature] + b_query)
        .astype(jnp.bfloat16)
        .reshape(seqs_dev, seq_len, feature)
    )
    key_rows = (
        projected[:, feature : 2 * feature].astype(jnp.bfloat16).reshape(seqs_dev, seq_len, feature)
    )
    values = (
        (projected[:, 2 * feature :] + b_value)
        .astype(jnp.bfloat16)
        .reshape(seqs_dev, seq_len, feature)
    )
    paired_query = split_pairs(queries)
    paired_key = split_pairs(key_rows)
    paired_value = split_pairs(values)
    attended_pairs, log_totals = lax.map(pair_forward, (paired_query, paired_key, paired_value))
    attended = join_pairs(attended_pairs, seqs_dev).reshape(token_count, feature)
    branch_a = (
        jnp.dot(attended, w_out, preferred_element_type=jnp.float32) + b_out
    ).reshape(seqs_dev, seq_len, feature)
    middle = resid_in + gate_a[:, None, :] * branch_a
    norm_m = modulate(middle, shift_m, scale_m).astype(jnp.bfloat16).reshape(token_count, feature)
    pre_act = jnp.dot(norm_m, w_expand, preferred_element_type=jnp.float32) + b_expand
    gelu_fn = partial(jax.nn.gelu, approximate=True)
    hidden = gelu_fn(pre_act).astype(jnp.bfloat16)
    branch_m = (
        jnp.dot(hidden, w_shrink, preferred_element_type=jnp.float32) + b_shrink
    ).reshape(seqs_dev, seq_len, feature)
    layer_out = middle + gate_m[:, None, :] * branch_m
    grad_out = upstream.astype(jnp.float32)
    d_branch_m = (gate_m[:, None, :] * grad_out).astype(jnp.bfloat16).reshape(token_count, feature)
    d_gate_m = jnp.sum(grad_out * branch_m, axis=1)
    g_shrinkbias = jnp.sum(d_branch_m, axis=0, dtype=jnp.float32)
    g_shrinker = scatter_rows(
        jnp.einsum("nf,nd->fd", hidden, d_branch_m, preferred_element_type=jnp.float32)
    )
    d_hidden = jnp.einsum("nd,fd->nf", d_branch_m, w_shrink, preferred_element_type=jnp.float32)
    _, gelu_pull = jax.vjp(gelu_fn, pre_act)
    d_pre = gelu_pull(d_hidden)[0].astype(jnp.bfloat16)
    g_expandbias = jnp.sum(d_pre, axis=0, dtype=jnp.float32)
    g_expander = scatter_rows(
        jnp.einsum("nd,nf->df", norm_m, d_pre, preferred_element_type=jnp.float32)
    )
    d_norm_m = jnp.einsum(
        "nf,df->nd", d_pre, w_expand, preferred_element_type=jnp.float32
    ).reshape(seqs_dev, seq_len, feature)
    _, norm_pull_m = jax.vjp(modulate, middle, shift_m, scale_m)
    d_mid_norm, d_shift_m, d_scale_m = norm_pull_m(d_norm_m)
    d_middle = grad_out + d_mid_norm
    d_branch_a = (gate_a[:, None, :] * d_middle).astype(jnp.bfloat16).reshape(token_count, feature)
    d_gate_a = jnp.sum(d_middle * branch_a, axis=1)
    g_outbiases = jnp.sum(d_branch_a, axis=0, dtype=jnp.float32)
    g_outweight = scatter_rows(
        jnp.einsum("nd,ne->de", attended, d_branch_a, preferred_element_type=jnp.float32)
    )
    d_attended = (
        jnp.einsum("ne,de->nd", d_branch_a, w_out, preferred_element_type=jnp.float32)
        .astype(jnp.bfloat16)
        .reshape(seqs_dev, seq_len, feature)
    )
    pair_query, pair_key, pair_value = lax.map(
        pair_backward, (paired_query, paired_key, paired_value, split_pairs(d_attended), log_totals)
    )
    d_projected = jnp.concatenate(
        [
            join_pairs(pair_query, seqs_dev).reshape(token_count, feature),
            join_pairs(pair_key, seqs_dev).reshape(token_count, feature),
            join_pairs(pair_value, seqs_dev).reshape(token_count, feature),
        ],
        axis=1,
    )
    g_querybias = jnp.sum(d_projected[:, :feature], axis=0, dtype=jnp.float32)
    g_valuebias = jnp.sum(d_projected[:, 2 * feature :], axis=0, dtype=jnp.float32)
    g_projector = scatter_rows(
        jnp.einsum("nd,ne->de", norm_a, d_projected, preferred_element_type=jnp.float32)
    )
    d_norm_a = jnp.einsum(
        "ne,de->nd", d_projected, w_proj, preferred_element_type=jnp.float32
    ).reshape(seqs_dev, seq_len, feature)
    _, norm_pull_a = jax.vjp(modulate, resid_in, shift_a, scale_a)
    d_in_norm, d_shift_a, d_scale_a = norm_pull_a(d_norm_a)
    latents_grad = d_middle + d_in_norm
    mod_partial = jnp.stack(
        [d_shift_a, d_scale_a, d_gate_a, d_shift_m, d_scale_m, d_gate_m], axis=1
    ).reshape(seqs_dev, 6 * feature)
    bias_sums = (g_querybias, g_valuebias, g_outbiases, g_expandbias, g_shrinkbias)
    small = jnp.concatenate(
        [mod_partial.astype(jnp.bfloat16).reshape(-1), cond_act.reshape(-1)]
        + [part.astype(jnp.bfloat16) for part in bias_sums]
    )
    gathered = lax.all_gather(small, ("rep", "fsdp"), axis=0, tiled=False)
    devices = gathered.shape[0]
    reps = devices // shards
    d_mod = gathered[:, :mod_width].reshape(devices * seqs_dev, 6 * feature)
    group = shards * seqs_dev
    cond_size = cond_act.shape[0] * own_rows
    cond_all = gathered[:, mod_width : mod_width + cond_size].reshape(reps, shards, cond_size)
    cond_all = lax.dynamic_index_in_dim(cond_all, shard_id, 1, keepdims=False)
    cond_all = cond_all.reshape(reps * cond_act.shape[0], own_rows)
    start = mod_width + cond_size
    bias_grads = []
    for part in bias_sums:
        width = part.shape[0] // shards
        own = lax.dynamic_slice_in_dim(gathered, start + shard_id * width, width, 1)
        bias_grads.append(jnp.sum(own, axis=0, dtype=jnp.float32))
        start += part.shape[0]
    g_modbias = jnp.sum(
        lax.dynamic_slice_in_dim(d_mod, shard_id * own_bias, own_bias, 1), axis=0, dtype=jnp.float32
    )
    g_modulator = jnp.einsum("sr,sc->rc", cond_all, d_mod, preferred_element_type=jnp.float32)
    own_mod = lax.dynamic_slice_in_dim(d_mod, lax.axis_index("rep") * group, group, 0)
    d_cond_act = jnp.einsum("sc,rc->sr", own_mod, modulator, preferred_element_type=jnp.float32)
    _, silu_pull = jax.vjp(jax.nn.silu, cond_slice)
    conditions_grad = silu_pull(d_cond_act)[0]
    return (
        layer_out,
        latents_grad,
        conditions_grad,
        g_modulator,
        g_modbias,
        g_projector,
        bias_grads[0],
        bias_grads[1],
        g_outweight,
        bias_grads[2],
        g_expander,
        bias_grads[3],
        g_shrinker,
        bias_grads[4],
    )


def solution(mesh):
    return jax.shard_map(
        on_device,
        mesh=mesh,
        in_specs=(
            P(("rep", "fsdp"), None, None),
            P("rep", None),
            P("fsdp", None),
            P("fsdp"),
            P("fsdp", None),
            P("fsdp"),
            P("fsdp"),
            P("fsdp", None),
            P("fsdp"),
            P("fsdp", None),
            P("fsdp"),
            P("fsdp", None),
            P("fsdp"),
            P(("rep", "fsdp"), None, None),
        ),
        out_specs=(
            P(("rep", "fsdp"), None, None),
            P(("rep", "fsdp"), None, None),
            P("rep", "fsdp"),
            P("fsdp", None),
            P("fsdp"),
            P("fsdp", None),
            P("fsdp"),
            P("fsdp"),
            P("fsdp", None),
            P("fsdp"),
            P("fsdp", None),
            P("fsdp"),
            P("fsdp", None),
            P("fsdp"),
        ),
        check_vma=False,
    )
```

time: 1600 us -> 950 us (0.59)
  waiting for transfers between devices: 930 us -> 356 us
  blocking collectives: 175 us -> 86.1 us
    reduce_scatter x4, waiting for transfers between devices: 638 us -> 196 us  [scatter_rows(): lax.psum_scatter(grad.astype(jnp.bfloat16), ('fsdp', 'rep'), scatter_dime...]
    all_gather x4 -> x6, waiting for transfers between devices: 256 us -> 160 us  [the longest x4 137 us: gather_rows(): return lax.all_gather(own, ('fsdp', 'rep'), axis=0, tiled=True)]
    all_gather x6 -> x3, blocking collectives: 133 us -> 86.1 us  [the longest x1 71.3 us: on_device(): gathered = lax.all_gather(small, ('rep', 'fsdp'), axis=0, tiled=False)]
    unnamed x1 -> x0, blocking collectives: 35.2 us -> none
    psum x1 -> x0, waiting for transfers between devices: 32.7 us -> none  [on_device(): lax.psum(g_modulator.astype(jnp.bfloat16), 'rep').astype(jnp.float32)]
  transfers between devices with their start and end apart: 10 -> 11, of which waited for: 7 -> 8; matrix products, arithmetic and copies ran while one was open for 24% -> 45% of each run, Pallas kernels for 0% -> 0%
where the time goes in v1:
time: 950 us; the launch traced here: 939 us
  waiting for transfers between devices  356 us (37%)
  matrix products  260 us (27%)
  local copies, waits for them, and re-layouts  141 us (15%)
  blocking collectives  86.1 us (9%)
  other arithmetic  72.1 us (8%)
  between operations  15.1 us (2%)
    reduce_scatter x4, waiting for transfers between devices, scatter_rows(): lax.psum_scatter(grad.astype(jnp.bfloat16), ('fsdp', 'rep'), scatter_dime...  196 us
    all_gather x4, waiting for transfers between devices, gather_rows(): return lax.all_gather(own, ('fsdp', 'rep'), axis=0, tiled=True)  137 us
    all_gather x1, blocking collectives, on_device(): gathered = lax.all_gather(small, ('rep', 'fsdp'), axis=0, tiled=False)  71.3 us
    dynamic_slice x48, local copies, waits for them, and re-layouts, on_device(): lax.map(pair_forward, (paired_query, paired_key, paired_value))  47.4 us
    unnamed x71, local copies, waits for them, and re-layouts  29 us
    dot_general x1, matrix products, on_device(): jnp.einsum('nd,fd->nf', d_branch_m, w_shrink, preferred_element_type=jnp....  27.2 us
    all_gather x2, waiting for transfers between devices, scatter_rows(): return lax.all_gather(own, 'rep', axis=0, tiled=True).astype(jnp.float32)  22.9 us
    dot_general x1, matrix products, on_device(): jnp.dot(norm_m, w_expand, preferred_element_type=jnp.float32) + b_expand  22.4 us
  transfers between devices with their start and end apart: 11, of which 8 were waited for; matrix products, arithmetic and copies ran while one was open for 45% of the time, Pallas kernels for 0%

profile of v1, /device:TPU:0, one launch (start us, length us, event | category | flops | bytes accessed | tf_op | source)
XLA Modules:
  0.0 939.2 jit_solution(2439608350267233966)
XLA Ops:
  19.4 7.3 all-to-all-start
  41.9 43.8 %all-gather.8.cloned.1.call-done = bf16[1024,3072]{1,0:T(8,128)(2,1)} async-done(((bf16[32,3072]{1,0:T(8,128)(2,1)}), bf16[1024,3072]{1,0:T(8,128)(2,1)}) %all-gather.8.cloned.1.call-update) | async-done | bytes 6291472 | tf_op jit(solution)/shard_map/all_gather | solution.py:92
  85.7 9.9 %fusion.80 = f32[1024,3072]{1,0:T(8,128)S(1)} fusion(bf16[1024,3072]{1,0:T(8,128)(2,1)} %all-gather.8.cloned.1.call-done, bf16[1,1024,1024]{1,2,0:T(8,128)(2,1)} %copy.80, f32[1024]{0:T(1024)S(1)} %bitcast.277, f32[1024]{0:T(1024)S(1)} %bitcast.264, f32[1024]{0:T(1024)S(1)} %fusion.67, f32[1024]{0:T(1024)S(1)} %broadcast_multiply_fusion.1), kind=kOutput, calls=%fused_computation.156 | convolution fusion | flops 6448742400 | bytes 20987904 | tf_op jit(solution)/shard_map/dot_general | solution.py:156
  104.5 4.0 copy.99
  114.0 63.1 %while.26 = (s32[]{:T(128)}, bf16[8,1024,128]{1,2,0:T(8,128)(2,1)}, f32[8,2,1024]{2,1,0:T(2,128)}, bf16[8,1024,128]{1,2,0:T(8,128)(2,1)}, bf16[8,1024,128]{1,2,0...) while((s32[]{:T(128)}, bf16[8,1024,128]{1,2,0:T(8,128)(2,1)}, f32[8,2,1024]{2,1,0:T(2,128)}, ...), condition=%wide.region_6.7_spmd, body=%wide.region_3.6_spmd.sunk | while | flops 555874304 | bytes 28378196 | solution.py:173
  177.1 7.9 fusion.87
  187.4 36.0 %all-gather.12.cloned.1.call-done = bf16[1024,4096]{1,0:T(8,128)(2,1)} async-done(((bf16[32,4096]{1,0:T(8,128)(2,1)}), bf16[1024,4096]{1,0:T(8,128)(2,1)}) %all-gather.12.cloned.1.call-update) | async-done | bytes 8388624 | tf_op jit(solution)/shard_map/all_gather | solution.py:92
  223.4 22.4 %multiply_convert_fusion.1 = (bf16[1024,4096]{1,0:T(8,128)(2,1)}, f32[1024,4096]{1,0:T(8,128)}) fusion(f32[4096]{0:T(1024)S(1)} %bitcast.275, bf16[1024,4096]{1,0:T(8,128)(2,1)} %all-gather.12.cloned.1.call-done, f32[1,1024,1024]{1,2,0:T(8,128)} %copy-done.2, f32[1024]{0:T(1024)S(1)} %bitcast.279, f32[1024]{0:T(1024)S(1)} %bitcast.260, ...), kind=kOutput, calls=%fused_computation.40 | convolution fusion | flops 8637120512 | bytes 37781504 | tf_op jit(solution)/shard_map/dot_general | solution.py:180
  245.8 57.1 %all-gather.14.cloned.1.call-done = bf16[4096,1024]{1,0:T(8,128)(2,1)} async-done(((bf16[128,1024]{1,0:T(8,128)(2,1)}), bf16[4096,1024]{1,0:T(8,128)(2,1)}) %all-gather.14.cloned.1.call-update) | async-done | bytes 8388624 | tf_op jit(solution)/shard_map/all_gather | solution.py:92
  302.9 27.2 %fusion.91 = (bf16[4096]{0:T(1024)(128)(2,1)}, bf16[1024,4096]{1,0:T(8,128)(2,1)}) fusion(f32[1024,4096]{1,0:T(8,128)} %get-tuple-element.228, f32[4096]{0:T(1024)S(1)} %bitcast.276, bf16[4096,1024]{1,0:T(8,128)(2,1)} %all-gather.14.cloned.1.call-done, bf16[1,1024,1024]{1,2,0:T(8,128)(2,1)} %copy.86, f32[1024]{0:T(1024)S(1)} %bitcast.269), kind=kOutput, calls=%fused_computation.164 | convolution fusion | flops 8685350912 | bytes 35680256 | tf_op jit(solution)/shard_map/nd,fd->nf/dot_general | solution.py:194
  330.1 15.6 %convolution_convert_fusion.1 = bf16[1024,4096]{1,0:T(8,128)(2,1)} fusion(bf16[1024,4096]{1,0:T(8,128)(2,1)} %get-tuple-element.234, f32[1,1024,1024]{1,2,0:T(8,128)} %copy-done.2, f32[1024]{0:T(1024)S(1)} %bitcast.280, f32[1024]{0:T(1024)S(1)} %bitcast.261, f32[1024]{0:T(1024)S(1)} %fusion.68, f32[1024]{0:T(1024)S(1)} %broadcast_multiply_fusion), kind=kOutput, calls=%fused_computation.42 | convolution fusion | flops 8599371776 | bytes 20987904 | tf_op jit(solution)/shard_map/nd,nf->df/dot_general | solution.py:199
  345.7 15.4 %convolution_convert_fusion = bf16[4096,1024]{1,0:T(8,128)(2,1)} fusion(bf16[1024,4096]{1,0:T(8,128)(2,1)} %get-tuple-element.227, bf16[1,1024,1024]{1,2,0:T(8,128)(2,1)} %copy.86, f32[1024]{0:T(1024)S(1)} %bitcast.270), kind=kOutput, calls=%fused_computation.41 | convolution fusion | flops 8597274624 | bytes 18878464 | tf_op jit(solution)/shard_map/nf,nd->fd/dot_general | solution.py:192
  361.2 16.2 %fusion.90 = (bf16[1024]{0:T(1024)(128)(2,1)}, f32[1024,1024]{1,0:T(8,128)}) fusion(bf16[1024,4096]{1,0:T(8,128)(2,1)} %get-tuple-element.234, bf16[1024,4096]{1,0:T(8,128)(2,1)} %all-gather.12.cloned.1.call-done), kind=kOutput, calls=%fused_computation.163 | convolution fusion | flops 8590982144 | bytes 20973568 | tf_op jit(solution)/shard_map/nf,df->nd/dot_general | solution.py:201
  377.4 5.4 copy.87
  382.8 5.5 fusion.35
  394.6 5.3 fusion.53
  400.0 5.8 fusion.50
  410.7 126.9 %while.27 = (s32[]{:T(128)}, bf16[8,1024,128]{1,2,0:T(8,128)(2,1)}, bf16[8,1024,128]{1,2,0:T(8,128)(2,1)}, bf16[8,1024,128]{1,2,0:T(8,128)(2,1)}, bf16[8,1024,12...) while((s32[]{:T(128)}, bf16[8,1024,128]{1,2,0:T(8,128)(2,1)}, ...), condition=%wide.region_13.14_spmd, body=%wide.region_11.13_spmd.sunk | while | flops 1367996416 | bytes 69264504 | solution.py:218
  537.6 12.9 %convolution_convert_fusion.2 = bf16[1024,3072]{1,0:T(8,128)(2,1)} fusion(bf16[1024,1024]{0,1:T(8,128)(2,1)} %bitcast.249, bf16[1024,1024]{0,1:T(8,128)(2,1)} %bitcast.253, bf16[1024,1024]{0,1:T(8,128)(2,1)} %bitcast.59, bf16[1,1024,1024]{1,2,0:T(8,128)(2,1)} %copy.80, f32[1024]{0:T(1024)S(1)} %bitcast.278, f32[1024]{0:T(1024)S(1)} %bitcast.265, ...), kind=kOutput, calls=%fused_computation.56 | convolution fusion | flops 6470762496 | bytes 14696448 | tf_op jit(solution)/shard_map/nd,ne->de/dot_general | solution.py:232
  550.6 12.4 %fusion.89 = (bf16[1024]{0:T(1024)(128)(2,1)S(1)}, f32[1024,1024]{1,0:T(8,128)}) fusion(bf16[1024,3072]{1,0:T(8,128)(2,1)} %all-gather.8.cloned.1.call-done, bf16[1024,1024]{0,1:T(8,128)(2,1)} %bitcast.250, bf16[1024,1024]{0,1:T(8,128)(2,1)} %bitcast.254, bf16[1024,1024]{0,1:T(8,128)(2,1)} %bitcast.59), kind=kOutput, calls=%fused_computation.162 | convolution fusion | flops 6462372864 | bytes 16779264 | tf_op jit(solution)/shard_map/ne,de->nd/dot_general | solution.py:234
  563.0 5.4 copy.88
  575.4 22.4 %fusion.32 = (bf16[1024]{0:T(1024)(128)(2,1)S(1)}, bf16[1024]{0:T(1024)(128)(2,1)S(1)}, f32[1,1024,1024]{1,2,0:T(8,128)}, f32[1,1024,1024]{1,2,0:T(8,128)}) fusion(bf16[1,1024,1024]{1,2,0:T(8,128)(2,1)} %copy.86, f32[1024]{0:T(1024)S(1)} %copy-done.23, f32[1024,1024]{0,1:T(8,128)} %get-tuple-element.226, f32[1024]{0:T(1024)S(1)} %copy-done.25, ...), kind=kOutput, calls=%fused_computation.65 | convolution fusion | flops 8610904064 | bytes 46178304 | tf_op jit(solution)/shard_map/dot_general | solution.py:184
  601.7 38.7 %reduce-scatter.11.cloned.1.call-done = bf16[128,1024]{1,0:T(8,128)(2,1)} async-done(((bf16[4096,1024]{1,0:T(8,128)(2,1)}), bf16[128,1024]{1,0:T(8,128)(2,1)}) %reduce-scatter.11.cloned.1.call-update) | async-done | bytes 262160 | tf_op jit(solution)/shard_map/reduce_scatter | solution.py:96
  640.4 71.3 %all-gather = bf16[491520]{0:T(1024)(128)(2,1)S(1)} all-gather(bf16[15360]{0:T(1024)(128)(2,1)S(1)} %constant_dynamic-update-slice_fusion.4), channel_id=2, replica_groups=mesh['rep'=4,'fsdp'=8] {'rep','fsdp'}, dimensions={0}, use_global_device_ids=true | all-gather | bytes 1013760 | tf_op jit(solution)/shard_map/all_gather | solution.py:248
  712.3 5.4 copy.91
  717.7 5.4 copy.92
  728.8 47.1 %reduce-scatter.7.cloned.1.call-done = bf16[32,1024]{1,0:T(8,128)(2,1)} async-done(((bf16[1024,1024]{1,0:T(8,128)(2,1)}), bf16[32,1024]{1,0:T(8,128)(2,1)}) %reduce-scatter.7.cloned.1.call-update) | async-done | bytes 65552 | tf_op jit(solution)/shard_map/reduce_scatter | solution.py:96
  775.9 6.0 all_gather.37
  782.8 110.7 %reduce-scatter.5.cloned.1.call-done = bf16[32,3072]{1,0:T(8,128)(2,1)} async-done(((bf16[1024,3072]{1,0:T(8,128)(2,1)}), bf16[32,3072]{1,0:T(8,128)(2,1)}) %reduce-scatter.5.cloned.1.call-update) | async-done | bytes 196624 | tf_op jit(solution)/shard_map/reduce_scatter | solution.py:96
  893.4 8.8 all_gather.36
  903.5 7.5 all-gather.16.cloned.1.call-done
  913.7 15.4 %all-gather.18.cloned.1.call-done = bf16[512,1024]{1,0:T(8,128)(2,1)} async-done(((bf16[128,1024]{1,0:T(8,128)(2,1)}), bf16[512,1024]{1,0:T(8,128)(2,1)}) %all-gather.18.cloned.1.call-update) | async-done | bytes 1048592 | tf_op jit(solution)/shard_map/all_gather | solution.py:99
  (318 shorter events, 269.2 us)
Async XLA Ops:
  7.2 10.2 %copy-start = (bf16[128,6144]{1,0:T(8,128)(2,1)S(1)}, bf16[128,6144]{1,0:T(8,128)(2,1)}, u32[]{:S(2)}) copy-start(bf16[128,6144]{1,0:T(8,128)(2,1)} %param.20) | copy-start | bytes 4718596
  7.2 78.5 %all-gather.8.cloned.1.call-start = ((), (), s32[]{:S(2)}) async-start(), calls=%async_computation.5 | async-start | bytes 6488064 | tf_op jit(solution)/shard_map/all_gather | solution.py:92
  9.0 168.1 %all-gather.10.cloned.1.call-start = ((), (), s32[]{:S(2)}) async-start(), calls=%async_computation.6 | async-start | bytes 2162688 | tf_op jit(solution)/shard_map/all_gather | solution.py:92
  10.5 212.9 %all-gather.12.cloned.1.call-start = ((), (), s32[]{:S(2)}) async-start(), calls=%async_computation.7 | async-start | bytes 8650752 | tf_op jit(solution)/shard_map/all_gather | solution.py:92
  19.4 21.7 %all-to-all-start = ((f32[8,1,7936]{2,1,0:T(1,128)}), f32[8,1,7936]{2,1,0:T(1,128)S(1)}, u32[]{:S(2)}, u32[]{:S(2)}) async-start(f32[8,1,7936]{2,1,0:T(1,128)} %copy.81), calls=%async_computation | async-start | bytes 507904 | tf_op jit(solution)/shard_map/all_to_all | solution.py:138
  26.6 276.3 %all-gather.14.cloned.1.call-start = ((), (), s32[]{:S(2)}) async-start(), calls=%async_computation.8 | async-start | bytes 8650752 | tf_op jit(solution)/shard_map/all_gather | solution.py:92
  28.4 546.9 %reduce-scatter.9.cloned.1.call-start = ((), (), s32[]{:S(2)}) async-start(), calls=%async_computation.11 | async-start | bytes 8650752 | tf_op jit(solution)/shard_map/reduce_scatter | solution.py:96
  34.3 61.3 %copy-start.9 = (f32[1024]{0:T(1024)}, f32[1024]{0:T(1024)S(1)}, u32[]{:S(2)}) copy-start(f32[1024]{0:T(1024)S(1)} %broadcast_multiply_fusion.1) | copy-start | bytes 12292
  41.1 54.5 %copy-start.11 = (f32[1024]{0:T(1024)}, f32[1024]{0:T(1024)S(1)}, u32[]{:S(2)}) copy-start(f32[1024]{0:T(1024)S(1)} %fusion.67) | copy-start | bytes 12292
  41.8 135.3 %copy-start.24 = (f32[1024]{0:T(1024)}, f32[1024]{0:T(1024)S(1)}, u32[]{:S(2)}) copy-start(f32[1024]{0:T(1024)S(1)} %get-tuple-element.217) | copy-start | bytes 12292
  41.9 53.8 %copy-start.15 = (f32[1,1,1024]{2,1,0:T(1,128)}, f32[1,1,1024]{2,1,0:T(1,128)S(1)}, u32[]{:S(2)}) copy-start(f32[1,1,1024]{2,1,0:T(1,128)S(1)} %get-tuple-element.224) | copy-start | bytes 12292
  41.9 53.8 %copy-start.21 = (f32[1,1,1024]{2,1,0:T(1,128)}, f32[1,1,1024]{2,1,0:T(1,128)S(1)}, u32[]{:S(2)}) copy-start(f32[1,1,1024]{2,1,0:T(1,128)S(1)} %get-tuple-element.223) | copy-start | bytes 12292
  345.7 294.7 %reduce-scatter.11.cloned.1.call-start = ((), (), s32[]{:S(2)}) async-start(), calls=%async_computation.13 | async-start | bytes 8650752 | tf_op jit(solution)/shard_map/reduce_scatter | solution.py:96
  361.2 414.7 %reduce-scatter.7.cloned.1.call-start = ((), (), s32[]{:S(2)}) async-start(), calls=%async_computation.10 | async-start | bytes 2162688 | tf_op jit(solution)/shard_map/reduce_scatter | solution.py:96
  382.8 5.5 copy-start.3
  382.8 6.1 copy-start.4
  390.0 3.3 copy-start.6
  400.0 493.4 %reduce-scatter.5.cloned.1.call-start = ((), (), s32[]{:S(2)}) async-start(), calls=%async_computation.9 | async-start | bytes 6488064 | tf_op jit(solution)/shard_map/reduce_scatter | solution.py:96
  410.6 126.9 %copy-start.10 = (f32[1024]{0:T(1024)S(1)}, f32[1024]{0:T(1024)}, u32[]{:S(2)}) copy-start(f32[1024]{0:T(1024)} %copy-done.9) | copy-start | bytes 12292
  410.6 126.9 %copy-start.12 = (f32[1024]{0:T(1024)S(1)}, f32[1024]{0:T(1024)}, u32[]{:S(2)}) copy-start(f32[1024]{0:T(1024)} %copy-done.11) | copy-start | bytes 12292
  410.7 126.9 %copy-start.16 = (f32[1,1,1024]{2,1,0:T(1,128)S(1)}, f32[1,1,1024]{2,1,0:T(1,128)}, u32[]{:S(2)}) copy-start(f32[1,1,1024]{2,1,0:T(1,128)} %copy-done.15) | copy-start | bytes 12292
  410.7 126.9 %copy-start.22 = (f32[1,1,1024]{2,1,0:T(1,128)S(1)}, f32[1,1,1024]{2,1,0:T(1,128)}, u32[]{:S(2)}) copy-start(f32[1,1,1024]{2,1,0:T(1,128)} %copy-done.21) | copy-start | bytes 12292
  550.5 360.4 %all-gather.16.cloned.1.call-start = ((), (), s32[]{:S(2)}) async-start(), calls=%async_computation.12 | async-start | bytes 1310720 | tf_op jit(solution)/shard_map/all_gather | solution.py:99
  568.4 3.8 copy-start.14
  568.4 3.8 copy-start.1
  568.4 4.8 copy-start.5
  575.3 353.8 %all-gather.18.cloned.1.call-start = ((), (), s32[]{:S(2)}) async-start(), calls=%async_computation.14 | async-start | bytes 1310720 | tf_op jit(solution)/shard_map/all_gather | solution.py:99
  575.4 22.5 %copy-start.17 = (bf16[1024]{0:T(1024)(128)(2,1)S(1)}, bf16[1024]{0:T(1024)(128)(2,1)}, u32[]{:S(2)}) copy-start(bf16[1024]{0:T(1024)(128)(2,1)} %get-tuple-element.157) | copy-start | bytes 6148
  575.4 22.5 %copy-start.26 = (bf16[1024]{0:T(1024)(128)(2,1)S(1)}, bf16[1024]{0:T(1024)(128)(2,1)}, u32[]{:S(2)}) copy-start(bf16[1024]{0:T(1024)(128)(2,1)} %get-tuple-element.231) | copy-start | bytes 6148
  597.8 3.8 copy-start.20
  597.8 3.8 copy-start.18
  597.8 3.8 copy-start.19
  (6 other events, 12.0 us)
Sparse Core Ops, SparseCore 0:
  11.5 74.1 all-gather.7
  88.5 54.9 all-gather.9
  147.0 76.3 all-gather.11
  226.7 76.1 all-gather.13
  345.8 147.4 reduce-scatter.8
  495.5 144.8 reduce-scatter.10
  642.7 133.2 reduce-scatter.6
  782.5 110.8 reduce-scatter.4
  895.0 15.9 all-gather.15
  912.3 16.7 all-gather.17

commit v2 on v1

v2 whole, which is shorter than its diff:
```python
from functools import partial

import jax
import jax.numpy as jnp
from jax import lax
from jax.experimental import pallas as pl
from jax.experimental.pallas import tpu as pltpu
from jax.sharding import PartitionSpec as P

HEADS = 16
HEAD_DIM = 64
PAIR = 2 * HEAD_DIM
CHUNK = 256
EPS_NORM = 1e-06
ROWS = 256
FF_BLOCK = 512
COL_BLOCK = 512
GELU_ROOT = 0.7978845608028654
GELU_CUBE = 0.044715


def dot_nn(left, right):
    return jnp.dot(left, right, preferred_element_type=jnp.float32)


def dot_nt(left, right):
    return lax.dot_general(left, right, (((1,), (1,)), ((), ())), preferred_element_type=jnp.float32)


def dot_tn(left, right):
    return lax.dot_general(left, right, (((0,), (0,)), ((), ())), preferred_element_type=jnp.float32)


def kernel_params(mebibytes):
    return pltpu.CompilerParams(vmem_limit_bytes=mebibytes * 2**20)


def cost(flops, moved, special=0):
    return pl.CostEstimate(flops=flops, bytes_accessed=moved, transcendentals=special)


def weight_spec(weight, first, width, order):
    if weight.ndim == 2:
        offset = first * weight.shape[0] // width
        return pl.BlockSpec((weight.shape[0], width), lambda *at: (0, offset + order(*at)))
    devices, _, rows, columns = weight.shape
    per = columns // width
    return pl.BlockSpec(
        (devices, 1, rows, width),
        lambda *at: (0, first + order(*at) // per, 0, order(*at) % per),
    )


def forward_dot_kernel(x_ref, w_ref, b_ref, out_ref):
    weight = w_ref[...].reshape(x_ref.shape[1], out_ref.shape[1])
    out_ref[...] = (dot_nn(x_ref[...], weight) + b_ref[...]).astype(out_ref.dtype)


def forward_dot(x, weight, first, bias, dtype, name):
    tokens, depth = x.shape
    columns = bias.shape[1]
    return pl.pallas_call(
        forward_dot_kernel,
        grid=(columns // COL_BLOCK,),
        in_specs=[
            pl.BlockSpec((tokens, depth), lambda i: (0, 0)),
            weight_spec(weight, first, COL_BLOCK, lambda i: i),
            pl.BlockSpec((1, COL_BLOCK), lambda i: (0, i)),
        ],
        out_specs=pl.BlockSpec((tokens, COL_BLOCK), lambda i: (0, i)),
        out_shape=jax.ShapeDtypeStruct((tokens, columns), dtype),
        compiler_params=kernel_params(40),
        cost_estimate=cost(2 * tokens * depth * columns, 4 * tokens * columns),
        name=name,
    )(x, weight, bias)


def backward_dot_kernel(dy_ref, w_ref, out_ref, sum_ref):
    step = pl.program_id(0)
    weight = w_ref[...].reshape(out_ref.shape[1], w_ref.shape[-1])
    part = dot_nt(dy_ref[0], weight)

    @pl.when(step == 0)
    def _():
        sum_ref[...] = part

    @pl.when(step > 0)
    def _():
        sum_ref[...] += part

    @pl.when(step == pl.num_programs(0) - 1)
    def _():
        out_ref[...] = sum_ref[...].astype(out_ref.dtype)


def backward_dot(dy, weight, first, dtype, name):
    groups, tokens, columns = dy.shape
    depth = columns
    per = columns // COL_BLOCK
    return pl.pallas_call(
        backward_dot_kernel,
        grid=(groups * per,),
        in_specs=[
            pl.BlockSpec((1, tokens, COL_BLOCK), lambda i: (i // per, 0, i % per)),
            weight_spec(weight, first, COL_BLOCK, lambda i: i),
        ],
        out_specs=pl.BlockSpec((tokens, depth), lambda i: (0, 0)),
        out_shape=jax.ShapeDtypeStruct((tokens, depth), dtype),
        scratch_shapes=[pltpu.VMEM((tokens, depth), jnp.float32)],
        compiler_params=kernel_params(40),
        cost_estimate=cost(2 * groups * tokens * depth * columns, 4 * tokens * columns),
        name=name,
    )(dy, weight)


def store_rows(total, own_core, own_slot, pieces, keep_ref, send_ref):
    rows = total.shape[0] // pieces
    low = total.astype(jnp.bfloat16).reshape(pieces // 2, 2, rows, total.shape[1])
    here = own_core == 0
    for slot in range(pieces // 2):
        first, second = low[slot, 0], low[slot, 1]
        place = pl.ds(pl.multiple_of((own_slot ^ slot) * rows, rows), rows)
        keep_ref[place, :] = jnp.where(here, first, second)
        send_ref[place, :] = jnp.where(here, second, first)


def grad_dot_kernel(pieces, own_ref, x_ref, dy_ref, keep_ref, send_ref):
    total = dot_tn(x_ref[...], dy_ref[0])
    store_rows(total, own_ref[0], own_ref[1], pieces, keep_ref, send_ref)


def grad_dot(own, x, dy, first, groups, pieces, name):
    tokens, depth = x.shape
    columns = dy.shape[2]
    per = columns // COL_BLOCK
    half = jax.ShapeDtypeStruct((depth // 2, groups * columns), jnp.bfloat16)
    block = pl.BlockSpec((depth // 2, COL_BLOCK), lambda i, own: (0, i))
    return pl.pallas_call(
        partial(grad_dot_kernel, pieces),
        grid_spec=pltpu.PrefetchScalarGridSpec(
            num_scalar_prefetch=1,
            grid=(groups * per,),
            in_specs=[
                pl.BlockSpec((tokens, depth), lambda i, own: (0, 0)),
                pl.BlockSpec((1, tokens, COL_BLOCK), lambda i, own: (first + i // per, 0, i % per)),
            ],
            out_specs=[block, block],
        ),
        out_shape=[half, half],
        compiler_params=kernel_params(40),
        cost_estimate=cost(2 * groups * tokens * depth * columns, 4 * tokens * columns),
        name=name,
    )(own, x, dy)


def feed_forward_kernel(
    depth_pieces,
    unit_pieces,
    own_ref,
    norm_ref,
    grad_ref,
    expand_ref,
    bias_ref,
    shrink_ref,
    branch_ref,
    d_norm_ref,
    keep_e_ref,
    send_e_ref,
    keep_s_ref,
    send_s_ref,
    d_bias_ref,
    norm_t,
    hidden,
    d_pre,
):
    tokens, depth = norm_ref.shape
    units = hidden.shape[1]
    step = pl.program_id(0)
    expand = expand_ref[...].reshape(depth, units)
    shrink = shrink_ref[...].reshape(units, depth)

    @pl.when(step == 0)
    def _():
        norm_t[...] = norm_ref[...].T
        branch_ref[...] = jnp.zeros_like(branch_ref)
        d_norm_ref[...] = jnp.zeros_like(d_norm_ref)

    bias_sum = jnp.zeros((1, units), jnp.float32)
    for start in range(0, tokens, ROWS):
        rows = slice(start, start + ROWS)
        pre = dot_nn(norm_ref[rows, :], expand) + bias_ref[...]
        square = pre * pre
        bend = jnp.tanh(GELU_ROOT * pre * (1.0 + GELU_CUBE * square))
        rise = 0.5 + 0.5 * bend
        unit = (pre * rise).astype(jnp.bfloat16)
        hidden[rows, :] = unit
        slope = rise + 0.5 * pre * (1.0 - bend * bend) * (
            GELU_ROOT + (3.0 * GELU_ROOT * GELU_CUBE) * square
        )
        branch_ref[rows, :] += dot_nn(unit, shrink)
        d_unit = dot_nt(grad_ref[rows, :], shrink)
        d_low = (d_unit * slope).astype(jnp.bfloat16)
        d_pre[rows, :] = d_low
        bias_sum = bias_sum + jnp.sum(d_low.astype(jnp.float32), axis=0, keepdims=True)
        d_norm_ref[rows, :] += dot_nt(d_low, expand)
    d_bias_ref[...] = bias_sum
    store_rows(
        dot_tn(hidden[...], grad_ref[...]), own_ref[0], own_ref[3], unit_pieces, keep_s_ref, send_s_ref
    )
    store_rows(
        dot_nn(norm_t[...], d_pre[...]), own_ref[0], own_ref[1], depth_pieces, keep_e_ref, send_e_ref
    )


def feed_forward(own, norm, grad, expand, bias, shrink, depth_pieces, unit_pieces):
    tokens, depth = norm.shape
    total = bias.shape[1]
    steps = total // FF_BLOCK
    whole = pl.BlockSpec((tokens, depth), lambda i, own: (0, 0))
    half_e = pl.BlockSpec((depth // 2, FF_BLOCK), lambda i, own: (0, i))
    half_s = pl.BlockSpec((FF_BLOCK // 2, depth), lambda i, own: (i ^ own[2], 0))
    line = pl.BlockSpec((1, FF_BLOCK), lambda i, own: (0, i))
    if shrink.ndim == 2:
        spec_e = weight_spec(expand, 0, FF_BLOCK, lambda i, own: i)
        spec_s = pl.BlockSpec((FF_BLOCK, depth), lambda i, own: (i, 0))
    else:
        devices, blocks, rows, columns = shrink.shape
        spec_e = weight_spec(expand, 4, FF_BLOCK, lambda i, own: i)
        spec_s = pl.BlockSpec((devices // steps, 4, rows, columns), lambda i, own: (i, 0, 0, 0))
    wide = jax.ShapeDtypeStruct((tokens, depth), jnp.float32)
    out_e = jax.ShapeDtypeStruct((depth // 2, total), jnp.bfloat16)
    out_s = jax.ShapeDtypeStruct((total // 2, depth), jnp.bfloat16)
    return pl.pallas_call(
        partial(feed_forward_kernel, depth_pieces, unit_pieces),
        grid_spec=pltpu.PrefetchScalarGridSpec(
            num_scalar_prefetch=1,
            grid=(steps,),
            in_specs=[whole, whole, spec_e, line, spec_s],
            out_specs=[whole, whole, half_e, half_e, half_s, half_s, line],
            scratch_shapes=[
                pltpu.VMEM((depth, tokens), jnp.bfloat16),
                pltpu.VMEM((tokens, FF_BLOCK), jnp.bfloat16),
                pltpu.VMEM((tokens, FF_BLOCK), jnp.bfloat16),
            ],
        ),
        out_shape=[
            wide,
            wide,
            out_e,
            out_e,
            out_s,
            out_s,
            jax.ShapeDtypeStruct((1, total), jnp.float32),
        ],
        compiler_params=kernel_params(56),
        cost_estimate=cost(12 * tokens * depth * total, 64 * 2**20, tokens * total),
        name="feed_forward",
    )(own, norm, grad, expand, bias, shrink)


def attention_forward_kernel(q_ref, k_ref, v_ref, out_ref, lse_ref):
    length = q_ref.shape[0]
    scaled = q_ref[...] * jnp.bfloat16(HEAD_DIM ** (-0.5))
    keys = k_ref[...]
    values_t = v_ref[...].T
    for start in range(0, length, CHUNK):
        rows = slice(start, start + CHUNK)
        pieces = []
        for head in range(2):
            cols = slice(head * HEAD_DIM, (head + 1) * HEAD_DIM)
            scores = dot_nt(keys[:, cols], scaled[rows, cols])
            top = jnp.max(scores, axis=0, keepdims=True)
            terms = jnp.exp(scores - top)
            total = jnp.sum(terms, axis=0, keepdims=True)
            part = dot_nn(values_t[cols, :], terms.astype(jnp.bfloat16))
            pieces.append(part / total)
            lse_ref[0, head : head + 1, rows] = top + jnp.log(total)
        out_ref[rows, :] = jnp.concatenate(pieces, axis=0).T.astype(jnp.bfloat16)


def attention_forward(projected):
    length = projected.shape[0]
    pairs = HEADS // 2
    return pl.pallas_call(
        attention_forward_kernel,
        grid=(pairs,),
        in_specs=[
            pl.BlockSpec((length, PAIR), lambda i: (0, i)),
            pl.BlockSpec((length, PAIR), lambda i: (0, pairs + i)),
            pl.BlockSpec((length, PAIR), lambda i: (0, 2 * pairs + i)),
        ],
        out_specs=[
            pl.BlockSpec((length, PAIR), lambda i: (0, i)),
            pl.BlockSpec((1, 2, length), lambda i: (i, 0, 0)),
        ],
        out_shape=[
            jax.ShapeDtypeStruct((length, HEADS * HEAD_DIM), jnp.bfloat16),
            jax.ShapeDtypeStruct((pairs, 2, length), jnp.float32),
        ],
        compiler_params=pltpu.CompilerParams(vmem_limit_bytes=48 * 2**20),
        cost_estimate=pl.CostEstimate(flops=16 * 2**30, bytes_accessed=8 * 2**20, transcendentals=16 * 2**20),
        name="attention_forward",
    )(projected, projected, projected)


def attention_backward_kernel(q_ref, k_ref, v_ref, g_ref, lse_ref, out_ref, qb_ref, vb_ref):
    length = q_ref.shape[0]
    root = HEAD_DIM ** (-0.5)
    scaled = q_ref[...] * jnp.bfloat16(root)
    keys = k_ref[...]
    values = v_ref[...]
    grads = g_ref[...]
    keys_t = keys.T
    sums_k = [None, None]
    sums_v = [None, None]
    sum_q = None
    for start in range(0, length, CHUNK):
        rows = slice(start, start + CHUNK)
        pieces = []
        for head in range(2):
            cols = slice(head * HEAD_DIM, (head + 1) * HEAD_DIM)
            query, grad = scaled[rows, cols], grads[rows, cols]
            scores = dot_nt(keys[:, cols], query)
            probs = jnp.exp(scores - lse_ref[0, head : head + 1, rows])
            d_probs = dot_nt(values[:, cols], grad)
            row_sum = jnp.sum(probs * d_probs, axis=0, keepdims=True)
            d_scores = (probs * (d_probs - row_sum)).astype(jnp.bfloat16)
            part_v = dot_nn(probs.astype(jnp.bfloat16), grad)
            part_k = dot_nn(d_scores, query)
            sums_v[head] = part_v if start == 0 else sums_v[head] + part_v
            sums_k[head] = part_k if start == 0 else sums_k[head] + part_k
            pieces.append(dot_nn(keys_t[cols, :], d_scores) * root)
        d_query = jnp.concatenate(pieces, axis=0).T.astype(jnp.bfloat16)
        out_ref[0, rows, :] = d_query
        part_q = jnp.sum(d_query.astype(jnp.float32), axis=0, keepdims=True)
        sum_q = part_q if start == 0 else sum_q + part_q
    out_ref[1] = jnp.concatenate(sums_k, axis=1).astype(jnp.bfloat16)
    d_value = jnp.concatenate(sums_v, axis=1).astype(jnp.bfloat16)
    out_ref[2] = d_value
    qb_ref[...] = sum_q
    vb_ref[...] = jnp.sum(d_value.astype(jnp.float32), axis=0, keepdims=True)


def attention_backward(projected, d_attended, lse):
    length = projected.shape[0]
    width = HEADS * HEAD_DIM
    pairs = HEADS // 2
    block = pl.BlockSpec((length, PAIR), lambda i: (0, i))
    row = pl.BlockSpec((1, PAIR), lambda i: (0, i))
    triple = pl.BlockSpec((3, length, PAIR), lambda i: (0, 0, i))
    whole = jax.ShapeDtypeStruct((3, length, width), jnp.bfloat16)
    line = jax.ShapeDtypeStruct((1, width), jnp.float32)
    return pl.pallas_call(
        attention_backward_kernel,
        grid=(pairs,),
        in_specs=[
            block,
            pl.BlockSpec((length, PAIR), lambda i: (0, pairs + i)),
            pl.BlockSpec((length, PAIR), lambda i: (0, 2 * pairs + i)),
            block,
            pl.BlockSpec((1, 2, length), lambda i: (i, 0, 0)),
        ],
        out_specs=[triple, row, row],
        out_shape=[whole, line, line],
        compiler_params=pltpu.CompilerParams(vmem_limit_bytes=48 * 2**20),
        cost_estimate=pl.CostEstimate(flops=40 * 2**30, bytes_accessed=16 * 2**20, transcendentals=16 * 2**20),
        name="attention_backward",
    )(projected, projected, projected, d_attended, lse)


def normalize(values):
    average = jnp.mean(values, axis=-1, keepdims=True)
    centred = values - average
    variance = jnp.mean(centred * centred, axis=-1, keepdims=True)
    return centred * lax.rsqrt(variance + EPS_NORM)


def modulate(values, shifts, scales):
    return normalize(values) * (1.0 + scales[:, None, :]) + shifts[:, None, :]


def exchange(value, rep_mask, fsdp_mask):
    reps, shards = lax.axis_size("rep"), lax.axis_size("fsdp")
    pairs = [
        (rep * shards + shard, (rep ^ rep_mask) * shards + (shard ^ fsdp_mask))
        for rep in range(reps)
        for shard in range(shards)
    ]
    return lax.ppermute(value, ("rep", "fsdp"), pairs)


def masks_of():
    reps, shards = lax.axis_size("rep"), lax.axis_size("fsdp")
    masks = [(1 << bit, 0) for bit in range(reps.bit_length() - 1)]
    return masks + [(0, 1 << bit) for bit in range(shards.bit_length() - 1)]


def gather_relative(row):
    rows = row[None, :]
    for masks in masks_of():
        rows = jnp.concatenate([rows, exchange(rows, *masks)], axis=0)
    return rows


def to_absolute(parts, own):
    parts = list(parts)
    bit = 1
    while bit < len(parts):
        flipped = (own & bit) != 0
        parts = [jnp.where(flipped, parts[i ^ bit], parts[i]) for i in range(len(parts))]
        bit *= 2
    return parts


def scatter_halves(keep, send, order):
    shards = lax.axis_size("fsdp")
    rows, columns = keep.shape[0] // (2 * shards), keep.shape[1]
    shape = (2, 2, 2, 2, rows, columns)
    masks = {"z2": (0, 4), "z1": (0, 2), "x": (0, 1), "y": (2, 0)}
    axes = ["z2", "z1", "x", "y"]
    arrived = exchange(send, 1, 0)
    total = keep.reshape(shape).astype(jnp.float32) + arrived.reshape(shape).astype(jnp.float32)
    for name in order:
        axis = axes.index(name)
        axes.pop(axis)
        away = lax.index_in_dim(total, 1, axis, keepdims=False).astype(jnp.bfloat16)
        stay = lax.index_in_dim(total, 0, axis, keepdims=False)
        total = stay + exchange(away, *masks[name]).astype(jnp.float32)
    own = total.astype(jnp.bfloat16)
    reps = [own] + [exchange(own, mask, 0) for mask in (1, 2, 3)]
    parts = to_absolute(reps, lax.axis_index("rep"))
    return jnp.concatenate(parts, axis=0).astype(jnp.float32)


def scatter_rows(grad):
    own = lax.psum_scatter(grad, ("fsdp", "rep"), scatter_dimension=0, tiled=True)
    return lax.all_gather(own, "rep", axis=0, tiled=True).astype(jnp.float32)


def own_quarter(weight):
    part = weight.shape[0] // lax.axis_size("rep")
    return lax.dynamic_slice_in_dim(weight, lax.axis_index("rep") * part, part, 0)


def gather_rows(weight):
    return lax.all_gather(own_quarter(weight), ("fsdp", "rep"), axis=0, tiled=True)


def column_blocks(quarter, width):
    rows = quarter.shape[0]
    blocks = quarter.shape[1] // width
    return quarter.reshape(rows, blocks, width).transpose(1, 0, 2).reshape(blocks * rows, width)


def gather_packed(parts, rows):
    packed = jnp.concatenate(parts, axis=0)
    blocks, width = packed.shape[0] // rows, packed.shape[1]
    full = lax.all_gather(packed, ("fsdp", "rep"), axis=0, tiled=True)
    return full.reshape(full.shape[0] // packed.shape[0], blocks, rows, width)


def on_device(
    latents,
    conditions,
    modulator,
    modulbias,
    projector,
    querybias,
    valuebias,
    outweight,
    outbiases,
    expander,
    expandbias,
    shrinker,
    shrinkbias,
    upstream,
):
    seqs_dev, seq_len, feature = latents.shape
    token_count = seqs_dev * seq_len
    shard_id, rep_id = lax.axis_index("fsdp"), lax.axis_index("rep")
    shards, reps = lax.axis_size("fsdp"), lax.axis_size("rep")
    halving = shards == 8 and reps == 4
    own_rows = modulator.shape[0]
    own_bias = modulbias.shape[0]

    if halving:
        quarter = own_rows // reps
        attn_weights = gather_packed(
            [column_blocks(own_quarter(projector), feature), own_quarter(outweight)], quarter
        )
        proj_at, out_at = (attn_weights, 0), (attn_weights, 3)
        ff_weights = gather_packed(
            [own_quarter(shrinker), column_blocks(own_quarter(expander), feature)], quarter
        )
        w_expand, w_shrink = ff_weights, ff_weights
        depth_pieces, unit_pieces = shards * reps, reps
        own = jnp.stack(
            [rep_id & 1, shard_id * 2 + (rep_id >> 1), shard_id, rep_id >> 1]
        ).astype(jnp.int32)
    else:
        proj_at, out_at = (gather_rows(projector), 0), (gather_rows(outweight), 0)
        w_expand, w_shrink = gather_rows(expander), gather_rows(shrinker)
        depth_pieces, unit_pieces = 2, 2
        own = jnp.zeros((4,), jnp.int32)

    def reduce_depth(halves, order):
        if halving:
            return scatter_halves(*halves, order)
        return scatter_rows(jnp.concatenate(halves, axis=0))

    def reduce_units(halves, order):
        if halving:
            return scatter_halves(*halves, order)
        blocks = [half.reshape(-1, 1, FF_BLOCK // 2, feature) for half in halves]
        return scatter_rows(jnp.concatenate(blocks, axis=1).reshape(-1, feature))

    cond_full = conditions.astype(jnp.float32)
    cond_slice = lax.dynamic_slice_in_dim(cond_full, shard_id * own_rows, own_rows, 1)
    cond_act = jax.nn.silu(cond_slice).astype(jnp.bfloat16)
    cond_own = lax.dynamic_slice_in_dim(cond_full, shard_id * seqs_dev, seqs_dev, 0)
    cond_own = jax.nn.silu(cond_own).astype(jnp.bfloat16)
    mod_term = jnp.dot(cond_act, modulator, preferred_element_type=jnp.float32)
    bias_parts = (modulbias, querybias, valuebias, outbiases, expandbias, shrinkbias)
    own_biases = jnp.concatenate([part.astype(jnp.float32) for part in bias_parts])
    mod_width = seqs_dev * 6 * feature
    sent = jnp.concatenate(
        [
            mod_term.reshape(shards, mod_width),
            jnp.broadcast_to(own_biases[None, :], (shards, own_biases.shape[0])),
        ],
        axis=1,
    )
    got = lax.all_to_all(sent, "fsdp", split_axis=0, concat_axis=0, tiled=True)
    full_biases = []
    start = mod_width
    for part in bias_parts:
        full_biases.append(got[:, start : start + part.shape[0]].reshape(1, -1))
        start += part.shape[0]
    full_modbias, b_query, b_value, b_out, b_expand, b_shrink = full_biases
    modvals = jnp.sum(got[:, :mod_width], axis=0).reshape(seqs_dev, 6, feature)
    modvals = modvals + full_modbias.reshape(1, 6, feature)
    shift_a, scale_a, gate_a = (modvals[:, 0], modvals[:, 1], modvals[:, 2])
    shift_m, scale_m, gate_m = (modvals[:, 3], modvals[:, 4], modvals[:, 5])

    resid_in = latents.astype(jnp.float32)
    norm_a = modulate(resid_in, shift_a, scale_a).astype(jnp.bfloat16).reshape(token_count, feature)
    b_proj = jnp.concatenate([b_query, jnp.zeros_like(b_query), b_value], axis=1)
    projected = forward_dot(norm_a, *proj_at, b_proj, jnp.bfloat16, "project")
    attended, log_totals = attention_forward(projected)
    branch_a = forward_dot(attended, *out_at, b_out, jnp.float32, "attention_out")
    branch_a = branch_a.reshape(seqs_dev, seq_len, feature)
    middle = resid_in + gate_a[:, None, :] * branch_a
    norm_m = modulate(middle, shift_m, scale_m).astype(jnp.bfloat16).reshape(token_count, feature)

    grad_out = upstream.astype(jnp.float32)
    d_branch_m = (gate_m[:, None, :] * grad_out).astype(jnp.bfloat16).reshape(token_count, feature)
    g_shrinkbias = jnp.sum(d_branch_m, axis=0, dtype=jnp.float32)
    branch_m, d_norm_m, keep_e, send_e, keep_s, send_s, g_expandbias = feed_forward(
        own, norm_m, d_branch_m, w_expand, b_expand, w_shrink, depth_pieces, unit_pieces
    )
    g_expander = reduce_depth((keep_e, send_e), ("y", "x", "z2", "z1"))
    g_shrinker = reduce_units((keep_s, send_s), ("x", "y", "z2", "z1"))
    branch_m = (branch_m + b_shrink).reshape(seqs_dev, seq_len, feature)
    layer_out = middle + gate_m[:, None, :] * branch_m
    d_gate_m = jnp.sum(grad_out * branch_m, axis=1)
    _, norm_pull_m = jax.vjp(modulate, middle, shift_m, scale_m)
    d_mid_norm, d_shift_m, d_scale_m = norm_pull_m(d_norm_m.reshape(seqs_dev, seq_len, feature))
    d_middle = grad_out + d_mid_norm
    d_branch_a = (gate_a[:, None, :] * d_middle).astype(jnp.bfloat16).reshape(token_count, feature)
    d_gate_a = jnp.sum(d_middle * branch_a, axis=1)
    g_outbiases = jnp.sum(d_branch_a, axis=0, dtype=jnp.float32)
    d_branch_one = d_branch_a[None]
    g_outweight = reduce_depth(
        grad_dot(own, attended, d_branch_one, 0, 1, depth_pieces, "outweight_grad"),
        ("x", "y", "z2", "z1"),
    )
    d_attended = backward_dot(d_branch_one, *out_at, jnp.bfloat16, "attention_out_back")
    early = gather_relative(
        jnp.concatenate(
            [cond_own.reshape(-1)]
            + [
                part.astype(jnp.bfloat16).reshape(-1)
                for part in (
                    d_gate_a, d_shift_m, d_scale_m, d_gate_m, g_outbiases, g_expandbias, g_shrinkbias
                )
            ]
        )
    )
    d_projected, g_querybias, g_valuebias = attention_backward(projected, d_attended, log_totals)
    g_projector = jnp.concatenate(
        [
            reduce_depth(
                grad_dot(own, norm_a, d_projected, 0, 2, depth_pieces, "projector_grad_qk"),
                ("y", "x", "z2", "z1"),
            ),
            reduce_depth(
                grad_dot(own, norm_a, d_projected, 2, 1, depth_pieces, "projector_grad_v"),
                ("x", "y", "z2", "z1"),
            ),
        ],
        axis=1,
    )
    d_norm_a = backward_dot(d_projected, *proj_at, jnp.float32, "project_back")
    _, norm_pull_a = jax.vjp(modulate, resid_in, shift_a, scale_a)
    d_in_norm, d_shift_a, d_scale_a = norm_pull_a(d_norm_a.reshape(seqs_dev, seq_len, feature))
    latents_grad = d_middle + d_in_norm
    late = gather_relative(
        jnp.concatenate(
            [
                part.astype(jnp.bfloat16).reshape(-1)
                for part in (d_shift_a, d_scale_a, g_querybias, g_valuebias)
            ]
        )
    )

    devices = reps * shards
    size = seqs_dev * feature
    cond_all = early[:, :size].reshape(devices * seqs_dev, feature)
    cond_all = lax.dynamic_slice_in_dim(cond_all, shard_id * own_rows, own_rows, 1)
    d_mod = jnp.stack(
        [late[:, i * size : (i + 1) * size] for i in range(2)]
        + [early[:, i * size : (i + 1) * size] for i in range(1, 5)],
        axis=1,
    )
    d_mod = d_mod.reshape(devices, 6, seqs_dev, feature).transpose(0, 2, 1, 3)
    d_mod = d_mod.reshape(devices * seqs_dev, 6 * feature)
    bias_grads = []
    for source, start, width in (
        (late, 2 * size, feature),
        (late, 2 * size + feature, feature),
        (early, 5 * size, feature),
        (early, 5 * size + feature, expandbias.shape[0] * shards),
        (early, 5 * size + feature + expandbias.shape[0] * shards, feature),
    ):
        part = width // shards
        own_part = lax.dynamic_slice_in_dim(source, start + shard_id * part, part, 1)
        bias_grads.append(jnp.sum(own_part, axis=0, dtype=jnp.float32))
    g_modbias = jnp.sum(
        lax.dynamic_slice_in_dim(d_mod, shard_id * own_bias, own_bias, 1), axis=0, dtype=jnp.float32
    )
    g_modulator = jnp.einsum("sr,sc->rc", cond_all, d_mod, preferred_element_type=jnp.float32)
    own_mod = d_mod.reshape(shards, reps, seqs_dev, 6 * feature)[:, 0].reshape(-1, 6 * feature)
    d_cond_act = jnp.einsum("sc,rc->sr", own_mod, modulator, preferred_element_type=jnp.float32)
    d_cond_act = jnp.stack(to_absolute(d_cond_act.reshape(shards, seqs_dev, own_rows), shard_id))
    d_cond_act = d_cond_act.reshape(shards * seqs_dev, own_rows)
    _, silu_pull = jax.vjp(jax.nn.silu, cond_slice)
    conditions_grad = silu_pull(d_cond_act)[0]
    return (
        layer_out,
        latents_grad,
        conditions_grad,
        g_modulator,
        g_modbias,
        g_projector,
        bias_grads[0],
        bias_grads[1],
        g_outweight,
        bias_grads[2],
        g_expander,
        bias_grads[3],
        g_shrinker,
        bias_grads[4],
    )


def solution(mesh):
    return jax.shard_map(
        on_device,
        mesh=mesh,
        in_specs=(
            P(("rep", "fsdp"), None, None),
            P("rep", None),
            P("fsdp", None),
            P("fsdp"),
            P("fsdp", None),
            P("fsdp"),
            P("fsdp"),
            P("fsdp", None),
            P("fsdp"),
            P("fsdp", None),
            P("fsdp"),
            P("fsdp", None),
            P("fsdp"),
            P(("rep", "fsdp"), None, None),
        ),
        out_specs=(
            P(("rep", "fsdp"), None, None),
            P(("rep", "fsdp"), None, None),
            P("rep", "fsdp"),
            P("fsdp", None),
            P("fsdp"),
            P("fsdp", None),
            P("fsdp"),
            P("fsdp"),
            P("fsdp", None),
            P("fsdp"),
            P("fsdp", None),
            P("fsdp"),
            P("fsdp", None),
            P("fsdp"),
        ),
        check_vma=False,
    )
```

time: 950 us -> 732 us (0.77)
  matrix products: 260 us -> 3.12 us
  Pallas kernels: 0 us -> 229 us
  local copies, waits for them, and re-layouts: 141 us -> 51.9 us
  blocking collectives: 86.1 us -> 0 us
  waiting for transfers between devices: 356 us -> 303 us
  starting transfers between devices: 7.66 us -> 47 us
    dot_general x68 -> x0, matrix products: 255 us -> none  [the longest x1 27.2 us: on_device(): jnp.einsum('nd,fd->nf', d_branch_m, w_shrink, preferred_element_type=jnp....]
    pallas_call x0 -> x10, Pallas kernels: none -> 229 us  [the longest x1 74.3 us: feed_forward(): pl.pallas_call(partial(feed_forward_kernel, depth_pieces, unit_pieces), g...]
    ppermute x0 -> x50, waiting for transfers between devices: none -> 202 us  [exchange(): return lax.ppermute(value, ('rep', 'fsdp'), pairs)]
    reduce_scatter x4 -> x0, waiting for transfers between devices: 196 us -> none  [scatter_rows(): lax.psum_scatter(grad.astype(jnp.bfloat16), ('fsdp', 'rep'), scatter_dime...]
    all_gather x3 -> x0, blocking collectives: 86.1 us -> none  [the longest x1 71.3 us: on_device(): gathered = lax.all_gather(small, ('rep', 'fsdp'), axis=0, tiled=False)]
    all_gather x6 -> x2, waiting for transfers between devices: 160 us -> 93.2 us  [gather_packed(): full = lax.all_gather(packed, ('fsdp', 'rep'), axis=0, tiled=True)]
    dynamic_slice x53 -> x4, local copies, waits for them, and re-layouts: 54 us -> 3.85 us  [own_quarter(): lax.dynamic_slice_in_dim(weight, lax.axis_index('rep') * part, part, 0)]
    ppermute x0 -> x50, starting transfers between devices: none -> 39.5 us  [exchange(): return lax.ppermute(value, ('rep', 'fsdp'), pairs)]
  transfers between devices with their start and end apart: 11 -> 53, of which waited for: 8 -> 28; matrix products, arithmetic and copies ran while one was open for 45% -> 12% of each run, Pallas kernels for 0% -> 10%
where the time goes in v2:
time: 732 us; the launch traced here: 727 us
  waiting for transfers between devices  303 us (41%)
  Pallas kernels  229 us (31%)
  other arithmetic  77.8 us (11%)
  local copies, waits for them, and re-layouts  51.9 us (7%)
  starting transfers between devices  47 us (6%)
  between operations  15.7 us (2%)
    ppermute x50, waiting for transfers between devices, exchange(): return lax.ppermute(value, ('rep', 'fsdp'), pairs)  202 us
    all_gather x2, waiting for transfers between devices, gather_packed(): full = lax.all_gather(packed, ('fsdp', 'rep'), axis=0, tiled=True)  93.2 us
    pallas_call x1, Pallas kernels, feed_forward(): pl.pallas_call(partial(feed_forward_kernel, depth_pieces, unit_pieces), g...  74.3 us
    pallas_call x1, Pallas kernels, attention_backward(): pl.pallas_call(attention_backward_kernel, grid=(pairs,), in_specs=[block,...  59.8 us
    pallas_call x1, Pallas kernels, attention_forward(): pl.pallas_call(attention_forward_kernel, grid=(pairs,), in_specs=[pl.Bloc...  49.4 us
    ppermute x50, starting transfers between devices, exchange(): return lax.ppermute(value, ('rep', 'fsdp'), pairs)  39.5 us
    unnamed x138, local copies, waits for them, and re-layouts  30 us
    pallas_call x2, Pallas kernels, backward_dot(): pl.pallas_call(backward_dot_kernel, grid=(groups * per,), in_specs=[pl.Bl...  16.1 us
  transfers between devices with their start and end apart: 53, of which 28 were waited for; matrix products, arithmetic and copies ran while one was open for 12% of the time, Pallas kernels for 10%

profile of v2, /device:TPU:0, one launch (start us, length us, event | category | flops | bytes accessed | tf_op | source)
XLA Modules:
  0.0 727.3 jit_solution(5171248873622987410)
XLA Ops:
  16.2 7.5 %all-to-all-start = ((f32[8,1,7936]{2,1,0:T(1,128)}), f32[8,1,7936]{2,1,0:T(1,128)S(1)}, u32[]{:S(2)}, u32[]{:S(2)}) async-start(f32[8,1,7936]{2,1,0:T(1,128)} %copy.66), calls=%async_computation | async-start | bytes 507904 | tf_op jit(solution)/shard_map/all_to_all | solution.py:533
  29.7 7.4 %all-to-all-done = f32[8,1,7936]{2,1,0:T(1,128)S(1)} async-done(((f32[8,1,7936]{2,1,0:T(1,128)}), f32[8,1,7936]{2,1,0:T(1,128)S(1)}, u32[]{:S(2)}, u32[]{:S(2)}) %all-to-all-start) | async-done | bytes 253984 | tf_op jit(solution)/shard_map/all_to_all | solution.py:533
  38.6 3.7 fusion.21.x_ref
  42.3 52.0 %all-gather.3.cloned.1.call-done = bf16[4096,1024]{1,0:T(8,128)(2,1)} async-done(((bf16[128,1024]{1,0:T(8,128)(2,1)}), bf16[4096,1024]{1,0:T(8,128)(2,1)}) %all-gather.3.cloned.1.call-update) | async-done | bytes 8388624 | tf_op jit(solution)/shard_map/all_gather | solution.py:458
  95.9 9.3 %project.1.q_ref.k_ref.v_ref = bf16[1024,3072]{1,0:T(8,128)(2,1)S(1)} custom-call(bf16[1024,1024]{1,0:T(8,128)(2,1)S(1)} %copy-done.4, bf16[32,4,32,1024]{3,2,1,0:T(8,128)(2,1)} %bitcast.269, f32[1,3072]{1,0:T(1,128)S(1)} %pad_maximum_fusion.8.b_ref), custom_call_target="tpu_custom_call" | custom-call | flops 6442450944 | bytes 12582912 | tf_op jit(solution)/shard_map/project/pallas_call | solution.py:62
  108.0 49.4 %attention_forward.1 = (bf16[1024,1024]{1,0:T(8,128)(2,1)S(1)}, f32[8,2,1024]{2,1,0:T(2,128)S(1)}) custom-call(bf16[1024,3072]{1,0:T(8,128)(2,1)} %copy-done.19, bf16[1024,3072]{1,0:T(8,128)(2,1)} %copy-done.19, bf16[1024,3072]{1,0:T(8,128)(2,1)} %copy-done.19), custom_call_target="tpu_custom_call" | custom-call | flops 17179869184 | bytes 8388608 | tf_op jit(solution)/shard_map/attention_forward/pallas_call | solution.py:284
  157.5 5.0 attention_out.1
  170.1 41.2 %all-gather.5.cloned.1.call-done = bf16[8192,1024]{1,0:T(8,128)(2,1)} async-done(((bf16[256,1024]{1,0:T(8,128)(2,1)}), bf16[8192,1024]{1,0:T(8,128)(2,1)}) %all-gather.5.cloned.1.call-update) | async-done | bytes 16777232 | tf_op jit(solution)/shard_map/all_gather | solution.py:458
  211.3 74.3 %feed_forward.1 = (f32[1024,1024]{1,0:T(8,128)}, f32[1024,1024]{1,0:T(8,128)}, bf16[512,4096]{1,0:T(8,128)(2,1)}, bf16[512,4096]{1,0:T(8,128)(2,1)}, bf16[2048,1...) custom-call(s32[4]{0:T(128)} %pad_add_fusion.own_ref, ...), custom_call_target="tpu_custom_call" | custom-call | flops 51539607552 | bytes 67108864 | tf_op jit(solution)/shard_map/feed_forward/pallas_call | solution.py:233
  293.2 4.1 attention_out_back.1.g_ref
  297.3 59.8 %attention_backward.1 = (bf16[3,1024,1024]{2,1,0:T(8,128)(2,1)}, f32[1,1024]{1,0:T(1,128)S(1)}, f32[1,1024]{1,0:T(1,128)S(1)}) custom-call(bf16[1024,3072]{1,0:T(8,128)(2,1)} %copy-done.19, bf16[1024,3072]{1,0:T(8,128)(2,1)} %copy-done.19, bf16[1024,3072]{1,0:T(8,128)(2,1)} %copy-done.19, bf16[1024,1024]{1,0:T(8,128)(2,1)S(1)} %attention_out_back.1.g_ref, ...), custom_call_target="tpu_custom_call" | custom-call | flops 42949672960 | bytes 16777216 | tf_op jit(solution)/shard_map/attention_backward/pallas_call | solution.py:353
  360.0 7.1 projector_grad_qk.1
  368.4 12.1 %project_back.1 = f32[1024,1024]{1,0:T(8,128)S(1)} custom-call(bf16[3,1024,1024]{2,1,0:T(8,128)(2,1)S(1)} %copy-done.9, bf16[32,4,32,1024]{3,2,1,0:T(8,128)(2,1)} %bitcast.271), custom_call_target="tpu_custom_call" | custom-call | flops 6442450944 | bytes 4194304 | tf_op jit(solution)/shard_map/project_back/pallas_call | solution.py:100
  391.2 4.7 fusion.8
  396.5 10.4 %fusion.12 = (bf16[1024]{0:T(1024)(128)(2,1)S(1)}, bf16[1024]{0:T(1024)(128)(2,1)S(1)}, f32[1,1024,1024]{2,1,0:T(8,128)}, f32[1,1024,1024]{2,1,0:T(8,128)}) fusion(bf16[1,1024,1024]{2,1,0:T(8,128)(2,1)} %param.27, f32[1024,1024]{1,0:T(8,128)} %get-tuple-element.33, f32[1024]{0:T(1024)S(1)} %copy-done.48, f32[1024,1024]{1,0:T(8,128)} %copy-done.3, ...), kind=kLoop, calls=%fused_computation.22 | loop fusion | flops 19920896 | bytes 33591296 | tf_op jit(solution)/shard_map/reduce_sum | solution.py:565
  417.4 4.3 outweight_grad.1
  442.8 16.7 %collective-permute-done.9 = bf16[16,11264]{1,0:T(8,128)(2,1)} collective-permute-done((bf16[16,11264]{1,0:T(8,128)(2,1)}, bf16[16,11264]{1,0:T(8,128)(2,1)}, u32[]{:S(2)}, u32[]{:S(2)}) %collective-permute-start.9) | collective-permute-done | bytes 360480 | tf_op jit(solution)/shard_map/ppermute | solution.py:389
  459.5 4.9 concatenate.100
  479.8 10.9 %collective-permute-done.27 = bf16[2,2,2,32,1024]{4,3,1,0,2:T(8,128)(2,1)S(1)} collective-permute-done((bf16[2,2,2,32,1024]{4,3,1,0,2:T(8,128)(2,1)S(1)}, bf16[2,2,2,32,1024]{4,3,1,0,2:T(8,128)(2,1)S(1)}, u32[]{:S(2)}, u32[]{:S(2)}) %collective-permute-start.27) | collective-permute-done | bytes 524320 | tf_op jit(solution)/shard_map/ppermute | solution.py:389
  491.9 9.7 %collective-permute-done.19 = bf16[2,2,2,32,1024]{4,3,1,0,2:T(8,128)(2,1)S(1)} collective-permute-done((bf16[2,2,2,32,1024]{4,3,1,0,2:T(8,128)(2,1)S(1)}, bf16[2,2,2,32,1024]{4,3,1,0,2:T(8,128)(2,1)S(1)}, u32[]{:S(2)}, u32[]{:S(2)}) %collective-permute-start.19) | collective-permute-done | bytes 524320 | tf_op jit(solution)/shard_map/ppermute | solution.py:389
  502.9 6.9 collective-permute-done.20
  519.2 18.0 %collective-permute-done.11 = bf16[2,2,2,32,2048]{4,3,1,0,2:T(8,128)(2,1)S(1)} collective-permute-done((bf16[2,2,2,32,2048]{4,3,1,0,2:T(8,128)(2,1)S(1)}, bf16[2,2,2,32,2048]{4,3,1,0,2:T(8,128)(2,1)S(1)}, u32[]{:S(2)}, u32[]{:S(2)}) %collective-permute-start.11) | collective-permute-done | bytes 1048608 | tf_op jit(solution)/shard_map/ppermute | solution.py:389
  553.3 4.2 convert_add_fusion
  575.2 31.6 %collective-permute-done.43 = bf16[2,2,2,128,1024]{4,3,1,0,2:T(8,128)(2,1)} collective-permute-done((bf16[2,2,2,128,1024]{4,3,1,0,2:T(8,128)(2,1)}, bf16[2,2,2,128,1024]{4,3,1,0,2:T(8,128)(2,1)}, u32[]{:S(2)}, u32[]{:S(2)}) %collective-permute-start.43) | collective-permute-done | bytes 2097184 | tf_op jit(solution)/shard_map/ppermute | solution.py:389
  610.7 3.7 collective-permute-done.35
  620.1 20.7 %collective-permute-done.44 = bf16[2,2,128,1024]{3,2,1,0:T(8,128)(2,1)S(1)} collective-permute-done((bf16[2,2,128,1024]{3,2,1,0:T(8,128)(2,1)S(1)}, bf16[2,2,128,1024]{3,2,1,0:T(8,128)(2,1)S(1)}, u32[]{:S(2)}, u32[]{:S(2)}) %collective-permute-start.44) | collective-permute-done | bytes 1048608 | tf_op jit(solution)/shard_map/ppermute | solution.py:389
  644.6 31.5 %collective-permute-done.45 = bf16[2,128,1024]{2,1,0:T(8,128)(2,1)S(1)} collective-permute-done((bf16[2,128,1024]{2,1,0:T(8,128)(2,1)S(1)}, bf16[2,128,1024]{2,1,0:T(8,128)(2,1)S(1)}, u32[]{:S(2)}, u32[]{:S(2)}) %collective-permute-start.45) | collective-permute-done | bytes 524320 | tf_op jit(solution)/shard_map/ppermute | solution.py:389
  676.4 10.9 %collective-permute-done.37 = bf16[2,32,4096]{2,1,0:T(8,128)(2,1)S(1)} collective-permute-done((bf16[2,32,4096]{2,1,0:T(8,128)(2,1)S(1)}, bf16[2,32,4096]{2,1,0:T(8,128)(2,1)S(1)}, u32[]{:S(2)}, u32[]{:S(2)}) %collective-permute-start.37) | collective-permute-done | bytes 524320 | tf_op jit(solution)/shard_map/ppermute | solution.py:389
  688.9 4.1 collective-permute-done.46
  701.7 5.7 collective-permute-done.48
  709.1 3.7 collective-permute-done.39
  712.8 5.7 collective-permute-done.40
  (368 shorter events, 170.1 us)
Async XLA Ops:
  7.3 87.1 %all-gather.3.cloned.1.call-start = ((), (), s32[]{:S(2)}) async-start(), calls=%async_computation.1 | async-start | bytes 8650752 | tf_op jit(solution)/shard_map/all_gather | solution.py:458
  10.3 200.9 %all-gather.5.cloned.1.call-start = ((), (), s32[]{:S(2)}) async-start(), calls=%async_computation.2 | async-start | bytes 17301504 | tf_op jit(solution)/shard_map/all_gather | solution.py:458
  16.2 21.0 %all-to-all-start = ((f32[8,1,7936]{2,1,0:T(1,128)}), f32[8,1,7936]{2,1,0:T(1,128)S(1)}, u32[]{:S(2)}, u32[]{:S(2)}) async-start(f32[8,1,7936]{2,1,0:T(1,128)} %copy.66), calls=%async_computation | async-start | bytes 507904 | tf_op jit(solution)/shard_map/all_to_all | solution.py:533
  421.8 128.9 %collective-permute-start.42 = (bf16[2048,1024]{1,0:T(8,128)(2,1)}, bf16[2048,1024]{1,0:T(8,128)(2,1)}, u32[]{:S(2)}, u32[]{:S(2)}) collective-permute-start(bf16[2048,1024]{1,0:T(8,128)(2,1)} %get-tuple-element.49), channel_id=1, source_target_pairs={{0,8},{1,9},{2,10},{3,11},{4,12},{5,13},{6,14},{7,15},{8,0},{9,1},... | collective-permute-start | bytes 12582920 | tf_op jit(solution)/shard_map/ppermute | solution.py:389
  421.8 137.4 %collective-permute-start.34 = (bf16[512,4096]{1,0:T(8,128)(2,1)}, bf16[512,4096]{1,0:T(8,128)(2,1)}, u32[]{:S(2)}, u32[]{:S(2)}) collective-permute-start(bf16[512,4096]{1,0:T(8,128)(2,1)} %get-tuple-element.47), channel_id=1, source_target_pairs={{0,8},{1,9},{2,10},{3,11},{4,12},{5,13},{6,14},{7,15},{8,0},{9,1},... | collective-permute-start | bytes 12582920 | tf_op jit(solution)/shard_map/ppermute | solution.py:389
  422.3 52.0 %collective-permute-start.26 = (bf16[512,1024]{1,0:T(8,128)(2,1)}, bf16[512,1024]{1,0:T(8,128)(2,1)}, u32[]{:S(2)}, u32[]{:S(2)}) collective-permute-start(bf16[512,1024]{1,0:T(8,128)(2,1)} %get-tuple-element.45), channel_id=1, source_target_pairs={{0,8},{1,9},{2,10},{3,11},{4,12},{5,13},{6,14},{7,15},{8,0},{9,1},... | collective-permute-start | bytes 3145736 | tf_op jit(solution)/shard_map/ppermute | solution.py:389
  436.5 73.5 %collective-permute-start.10 = (bf16[512,2048]{1,0:T(8,128)(2,1)}, bf16[512,2048]{1,0:T(8,128)(2,1)}, u32[]{:S(2)}, u32[]{:S(2)}) collective-permute-start(bf16[512,2048]{1,0:T(8,128)(2,1)} %get-tuple-element.41), channel_id=1, source_target_pairs={{0,8},{1,9},{2,10},{3,11},{4,12},{5,13},{6,14},{7,15},{8,0},{9,1},... | collective-permute-start | bytes 6291464 | tf_op jit(solution)/shard_map/ppermute | solution.py:389
  439.7 19.8 %collective-permute-start.9 = (bf16[16,11264]{1,0:T(8,128)(2,1)}, bf16[16,11264]{1,0:T(8,128)(2,1)}, u32[]{:S(2)}, u32[]{:S(2)}) collective-permute-start(bf16[16,11264]{1,0:T(8,128)(2,1)} %concatenate.99), channel_id=1, source_target_pairs={{0,4},{1,5},{2,6},{3,7},{4,0},{5,1},{6,2},{7,3},{8,12},{9,13},{10,... | collective-permute-start | bytes 1081352 | tf_op jit(solution)/shard_map/ppermute | solution.py:389
  459.5 17.3 %collective-permute-start.18 = (bf16[512,1024]{1,0:T(8,128)(2,1)}, bf16[512,1024]{1,0:T(8,128)(2,1)}, u32[]{:S(2)}, u32[]{:S(2)}) collective-permute-start(bf16[512,1024]{1,0:T(8,128)(2,1)} %copy-done.18), channel_id=1, source_target_pairs={{0,8},{1,9},{2,10},{3,11},{4,12},{5,13},{6,14},{7,15},{8,0},{9,1},... | collective-permute-start | bytes 3145736 | tf_op jit(solution)/shard_map/ppermute | solution.py:389
  475.9 14.8 %collective-permute-start.27 = (bf16[2,2,2,32,1024]{4,3,1,0,2:T(8,128)(2,1)S(1)}, bf16[2,2,2,32,1024]{4,3,1,0,2:T(8,128)(2,1)S(1)}, u32[]{:S(2)}, u32[]{:S(2)}) collective-permute-start(bf16[2,2,2,32,1024]{4,3,1,0,2:T(8,128)(2,1)S(1)} %fusion.39), channel_id=1, source_target_pairs={{0,1},{1,0},{2,3},{3,2},{4,5},{5,4},{6,7},{7,6},{8,9},{9,8},{10,11... | collective-permute-start | bytes 1572872 | tf_op jit(solution)/shard_map/ppermute | solution.py:389
  478.5 23.1 %collective-permute-start.19 = (bf16[2,2,2,32,1024]{4,3,1,0,2:T(8,128)(2,1)S(1)}, bf16[2,2,2,32,1024]{4,3,1,0,2:T(8,128)(2,1)S(1)}, u32[]{:S(2)}, u32[]{:S(2)}) collective-permute-start(bf16[2,2,2,32,1024]{4,3,1,0,2:T(8,128)(2,1)S(1)} %fusion.38), channel_id=1, source_target_pairs={{0,1},{1,0},{2,3},{3,2},{4,5},{5,4},{6,7},{7,6},{8,9},{9,8},{10,11... | collective-permute-start | bytes 1572872 | tf_op jit(solution)/shard_map/ppermute | solution.py:389
  512.5 24.7 %collective-permute-start.11 = (bf16[2,2,2,32,2048]{4,3,1,0,2:T(8,128)(2,1)S(1)}, bf16[2,2,2,32,2048]{4,3,1,0,2:T(8,128)(2,1)S(1)}, u32[]{:S(2)}, u32[]{:S(2)}) collective-permute-start(bf16[2,2,2,32,2048]{4,3,1,0,2:T(8,128)(2,1)S(1)} %fusion.29), channel_id=1, source_target_pairs={{0,16},{1,17},{2,18},{3,19},{4,20},{5,21},{6,22},{7,23},{8,24},{9,... | collective-permute-start | bytes 3145736 | tf_op jit(solution)/shard_map/ppermute | solution.py:389
  517.2 25.7 %collective-permute-start.22 = (bf16[32,1024]{1,0:T(8,128)(2,1)S(1)}, bf16[32,1024]{1,0:T(8,128)(2,1)S(1)}, u32[]{:S(2)}, u32[]{:S(2)}) collective-permute-start(bf16[32,1024]{1,0:T(8,128)(2,1)S(1)} %fusion.66), channel_id=1, source_target_pairs={{0,2},{1,3},{2,0},{3,1},{4,6},{5,7},{6,4},{7,5},{8,10},{9,11},{10,... | collective-permute-start | bytes 196616 | tf_op jit(solution)/shard_map/ppermute | solution.py:389
  518.5 25.8 %collective-permute-start.31 = (bf16[32,1024]{1,0:T(8,128)(2,1)S(1)}, bf16[32,1024]{1,0:T(8,128)(2,1)S(1)}, u32[]{:S(2)}, u32[]{:S(2)}) collective-permute-start(bf16[32,1024]{1,0:T(8,128)(2,1)S(1)} %fusion.60), channel_id=1, source_target_pairs={{0,24},{1,25},{2,26},{3,27},{4,28},{5,29},{6,30},{7,31},{8,16},{9,... | collective-permute-start | bytes 196616 | tf_op jit(solution)/shard_map/ppermute | solution.py:389
  547.1 21.1 %collective-permute-start.23 = (bf16[32,1024]{1,0:T(8,128)(2,1)}, bf16[32,1024]{1,0:T(8,128)(2,1)}, u32[]{:S(2)}, u32[]{:S(2)}) collective-permute-start(bf16[32,1024]{1,0:T(8,128)(2,1)} %fusion.62), channel_id=1, source_target_pairs={{0,24},{1,25},{2,26},{3,27},{4,28},{5,29},{6,30},{7,31},{8,16},{9,... | collective-permute-start | bytes 196616 | tf_op jit(solution)/shard_map/ppermute | solution.py:389
  547.1 21.2 %collective-permute-start.24 = (bf16[32,1024]{1,0:T(8,128)(2,1)}, bf16[32,1024]{1,0:T(8,128)(2,1)}, u32[]{:S(2)}, u32[]{:S(2)}) collective-permute-start(bf16[32,1024]{1,0:T(8,128)(2,1)} %fusion.62), channel_id=1, source_target_pairs={{0,16},{1,17},{2,18},{3,19},{4,20},{5,21},{6,22},{7,23},{8,24},{9,... | collective-permute-start | bytes 196616 | tf_op jit(solution)/shard_map/ppermute | solution.py:389
  549.4 19.0 %collective-permute-start.25 = (bf16[32,1024]{1,0:T(8,128)(2,1)}, bf16[32,1024]{1,0:T(8,128)(2,1)}, u32[]{:S(2)}, u32[]{:S(2)}) collective-permute-start(bf16[32,1024]{1,0:T(8,128)(2,1)} %fusion.62), channel_id=1, source_target_pairs={{0,8},{1,9},{2,10},{3,11},{4,12},{5,13},{6,14},{7,15},{8,0},{9,1},... | collective-permute-start | bytes 196616 | tf_op jit(solution)/shard_map/ppermute | solution.py:389
  550.7 15.2 %collective-permute-start.13 = (bf16[2,32,2048]{2,1,0:T(8,128)(2,1)}, bf16[2,32,2048]{2,1,0:T(8,128)(2,1)}, u32[]{:S(2)}, u32[]{:S(2)}) collective-permute-start(bf16[2,32,2048]{2,1,0:T(8,128)(2,1)} %fusion.47), channel_id=1, source_target_pairs={{0,4},{1,5},{2,6},{3,7},{4,0},{5,1},{6,2},{7,3},{8,12},{9,13},{10,... | collective-permute-start | bytes 786440 | tf_op jit(solution)/shard_map/ppermute | solution.py:389
  559.1 47.7 %collective-permute-start.43 = (bf16[2,2,2,128,1024]{4,3,1,0,2:T(8,128)(2,1)}, bf16[2,2,2,128,1024]{4,3,1,0,2:T(8,128)(2,1)}, u32[]{:S(2)}, u32[]{:S(2)}) collective-permute-start(bf16[2,2,2,128,1024]{4,3,1,0,2:T(8,128)(2,1)} %fusion.20), channel_id=1, source_target_pairs={{0,1},{1,0},{2,3},{3,2},{4,5},{5,4},{6,7},{7,6},{8,9},{9,8},{10,11... | collective-permute-start | bytes 6291464 | tf_op jit(solution)/shard_map/ppermute | solution.py:389
  565.9 48.6 %collective-permute-start.35 = (bf16[2,2,2,32,4096]{4,3,1,0,2:T(8,128)(2,1)S(1)}, bf16[2,2,2,32,4096]{4,3,1,0,2:T(8,128)(2,1)S(1)}, u32[]{:S(2)}, u32[]{:S(2)}) collective-permute-start(bf16[2,2,2,32,4096]{4,3,1,0,2:T(8,128)(2,1)S(1)} %fusion.19), channel_id=1, source_target_pairs={{0,16},{1,17},{2,18},{3,19},{4,20},{5,21},{6,22},{7,23},{8,24},{9,... | collective-permute-start | bytes 6291464 | tf_op jit(solution)/shard_map/ppermute | solution.py:389
  573.3 43.2 %collective-permute-start.15 = (bf16[32,2048]{1,0:T(8,128)(2,1)S(1)}, bf16[32,2048]{1,0:T(8,128)(2,1)S(1)}, u32[]{:S(2)}, u32[]{:S(2)}) collective-permute-start(bf16[32,2048]{1,0:T(8,128)(2,1)S(1)} %fusion.55), channel_id=1, source_target_pairs={{0,24},{1,25},{2,26},{3,27},{4,28},{5,29},{6,30},{7,31},{8,16},{9,... | collective-permute-start | bytes 393224 | tf_op jit(solution)/shard_map/ppermute | solution.py:389
  573.4 46.7 %collective-permute-start.16 = (bf16[32,2048]{1,0:T(8,128)(2,1)S(1)}, bf16[32,2048]{1,0:T(8,128)(2,1)S(1)}, u32[]{:S(2)}, u32[]{:S(2)}) collective-permute-start(bf16[32,2048]{1,0:T(8,128)(2,1)S(1)} %fusion.55), channel_id=1, source_target_pairs={{0,16},{1,17},{2,18},{3,19},{4,20},{5,21},{6,22},{7,23},{8,24},{9,... | collective-permute-start | bytes 393224 | tf_op jit(solution)/shard_map/ppermute | solution.py:389
  574.2 45.9 %collective-permute-start.17 = (bf16[32,2048]{1,0:T(8,128)(2,1)S(1)}, bf16[32,2048]{1,0:T(8,128)(2,1)S(1)}, u32[]{:S(2)}, u32[]{:S(2)}) collective-permute-start(bf16[32,2048]{1,0:T(8,128)(2,1)S(1)} %fusion.55), channel_id=1, source_target_pairs={{0,8},{1,9},{2,10},{3,11},{4,12},{5,13},{6,14},{7,15},{8,0},{9,1},... | collective-permute-start | bytes 393224 | tf_op jit(solution)/shard_map/ppermute | solution.py:389
  609.3 31.5 %collective-permute-start.44 = (bf16[2,2,128,1024]{3,2,1,0:T(8,128)(2,1)S(1)}, bf16[2,2,128,1024]{3,2,1,0:T(8,128)(2,1)S(1)}, u32[]{:S(2)}, u32[]{:S(2)}) collective-permute-start(bf16[2,2,128,1024]{3,2,1,0:T(8,128)(2,1)S(1)} %fusion.28), channel_id=1, source_target_pairs={{0,16},{1,17},{2,18},{3,19},{4,20},{5,21},{6,22},{7,23},{8,24},{9,... | collective-permute-start | bytes 3145736 | tf_op jit(solution)/shard_map/ppermute | solution.py:389
  615.3 26.0 %collective-permute-start.36 = (bf16[2,2,32,4096]{3,2,1,0:T(8,128)(2,1)S(1)}, bf16[2,2,32,4096]{3,2,1,0:T(8,128)(2,1)S(1)}, u32[]{:S(2)}, u32[]{:S(2)}) collective-permute-start(bf16[2,2,32,4096]{3,2,1,0:T(8,128)(2,1)S(1)} %fusion.27), channel_id=1, source_target_pairs={{0,1},{1,0},{2,3},{3,2},{4,5},{5,4},{6,7},{7,6},{8,9},{9,8},{10,11... | collective-permute-start | bytes 3145736 | tf_op jit(solution)/shard_map/ppermute | solution.py:389
  641.2 34.9 %collective-permute-start.45 = (bf16[2,128,1024]{2,1,0:T(8,128)(2,1)S(1)}, bf16[2,128,1024]{2,1,0:T(8,128)(2,1)S(1)}, u32[]{:S(2)}, u32[]{:S(2)}) collective-permute-start(bf16[2,128,1024]{2,1,0:T(8,128)(2,1)S(1)} %fusion.37), channel_id=1, source_target_pairs={{0,4},{1,5},{2,6},{3,7},{4,0},{5,1},{6,2},{7,3},{8,12},{9,13},{10,... | collective-permute-start | bytes 1572872 | tf_op jit(solution)/shard_map/ppermute | solution.py:389
  641.6 45.8 %collective-permute-start.37 = (bf16[2,32,4096]{2,1,0:T(8,128)(2,1)S(1)}, bf16[2,32,4096]{2,1,0:T(8,128)(2,1)S(1)}, u32[]{:S(2)}, u32[]{:S(2)}) collective-permute-start(bf16[2,32,4096]{2,1,0:T(8,128)(2,1)S(1)} %fusion.36), channel_id=1, source_target_pairs={{0,4},{1,5},{2,6},{3,7},{4,0},{5,1},{6,2},{7,3},{8,12},{9,13},{10,... | collective-permute-start | bytes 1572872 | tf_op jit(solution)/shard_map/ppermute | solution.py:389
  676.3 16.6 %collective-permute-start.46 = (bf16[128,1024]{1,0:T(8,128)(2,1)S(1)}, bf16[128,1024]{1,0:T(8,128)(2,1)S(1)}, u32[]{:S(2)}, u32[]{:S(2)}) collective-permute-start(bf16[128,1024]{1,0:T(8,128)(2,1)S(1)} %fusion.51), channel_id=1, source_target_pairs={{0,2},{1,3},{2,0},{3,1},{4,6},{5,7},{6,4},{7,5},{8,10},{9,11},{10,... | collective-permute-start | bytes 786440 | tf_op jit(solution)/shard_map/ppermute | solution.py:389
  693.4 14.0 %collective-permute-start.48 = (bf16[128,1024]{1,0:T(8,128)(2,1)S(1)}, bf16[128,1024]{1,0:T(8,128)(2,1)S(1)}, u32[]{:S(2)}, u32[]{:S(2)}) collective-permute-start(bf16[128,1024]{1,0:T(8,128)(2,1)S(1)} %fusion.41), channel_id=1, source_target_pairs={{0,16},{1,17},{2,18},{3,19},{4,20},{5,21},{6,22},{7,23},{8,24},{9,... | collective-permute-start | bytes 786440 | tf_op jit(solution)/shard_map/ppermute | solution.py:389
  698.5 14.3 %collective-permute-start.39 = (bf16[32,4096]{1,0:T(8,128)(2,1)S(1)}, bf16[32,4096]{1,0:T(8,128)(2,1)S(1)}, u32[]{:S(2)}, u32[]{:S(2)}) collective-permute-start(bf16[32,4096]{1,0:T(8,128)(2,1)S(1)} %fusion.43), channel_id=1, source_target_pairs={{0,24},{1,25},{2,26},{3,27},{4,28},{5,29},{6,30},{7,31},{8,16},{9,... | collective-permute-start | bytes 786440 | tf_op jit(solution)/shard_map/ppermute | solution.py:389
  699.0 19.5 %collective-permute-start.40 = (bf16[32,4096]{1,0:T(8,128)(2,1)S(1)}, bf16[32,4096]{1,0:T(8,128)(2,1)S(1)}, u32[]{:S(2)}, u32[]{:S(2)}) collective-permute-start(bf16[32,4096]{1,0:T(8,128)(2,1)S(1)} %fusion.43), channel_id=1, source_target_pairs={{0,16},{1,17},{2,18},{3,19},{4,20},{5,21},{6,22},{7,23},{8,24},{9,... | collective-permute-start | bytes 786440 | tf_op jit(solution)/shard_map/ppermute | solution.py:389
  701.6 17.0 %collective-permute-start.41 = (bf16[32,4096]{1,0:T(8,128)(2,1)S(1)}, bf16[32,4096]{1,0:T(8,128)(2,1)S(1)}, u32[]{:S(2)}, u32[]{:S(2)}) collective-permute-start(bf16[32,4096]{1,0:T(8,128)(2,1)S(1)} %fusion.43), channel_id=1, source_target_pairs={{0,8},{1,9},{2,10},{3,11},{4,12},{5,13},{6,14},{7,15},{8,0},{9,1},... | collective-permute-start | bytes 786440 | tf_op jit(solution)/shard_map/ppermute | solution.py:389
  (80 other events, 841.8 us)
Sparse Core Ops, SparseCore 0:
  11.5 82.7 all-gather.2
  97.8 113.4 all-gather.4

commit v3 on v2

--- a/solution.py
+++ b/solution.py
@@ -11,8 +11,9 @@
 HEAD_DIM = 64
 PAIR = 2 * HEAD_DIM
 CHUNK = 256
+KEY_BLOCK = 128
 EPS_NORM = 1e-06
-ROWS = 256
+ROWS = 512
 FF_BLOCK = 512
 COL_BLOCK = 512
 GELU_ROOT = 0.7978845608028654
@@ -70,15 +71,69 @@
         out_specs=pl.BlockSpec((tokens, COL_BLOCK), lambda i: (0, i)),
         out_shape=jax.ShapeDtypeStruct((tokens, columns), dtype),
         compiler_params=kernel_params(40),
-        cost_estimate=cost(2 * tokens * depth * columns, 4 * tokens * columns),
+        cost_estimate=cost(tokens * depth * columns, tokens * columns),
         name=name,
     )(x, weight, bias)
+
+
+def project_kernel(maps, own_ref, x_ref, b_ref, *refs):
+    sources, (out_ref, full_ref) = refs[:4], refs[4:]
+    step = pl.program_id(0)
+    rows = sources[0].shape[1]
+    half = pl.num_programs(0) // 2
+    for chain in range(2):
+
+        @pl.when((step >= half) == (chain == 1))
+        def _():
+            for flip in range(2):
+                source = sources[2 * chain + flip]
+                for index, relative in enumerate(maps[chain]):
+                    place = pl.multiple_of((own_ref[0] ^ (relative ^ flip)) * rows, rows)
+                    full_ref[pl.ds(place, rows), :] = source[index]
+
+    out_ref[...] = (dot_nn(x_ref[...], full_ref[...]) + b_ref[...]).astype(out_ref.dtype)
+
+
+def project(flat, x, bias, chains, maps):
+    tokens, depth = x.shape
+    columns = bias.shape[1]
+    steps = columns // COL_BLOCK
+    half = steps // 2
+    blocks, rows, _ = chains[0][0].shape
+    first = pl.BlockSpec((blocks, rows, COL_BLOCK), lambda i, own: (0, 0, jnp.minimum(i, half - 1)))
+    second = pl.BlockSpec((blocks, rows, COL_BLOCK), lambda i, own: (0, 0, jnp.maximum(i - half, 0)))
+    return pl.pallas_call(
+        partial(project_kernel, maps),
+        grid_spec=pltpu.PrefetchScalarGridSpec(
+            num_scalar_prefetch=1,
+            grid=(steps,),
+            in_specs=[
+                pl.BlockSpec((tokens, depth), lambda i, own: (0, 0)),
+                pl.BlockSpec((1, COL_BLOCK), lambda i, own: (0, i)),
+                first,
+                first,
+                second,
+                second,
+            ],
+            out_specs=[
+                pl.BlockSpec((tokens, COL_BLOCK), lambda i, own: (0, i)),
+                pl.BlockSpec((depth, COL_BLOCK), lambda i, own: (0, i)),
+            ],
+        ),
+        out_shape=[
+            jax.ShapeDtypeStruct((tokens, columns), jnp.bfloat16),
+            jax.ShapeDtypeStruct((depth, columns), jnp.bfloat16),
+        ],
+        compiler_params=kernel_params(40),
+        cost_estimate=cost(tokens * depth * columns, tokens * columns),
+        name="project",
+    )(flat, x, bias, *chains[0], *chains[1])
 
 
 def backward_dot_kernel(dy_ref, w_ref, out_ref, sum_ref):
     step = pl.program_id(0)
     weight = w_ref[...].reshape(out_ref.shape[1], w_ref.shape[-1])
-    part = dot_nt(dy_ref[0], weight)
+    part = dot_nt(dy_ref[...], weight)
 
     @pl.when(step == 0)
     def _():
@@ -94,23 +149,54 @@
 
 
 def backward_dot(dy, weight, first, dtype, name):
-    groups, tokens, columns = dy.shape
+    tokens, columns = dy.shape
     depth = columns
-    per = columns // COL_BLOCK
     return pl.pallas_call(
         backward_dot_kernel,
-        grid=(groups * per,),
+        grid=(columns // COL_BLOCK,),
         in_specs=[
-            pl.BlockSpec((1, tokens, COL_BLOCK), lambda i: (i // per, 0, i % per)),
+            pl.BlockSpec((tokens, COL_BLOCK), lambda i: (0, i)),
             weight_spec(weight, first, COL_BLOCK, lambda i: i),
         ],
         out_specs=pl.BlockSpec((tokens, depth), lambda i: (0, 0)),
         out_shape=jax.ShapeDtypeStruct((tokens, depth), dtype),
         scratch_shapes=[pltpu.VMEM((tokens, depth), jnp.float32)],
         compiler_params=kernel_params(40),
-        cost_estimate=cost(2 * groups * tokens * depth * columns, 4 * tokens * columns),
+        cost_estimate=cost(tokens * depth * columns, tokens * columns),
         name=name,
     )(dy, weight)
+
+
+def project_back_kernel(low_ref, high_ref, w_ref, out_ref):
+    step = pl.program_id(0)
+
+    @pl.when(step == 0)
+    def _():
+        out_ref[...] = dot_nt(low_ref[0], w_ref[...])
+
+    @pl.when((step > 0) & (step % 2 == 0))
+    def _():
+        out_ref[...] += dot_nt(low_ref[0], w_ref[...])
+
+    @pl.when(step % 2 == 1)
+    def _():
+        out_ref[...] += dot_nt(high_ref[0], w_ref[...])
+
+
+def project_back(low, high, weight):
+    groups, tokens, width = low.shape
+    depth = weight.shape[0]
+    block = pl.BlockSpec((1, tokens, width), lambda i: (i // 2, 0, 0))
+    return pl.pallas_call(
+        project_back_kernel,
+        grid=(2 * groups,),
+        in_specs=[block, block, pl.BlockSpec((depth, width), lambda i: (0, i))],
+        out_specs=pl.BlockSpec((tokens, depth), lambda i: (0, 0)),
+        out_shape=jax.ShapeDtypeStruct((tokens, depth), jnp.float32),
+        compiler_params=kernel_params(40),
+        cost_estimate=cost(groups * tokens * depth * width, tokens * width),
+        name="project_back",
+    )(low, high, weight)
 
 
 def store_rows(total, own_core, own_slot, pieces, keep_ref, send_ref):
@@ -129,9 +215,9 @@
     store_rows(total, own_ref[0], own_ref[1], pieces, keep_ref, send_ref)
 
 
-def grad_dot(own, x, dy, first, groups, pieces, name):
+def grad_dot(own, x, dy, pieces, name):
     tokens, depth = x.shape
-    columns = dy.shape[2]
+    groups, _, columns = dy.shape
     per = columns // COL_BLOCK
     half = jax.ShapeDtypeStruct((depth // 2, groups * columns), jnp.bfloat16)
     block = pl.BlockSpec((depth // 2, COL_BLOCK), lambda i, own: (0, i))
@@ -142,13 +228,13 @@
             grid=(groups * per,),
             in_specs=[
                 pl.BlockSpec((tokens, depth), lambda i, own: (0, 0)),
-                pl.BlockSpec((1, tokens, COL_BLOCK), lambda i, own: (first + i // per, 0, i % per)),
+                pl.BlockSpec((1, tokens, COL_BLOCK), lambda i, own: (i // per, 0, i % per)),
             ],
             out_specs=[block, block],
         ),
         out_shape=[half, half],
         compiler_params=kernel_params(40),
-        cost_estimate=cost(2 * groups * tokens * depth * columns, 4 * tokens * columns),
+        cost_estimate=cost(groups * tokens * depth * columns, tokens * columns),
         name=name,
     )(own, x, dy)
 
@@ -186,9 +272,19 @@
         d_norm_ref[...] = jnp.zeros_like(d_norm_ref)
 
     bias_sum = jnp.zeros((1, units), jnp.float32)
-    for start in range(0, tokens, ROWS):
+    starts = list(range(0, tokens, ROWS))
+
+    def entering(start):
         rows = slice(start, start + ROWS)
-        pre = dot_nn(norm_ref[rows, :], expand) + bias_ref[...]
+        return dot_nn(norm_ref[rows, :], expand), dot_nt(grad_ref[rows, :], shrink)
+
+    upcoming = entering(starts[0])
+    for number, start in enumerate(starts):
+        rows = slice(start, start + ROWS)
+        pre, d_unit = upcoming
+        if number + 1 < len(starts):
+            upcoming = entering(starts[number + 1])
+        pre = pre + bias_ref[...]
         square = pre * pre
         bend = jnp.tanh(GELU_ROOT * pre * (1.0 + GELU_CUBE * square))
         rise = 0.5 + 0.5 * bend
@@ -197,11 +293,10 @@
         slope = rise + 0.5 * pre * (1.0 - bend * bend) * (
             GELU_ROOT + (3.0 * GELU_ROOT * GELU_CUBE) * square
         )
-        branch_ref[rows, :] += dot_nn(unit, shrink)
-        d_unit = dot_nt(grad_ref[rows, :], shrink)
         d_low = (d_unit * slope).astype(jnp.bfloat16)
         d_pre[rows, :] = d_low
         bias_sum = bias_sum + jnp.sum(d_low.astype(jnp.float32), axis=0, keepdims=True)
+        branch_ref[rows, :] += dot_nn(unit, shrink)
         d_norm_ref[rows, :] += dot_nt(d_low, expand)
     d_bias_ref[...] = bias_sum
     store_rows(
@@ -253,29 +348,46 @@
             jax.ShapeDtypeStruct((1, total), jnp.float32),
         ],
         compiler_params=kernel_params(56),
-        cost_estimate=cost(12 * tokens * depth * total, 64 * 2**20, tokens * total),
+        cost_estimate=cost(6 * tokens * depth * total, 16 * 2**20, tokens * total),
         name="feed_forward",
     )(own, norm, grad, expand, bias, shrink)
 
 
-def attention_forward_kernel(q_ref, k_ref, v_ref, out_ref, lse_ref):
+def attention_forward_kernel(q_ref, k_ref, v_ref, out_ref, out_t_ref, lse_ref):
     length = q_ref.shape[0]
     scaled = q_ref[...] * jnp.bfloat16(HEAD_DIM ** (-0.5))
     keys = k_ref[...]
     values_t = v_ref[...].T
-    for start in range(0, length, CHUNK):
+    ones = jnp.ones((16, length), jnp.bfloat16)
+    extended = [
+        jnp.concatenate([values_t[head * HEAD_DIM : (head + 1) * HEAD_DIM], ones], axis=0)
+        for head in range(2)
+    ]
+    tasks = [(start, head) for start in range(0, length, CHUNK) for head in range(2)]
+
+    def scores_of(task):
+        start, head = task
+        cols = slice(head * HEAD_DIM, (head + 1) * HEAD_DIM)
+        return dot_nt(keys[:, cols], scaled[start : start + CHUNK, cols])
+
+    upcoming = scores_of(tasks[0])
+    pieces = []
+    for number, (start, head) in enumerate(tasks):
+        scores = upcoming
+        if number + 1 < len(tasks):
+            upcoming = scores_of(tasks[number + 1])
         rows = slice(start, start + CHUNK)
-        pieces = []
-        for head in range(2):
-            cols = slice(head * HEAD_DIM, (head + 1) * HEAD_DIM)
-            scores = dot_nt(keys[:, cols], scaled[rows, cols])
-            top = jnp.max(scores, axis=0, keepdims=True)
-            terms = jnp.exp(scores - top)
-            total = jnp.sum(terms, axis=0, keepdims=True)
-            part = dot_nn(values_t[cols, :], terms.astype(jnp.bfloat16))
-            pieces.append(part / total)
-            lse_ref[0, head : head + 1, rows] = top + jnp.log(total)
-        out_ref[rows, :] = jnp.concatenate(pieces, axis=0).T.astype(jnp.bfloat16)
+        top = jnp.max(scores, axis=0, keepdims=True)
+        terms = jnp.exp(scores - top).astype(jnp.bfloat16)
+        part = dot_nn(extended[head], terms)
+        total = part[HEAD_DIM : HEAD_DIM + 1]
+        piece = part[:HEAD_DIM] / total
+        lse_ref[0, head : head + 1, rows] = top + jnp.log(total)
+        out_t_ref[head * HEAD_DIM : (head + 1) * HEAD_DIM, rows] = piece
+        pieces.append(piece)
+        if head == 1:
+            out_ref[rows, :] = jnp.concatenate(pieces, axis=0).T.astype(jnp.bfloat16)
+            pieces = []
 
 
 def attention_forward(projected):
@@ -291,19 +403,23 @@
         ],
         out_specs=[
             pl.BlockSpec((length, PAIR), lambda i: (0, i)),
+            pl.BlockSpec((PAIR, length), lambda i: (i, 0)),
             pl.BlockSpec((1, 2, length), lambda i: (i, 0, 0)),
         ],
         out_shape=[
             jax.ShapeDtypeStruct((length, HEADS * HEAD_DIM), jnp.bfloat16),
+            jax.ShapeDtypeStruct((HEADS * HEAD_DIM, length), jnp.float32),
             jax.ShapeDtypeStruct((pairs, 2, length), jnp.float32),
         ],
-        compiler_params=pltpu.CompilerParams(vmem_limit_bytes=48 * 2**20),
-        cost_estimate=pl.CostEstimate(flops=16 * 2**30, bytes_accessed=8 * 2**20, transcendentals=16 * 2**20),
+        compiler_params=kernel_params(48),
+        cost_estimate=cost(2**32, 8 * 2**20, 2**24),
         name="attention_forward",
     )(projected, projected, projected)
 
 
-def attention_backward_kernel(q_ref, k_ref, v_ref, g_ref, lse_ref, out_ref, qb_ref, vb_ref):
+def attention_backward_kernel(
+    q_ref, k_ref, v_ref, g_ref, o_ref, lse_ref, out_ref, qb_ref, vb_ref, probs, d_scores
+):
     length = q_ref.shape[0]
     root = HEAD_DIM ** (-0.5)
     scaled = q_ref[...] * jnp.bfloat16(root)
@@ -311,29 +427,36 @@
     values = v_ref[...]
     grads = g_ref[...]
     keys_t = keys.T
+    product = grads.T.astype(jnp.float32) * o_ref[...]
     sums_k = [None, None]
     sums_v = [None, None]
     sum_q = None
-    for start in range(0, length, CHUNK):
+    pieces = []
+    tasks = [(start, head) for start in range(0, length, CHUNK) for head in range(2)]
+    for number, (start, head) in enumerate(tasks):
         rows = slice(start, start + CHUNK)
-        pieces = []
-        for head in range(2):
-            cols = slice(head * HEAD_DIM, (head + 1) * HEAD_DIM)
-            query, grad = scaled[rows, cols], grads[rows, cols]
-            scores = dot_nt(keys[:, cols], query)
-            probs = jnp.exp(scores - lse_ref[0, head : head + 1, rows])
-            d_probs = dot_nt(values[:, cols], grad)
-            row_sum = jnp.sum(probs * d_probs, axis=0, keepdims=True)
-            d_scores = (probs * (d_probs - row_sum)).astype(jnp.bfloat16)
-            part_v = dot_nn(probs.astype(jnp.bfloat16), grad)
-            part_k = dot_nn(d_scores, query)
-            sums_v[head] = part_v if start == 0 else sums_v[head] + part_v
-            sums_k[head] = part_k if start == 0 else sums_k[head] + part_k
-            pieces.append(dot_nn(keys_t[cols, :], d_scores) * root)
-        d_query = jnp.concatenate(pieces, axis=0).T.astype(jnp.bfloat16)
-        out_ref[0, rows, :] = d_query
-        part_q = jnp.sum(d_query.astype(jnp.float32), axis=0, keepdims=True)
-        sum_q = part_q if start == 0 else sum_q + part_q
+        slot = number % 2
+        cols = slice(head * HEAD_DIM, (head + 1) * HEAD_DIM)
+        query, grad = scaled[rows, cols], grads[rows, cols]
+        lse = lse_ref[0, head : head + 1, rows]
+        row_sum = jnp.sum(product[cols, rows], axis=0, keepdims=True)
+        for block in range(0, length, KEY_BLOCK):
+            some = slice(block, block + KEY_BLOCK)
+            prob = jnp.exp(dot_nt(keys[some, cols], query) - lse)
+            d_prob = dot_nt(values[some, cols], grad)
+            probs[slot, some, :] = prob.astype(jnp.bfloat16)
+            d_scores[slot, some, :] = (prob * (d_prob - row_sum)).astype(jnp.bfloat16)
+        part_v = dot_nn(probs[slot], grad)
+        part_k = dot_nn(d_scores[slot], query)
+        sums_v[head] = part_v if start == 0 else sums_v[head] + part_v
+        sums_k[head] = part_k if start == 0 else sums_k[head] + part_k
+        pieces.append(dot_nn(keys_t[cols, :], d_scores[slot]) * root)
+        if head == 1:
+            d_query = jnp.concatenate(pieces, axis=0).T.astype(jnp.bfloat16)
+            pieces = []
+            out_ref[0, rows, :] = d_query
+            part_q = jnp.sum(d_query.astype(jnp.float32), axis=0, keepdims=True)
+            sum_q = part_q if start == 0 else sum_q + part_q
     out_ref[1] = jnp.concatenate(sums_k, axis=1).astype(jnp.bfloat16)
     d_value = jnp.concatenate(sums_v, axis=1).astype(jnp.bfloat16)
     out_ref[2] = d_value
@@ -341,31 +464,33 @@
     vb_ref[...] = jnp.sum(d_value.astype(jnp.float32), axis=0, keepdims=True)
 
 
-def attention_backward(projected, d_attended, lse):
+def attention_backward(projected, d_attended, attended_t, lse, first, count, name):
     length = projected.shape[0]
-    width = HEADS * HEAD_DIM
+    width = count * PAIR
     pairs = HEADS // 2
-    block = pl.BlockSpec((length, PAIR), lambda i: (0, i))
     row = pl.BlockSpec((1, PAIR), lambda i: (0, i))
-    triple = pl.BlockSpec((3, length, PAIR), lambda i: (0, 0, i))
-    whole = jax.ShapeDtypeStruct((3, length, width), jnp.bfloat16)
     line = jax.ShapeDtypeStruct((1, width), jnp.float32)
     return pl.pallas_call(
         attention_backward_kernel,
-        grid=(pairs,),
+        grid=(count,),
         in_specs=[
-            block,
-            pl.BlockSpec((length, PAIR), lambda i: (0, pairs + i)),
-            pl.BlockSpec((length, PAIR), lambda i: (0, 2 * pairs + i)),
-            block,
-            pl.BlockSpec((1, 2, length), lambda i: (i, 0, 0)),
-        ],
-        out_specs=[triple, row, row],
-        out_shape=[whole, line, line],
-        compiler_params=pltpu.CompilerParams(vmem_limit_bytes=48 * 2**20),
-        cost_estimate=pl.CostEstimate(flops=40 * 2**30, bytes_accessed=16 * 2**20, transcendentals=16 * 2**20),
-        name="attention_backward",
-    )(projected, projected, projected, d_attended, lse)
+            pl.BlockSpec((length, PAIR), lambda i: (0, first + i)),
+            pl.BlockSpec((length, PAIR), lambda i: (0, pairs + first + i)),
+            pl.BlockSpec((length, PAIR), lambda i: (0, 2 * pairs + first + i)),
+            pl.BlockSpec((length, PAIR), lambda i: (0, first + i)),
+            pl.BlockSpec((PAIR, length), lambda i: (first + i, 0)),
+            pl.BlockSpec((1, 2, length), lambda i: (first + i, 0, 0)),
+        ],
+        out_specs=[pl.BlockSpec((3, length, PAIR), lambda i: (0, 0, i)), row, row],
+        out_shape=[jax.ShapeDtypeStruct((3, length, width), jnp.bfloat16), line, line],
+        scratch_shapes=[
+            pltpu.VMEM((2, length, CHUNK), jnp.bfloat16),
+            pltpu.VMEM((2, length, CHUNK), jnp.bfloat16),
+        ],
+        compiler_params=kernel_params(48),
+        cost_estimate=cost(count * 2**29, count * 2 * 2**20, count * 2**21),
+        name=name,
+    )(projected, projected, projected, d_attended, attended_t, lse)
 
 
 def normalize(values):
@@ -377,6 +502,10 @@
 
 def modulate(values, shifts, scales):
     return normalize(values) * (1.0 + scales[:, None, :]) + shifts[:, None, :]
+
+
+MASKS = {"core": (1, 0), "y": (2, 0), "x": (0, 1), "z1": (0, 2), "z2": (0, 4)}
+GATHER_ORDERS = (("z1", "z2", "x", "y"), ("z1", "z2", "y", "x"))
 
 
 def exchange(value, rep_mask, fsdp_mask):
@@ -389,17 +518,29 @@
     return lax.ppermute(value, ("rep", "fsdp"), pairs)
 
 
-def masks_of():
+def gather_relative(row):
     reps, shards = lax.axis_size("rep"), lax.axis_size("fsdp")
-    masks = [(1 << bit, 0) for bit in range(reps.bit_length() - 1)]
-    return masks + [(0, 1 << bit) for bit in range(shards.bit_length() - 1)]
-
-
-def gather_relative(row):
-    rows = row[None, :]
-    for masks in masks_of():
-        rows = jnp.concatenate([rows, exchange(rows, *masks)], axis=0)
+    masks = [(0, 1 << bit) for bit in reversed(range(shards.bit_length() - 1))]
+    masks += [(1 << bit, 0) for bit in reversed(range(reps.bit_length() - 1))]
+    rows = row[None]
+    for pair in masks:
+        rows = jnp.stack([rows, exchange(rows, *pair)], axis=1).reshape(-1, *row.shape)
     return rows
+
+
+def gather_chain(quarter, order):
+    rows = quarter[None]
+    for name in order:
+        rows = jnp.concatenate([rows, exchange(rows, *MASKS[name])], axis=0)
+    return rows, exchange(rows, *MASKS["core"])
+
+
+def chain_map(order):
+    offsets = [0]
+    for name in order:
+        rep_mask, fsdp_mask = MASKS[name]
+        offsets += [offset ^ (fsdp_mask * 4 + rep_mask) for offset in offsets]
+    return tuple(offsets)
 
 
 def to_absolute(parts, own):
@@ -412,24 +553,55 @@
     return parts
 
 
-def scatter_halves(keep, send, order):
-    shards = lax.axis_size("fsdp")
-    rows, columns = keep.shape[0] // (2 * shards), keep.shape[1]
-    shape = (2, 2, 2, 2, rows, columns)
-    masks = {"z2": (0, 4), "z1": (0, 2), "x": (0, 1), "y": (2, 0)}
-    axes = ["z2", "z1", "x", "y"]
-    arrived = exchange(send, 1, 0)
-    total = keep.reshape(shape).astype(jnp.float32) + arrived.reshape(shape).astype(jnp.float32)
-    for name in order:
-        axis = axes.index(name)
-        axes.pop(axis)
-        away = lax.index_in_dim(total, 1, axis, keepdims=False).astype(jnp.bfloat16)
-        stay = lax.index_in_dim(total, 0, axis, keepdims=False)
-        total = stay + exchange(away, *masks[name]).astype(jnp.float32)
-    own = total.astype(jnp.bfloat16)
-    reps = [own] + [exchange(own, mask, 0) for mask in (1, 2, 3)]
-    parts = to_absolute(reps, lax.axis_index("rep"))
-    return jnp.concatenate(parts, axis=0).astype(jnp.float32)
+class HalvingSum:
+    def __init__(self, keep, send, order):
+        rows, columns = keep.shape[0] // 16, keep.shape[1]
+        self.shape = (2, 2, 2, 2, rows, columns)
+        self.axes = ["z2", "z1", "x", "y"]
+        self.order = list(order)
+        self.stay = keep.reshape(self.shape)
+        self.arrived = exchange(send, *MASKS["core"])
+
+    def half(self, axis, side):
+        stay = lax.index_in_dim(self.stay, side, axis, keepdims=False)
+        arrived = lax.index_in_dim(self.arrived.reshape(self.stay.shape), side, axis, keepdims=False)
+        return (stay.astype(jnp.float32) + arrived.astype(jnp.float32)).astype(jnp.bfloat16)
+
+    def step(self):
+        name = self.order.pop(0)
+        axis = self.axes.index(name)
+        self.axes.pop(axis)
+        away, stay = self.half(axis, 1), self.half(axis, 0)
+        self.stay, self.arrived = stay, exchange(away, *MASKS[name])
+
+    def finish(self):
+        while self.order:
+            self.step()
+        own = self.stay.astype(jnp.float32) + self.arrived.reshape(self.stay.shape).astype(jnp.float32)
+        own = own.astype(jnp.bfloat16)
+        pair = [own, exchange(own, *MASKS["core"])]
+        both = jnp.stack(pair)
+        other = exchange(both, *MASKS["y"])
+        parts = to_absolute([*pair, other[0], other[1]], lax.axis_index("rep"))
+        return jnp.concatenate(parts, axis=0).astype(jnp.float32)
+
+
+class PlainSum:
+    def __init__(self, grad):
+        self.arrived = grad
+
+    def step(self):
+        pass
+
+    def finish(self):
+        return scatter_rows(self.arrived)
+
+
+def hold(value, *sums):
+    held = lax.optimization_barrier((value, *[total.arrived for total in sums]))
+    for total, arrived in zip(sums, held[1:]):
+        total.arrived = arrived
+    return held[0]
 
 
 def scatter_rows(grad):
@@ -483,36 +655,45 @@
     own_rows = modulator.shape[0]
     own_bias = modulbias.shape[0]
 
+    width = projector.shape[1]
     if halving:
         quarter = own_rows // reps
-        attn_weights = gather_packed(
-            [column_blocks(own_quarter(projector), feature), own_quarter(outweight)], quarter
+        proj_quarter = own_quarter(projector)
+        chains = [
+            gather_chain(proj_quarter[:, part * (width // 2) : (part + 1) * (width // 2)], order)
+            for part, order in enumerate(GATHER_ORDERS)
+        ]
+        maps = [chain_map(order) for order in GATHER_ORDERS]
+        packed = gather_packed(
+            [
+                own_quarter(shrinker),
+                column_blocks(own_quarter(expander), feature),
+                own_quarter(outweight),
+            ],
+            quarter,
         )
-        proj_at, out_at = (attn_weights, 0), (attn_weights, 3)
-        ff_weights = gather_packed(
-            [own_quarter(shrinker), column_blocks(own_quarter(expander), feature)], quarter
-        )
-        w_expand, w_shrink = ff_weights, ff_weights
+        out_at = (packed, 8)
+        w_expand, w_shrink = packed, packed
         depth_pieces, unit_pieces = shards * reps, reps
         own = jnp.stack(
             [rep_id & 1, shard_id * 2 + (rep_id >> 1), shard_id, rep_id >> 1]
         ).astype(jnp.int32)
     else:
-        proj_at, out_at = (gather_rows(projector), 0), (gather_rows(outweight), 0)
+        w_proj, out_at = gather_rows(projector), (gather_rows(outweight), 0)
         w_expand, w_shrink = gather_rows(expander), gather_rows(shrinker)
         depth_pieces, unit_pieces = 2, 2
         own = jnp.zeros((4,), jnp.int32)
 
-    def reduce_depth(halves, order):
+    def depth_sum(halves, order):
         if halving:
-            return scatter_halves(*halves, order)
-        return scatter_rows(jnp.concatenate(halves, axis=0))
-
-    def reduce_units(halves, order):
+            return HalvingSum(*halves, order)
+        return PlainSum(jnp.concatenate(halves, axis=0))
+
+    def unit_sum(halves, order):
         if halving:
-            return scatter_halves(*halves, order)
+            return HalvingSum(*halves, order)
         blocks = [half.reshape(-1, 1, FF_BLOCK // 2, feature) for half in halves]
-        return scatter_rows(jnp.concatenate(blocks, axis=1).reshape(-1, feature))
+        return PlainSum(jnp.concatenate(blocks, axis=1).reshape(-1, feature))
 
     cond_full = conditions.astype(jnp.float32)
     cond_slice = lax.dynamic_slice_in_dim(cond_full, shard_id * own_rows, own_rows, 1)
@@ -545,8 +726,12 @@
     resid_in = latents.astype(jnp.float32)
     norm_a = modulate(resid_in, shift_a, scale_a).astype(jnp.bfloat16).reshape(token_count, feature)
     b_proj = jnp.concatenate([b_query, jnp.zeros_like(b_query), b_value], axis=1)
-    projected = forward_dot(norm_a, *proj_at, b_proj, jnp.bfloat16, "project")
-    attended, log_totals = attention_forward(projected)
+    if halving:
+        flat = (shard_id * reps + rep_id).astype(jnp.int32)[None]
+        projected, w_proj = project(flat, norm_a, b_proj, chains, maps)
+    else:
+        projected = forward_dot(norm_a, w_proj, 0, b_proj, jnp.bfloat16, "project")
+    attended, attended_t, log_totals = attention_forward(projected)
     branch_a = forward_dot(attended, *out_at, b_out, jnp.float32, "attention_out")
     branch_a = branch_a.reshape(seqs_dev, seq_len, feature)
     middle = resid_in + gate_a[:, None, :] * branch_a
@@ -558,8 +743,8 @@
     branch_m, d_norm_m, keep_e, send_e, keep_s, send_s, g_expandbias = feed_forward(
         own, norm_m, d_branch_m, w_expand, b_expand, w_shrink, depth_pieces, unit_pieces
     )
-    g_expander = reduce_depth((keep_e, send_e), ("y", "x", "z2", "z1"))
-    g_shrinker = reduce_units((keep_s, send_s), ("x", "y", "z2", "z1"))
+    sum_e = depth_sum((keep_e, send_e), ("y", "x", "z2", "z1"))
+    sum_s = unit_sum((keep_s, send_s), ("x", "y", "z2", "z1"))
     branch_m = (branch_m + b_shrink).reshape(seqs_dev, seq_len, feature)
     layer_out = middle + gate_m[:, None, :] * branch_m
     d_gate_m = jnp.sum(grad_out * branch_m, axis=1)
@@ -569,72 +754,82 @@
     d_branch_a = (gate_a[:, None, :] * d_middle).astype(jnp.bfloat16).reshape(token_count, feature)
     d_gate_a = jnp.sum(d_middle * branch_a, axis=1)
     g_outbiases = jnp.sum(d_branch_a, axis=0, dtype=jnp.float32)
-    d_branch_one = d_branch_a[None]
-    g_outweight = reduce_depth(
-        grad_dot(own, attended, d_branch_one, 0, 1, depth_pieces, "outweight_grad"),
+    d_attended = backward_dot(d_branch_a, *out_at, jnp.bfloat16, "attention_out_back")
+    d_attended = hold(d_attended, sum_e, sum_s)
+    sum_e.step()
+    sum_s.step()
+    half_pairs = HEADS // 4
+    d_low, q_low, v_low = attention_backward(
+        projected, d_attended, attended_t, log_totals, 0, half_pairs, "attention_backward_low"
+    )
+    sum_low = depth_sum(
+        grad_dot(own, norm_a, d_low, depth_pieces, "projector_grad_low"), ("y", "x", "z2", "z1")
+    )
+    sum_out = depth_sum(
+        grad_dot(own, attended, d_branch_a[None], depth_pieces, "outweight_grad"),
         ("x", "y", "z2", "z1"),
     )
-    d_attended = backward_dot(d_branch_one, *out_at, jnp.bfloat16, "attention_out_back")
-    early = gather_relative(
-        jnp.concatenate(
-            [cond_own.reshape(-1)]
-            + [
-                part.astype(jnp.bfloat16).reshape(-1)
-                for part in (
-                    d_gate_a, d_shift_m, d_scale_m, d_gate_m, g_outbiases, g_expandbias, g_shrinkbias
-                )
-            ]
-        )
-    )
-    d_projected, g_querybias, g_valuebias = attention_backward(projected, d_attended, log_totals)
-    g_projector = jnp.concatenate(
-        [
-            reduce_depth(
-                grad_dot(own, norm_a, d_projected, 0, 2, depth_pieces, "projector_grad_qk"),
-                ("y", "x", "z2", "z1"),
-            ),
-            reduce_depth(
-                grad_dot(own, norm_a, d_projected, 2, 1, depth_pieces, "projector_grad_v"),
-                ("x", "y", "z2", "z1"),
-            ),
-        ],
-        axis=1,
-    )
-    d_norm_a = backward_dot(d_projected, *proj_at, jnp.float32, "project_back")
+    d_attended = hold(d_attended, sum_e, sum_s, sum_low, sum_out)
+    for total in (sum_e, sum_s, sum_low, sum_out):
+        total.step()
+    d_high, q_high, v_high = attention_backward(
+        projected, d_attended, attended_t, log_totals, half_pairs, half_pairs, "attention_backward_high"
+    )
+    d_high = hold(d_high, sum_e, sum_s, sum_low, sum_out)
+    for total in (sum_e, sum_s, sum_low, sum_out):
+        total.step()
+    sum_high = depth_sum(
+        grad_dot(own, norm_a, d_high, depth_pieces, "projector_grad_high"), ("x", "y", "z2", "z1")
+    )
+    d_norm_a = project_back(d_low, d_high, w_proj)
+    d_norm_a = hold(d_norm_a, sum_high)
+    sum_high.step()
+    g_querybias = jnp.concatenate([q_low, q_high], axis=1)
+    g_valuebias = jnp.concatenate([v_low, v_high], axis=1)
     _, norm_pull_a = jax.vjp(modulate, resid_in, shift_a, scale_a)
     d_in_norm, d_shift_a, d_scale_a = norm_pull_a(d_norm_a.reshape(seqs_dev, seq_len, feature))
     latents_grad = d_middle + d_in_norm
-    late = gather_relative(
-        jnp.concatenate(
-            [
-                part.astype(jnp.bfloat16).reshape(-1)
-                for part in (d_shift_a, d_scale_a, g_querybias, g_valuebias)
-            ]
-        )
-    )
-
+    small = jnp.concatenate(
+        [
+            part.astype(jnp.bfloat16).reshape(-1)
+            for part in (
+                d_shift_a,
+                d_scale_a,
+                d_gate_a,
+                d_shift_m,
+                d_scale_m,
+                d_gate_m,
+                cond_own,
+                g_querybias,
+                g_valuebias,
+                g_outbiases,
+                g_expandbias,
+                g_shrinkbias,
+            )
+        ]
+    )
     devices = reps * shards
     size = seqs_dev * feature
-    cond_all = early[:, :size].reshape(devices * seqs_dev, feature)
+    gathered = gather_relative(small.reshape(-1, 128)).reshape(devices, -1)
+    g_expander, g_shrinker = sum_e.finish(), sum_s.finish()
+    g_outweight = sum_out.finish()
+    low, high = sum_low.finish(), sum_high.finish()
+    g_projector = jnp.stack(
+        [low.reshape(own_rows, 3, feature // 2), high.reshape(own_rows, 3, feature // 2)], axis=2
+    ).reshape(own_rows, 3 * feature)
+
+    cond_all = gathered[:, 6 * size : 7 * size].reshape(devices * seqs_dev, feature)
     cond_all = lax.dynamic_slice_in_dim(cond_all, shard_id * own_rows, own_rows, 1)
-    d_mod = jnp.stack(
-        [late[:, i * size : (i + 1) * size] for i in range(2)]
-        + [early[:, i * size : (i + 1) * size] for i in range(1, 5)],
-        axis=1,
-    )
+    d_mod = gathered[:, : 6 * size]
     d_mod = d_mod.reshape(devices, 6, seqs_dev, feature).transpose(0, 2, 1, 3)
     d_mod = d_mod.reshape(devices * seqs_dev, 6 * feature)
     bias_grads = []
-    for source, start, width in (
-        (late, 2 * size, feature),
-        (late, 2 * size + feature, feature),
-        (early, 5 * size, feature),
-        (early, 5 * size + feature, expandbias.shape[0] * shards),
-        (early, 5 * size + feature + expandbias.shape[0] * shards, feature),
-    ):
-        part = width // shards
-        own_part = lax.dynamic_slice_in_dim(source, start + shard_id * part, part, 1)
+    start = 7 * size
+    for total in (feature, feature, feature, expandbias.shape[0] * shards, feature):
+        part = total // shards
+        own_part = lax.dynamic_slice_in_dim(gathered, start + shard_id * part, part, 1)
         bias_grads.append(jnp.sum(own_part, axis=0, dtype=jnp.float32))
+        start += total
     g_modbias = jnp.sum(
         lax.dynamic_slice_in_dim(d_mod, shard_id * own_bias, own_bias, 1), axis=0, dtype=jnp.float32
     )

time: 732 us -> 632 us (0.86)
  waiting for transfers between devices: 303 us -> 216 us
  Pallas kernels: 229 us -> 197 us
  other arithmetic: 77.8 us -> 86.3 us
    all_gather x2 -> x1, waiting for transfers between devices: 93.2 us -> 14.5 us  [gather_packed(): full = lax.all_gather(packed, ('fsdp', 'rep'), axis=0, tiled=True)]
    convert_element_type x8 -> x33, other arithmetic: 4.74 us -> 24.5 us  [the longest x25 19.5 us: half(): (stay.astype(jnp.float32) + arrived.astype(jnp.float32)).astype(jnp.bfloa...]
    pallas_call x1, Pallas kernels: 49.4 us -> 30.1 us  [attention_forward(): pl.pallas_call(attention_forward_kernel, grid=(pairs,), in_specs=[pl.Bloc...]
    add x20 -> x0, other arithmetic: 19.2 us -> none  [the longest x5 13.4 us: scatter_halves(): keep.reshape(shape).astype(jnp.float32)]
    slice x1 -> x10, local copies, waits for them, and re-layouts: 0.85 us -> 14.6 us  [the longest x5 10.5 us: half(): stay = lax.index_in_dim(self.stay, side, axis, keepdims=False)]
    pallas_call x2 -> x1, Pallas kernels: 14.4 us -> 4.19 us  [forward_dot(): pl.pallas_call(forward_dot_kernel, grid=(columns // COL_BLOCK,), in_specs...]
    all_to_all x1, waiting for transfers between devices: 7.44 us -> 0.01 us  [on_device(): got = lax.all_to_all(sent, 'fsdp', split_axis=0, concat_axis=0, tiled=True)]
    unnamed x138 -> x170, local copies, waits for them, and re-layouts: 30 us -> 25.3 us
  transfers between devices with their start and end apart: 53 -> 52, of which waited for: 28 -> 24; matrix products, arithmetic and copies ran while one was open for 12% -> 19% of each run, Pallas kernels for 10% -> 15%
where the time goes in v3:
time: 632 us; the launch traced here: 628 us
  waiting for transfers between devices  216 us (34%)
  Pallas kernels  197 us (31%)
  other arithmetic  86.3 us (14%)
  local copies, waits for them, and re-layouts  59 us (9%)
  starting transfers between devices  51.3 us (8%)
  between operations  15.7 us (2%)
    ppermute x50, waiting for transfers between devices, exchange(): return lax.ppermute(value, ('rep', 'fsdp'), pairs)  202 us
    pallas_call x1, Pallas kernels, feed_forward(): pl.pallas_call(partial(feed_forward_kernel, depth_pieces, unit_pieces), g...  74.4 us
    pallas_call x2, Pallas kernels, attention_backward(): pl.pallas_call(attention_backward_kernel, grid=(count,), in_specs=[pl.Blo...  48.1 us
    ppermute x50, starting transfers between devices, exchange(): return lax.ppermute(value, ('rep', 'fsdp'), pairs)  43.6 us
    pallas_call x1, Pallas kernels, attention_forward(): pl.pallas_call(attention_forward_kernel, grid=(pairs,), in_specs=[pl.Bloc...  30.1 us
    unnamed x170, local copies, waits for them, and re-layouts  25.3 us
    convert_element_type x25, other arithmetic, half(): (stay.astype(jnp.float32) + arrived.astype(jnp.float32)).astype(jnp.bfloa...  19.5 us
    all_gather x1, waiting for transfers between devices, gather_packed(): full = lax.all_gather(packed, ('fsdp', 'rep'), axis=0, tiled=True)  14.5 us
  transfers between devices with their start and end apart: 52, of which 24 were waited for; matrix products, arithmetic and copies ran while one was open for 19% of the time, Pallas kernels for 15%

profile of v3, /device:TPU:0, one launch (start us, length us, event | category | flops | bytes accessed | tf_op | source)
XLA Modules:
  0.0 628.2 jit_solution(14889022335476454571)
XLA Ops:
  14.1 7.6 %all-to-all-start = ((f32[8,1,7936]{2,1,0:T(1,128)}), f32[8,1,7936]{2,1,0:T(1,128)}, u32[]{:S(2)}, u32[]{:S(2)}) async-start(f32[8,1,7936]{2,1,0:T(1,128)} %copy.136), calls=%async_computation | async-start | bytes 507904 | tf_op jit(solution)/shard_map/all_to_all | solution.py:714
  29.6 8.6 %collective-permute-done.5 = bf16[1,32,1536]{2,1,0:T(8,128)(2,1)S(1)} collective-permute-done((bf16[1,32,1536]{2,1,0:T(8,128)(2,1)S(1)}, bf16[1,32,1536]{2,1,0:T(8,128)(2,1)S(1)}, u32[]{:S(2)}, u32[]{:S(2)}) %collective-permute-start.5) | collective-permute-done | bytes 98336 | tf_op jit(solution)/shard_map/ppermute | solution.py:518
  39.8 4.8 collective-permute-done
  47.8 10.2 %collective-permute-done.6 = bf16[2,32,1536]{2,1,0:T(8,128)(2,1)S(1)} collective-permute-done((bf16[2,32,1536]{2,1,0:T(8,128)(2,1)S(1)}, bf16[2,32,1536]{2,1,0:T(8,128)(2,1)S(1)}, u32[]{:S(2)}, u32[]{:S(2)}) %collective-permute-start.6) | collective-permute-done | bytes 196640 | tf_op jit(solution)/shard_map/ppermute | solution.py:518
  66.2 11.4 %collective-permute-done.7 = bf16[4,32,1536]{2,1,0:T(8,128)(2,1)} collective-permute-done((bf16[4,32,1536]{2,1,0:T(8,128)(2,1)}, bf16[4,32,1536]{2,1,0:T(8,128)(2,1)}, u32[]{:S(2)}, u32[]{:S(2)}) %collective-permute-start.7) | collective-permute-done | bytes 393248 | tf_op jit(solution)/shard_map/ppermute | solution.py:518
  89.8 14.0 %collective-permute-done.8 = bf16[8,32,1536]{2,1,0:T(8,128)(2,1)S(1)} collective-permute-done((bf16[8,32,1536]{2,1,0:T(8,128)(2,1)S(1)}, bf16[8,32,1536]{2,1,0:T(8,128)(2,1)S(1)}, u32[]{:S(2)}, u32[]{:S(2)}) %collective-permute-start.8) | collective-permute-done | bytes 786464 | tf_op jit(solution)/shard_map/ppermute | solution.py:518
  110.7 12.3 %project.1 = (bf16[1024,3072]{1,0:T(8,128)(2,1)}, bf16[1024,3072]{1,0:T(8,128)(2,1)}) custom-call(s32[1]{0:T(128)} %bitcast.2.own_ref, bf16[1024,1024]{1,0:T(8,128)(2,1)S(1)} %fusion.21.x_ref, f32[1,3072]{1,0:T(1,128)S(1)} %pad_maximum_fusion.17.b_ref, bf16[16,32,1536]{2,1,0:T(8,128)(2,1)S(1)} %constant_dynamic-update-slice_fusion.refs_0_, ...), custom_call_target="tpu_custom_call" | custom-call | flops 3221225472 | bytes 3145728 | tf_op jit(solution)/shard_map/project/pallas_call | solution.py:105
  123.0 30.1 %attention_forward.1 = (bf16[1024,1024]{1,0:T(8,128)(2,1)S(1)}, f32[1024,1024]{1,0:T(8,128)}, f32[8,2,1024]{2,1,0:T(2,128)S(1)}) custom-call(bf16[1024,3072]{1,0:T(8,128)(2,1)} %get-tuple-element.53.q_ref.k_ref.v_ref, bf16[1024,3072]{1,0:T(8,128)(2,1)} %get-tuple-element.53.q_ref.k_ref.v_ref, bf16[1024,3072]{1,0:T(8,128)(2,1)} %get-tuple-element.53.q_ref.k_ref.v_ref), custom_call_target="tpu_custom_call" | custom-call | flops 4294967296 | bytes 8388608 | tf_op jit(solution)/shard_map/attention_forward/pallas_call | solution.py:396
  154.4 14.5 %all-gather.2.cloned.1.call-done = bf16[9216,1024]{1,0:T(8,128)(2,1)} async-done(((bf16[288,1024]{1,0:T(8,128)(2,1)}), bf16[9216,1024]{1,0:T(8,128)(2,1)}) %all-gather.2.cloned.1.call-update) | async-done | bytes 18874384 | tf_op jit(solution)/shard_map/all_gather | solution.py:630
  170.4 4.2 attention_out.1
  180.6 74.4 %feed_forward.1 = (f32[1024,1024]{1,0:T(8,128)}, f32[1024,1024]{1,0:T(8,128)}, bf16[512,4096]{1,0:T(8,128)(2,1)}, bf16[512,4096]{1,0:T(8,128)(2,1)}, bf16[2048,1...) custom-call(s32[4]{0:T(128)} %pad_add_fusion.own_ref, bf16[1024,1024]{1,0:T(8,128)(2,1)} %fusion.16.norm_ref, ...), custom_call_target="tpu_custom_call" | custom-call | flops 25769803776 | bytes 16777216 | tf_op jit(solution)/shard_map/feed_forward/pallas_call | solution.py:328
  260.0 5.3 fusion.13
  274.8 5.0 attention_out_back.1.g_ref
  296.0 24.1 %attention_backward_low.1 = (bf16[3,1024,512]{2,1,0:T(8,128)(2,1)S(1)}, f32[1,512]{1,0:T(1,128)S(1)}, f32[1,512]{1,0:T(1,128)S(1)}) custom-call(bf16[1024,3072]{1,0:T(8,128)(2,1)} %get-tuple-element.53.q_ref.k_ref.v_ref, bf16[1024,3072]{1,0:T(8,128)(2,1)} %get-tuple-element.53.q_ref.k_ref.v_ref, bf16[1024,3072]{1,0:T(8,128)(2,1)} %get-tuple-element.53.q_ref.k_ref.v_ref, ...), custom_call_target="tpu_custom_call" | custom-call | flops 2147483648 | bytes 8388608 | tf_op jit(solution)/shard_map/attention_backward_low/pallas_call | solution.py:473
  320.2 4.9 projector_grad_low.1
  331.8 4.2 collective-permute-done.13
  335.9 7.3 %collective-permute-done.12 = bf16[2,2,2,32,4096]{4,3,1,2,0:T(8,128)(2,1)} collective-permute-done((bf16[2,2,2,32,4096]{4,3,1,2,0:T(8,128)(2,1)}, bf16[2,2,2,32,4096]{4,3,1,2,0:T(8,128)(2,1)}, u32[]{:S(2)}, u32[]{:S(2)}) %collective-permute-start.12) | collective-permute-done | bytes 2097184 | tf_op jit(solution)/shard_map/ppermute | solution.py:518
  343.3 24.0 %attention_backward_high.1 = (bf16[3,1024,512]{2,1,0:T(8,128)(2,1)S(1)}, f32[1,512]{1,0:T(1,128)S(1)}, f32[1,512]{1,0:T(1,128)S(1)}) custom-call(bf16[1024,3072]{1,0:T(8,128)(2,1)} %get-tuple-element.53.q_ref.k_ref.v_ref, bf16[1024,3072]{1,0:T(8,128)(2,1)} %get-tuple-element.53.q_ref.k_ref.v_ref, bf16[1024,3072]{1,0:T(8,128)(2,1)} %get-tuple-element.53.q_ref.k_ref.v_ref, ...), custom_call_target="tpu_custom_call" | custom-call | flops 2147483648 | bytes 8388608 | tf_op jit(solution)/shard_map/attention_backward_high/pallas_call | solution.py:473
  383.9 29.3 %collective-permute-done.18 = bf16[2,2,2,32,1536]{4,3,1,2,0:T(8,128)(2,1)S(1)} collective-permute-done((bf16[2,2,2,32,1536]{4,3,1,2,0:T(8,128)(2,1)S(1)}, bf16[2,2,2,32,1536]{4,3,1,2,0:T(8,128)(2,1)S(1)}, u32[]{:S(2)}, u32[]{:S(2)}) %collective-permute-start.18) | collective-permute-done | bytes 786464 | tf_op jit(solution)/shard_map/ppermute | solution.py:518
  419.5 5.1 projector_grad_high.1
  427.6 40.0 %collective-permute-done.38 = bf16[2,32,1024]{2,1,0:T(8,128)(2,1)S(1)} collective-permute-done((bf16[2,32,1024]{2,1,0:T(8,128)(2,1)S(1)}, bf16[2,32,1024]{2,1,0:T(8,128)(2,1)S(1)}, u32[]{:S(2)}, u32[]{:S(2)}) %collective-permute-start.38) | collective-permute-done | bytes 131104 | tf_op jit(solution)/shard_map/ppermute | solution.py:518
  467.7 9.2 %project_back.1 = f32[1024,1024]{1,0:T(8,128)S(1)} custom-call(bf16[3,1024,512]{2,1,0:T(8,128)(2,1)S(1)} %get-tuple-element.62.dy_ref.low_ref, bf16[3,1024,512]{2,1,0:T(8,128)(2,1)S(1)} %get-tuple-element.77.high_ref.dy_ref, bf16[1024,3072]{1,0:T(8,128)(2,1)} %get-tuple-element.78.w_ref), custom_call_target="tpu_custom_call" | custom-call | flops 1610612736 | bytes 524288 | tf_op jit(solution)/shard_map/project_back/pallas_call | solution.py:190
  483.3 6.4 %collective-permute-done.27 = bf16[2,32,1536]{2,1,0:T(8,128)(2,1)S(1)} collective-permute-done((bf16[2,32,1536]{2,1,0:T(8,128)(2,1)S(1)}, bf16[2,32,1536]{2,1,0:T(8,128)(2,1)S(1)}, u32[]{:S(2)}, u32[]{:S(2)}) %collective-permute-start.27) | collective-permute-done | bytes 196640 | tf_op jit(solution)/shard_map/ppermute | solution.py:518
  489.9 10.2 %collective-permute-done.28 = bf16[32,1536]{1,0:T(8,128)(2,1)S(1)} collective-permute-done((bf16[32,1536]{1,0:T(8,128)(2,1)S(1)}, bf16[32,1536]{1,0:T(8,128)(2,1)S(1)}, u32[]{:S(2)}, u32[]{:S(2)}) %collective-permute-start.28) | collective-permute-done | bytes 98336 | tf_op jit(solution)/shard_map/ppermute | solution.py:518
  504.3 4.2 collective-permute-done.30
  533.1 8.0 %fusion.12 = (bf16[1024]{0:T(1024)(128)(2,1)S(1)}, bf16[1024]{0:T(1024)(128)(2,1)S(1)}, f32[1,1024,1024]{2,1,0:T(8,128)}, f32[1,1024,1024]{2,1,0:T(8,128)}) fusion(bf16[1,1024,1024]{2,1,0:T(8,128)(2,1)} %param.27, f32[1024,1024]{1,0:T(8,128)} %get-tuple-element.55, f32[1024]{0:T(1024)S(1)} %copy-done.52, f32[1024,1024]{1,0:T(8,128)S(1)} %copy-done.4, ...), kind=kLoop, calls=%fused_computation.20 | loop fusion | flops 19920896 | bytes 33591296 | tf_op jit(solution)/shard_map/reduce_sum | solution.py:750
  554.0 11.1 %collective-permute-done.23 = bf16[4,120,128]{2,1,0:T(8,128)(2,1)S(1)} collective-permute-done((bf16[4,120,128]{2,1,0:T(8,128)(2,1)S(1)}, bf16[4,120,128]{2,1,0:T(8,128)(2,1)S(1)}, u32[]{:S(2)}, u32[]{:S(2)}) %collective-permute-start.23) | collective-permute-done | bytes 122912 | tf_op jit(solution)/shard_map/ppermute | solution.py:518
  567.3 4.2 collective-permute-done.24
  580.3 5.7 collective-permute-done.32
  589.4 9.5 %collective-permute-done.33 = bf16[2,32,1536]{2,1,0:T(8,128)(2,1)S(1)} collective-permute-done((bf16[2,32,1536]{2,1,0:T(8,128)(2,1)S(1)}, bf16[2,32,1536]{2,1,0:T(8,128)(2,1)S(1)}, u32[]{:S(2)}, u32[]{:S(2)}) %collective-permute-start.33) | collective-permute-done | bytes 196640 | tf_op jit(solution)/shard_map/ppermute | solution.py:518
  599.0 4.6 collective-permute-done.34
  607.7 5.2 collective-permute-done.36
  (410 shorter events, 192.9 us)
Async XLA Ops:
  7.3 161.6 %all-gather.2.cloned.1.call-start = ((), (), s32[]{:S(2)}) async-start(), calls=%async_computation.1 | async-start | bytes 19464192 | tf_op jit(solution)/shard_map/all_gather | solution.py:630
  14.1 51.1 %all-to-all-start = ((f32[8,1,7936]{2,1,0:T(1,128)}), f32[8,1,7936]{2,1,0:T(1,128)}, u32[]{:S(2)}, u32[]{:S(2)}) async-start(f32[8,1,7936]{2,1,0:T(1,128)} %copy.136), calls=%async_computation | async-start | bytes 507904 | tf_op jit(solution)/shard_map/all_to_all | solution.py:714
  23.3 14.9 %collective-permute-start.5 = (bf16[1,32,1536]{2,1,0:T(8,128)(2,1)S(1)}, bf16[1,32,1536]{2,1,0:T(8,128)(2,1)S(1)}, u32[]{:S(2)}, u32[]{:S(2)}) collective-permute-start(bf16[1,32,1536]{2,1,0:T(8,128)(2,1)S(1)} %get-tuple-element.161), channel_id=1, source_target_pairs={{0,2},{1,3},{2,0},{3,1},{4,6},{5,7},{6,4},{7,5},{8,10},{9,11},{10,... | collective-permute-start | bytes 294920 | tf_op jit(solution)/shard_map/ppermute | solution.py:518
  25.3 19.3 %collective-permute-start = (bf16[1,32,1536]{2,1,0:T(8,128)(2,1)S(1)}, bf16[1,32,1536]{2,1,0:T(8,128)(2,1)S(1)}, u32[]{:S(2)}, u32[]{:S(2)}) collective-permute-start(bf16[1,32,1536]{2,1,0:T(8,128)(2,1)S(1)} %get-tuple-element.214), channel_id=1, source_target_pairs={{0,2},{1,3},{2,0},{3,1},{4,6},{5,7},{6,4},{7,5},{8,10},{9,11},{10,... | collective-permute-start | bytes 294920 | tf_op jit(solution)/shard_map/ppermute | solution.py:518
  38.9 19.2 %collective-permute-start.6 = (bf16[2,32,1536]{2,1,0:T(8,128)(2,1)S(1)}, bf16[2,32,1536]{2,1,0:T(8,128)(2,1)S(1)}, u32[]{:S(2)}, u32[]{:S(2)}) collective-permute-start(bf16[2,32,1536]{2,1,0:T(8,128)(2,1)S(1)} %pad_maximum_fusion.11), channel_id=1, source_target_pairs={{0,4},{1,5},{2,6},{3,7},{4,0},{5,1},{6,2},{7,3},{8,12},{9,13},{10,... | collective-permute-start | bytes 589832 | tf_op jit(solution)/shard_map/ppermute | solution.py:518
  45.3 16.0 %collective-permute-start.1 = (bf16[2,32,1536]{2,1,0:T(8,128)(2,1)S(1)}, bf16[2,32,1536]{2,1,0:T(8,128)(2,1)S(1)}, u32[]{:S(2)}, u32[]{:S(2)}) collective-permute-start(bf16[2,32,1536]{2,1,0:T(8,128)(2,1)S(1)} %pad_maximum_fusion.10), channel_id=1, source_target_pairs={{0,4},{1,5},{2,6},{3,7},{4,0},{5,1},{6,2},{7,3},{8,12},{9,13},{10,... | collective-permute-start | bytes 589832 | tf_op jit(solution)/shard_map/ppermute | solution.py:518
  59.8 17.9 %collective-permute-start.7 = (bf16[4,32,1536]{2,1,0:T(8,128)(2,1)}, bf16[4,32,1536]{2,1,0:T(8,128)(2,1)}, u32[]{:S(2)}, u32[]{:S(2)}) collective-permute-start(bf16[4,32,1536]{2,1,0:T(8,128)(2,1)} %pad_maximum_fusion.8), channel_id=1, source_target_pairs={{0,16},{1,17},{2,18},{3,19},{4,20},{5,21},{6,22},{7,23},{8,24},{9,... | collective-permute-start | bytes 1179656 | tf_op jit(solution)/shard_map/ppermute | solution.py:518
  63.0 20.7 %collective-permute-start.2 = (bf16[4,32,1536]{2,1,0:T(8,128)(2,1)}, bf16[4,32,1536]{2,1,0:T(8,128)(2,1)}, u32[]{:S(2)}, u32[]{:S(2)}) collective-permute-start(bf16[4,32,1536]{2,1,0:T(8,128)(2,1)} %pad_maximum_fusion.7), channel_id=1, source_target_pairs={{0,1},{1,0},{2,3},{3,2},{4,5},{5,4},{6,7},{7,6},{8,9},{9,8},{10,11... | collective-permute-start | bytes 1179656 | tf_op jit(solution)/shard_map/ppermute | solution.py:518
  78.8 25.0 %collective-permute-start.8 = (bf16[8,32,1536]{2,1,0:T(8,128)(2,1)S(1)}, bf16[8,32,1536]{2,1,0:T(8,128)(2,1)S(1)}, u32[]{:S(2)}, u32[]{:S(2)}) collective-permute-start(bf16[8,32,1536]{2,1,0:T(8,128)(2,1)S(1)} %pad_maximum_fusion.2), channel_id=1, source_target_pairs={{0,1},{1,0},{2,3},{3,2},{4,5},{5,4},{6,7},{7,6},{8,9},{9,8},{10,11... | collective-permute-start | bytes 2359304 | tf_op jit(solution)/shard_map/ppermute | solution.py:518
  84.8 19.9 %collective-permute-start.3 = (bf16[8,32,1536]{2,1,0:T(8,128)(2,1)S(1)}, bf16[8,32,1536]{2,1,0:T(8,128)(2,1)S(1)}, u32[]{:S(2)}, u32[]{:S(2)}) collective-permute-start(bf16[8,32,1536]{2,1,0:T(8,128)(2,1)S(1)} %pad_maximum_fusion.1), channel_id=1, source_target_pairs={{0,16},{1,17},{2,18},{3,19},{4,20},{5,21},{6,22},{7,23},{8,24},{9,... | collective-permute-start | bytes 2359304 | tf_op jit(solution)/shard_map/ppermute | solution.py:518
  255.0 26.5 %collective-permute-start.10 = (bf16[512,4096]{1,0:T(8,128)(2,1)}, bf16[512,4096]{1,0:T(8,128)(2,1)}, u32[]{:S(2)}, u32[]{:S(2)}) collective-permute-start(bf16[512,4096]{1,0:T(8,128)(2,1)} %get-tuple-element.57), channel_id=1, source_target_pairs={{0,8},{1,9},{2,10},{3,11},{4,12},{5,13},{6,14},{7,15},{8,0},{9,1},... | collective-permute-start | bytes 12582920 | tf_op jit(solution)/shard_map/ppermute | solution.py:518
  255.3 26.2 %collective-permute-start.11 = (bf16[2048,1024]{1,0:T(8,128)(2,1)}, bf16[2048,1024]{1,0:T(8,128)(2,1)}, u32[]{:S(2)}, u32[]{:S(2)}) collective-permute-start(bf16[2048,1024]{1,0:T(8,128)(2,1)} %get-tuple-element.58), channel_id=1, source_target_pairs={{0,8},{1,9},{2,10},{3,11},{4,12},{5,13},{6,14},{7,15},{8,0},{9,1},... | collective-permute-start | bytes 12582920 | tf_op jit(solution)/shard_map/ppermute | solution.py:518
  274.4 57.3 %collective-permute-start.15 = (bf16[512,1024]{1,0:T(8,128)(2,1)S(1)}, bf16[512,1024]{1,0:T(8,128)(2,1)}, u32[]{:S(2)}, u32[]{:S(2)}) collective-permute-start(bf16[512,1024]{1,0:T(8,128)(2,1)S(1)} %get-tuple-element.68), channel_id=1, source_target_pairs={{0,8},{1,9},{2,10},{3,11},{4,12},{5,13},{6,14},{7,15},{8,0},{9,1},... | collective-permute-start | bytes 3145736 | tf_op jit(solution)/shard_map/ppermute | solution.py:518
  287.8 48.1 %collective-permute-start.13 = (bf16[2,2,2,128,1024]{4,3,1,2,0:T(8,128)(2,1)}, bf16[2,2,2,128,1024]{4,3,1,2,0:T(8,128)(2,1)}, u32[]{:S(2)}, u32[]{:S(2)}) collective-permute-start(bf16[2,2,2,128,1024]{4,3,1,2,0:T(8,128)(2,1)} %fusion.18), channel_id=1, source_target_pairs={{0,1},{1,0},{2,3},{3,2},{4,5},{5,4},{6,7},{7,6},{8,9},{9,8},{10,11... | collective-permute-start | bytes 6291464 | tf_op jit(solution)/shard_map/ppermute | solution.py:518
  295.4 47.8 %collective-permute-start.12 = (bf16[2,2,2,32,4096]{4,3,1,2,0:T(8,128)(2,1)}, bf16[2,2,2,32,4096]{4,3,1,2,0:T(8,128)(2,1)}, u32[]{:S(2)}, u32[]{:S(2)}) collective-permute-start(bf16[2,2,2,32,4096]{4,3,1,2,0:T(8,128)(2,1)} %fusion.17), channel_id=1, source_target_pairs={{0,16},{1,17},{2,18},{3,19},{4,20},{5,21},{6,22},{7,23},{8,24},{9,... | collective-permute-start | bytes 6291464 | tf_op jit(solution)/shard_map/ppermute | solution.py:518
  369.0 14.9 %collective-permute-start.19 = (bf16[2,2,2,32,1024]{4,3,1,2,0:T(8,128)(2,1)S(1)}, bf16[2,2,2,32,1024]{4,3,1,2,0:T(8,128)(2,1)S(1)}, u32[]{:S(2)}, u32[]{:S(2)}) collective-permute-start(bf16[2,2,2,32,1024]{4,3,1,2,0:T(8,128)(2,1)S(1)} %fusion.34), channel_id=1, source_target_pairs={{0,1},{1,0},{2,3},{3,2},{4,5},{5,4},{6,7},{7,6},{8,9},{9,8},{10,11... | collective-permute-start | bytes 1572872 | tf_op jit(solution)/shard_map/ppermute | solution.py:518
  372.2 41.0 %collective-permute-start.17 = (bf16[2,2,128,1024]{3,2,1,0:T(8,128)(2,1)S(1)}, bf16[2,2,128,1024]{3,2,1,0:T(8,128)(2,1)S(1)}, u32[]{:S(2)}, u32[]{:S(2)}) collective-permute-start(bf16[2,2,128,1024]{3,2,1,0:T(8,128)(2,1)S(1)} %get-tuple-element.167), channel_id=1, source_target_pairs={{0,16},{1,17},{2,18},{3,19},{4,20},{5,21},{6,22},{7,23},{8,24},{9,... | collective-permute-start | bytes 3145736 | tf_op jit(solution)/shard_map/ppermute | solution.py:518
  375.9 37.3 %collective-permute-start.16 = (bf16[2,2,32,4096]{3,2,1,0:T(8,128)(2,1)S(1)}, bf16[2,2,32,4096]{3,2,1,0:T(8,128)(2,1)S(1)}, u32[]{:S(2)}, u32[]{:S(2)}) collective-permute-start(bf16[2,2,32,4096]{3,2,1,0:T(8,128)(2,1)S(1)} %get-tuple-element.169), channel_id=1, source_target_pairs={{0,1},{1,0},{2,3},{3,2},{4,5},{5,4},{6,7},{7,6},{8,9},{9,8},{10,11... | collective-permute-start | bytes 3145736 | tf_op jit(solution)/shard_map/ppermute | solution.py:518
  377.0 36.2 %collective-permute-start.18 = (bf16[2,2,2,32,1536]{4,3,1,2,0:T(8,128)(2,1)S(1)}, bf16[2,2,2,32,1536]{4,3,1,2,0:T(8,128)(2,1)S(1)}, u32[]{:S(2)}, u32[]{:S(2)}) collective-permute-start(bf16[2,2,2,32,1536]{4,3,1,2,0:T(8,128)(2,1)S(1)} %fusion.30), channel_id=1, source_target_pairs={{0,16},{1,17},{2,18},{3,19},{4,20},{5,21},{6,22},{7,23},{8,24},{9,... | collective-permute-start | bytes 2359304 | tf_op jit(solution)/shard_map/ppermute | solution.py:518
  414.8 62.7 %collective-permute-start.26 = (bf16[2,2,32,1536]{3,2,1,0:T(8,128)(2,1)S(1)}, bf16[2,2,32,1536]{3,2,1,0:T(8,128)(2,1)S(1)}, u32[]{:S(2)}, u32[]{:S(2)}) collective-permute-start(bf16[2,2,32,1536]{3,2,1,0:T(8,128)(2,1)S(1)} %get-tuple-element.184), channel_id=1, source_target_pairs={{0,1},{1,0},{2,3},{3,2},{4,5},{5,4},{6,7},{7,6},{8,9},{9,8},{10,11... | collective-permute-start | bytes 1179656 | tf_op jit(solution)/shard_map/ppermute | solution.py:518
  416.2 64.8 %collective-permute-start.46 = (bf16[2,128,1024]{2,1,0:T(8,128)(2,1)S(1)}, bf16[2,128,1024]{2,1,0:T(8,128)(2,1)S(1)}, u32[]{:S(2)}, u32[]{:S(2)}) collective-permute-start(bf16[2,128,1024]{2,1,0:T(8,128)(2,1)S(1)} %get-tuple-element.179), channel_id=1, source_target_pairs={{0,4},{1,5},{2,6},{3,7},{4,0},{5,1},{6,2},{7,3},{8,12},{9,13},{10,... | collective-permute-start | bytes 1572872 | tf_op jit(solution)/shard_map/ppermute | solution.py:518
  418.1 65.1 %collective-permute-start.42 = (bf16[2,32,4096]{2,1,0:T(8,128)(2,1)S(1)}, bf16[2,32,4096]{2,1,0:T(8,128)(2,1)S(1)}, u32[]{:S(2)}, u32[]{:S(2)}) collective-permute-start(bf16[2,32,4096]{2,1,0:T(8,128)(2,1)S(1)} %get-tuple-element.181), channel_id=1, source_target_pairs={{0,4},{1,5},{2,6},{3,7},{4,0},{5,1},{6,2},{7,3},{8,12},{9,13},{10,... | collective-permute-start | bytes 1572872 | tf_op jit(solution)/shard_map/ppermute | solution.py:518
  424.7 42.9 %collective-permute-start.38 = (bf16[2,32,1024]{2,1,0:T(8,128)(2,1)S(1)}, bf16[2,32,1024]{2,1,0:T(8,128)(2,1)S(1)}, u32[]{:S(2)}, u32[]{:S(2)}) collective-permute-start(bf16[2,32,1024]{2,1,0:T(8,128)(2,1)S(1)} %get-tuple-element.216), channel_id=1, source_target_pairs={{0,4},{1,5},{2,6},{3,7},{4,0},{5,1},{6,2},{7,3},{8,12},{9,13},{10,... | collective-permute-start | bytes 393224 | tf_op jit(solution)/shard_map/ppermute | solution.py:518
  476.9 44.6 %collective-permute-start.20 = (bf16[512,1536]{1,0:T(8,128)(2,1)S(1)}, bf16[512,1536]{1,0:T(8,128)(2,1)}, u32[]{:S(2)}, u32[]{:S(2)}) collective-permute-start(bf16[512,1536]{1,0:T(8,128)(2,1)S(1)} %get-tuple-element.79), channel_id=1, source_target_pairs={{0,8},{1,9},{2,10},{3,11},{4,12},{5,13},{6,14},{7,15},{8,0},{9,1},... | collective-permute-start | bytes 4718600 | tf_op jit(solution)/shard_map/ppermute | solution.py:518
  481.1 21.7 %collective-permute-start.47 = (bf16[128,1024]{1,0:T(8,128)(2,1)S(1)}, bf16[128,1024]{1,0:T(8,128)(2,1)S(1)}, u32[]{:S(2)}, u32[]{:S(2)}) collective-permute-start(bf16[128,1024]{1,0:T(8,128)(2,1)S(1)} %fusion.54), channel_id=1, source_target_pairs={{0,2},{1,3},{2,0},{3,1},{4,6},{5,7},{6,4},{7,5},{8,10},{9,11},{10,... | collective-permute-start | bytes 786440 | tf_op jit(solution)/shard_map/ppermute | solution.py:518
  483.2 19.8 %collective-permute-start.43 = (bf16[32,4096]{1,0:T(8,128)(2,1)S(1)}, bf16[32,4096]{1,0:T(8,128)(2,1)S(1)}, u32[]{:S(2)}, u32[]{:S(2)}) collective-permute-start(bf16[32,4096]{1,0:T(8,128)(2,1)S(1)} %fusion.52), channel_id=1, source_target_pairs={{0,2},{1,3},{2,0},{3,1},{4,6},{5,7},{6,4},{7,5},{8,10},{9,11},{10,... | collective-permute-start | bytes 786440 | tf_op jit(solution)/shard_map/ppermute | solution.py:518
  502.9 12.9 %collective-permute-start.48 = (bf16[128,1024]{1,0:T(8,128)(2,1)S(1)}, bf16[128,1024]{1,0:T(8,128)(2,1)}, u32[]{:S(2)}, u32[]{:S(2)}) collective-permute-start(bf16[128,1024]{1,0:T(8,128)(2,1)S(1)} %fusion.39), channel_id=1, source_target_pairs={{0,8},{1,9},{2,10},{3,11},{4,12},{5,13},{6,14},{7,15},{8,0},{9,1},... | collective-permute-start | bytes 786440 | tf_op jit(solution)/shard_map/ppermute | solution.py:518
  503.8 15.0 %collective-permute-start.44 = (bf16[32,4096]{1,0:T(8,128)(2,1)}, bf16[32,4096]{1,0:T(8,128)(2,1)}, u32[]{:S(2)}, u32[]{:S(2)}) collective-permute-start(bf16[32,4096]{1,0:T(8,128)(2,1)} %fusion.42), channel_id=1, source_target_pairs={{0,8},{1,9},{2,10},{3,11},{4,12},{5,13},{6,14},{7,15},{8,0},{9,1},... | collective-permute-start | bytes 786440 | tf_op jit(solution)/shard_map/ppermute | solution.py:518
  517.6 48.5 %collective-permute-start.49 = (bf16[2,128,1024]{2,1,0:T(8,128)(2,1)}, bf16[2,128,1024]{2,1,0:T(8,128)(2,1)}, u32[]{:S(2)}, u32[]{:S(2)}) collective-permute-start(bf16[2,128,1024]{2,1,0:T(8,128)(2,1)} %pad_maximum_fusion.5), channel_id=1, source_target_pairs={{0,16},{1,17},{2,18},{3,19},{4,20},{5,21},{6,22},{7,23},{8,24},{9,... | collective-permute-start | bytes 1572872 | tf_op jit(solution)/shard_map/ppermute | solution.py:518
  520.7 24.9 %collective-permute-start.45 = (bf16[2,32,4096]{2,1,0:T(8,128)(2,1)}, bf16[2,32,4096]{2,1,0:T(8,128)(2,1)}, u32[]{:S(2)}, u32[]{:S(2)}) collective-permute-start(bf16[2,32,4096]{2,1,0:T(8,128)(2,1)} %pad_maximum_fusion.4), channel_id=1, source_target_pairs={{0,16},{1,17},{2,18},{3,19},{4,20},{5,21},{6,22},{7,23},{8,24},{9,... | collective-permute-start | bytes 1572872 | tf_op jit(solution)/shard_map/ppermute | solution.py:518
  544.5 28.7 %collective-permute-start.31 = (bf16[2,2,2,32,1536]{4,3,1,2,0:T(8,128)(2,1)S(1)}, bf16[2,2,2,32,1536]{4,3,1,2,0:T(8,128)(2,1)S(1)}, u32[]{:S(2)}, u32[]{:S(2)}) collective-permute-start(bf16[2,2,2,32,1536]{4,3,1,2,0:T(8,128)(2,1)S(1)} %fusion.33), channel_id=1, source_target_pairs={{0,1},{1,0},{2,3},{3,2},{4,5},{5,4},{6,7},{7,6},{8,9},{9,8},{10,11... | collective-permute-start | bytes 2359304 | tf_op jit(solution)/shard_map/ppermute | solution.py:518
  551.5 13.7 %collective-permute-start.23 = (bf16[4,120,128]{2,1,0:T(8,128)(2,1)S(1)}, bf16[4,120,128]{2,1,0:T(8,128)(2,1)S(1)}, u32[]{:S(2)}, u32[]{:S(2)}) collective-permute-start(bf16[4,120,128]{2,1,0:T(8,128)(2,1)S(1)} %bitcast.395), channel_id=1, source_target_pairs={{0,1},{1,0},{2,3},{3,2},{4,5},{5,4},{6,7},{7,6},{8,9},{9,8},{10,11... | collective-permute-start | bytes 368648 | tf_op jit(solution)/shard_map/ppermute | solution.py:518
  (90 other events, 715.5 us)
Sparse Core Ops, SparseCore 0:
  11.6 157.2 all-gather.1

commit v4 on v3

--- a/solution.py
+++ b/solution.py
@@ -13,7 +13,8 @@
 CHUNK = 256
 KEY_BLOCK = 128
 EPS_NORM = 1e-06
-ROWS = 512
+UNIT_SHARDS = 8
+ROWS = 256
 FF_BLOCK = 512
 COL_BLOCK = 512
 GELU_ROOT = 0.7978845608028654
@@ -307,21 +308,27 @@
     )
 
 
-def feed_forward(own, norm, grad, expand, bias, shrink, depth_pieces, unit_pieces):
+def feed_forward(own, norm, grad, expand, bias, shrink, half, pieces, name):
     tokens, depth = norm.shape
-    total = bias.shape[1]
+    depth_pieces, unit_pieces = pieces
+    total = bias.shape[1] // 2
     steps = total // FF_BLOCK
     whole = pl.BlockSpec((tokens, depth), lambda i, own: (0, 0))
     half_e = pl.BlockSpec((depth // 2, FF_BLOCK), lambda i, own: (0, i))
-    half_s = pl.BlockSpec((FF_BLOCK // 2, depth), lambda i, own: (i ^ own[2], 0))
-    line = pl.BlockSpec((1, FF_BLOCK), lambda i, own: (0, i))
+    half_s = pl.BlockSpec((FF_BLOCK // 2, depth), lambda i, own: (i, 0))
     if shrink.ndim == 2:
-        spec_e = weight_spec(expand, 0, FF_BLOCK, lambda i, own: i)
-        spec_s = pl.BlockSpec((FF_BLOCK, depth), lambda i, own: (i, 0))
+        spec_e = weight_spec(expand, 2 * half, FF_BLOCK, lambda i, own: i)
+        spec_s = pl.BlockSpec((FF_BLOCK, depth), lambda i, own: (steps * half + i, 0))
     else:
         devices, blocks, rows, columns = shrink.shape
-        spec_e = weight_spec(expand, 4, FF_BLOCK, lambda i, own: i)
-        spec_s = pl.BlockSpec((devices // steps, 4, rows, columns), lambda i, own: (i, 0, 0, 0))
+        shards = devices // 4
+        spec_e = weight_spec(expand, 4 + 2 * half, FF_BLOCK, lambda i, own: i)
+        shrink = shrink.reshape(shards, 2, 2, blocks, rows, columns)
+        spec_s = pl.BlockSpec(
+            (shards // steps, 1, 2, 4, rows, columns), lambda i, own: (i, half, 0, 0, 0, 0)
+        )
+    line = pl.BlockSpec((1, FF_BLOCK), lambda i, own: (0, steps * half + i))
+    line_out = pl.BlockSpec((1, FF_BLOCK), lambda i, own: (0, i))
     wide = jax.ShapeDtypeStruct((tokens, depth), jnp.float32)
     out_e = jax.ShapeDtypeStruct((depth // 2, total), jnp.bfloat16)
     out_s = jax.ShapeDtypeStruct((total // 2, depth), jnp.bfloat16)
@@ -331,7 +338,7 @@
             num_scalar_prefetch=1,
             grid=(steps,),
             in_specs=[whole, whole, spec_e, line, spec_s],
-            out_specs=[whole, whole, half_e, half_e, half_s, half_s, line],
+            out_specs=[whole, whole, half_e, half_e, half_s, half_s, line_out],
             scratch_shapes=[
                 pltpu.VMEM((depth, tokens), jnp.bfloat16),
                 pltpu.VMEM((tokens, FF_BLOCK), jnp.bfloat16),
@@ -349,7 +356,7 @@
         ],
         compiler_params=kernel_params(56),
         cost_estimate=cost(6 * tokens * depth * total, 16 * 2**20, tokens * total),
-        name="feed_forward",
+        name=name,
     )(own, norm, grad, expand, bias, shrink)
 
 
@@ -578,12 +585,37 @@
         while self.order:
             self.step()
         own = self.stay.astype(jnp.float32) + self.arrived.reshape(self.stay.shape).astype(jnp.float32)
-        own = own.astype(jnp.bfloat16)
-        pair = [own, exchange(own, *MASKS["core"])]
-        both = jnp.stack(pair)
-        other = exchange(both, *MASKS["y"])
-        parts = to_absolute([*pair, other[0], other[1]], lax.axis_index("rep"))
-        return jnp.concatenate(parts, axis=0).astype(jnp.float32)
+        return gather_reps(own.astype(jnp.bfloat16))
+
+
+def gather_reps(own):
+    pair = [own, exchange(own, *MASKS["core"])]
+    other = exchange(jnp.stack(pair), *MASKS["y"])
+    parts = to_absolute([*pair, other[0], other[1]], lax.axis_index("rep"))
+    return jnp.concatenate(parts, axis=0).astype(jnp.float32)
+
+
+class GroupSum:
+    def __init__(self, keep, send):
+        self.keep = keep
+        self.arrived = exchange(send, *MASKS["core"])
+
+    def step(self):
+        total = self.keep.astype(jnp.float32) + self.arrived.astype(jnp.float32)
+        self.arrived = total.astype(jnp.bfloat16)
+
+    def launch(self):
+        shards = lax.axis_size("fsdp")
+        groups = [
+            [(2 * y + core) * shards + shard for shard in range(shards) for y in range(2)]
+            for core in range(2)
+        ]
+        self.arrived = lax.psum_scatter(
+            self.arrived, ("rep", "fsdp"), scatter_dimension=0, axis_index_groups=groups, tiled=True
+        )
+
+    def finish(self):
+        return gather_reps(self.arrived)
 
 
 class PlainSum:
@@ -591,6 +623,9 @@
         self.arrived = grad
 
     def step(self):
+        pass
+
+    def launch(self):
         pass
 
     def finish(self):
@@ -616,6 +651,18 @@
 
 def gather_rows(weight):
     return lax.all_gather(own_quarter(weight), ("fsdp", "rep"), axis=0, tiled=True)
+
+
+def by_half(columns):
+    rows, count = columns.shape
+    split = columns.reshape(rows, UNIT_SHARDS, 2, count // (2 * UNIT_SHARDS))
+    return split.transpose(0, 2, 1, 3).reshape(rows, count)
+
+
+def undo_by_half(first, second):
+    rows, count = first.shape
+    split = [half.reshape(rows, UNIT_SHARDS, count // UNIT_SHARDS) for half in (first, second)]
+    return jnp.stack(split, axis=2).reshape(rows, 2 * count)
 
 
 def column_blocks(quarter, width):
@@ -667,31 +714,33 @@
         packed = gather_packed(
             [
                 own_quarter(shrinker),
-                column_blocks(own_quarter(expander), feature),
+                column_blocks(by_half(own_quarter(expander)), feature),
                 own_quarter(outweight),
             ],
             quarter,
         )
         out_at = (packed, 8)
         w_expand, w_shrink = packed, packed
-        depth_pieces, unit_pieces = shards * reps, reps
+        depth_pieces, unit_pieces = shards * reps, 2 * reps
+        own_core = jnp.stack([rep_id & 1] + [jnp.zeros_like(rep_id)] * 3).astype(jnp.int32)
         own = jnp.stack(
             [rep_id & 1, shard_id * 2 + (rep_id >> 1), shard_id, rep_id >> 1]
         ).astype(jnp.int32)
     else:
         w_proj, out_at = gather_rows(projector), (gather_rows(outweight), 0)
-        w_expand, w_shrink = gather_rows(expander), gather_rows(shrinker)
+        w_expand = by_half(gather_rows(expander))
+        w_shrink = by_half(gather_rows(shrinker).T).T
         depth_pieces, unit_pieces = 2, 2
-        own = jnp.zeros((4,), jnp.int32)
-
-    def depth_sum(halves, order):
+        own = own_core = jnp.zeros((4,), jnp.int32)
+
+    def depth_sum(halves, order=None):
         if halving:
-            return HalvingSum(*halves, order)
+            return HalvingSum(*halves, order) if order else GroupSum(*halves)
         return PlainSum(jnp.concatenate(halves, axis=0))
 
-    def unit_sum(halves, order):
+    def unit_sum(halves):
         if halving:
-            return HalvingSum(*halves, order)
+            return GroupSum(*halves)
         blocks = [half.reshape(-1, 1, FF_BLOCK // 2, feature) for half in halves]
         return PlainSum(jnp.concatenate(blocks, axis=1).reshape(-1, feature))
 
@@ -740,12 +789,37 @@
     grad_out = upstream.astype(jnp.float32)
     d_branch_m = (gate_m[:, None, :] * grad_out).astype(jnp.bfloat16).reshape(token_count, feature)
     g_shrinkbias = jnp.sum(d_branch_m, axis=0, dtype=jnp.float32)
-    branch_m, d_norm_m, keep_e, send_e, keep_s, send_s, g_expandbias = feed_forward(
-        own, norm_m, d_branch_m, w_expand, b_expand, w_shrink, depth_pieces, unit_pieces
-    )
-    sum_e = depth_sum((keep_e, send_e), ("y", "x", "z2", "z1"))
-    sum_s = unit_sum((keep_s, send_s), ("x", "y", "z2", "z1"))
-    branch_m = (branch_m + b_shrink).reshape(seqs_dev, seq_len, feature)
+    b_units = by_half(b_expand)
+    branch_parts, norm_parts, bias_parts, sums_e, sums_s = [], [], [], [], []
+    norm_now = norm_m
+    for half in range(2):
+        branch, d_norm, keep_e, send_e, keep_s, send_s, d_bias = feed_forward(
+            own_core,
+            norm_now,
+            d_branch_m,
+            w_expand,
+            b_units,
+            w_shrink,
+            half,
+            (depth_pieces, unit_pieces),
+            ("feed_forward_low", "feed_forward_high")[half],
+        )
+        branch_parts.append(branch)
+        norm_parts.append(d_norm)
+        bias_parts.append(d_bias)
+        sum_e, sum_s = depth_sum((keep_e, send_e)), unit_sum((keep_s, send_s))
+        sums_e.append(sum_e)
+        sums_s.append(sum_s)
+        sum_e.step()
+        sum_s.step()
+        if half == 0:
+            norm_now = hold(norm_m, sum_e, sum_s)
+            sum_e.launch()
+            sum_s.launch()
+    g_expandbias = undo_by_half(*bias_parts)
+    d_norm_m = norm_parts[0] + norm_parts[1]
+    branch_m = branch_parts[0] + branch_parts[1] + b_shrink
+    branch_m = branch_m.reshape(seqs_dev, seq_len, feature)
     layer_out = middle + gate_m[:, None, :] * branch_m
     d_gate_m = jnp.sum(grad_out * branch_m, axis=1)
     _, norm_pull_m = jax.vjp(modulate, middle, shift_m, scale_m)
@@ -755,31 +829,29 @@
     d_gate_a = jnp.sum(d_middle * branch_a, axis=1)
     g_outbiases = jnp.sum(d_branch_a, axis=0, dtype=jnp.float32)
     d_attended = backward_dot(d_branch_a, *out_at, jnp.bfloat16, "attention_out_back")
+    sum_e, sum_s = sums_e[1], sums_s[1]
     d_attended = hold(d_attended, sum_e, sum_s)
-    sum_e.step()
-    sum_s.step()
+    sum_e.launch()
+    sum_s.launch()
     half_pairs = HEADS // 4
     d_low, q_low, v_low = attention_backward(
         projected, d_attended, attended_t, log_totals, 0, half_pairs, "attention_backward_low"
     )
-    sum_low = depth_sum(
-        grad_dot(own, norm_a, d_low, depth_pieces, "projector_grad_low"), ("y", "x", "z2", "z1")
-    )
     sum_out = depth_sum(
-        grad_dot(own, attended, d_branch_a[None], depth_pieces, "outweight_grad"),
-        ("x", "y", "z2", "z1"),
-    )
-    d_attended = hold(d_attended, sum_e, sum_s, sum_low, sum_out)
-    for total in (sum_e, sum_s, sum_low, sum_out):
-        total.step()
+        grad_dot(own_core, attended, d_branch_a[None], depth_pieces, "outweight_grad")
+    )
+    sum_low = depth_sum(grad_dot(own_core, norm_a, d_low, depth_pieces, "projector_grad_low"))
+    d_attended = hold(d_attended, sum_low, sum_out)
     d_high, q_high, v_high = attention_backward(
         projected, d_attended, attended_t, log_totals, half_pairs, half_pairs, "attention_backward_high"
     )
-    d_high = hold(d_high, sum_e, sum_s, sum_low, sum_out)
-    for total in (sum_e, sum_s, sum_low, sum_out):
-        total.step()
+    sum_out.step()
+    sum_low.step()
+    d_high = hold(d_high, sum_low, sum_out)
+    sum_out.launch()
+    sum_low.launch()
     sum_high = depth_sum(
-        grad_dot(own, norm_a, d_high, depth_pieces, "projector_grad_high"), ("x", "y", "z2", "z1")
+        grad_dot(own, norm_a, d_high, depth_pieces, "projector_grad_high"), ("y", "x", "z2", "z1")
     )
     d_norm_a = project_back(d_low, d_high, w_proj)
     d_norm_a = hold(d_norm_a, sum_high)
@@ -811,7 +883,12 @@
     devices = reps * shards
     size = seqs_dev * feature
     gathered = gather_relative(small.reshape(-1, 128)).reshape(devices, -1)
-    g_expander, g_shrinker = sum_e.finish(), sum_s.finish()
+    g_expander = undo_by_half(sums_e[0].finish(), sums_e[1].finish())
+    if halving:
+        g_shrinker = jnp.concatenate([sums_s[0].finish(), sums_s[1].finish()], axis=0)
+    else:
+        units = [total.arrived.reshape(UNIT_SHARDS, 1, -1, feature) for total in sums_s]
+        g_shrinker = scatter_rows(jnp.concatenate(units, axis=1).reshape(-1, feature))
     g_outweight = sum_out.finish()
     low, high = sum_low.finish(), sum_high.finish()
     g_projector = jnp.stack(

time: 632 us -> 794 us (1.26)
  waiting for transfers between devices: 216 us -> 338 us
  other arithmetic: 86.3 us -> 111 us
  local copies, waits for them, and re-layouts: 59 us -> 78.7 us
  starting transfers between devices: 51.3 us -> 35.3 us
  Pallas kernels: 197 us -> 208 us
    reduce_scatter x0 -> x6, waiting for transfers between devices: none -> 176 us  [launch(): lax.psum_scatter(self.arrived, ('rep', 'fsdp'), scatter_dimension=0, axis...]
    ppermute x50 -> x40, waiting for transfers between devices: 202 us -> 146 us  [exchange(): return lax.ppermute(value, ('rep', 'fsdp'), pairs)]
    unnamed x170 -> x168, local copies, waits for them, and re-layouts: 25.3 us -> 54.7 us
    ppermute x50 -> x40, starting transfers between devices: 43.6 us -> 27.3 us  [exchange(): return lax.ppermute(value, ('rep', 'fsdp'), pairs)]
    convert_element_type x9 -> x8, other arithmetic: 5.62 us -> 21.9 us  [the longest x6 21 us: step(): self.arrived = total.astype(jnp.bfloat16)]
    convert_element_type x25 -> x5, other arithmetic: 19.5 us -> 4.49 us  [half(): (stay.astype(jnp.float32) + arrived.astype(jnp.float32)).astype(jnp.bfloa...]
    pallas_call x1 -> x2, Pallas kernels: 74.4 us -> 84.7 us  [feed_forward(): pl.pallas_call(partial(feed_forward_kernel, depth_pieces, unit_pieces), g...]
    unnamed x8 -> x16, other arithmetic: 0.11 us -> 8.82 us
  transfers between devices with their start and end apart: 52 -> 48, of which waited for: 24 -> 23; matrix products, arithmetic and copies ran while one was open for 19% -> 19% of each run, Pallas kernels for 15% -> 20%
where the time goes in v4:
time: 794 us; the launch traced here: 789 us
  waiting for transfers between devices  338 us (43%)
  Pallas kernels  208 us (26%)
  other arithmetic  111 us (14%)
  local copies, waits for them, and re-layouts  78.7 us (10%)
  starting transfers between devices  35.3 us (4%)
  between operations  15.7 us (2%)
    reduce_scatter x6, waiting for transfers between devices, launch(): lax.psum_scatter(self.arrived, ('rep', 'fsdp'), scatter_dimension=0, axis...  176 us
    ppermute x40, waiting for transfers between devices, exchange(): return lax.ppermute(value, ('rep', 'fsdp'), pairs)  146 us
    pallas_call x2, Pallas kernels, feed_forward(): pl.pallas_call(partial(feed_forward_kernel, depth_pieces, unit_pieces), g...  84.7 us
    unnamed x168, local copies, waits for them, and re-layouts  54.7 us
    pallas_call x2, Pallas kernels, attention_backward(): pl.pallas_call(attention_backward_kernel, grid=(count,), in_specs=[pl.Blo...  48 us
    pallas_call x1, Pallas kernels, attention_forward(): pl.pallas_call(attention_forward_kernel, grid=(pairs,), in_specs=[pl.Bloc...  30.1 us
    ppermute x40, starting transfers between devices, exchange(): return lax.ppermute(value, ('rep', 'fsdp'), pairs)  27.3 us
    convert_element_type x6, other arithmetic, step(): self.arrived = total.astype(jnp.bfloat16)  21 us
  transfers between devices with their start and end apart: 48, of which 23 were waited for; matrix products, arithmetic and copies ran while one was open for 19% of the time, Pallas kernels for 20%

profile of v4, /device:TPU:0, one launch (start us, length us, event | category | flops | bytes accessed | tf_op | source)
XLA Modules:
  0.0 789.4 jit_solution(17692687390866008051)
XLA Ops:
  14.2 7.3 all-to-all-start
  31.2 6.6 collective-permute-done.5
  46.4 11.5 %collective-permute-done.6 = bf16[2,32,1536]{2,1,0:T(8,128)(2,1)S(1)} collective-permute-done((bf16[2,32,1536]{2,1,0:T(8,128)(2,1)S(1)}, bf16[2,32,1536]{2,1,0:T(8,128)(2,1)S(1)}, u32[]{:S(2)}, u32[]{:S(2)}) %collective-permute-start.6) | collective-permute-done | bytes 196640 | tf_op jit(solution)/shard_map/ppermute | solution.py:525
  66.7 12.2 %collective-permute-done.7 = bf16[4,32,1536]{2,1,0:T(8,128)(2,1)} collective-permute-done((bf16[4,32,1536]{2,1,0:T(8,128)(2,1)}, bf16[4,32,1536]{2,1,0:T(8,128)(2,1)}, u32[]{:S(2)}, u32[]{:S(2)}) %collective-permute-start.7) | collective-permute-done | bytes 393248 | tf_op jit(solution)/shard_map/ppermute | solution.py:525
  90.3 13.9 %collective-permute-done.8 = bf16[8,32,1536]{2,1,0:T(8,128)(2,1)S(1)} collective-permute-done((bf16[8,32,1536]{2,1,0:T(8,128)(2,1)S(1)}, bf16[8,32,1536]{2,1,0:T(8,128)(2,1)S(1)}, u32[]{:S(2)}, u32[]{:S(2)}) %collective-permute-start.8) | collective-permute-done | bytes 786464 | tf_op jit(solution)/shard_map/ppermute | solution.py:525
  111.1 12.3 %project.1 = (bf16[1024,3072]{1,0:T(8,128)(2,1)}, bf16[1024,3072]{1,0:T(8,128)(2,1)}) custom-call(s32[1]{0:T(128)} %bitcast.2.own_ref, bf16[1024,1024]{1,0:T(8,128)(2,1)S(1)} %fusion.17.x_ref, f32[1,3072]{1,0:T(1,128)S(1)} %pad_maximum_fusion.19.b_ref, bf16[16,32,1536]{2,1,0:T(8,128)(2,1)S(1)} %constant_dynamic-update-slice_fusion.refs_0_, ...), custom_call_target="tpu_custom_call" | custom-call | flops 3221225472 | bytes 3145728 | tf_op jit(solution)/shard_map/project/pallas_call | solution.py:106
  123.4 30.1 %attention_forward.1 = (bf16[1024,1024]{1,0:T(8,128)(2,1)S(1)}, f32[1024,1024]{1,0:T(8,128)}, f32[8,2,1024]{2,1,0:T(2,128)S(1)}) custom-call(bf16[1024,3072]{1,0:T(8,128)(2,1)} %get-tuple-element.59.q_ref.k_ref.v_ref, bf16[1024,3072]{1,0:T(8,128)(2,1)} %get-tuple-element.59.q_ref.k_ref.v_ref, bf16[1024,3072]{1,0:T(8,128)(2,1)} %get-tuple-element.59.q_ref.k_ref.v_ref), custom_call_target="tpu_custom_call" | custom-call | flops 4294967296 | bytes 8388608 | tf_op jit(solution)/shard_map/attention_forward/pallas_call | solution.py:403
  154.8 14.5 %all-gather.2.cloned.1.call-done = bf16[9216,1024]{1,0:T(8,128)(2,1)} async-done(((bf16[288,1024]{1,0:T(8,128)(2,1)}), bf16[9216,1024]{1,0:T(8,128)(2,1)}) %all-gather.2.cloned.1.call-update) | async-done | bytes 18874384 | tf_op jit(solution)/shard_map/all_gather | solution.py:677
  170.9 4.2 attention_out.1
  179.8 42.1 %feed_forward_low.1 = (f32[1024,1024]{1,0:T(8,128)}, f32[1024,1024]{1,0:T(8,128)}, bf16[512,2048]{1,0:T(8,128)(2,1)}, bf16[512,2048]{1,0:T(8,128)(2,1)}, bf16[10...) custom-call(s32[4]{0:T(128)} %pad_add_fusion.own_ref, bf16[1024,1024]{1,0:T(8,128)(2,1)} %fusion.16.norm_ref, ...), custom_call_target="tpu_custom_call" | custom-call | flops 12884901888 | bytes 16777216 | tf_op jit(solution)/shard_map/feed_forward_low/pallas_call | solution.py:335
  222.5 4.3 collective-permute-done.10
  230.5 4.5 add_convert_fusion.2
  235.1 42.6 %feed_forward_high.1 = (f32[1024,1024]{1,0:T(8,128)}, f32[1024,1024]{1,0:T(8,128)}, bf16[512,2048]{1,0:T(8,128)(2,1)}, bf16[512,2048]{1,0:T(8,128)(2,1)}, bf16[1...) custom-call(s32[4]{0:T(128)} %pad_add_fusion.own_ref, bf16[1024,1024]{1,0:T(8,128)(2,1)} %fusion.16.norm_ref, ...), custom_call_target="tpu_custom_call" | custom-call | flops 12884901888 | bytes 16777216 | tf_op jit(solution)/shard_map/feed_forward_high/pallas_call | solution.py:335
  286.5 5.0 fusion.66
  293.5 5.5 attention_out_back.1.g_ref
  300.4 3.9 add_convert_fusion
  304.3 4.5 add_convert_fusion.1
  310.4 24.1 %attention_backward_low.1 = (bf16[3,1024,512]{2,1,0:T(8,128)(2,1)S(1)}, f32[1,512]{1,0:T(1,128)S(1)}, f32[1,512]{1,0:T(1,128)S(1)}) custom-call(bf16[1024,3072]{1,0:T(8,128)(2,1)} %get-tuple-element.59.q_ref.k_ref.v_ref, bf16[1024,3072]{1,0:T(8,128)(2,1)} %get-tuple-element.59.q_ref.k_ref.v_ref, bf16[1024,3072]{1,0:T(8,128)(2,1)} %get-tuple-element.59.q_ref.k_ref.v_ref, ...), custom_call_target="tpu_custom_call" | custom-call | flops 2147483648 | bytes 8388608 | tf_op jit(solution)/shard_map/attention_backward_low/pallas_call | solution.py:480
  334.5 4.9 projector_grad_low.1
  346.1 24.0 %attention_backward_high.1 = (bf16[3,1024,512]{2,1,0:T(8,128)(2,1)S(1)}, f32[1,512]{1,0:T(1,128)S(1)}, f32[1,512]{1,0:T(1,128)S(1)}) custom-call(bf16[1024,3072]{1,0:T(8,128)(2,1)} %get-tuple-element.59.q_ref.k_ref.v_ref, bf16[1024,3072]{1,0:T(8,128)(2,1)} %get-tuple-element.59.q_ref.k_ref.v_ref, bf16[1024,3072]{1,0:T(8,128)(2,1)} %get-tuple-element.59.q_ref.k_ref.v_ref, ...), custom_call_target="tpu_custom_call" | custom-call | flops 2147483648 | bytes 8388608 | tf_op jit(solution)/shard_map/attention_backward_high/pallas_call | solution.py:480
  383.6 5.6 projector_grad_high.1
  393.6 9.1 %project_back.1 = f32[1024,1024]{1,0:T(8,128)S(1)} custom-call(bf16[3,1024,512]{2,1,0:T(8,128)(2,1)S(1)} %copy-done.13, bf16[3,1024,512]{2,1,0:T(8,128)(2,1)S(1)} %copy-done.16, bf16[1024,3072]{1,0:T(8,128)(2,1)} %get-tuple-element.87.w_ref), custom_call_target="tpu_custom_call" | custom-call | flops 1610612736 | bytes 524288 | tf_op jit(solution)/shard_map/project_back/pallas_call | solution.py:191
  409.4 8.0 %collective-permute-done.37 = bf16[2,64,1024]{2,1,0:T(8,128)(2,1)S(1)} collective-permute-done((bf16[2,64,1024]{2,1,0:T(8,128)(2,1)S(1)}, bf16[2,64,1024]{2,1,0:T(8,128)(2,1)S(1)}, u32[]{:S(2)}, u32[]{:S(2)}) %collective-permute-start.37) | collective-permute-done | bytes 262176 | tf_op jit(solution)/shard_map/ppermute | solution.py:525
  420.5 5.2 collective-permute-done.33
  435.6 4.2 fusion.8
  441.0 9.8 %fusion.12 = (bf16[1024]{0:T(1024)(128)(2,1)S(1)}, bf16[1024]{0:T(1024)(128)(2,1)S(1)}, f32[1,1024,1024]{2,1,0:T(8,128)}, f32[1,1024,1024]{2,1,0:T(8,128)}) fusion(bf16[1,1024,1024]{2,1,0:T(8,128)(2,1)} %param.27, f32[1024]{0:T(1024)S(1)} %copy-done.51, f32[1024,1024]{1,0:T(8,128)} %get-tuple-element.61, f32[1024,1024]{1,0:T(8,128)} %get-tuple-element.67, ...), kind=kLoop, calls=%fused_computation.20 | loop fusion | flops 20969472 | bytes 37785600 | tf_op jit(solution)/shard_map/reduce_sum | solution.py:824
  490.7 52.7 %collective-permute-done.20 = bf16[8,120,128]{2,1,0:T(8,128)(2,1)S(1)} collective-permute-done((bf16[8,120,128]{2,1,0:T(8,128)(2,1)S(1)}, bf16[8,120,128]{2,1,0:T(8,128)(2,1)S(1)}, u32[]{:S(2)}, u32[]{:S(2)}) %collective-permute-start.20) | collective-permute-done | bytes 245792 | tf_op jit(solution)/shard_map/ppermute | solution.py:525
  557.4 77.3 %reduce-scatter.13.cloned.1.call-done = bf16[32,2048]{1,0:T(8,128)(2,1)} async-done(((bf16[512,2048]{1,0:T(8,128)(2,1)}), bf16[32,2048]{1,0:T(8,128)(2,1)}) %reduce-scatter.13.cloned.1.call-update) | async-done | bytes 131088 | tf_op jit(solution)/shard_map/reduce_scatter | solution.py:613
  640.0 5.1 collective-permute-done.26
  656.0 3.9 reshape.696
  662.7 98.8 %reduce-scatter.7.cloned.1.call-done = bf16[32,1536]{1,0:T(8,128)(2,1)} async-done(((bf16[512,1536]{1,0:T(8,128)(2,1)}), bf16[32,1536]{1,0:T(8,128)(2,1)}) %reduce-scatter.7.cloned.1.call-update) | async-done | bytes 98320 | tf_op jit(solution)/shard_map/reduce_scatter | solution.py:613
  765.3 4.0 collective-permute-done.29
  (400 shorter events, 212.1 us)
Async XLA Ops:
  7.3 162.1 %all-gather.2.cloned.1.call-start = ((), (), s32[]{:S(2)}) async-start(), calls=%async_computation.7 | async-start | bytes 19464192 | tf_op jit(solution)/shard_map/all_gather | solution.py:677
  14.2 51.5 %all-to-all-start = ((f32[8,1,7936]{2,1,0:T(1,128)}), f32[8,1,7936]{2,1,0:T(1,128)}, u32[]{:S(2)}, u32[]{:S(2)}) async-start(f32[8,1,7936]{2,1,0:T(1,128)} %copy.77), calls=%async_computation | async-start | bytes 507904 | tf_op jit(solution)/shard_map/all_to_all | solution.py:763
  21.5 368.0 %reduce-scatter.15.cloned.1.call-start = ((), (), s32[]{:S(2)}) async-start(), calls=%async_computation.12 | async-start | bytes 2228224 | tf_op jit(solution)/shard_map/reduce_scatter | solution.py:613
  23.7 14.1 %collective-permute-start.5 = (bf16[1,32,1536]{2,1,0:T(8,128)(2,1)S(1)}, bf16[1,32,1536]{2,1,0:T(8,128)(2,1)S(1)}, u32[]{:S(2)}, u32[]{:S(2)}) collective-permute-start(bf16[1,32,1536]{2,1,0:T(8,128)(2,1)S(1)} %get-tuple-element.175), channel_id=1, source_target_pairs={{0,2},{1,3},{2,0},{3,1},{4,6},{5,7},{6,4},{7,5},{8,10},{9,11},{10,... | collective-permute-start | bytes 294920 | tf_op jit(solution)/shard_map/ppermute | solution.py:525
  25.7 17.5 %collective-permute-start = (bf16[1,32,1536]{2,1,0:T(8,128)(2,1)S(1)}, bf16[1,32,1536]{2,1,0:T(8,128)(2,1)S(1)}, u32[]{:S(2)}, u32[]{:S(2)}) collective-permute-start(bf16[1,32,1536]{2,1,0:T(8,128)(2,1)S(1)} %get-tuple-element.190), channel_id=1, source_target_pairs={{0,2},{1,3},{2,0},{3,1},{4,6},{5,7},{6,4},{7,5},{8,10},{9,11},{10,... | collective-permute-start | bytes 294920 | tf_op jit(solution)/shard_map/ppermute | solution.py:525
  38.4 19.5 %collective-permute-start.6 = (bf16[2,32,1536]{2,1,0:T(8,128)(2,1)S(1)}, bf16[2,32,1536]{2,1,0:T(8,128)(2,1)S(1)}, u32[]{:S(2)}, u32[]{:S(2)}) collective-permute-start(bf16[2,32,1536]{2,1,0:T(8,128)(2,1)S(1)} %pad_maximum_fusion.13), channel_id=1, source_target_pairs={{0,4},{1,5},{2,6},{3,7},{4,0},{5,1},{6,2},{7,3},{8,12},{9,13},{10,... | collective-permute-start | bytes 589832 | tf_op jit(solution)/shard_map/ppermute | solution.py:525
  43.9 17.9 %collective-permute-start.1 = (bf16[2,32,1536]{2,1,0:T(8,128)(2,1)S(1)}, bf16[2,32,1536]{2,1,0:T(8,128)(2,1)S(1)}, u32[]{:S(2)}, u32[]{:S(2)}) collective-permute-start(bf16[2,32,1536]{2,1,0:T(8,128)(2,1)S(1)} %pad_maximum_fusion.12), channel_id=1, source_target_pairs={{0,4},{1,5},{2,6},{3,7},{4,0},{5,1},{6,2},{7,3},{8,12},{9,13},{10,... | collective-permute-start | bytes 589832 | tf_op jit(solution)/shard_map/ppermute | solution.py:525
  59.7 19.2 %collective-permute-start.7 = (bf16[4,32,1536]{2,1,0:T(8,128)(2,1)}, bf16[4,32,1536]{2,1,0:T(8,128)(2,1)}, u32[]{:S(2)}, u32[]{:S(2)}) collective-permute-start(bf16[4,32,1536]{2,1,0:T(8,128)(2,1)} %pad_maximum_fusion.6), channel_id=1, source_target_pairs={{0,16},{1,17},{2,18},{3,19},{4,20},{5,21},{6,22},{7,23},{8,24},{9,... | collective-permute-start | bytes 1179656 | tf_op jit(solution)/shard_map/ppermute | solution.py:525
  63.5 20.7 %collective-permute-start.2 = (bf16[4,32,1536]{2,1,0:T(8,128)(2,1)}, bf16[4,32,1536]{2,1,0:T(8,128)(2,1)}, u32[]{:S(2)}, u32[]{:S(2)}) collective-permute-start(bf16[4,32,1536]{2,1,0:T(8,128)(2,1)} %pad_maximum_fusion.5), channel_id=1, source_target_pairs={{0,1},{1,0},{2,3},{3,2},{4,5},{5,4},{6,7},{7,6},{8,9},{9,8},{10,11... | collective-permute-start | bytes 1179656 | tf_op jit(solution)/shard_map/ppermute | solution.py:525
  80.0 24.2 %collective-permute-start.8 = (bf16[8,32,1536]{2,1,0:T(8,128)(2,1)S(1)}, bf16[8,32,1536]{2,1,0:T(8,128)(2,1)S(1)}, u32[]{:S(2)}, u32[]{:S(2)}) collective-permute-start(bf16[8,32,1536]{2,1,0:T(8,128)(2,1)S(1)} %pad_maximum_fusion.2), channel_id=1, source_target_pairs={{0,1},{1,0},{2,3},{3,2},{4,5},{5,4},{6,7},{7,6},{8,9},{9,8},{10,11... | collective-permute-start | bytes 2359304 | tf_op jit(solution)/shard_map/ppermute | solution.py:525
  85.4 19.8 %collective-permute-start.3 = (bf16[8,32,1536]{2,1,0:T(8,128)(2,1)S(1)}, bf16[8,32,1536]{2,1,0:T(8,128)(2,1)S(1)}, u32[]{:S(2)}, u32[]{:S(2)}) collective-permute-start(bf16[8,32,1536]{2,1,0:T(8,128)(2,1)S(1)} %pad_maximum_fusion.1), channel_id=1, source_target_pairs={{0,16},{1,17},{2,18},{3,19},{4,20},{5,21},{6,22},{7,23},{8,24},{9,... | collective-permute-start | bytes 2359304 | tf_op jit(solution)/shard_map/ppermute | solution.py:525
  235.1 169.7 %reduce-scatter.11.cloned.1.call-start = ((), (), s32[]{:S(2)}) async-start(), calls=%async_computation.10 | async-start | bytes 2228224 | tf_op jit(solution)/shard_map/reduce_scatter | solution.py:613
  277.7 26.6 %collective-permute-start.12 = (bf16[512,2048]{1,0:T(8,128)(2,1)}, bf16[512,2048]{1,0:T(8,128)(2,1)}, u32[]{:S(2)}, u32[]{:S(2)}) collective-permute-start(bf16[512,2048]{1,0:T(8,128)(2,1)} %get-tuple-element.71), channel_id=1, source_target_pairs={{0,8},{1,9},{2,10},{3,11},{4,12},{5,13},{6,14},{7,15},{8,0},{9,1},... | collective-permute-start | bytes 6291464 | tf_op jit(solution)/shard_map/ppermute | solution.py:525
  278.0 22.3 %collective-permute-start.13 = (bf16[1024,1024]{1,0:T(8,128)(2,1)}, bf16[1024,1024]{1,0:T(8,128)(2,1)}, u32[]{:S(2)}, u32[]{:S(2)}) collective-permute-start(bf16[1024,1024]{1,0:T(8,128)(2,1)} %get-tuple-element.73), channel_id=1, source_target_pairs={{0,8},{1,9},{2,10},{3,11},{4,12},{5,13},{6,14},{7,15},{8,0},{9,1},... | collective-permute-start | bytes 6291464 | tf_op jit(solution)/shard_map/ppermute | solution.py:525
  286.4 196.2 %reduce-scatter.9.cloned.1.call-start = ((), (), s32[]{:S(2)}) async-start(), calls=%async_computation.9 | async-start | bytes 1114112 | tf_op jit(solution)/shard_map/reduce_scatter | solution.py:613
  376.1 179.9 %reduce-scatter.17.cloned.1.call-start = ((), (), s32[]{:S(2)}) async-start(), calls=%async_computation.13 | async-start | bytes 2228224 | tf_op jit(solution)/shard_map/reduce_scatter | solution.py:613
  376.7 258.0 %reduce-scatter.13.cloned.1.call-start = ((), (), s32[]{:S(2)}) async-start(), calls=%async_computation.11 | async-start | bytes 2228224 | tf_op jit(solution)/shard_map/reduce_scatter | solution.py:613
  377.3 384.2 %reduce-scatter.7.cloned.1.call-start = ((), (), s32[]{:S(2)}) async-start(), calls=%async_computation.8 | async-start | bytes 1671168 | tf_op jit(solution)/shard_map/reduce_scatter | solution.py:613
  389.2 38.3 %collective-permute-start.16 = (bf16[512,1536]{1,0:T(8,128)(2,1)}, bf16[512,1536]{1,0:T(8,128)(2,1)}, u32[]{:S(2)}, u32[]{:S(2)}) collective-permute-start(bf16[512,1536]{1,0:T(8,128)(2,1)} %get-tuple-element.88), channel_id=1, source_target_pairs={{0,8},{1,9},{2,10},{3,11},{4,12},{5,13},{6,14},{7,15},{8,0},{9,1},... | collective-permute-start | bytes 4718600 | tf_op jit(solution)/shard_map/ppermute | solution.py:525
  389.5 15.5 %collective-permute-start.36 = (bf16[64,1024]{1,0:T(8,128)(2,1)}, bf16[64,1024]{1,0:T(8,128)(2,1)S(1)}, u32[]{:S(2)}, u32[]{:S(2)}) collective-permute-start(bf16[64,1024]{1,0:T(8,128)(2,1)} %reduce-scatter.15.cloned.1.call-done), channel_id=1, source_target_pairs={{0,8},{1,9},{2,10},{3,11},{4,12},{5,13},{6,14},{7,15},{8,0},{9,1},... | collective-permute-start | bytes 393224 | tf_op jit(solution)/shard_map/ppermute | solution.py:525
  405.7 11.7 %collective-permute-start.37 = (bf16[2,64,1024]{2,1,0:T(8,128)(2,1)S(1)}, bf16[2,64,1024]{2,1,0:T(8,128)(2,1)S(1)}, u32[]{:S(2)}, u32[]{:S(2)}) collective-permute-start(bf16[2,64,1024]{2,1,0:T(8,128)(2,1)S(1)} %pad_maximum_fusion.9), channel_id=1, source_target_pairs={{0,16},{1,17},{2,18},{3,19},{4,20},{5,21},{6,22},{7,23},{8,24},{9,... | collective-permute-start | bytes 786440 | tf_op jit(solution)/shard_map/ppermute | solution.py:525
  408.7 17.0 %collective-permute-start.33 = (bf16[2,32,2048]{2,1,0:T(8,128)(2,1)S(1)}, bf16[2,32,2048]{2,1,0:T(8,128)(2,1)S(1)}, u32[]{:S(2)}, u32[]{:S(2)}) collective-permute-start(bf16[2,32,2048]{2,1,0:T(8,128)(2,1)S(1)} %pad_maximum_fusion.7), channel_id=1, source_target_pairs={{0,16},{1,17},{2,18},{3,19},{4,20},{5,21},{6,22},{7,23},{8,24},{9,... | collective-permute-start | bytes 786440 | tf_op jit(solution)/shard_map/ppermute | solution.py:525
  463.5 11.1 %collective-permute-start.17 = (bf16[1,120,128]{2,1,0:T(8,128)(2,1)}, bf16[1,120,128]{2,1,0:T(8,128)(2,1)S(1)}, u32[]{:S(2)}, u32[]{:S(2)}) collective-permute-start(bf16[1,120,128]{2,1,0:T(8,128)(2,1)} %bitcast.42), channel_id=1, source_target_pairs={{0,4},{1,5},{2,6},{3,7},{4,0},{5,1},{6,2},{7,3},{8,12},{9,13},{10,... | collective-permute-start | bytes 92168 | tf_op jit(solution)/shard_map/ppermute | solution.py:525
  481.9 64.4 %collective-permute-start.24 = (bf16[2,2,2,32,1536]{4,3,1,2,0:T(8,128)(2,1)}, bf16[2,2,2,32,1536]{4,3,1,2,0:T(8,128)(2,1)}, u32[]{:S(2)}, u32[]{:S(2)}) collective-permute-start(bf16[2,2,2,32,1536]{4,3,1,2,0:T(8,128)(2,1)} %fusion.21), channel_id=1, source_target_pairs={{0,16},{1,17},{2,18},{3,19},{4,20},{5,21},{6,22},{7,23},{8,24},{9,... | collective-permute-start | bytes 2359304 | tf_op jit(solution)/shard_map/ppermute | solution.py:525
  487.4 55.9 %collective-permute-start.20 = (bf16[8,120,128]{2,1,0:T(8,128)(2,1)S(1)}, bf16[8,120,128]{2,1,0:T(8,128)(2,1)S(1)}, u32[]{:S(2)}, u32[]{:S(2)}) collective-permute-start(bf16[8,120,128]{2,1,0:T(8,128)(2,1)S(1)} %bitcast.318), channel_id=1, source_target_pairs={{0,16},{1,17},{2,18},{3,19},{4,20},{5,21},{6,22},{7,23},{8,24},{9,... | collective-permute-start | bytes 737288 | tf_op jit(solution)/shard_map/ppermute | solution.py:525
  488.4 57.0 %collective-permute-start.31 = (bf16[2,32,1024]{2,1,0:T(8,128)(2,1)S(1)}, bf16[2,32,1024]{2,1,0:T(8,128)(2,1)S(1)}, u32[]{:S(2)}, u32[]{:S(2)}) collective-permute-start(bf16[2,32,1024]{2,1,0:T(8,128)(2,1)S(1)} %pad_maximum_fusion.16), channel_id=1, source_target_pairs={{0,16},{1,17},{2,18},{3,19},{4,20},{5,21},{6,22},{7,23},{8,24},{9,... | collective-permute-start | bytes 393224 | tf_op jit(solution)/shard_map/ppermute | solution.py:525
  548.4 87.4 %collective-permute-start.25 = (bf16[2,2,32,1536]{3,2,1,0:T(8,128)(2,1)}, bf16[2,2,32,1536]{3,2,1,0:T(8,128)(2,1)}, u32[]{:S(2)}, u32[]{:S(2)}) collective-permute-start(bf16[2,2,32,1536]{3,2,1,0:T(8,128)(2,1)} %get-tuple-element.182), channel_id=1, source_target_pairs={{0,1},{1,0},{2,3},{3,2},{4,5},{5,4},{6,7},{7,6},{8,9},{9,8},{10,11... | collective-permute-start | bytes 1179656 | tf_op jit(solution)/shard_map/ppermute | solution.py:525
  556.1 78.6 %collective-permute-start.38 = (bf16[64,1024]{1,0:T(8,128)(2,1)}, bf16[64,1024]{1,0:T(8,128)(2,1)S(1)}, u32[]{:S(2)}, u32[]{:S(2)}) collective-permute-start(bf16[64,1024]{1,0:T(8,128)(2,1)} %reduce-scatter.17.cloned.1.call-done), channel_id=1, source_target_pairs={{0,8},{1,9},{2,10},{3,11},{4,12},{5,13},{6,14},{7,15},{8,0},{9,1},... | collective-permute-start | bytes 393224 | tf_op jit(solution)/shard_map/ppermute | solution.py:525
  635.7 9.6 %collective-permute-start.39 = (bf16[2,64,1024]{2,1,0:T(8,128)(2,1)S(1)}, bf16[2,64,1024]{2,1,0:T(8,128)(2,1)S(1)}, u32[]{:S(2)}, u32[]{:S(2)}) collective-permute-start(bf16[2,64,1024]{2,1,0:T(8,128)(2,1)S(1)} %pad_maximum_fusion.10), channel_id=1, source_target_pairs={{0,16},{1,17},{2,18},{3,19},{4,20},{5,21},{6,22},{7,23},{8,24},{9,... | collective-permute-start | bytes 786440 | tf_op jit(solution)/shard_map/ppermute | solution.py:525
  637.9 12.8 %collective-permute-start.35 = (bf16[2,32,2048]{2,1,0:T(8,128)(2,1)S(1)}, bf16[2,32,2048]{2,1,0:T(8,128)(2,1)S(1)}, u32[]{:S(2)}, u32[]{:S(2)}) collective-permute-start(bf16[2,32,2048]{2,1,0:T(8,128)(2,1)S(1)} %pad_maximum_fusion.8), channel_id=1, source_target_pairs={{0,16},{1,17},{2,18},{3,19},{4,20},{5,21},{6,22},{7,23},{8,24},{9,... | collective-permute-start | bytes 786440 | tf_op jit(solution)/shard_map/ppermute | solution.py:525
  651.7 109.8 %collective-permute-start.28 = (bf16[32,1536]{1,0:T(8,128)(2,1)S(1)}, bf16[32,1536]{1,0:T(8,128)(2,1)S(1)}, u32[]{:S(2)}, u32[]{:S(2)}) collective-permute-start(bf16[32,1536]{1,0:T(8,128)(2,1)S(1)} %fusion.27), channel_id=1, source_target_pairs={{0,8},{1,9},{2,10},{3,11},{4,12},{5,13},{6,14},{7,15},{8,0},{9,1},... | collective-permute-start | bytes 294920 | tf_op jit(solution)/shard_map/ppermute | solution.py:525
  763.9 9.2 %collective-permute-start.23 = (bf16[2,32,1536]{2,1,0:T(8,128)(2,1)S(1)}, bf16[2,32,1536]{2,1,0:T(8,128)(2,1)S(1)}, u32[]{:S(2)}, u32[]{:S(2)}) collective-permute-start(bf16[2,32,1536]{2,1,0:T(8,128)(2,1)S(1)} %pad_maximum_fusion.14), channel_id=1, source_target_pairs={{0,16},{1,17},{2,18},{3,19},{4,20},{5,21},{6,22},{7,23},{8,24},{9,... | collective-permute-start | bytes 589832 | tf_op jit(solution)/shard_map/ppermute | solution.py:525
  (81 other events, 917.2 us)
Sparse Core Ops, SparseCore 0:
  11.6 157.6 all-gather.1
  235.2 79.0 reduce-scatter.14
  316.6 78.0 reduce-scatter.10
  397.4 74.4 reduce-scatter.8
  474.1 79.0 reduce-scatter.16
  555.5 79.1 reduce-scatter.12
  640.2 121.2 reduce-scatter.6

commit v5 on v3

--- a/solution.py
+++ b/solution.py
@@ -12,6 +12,7 @@
 PAIR = 2 * HEAD_DIM
 CHUNK = 256
 KEY_BLOCK = 128
+NORM_ROWS = 128
 EPS_NORM = 1e-06
 ROWS = 512
 FF_BLOCK = 512
@@ -167,36 +168,71 @@
     )(dy, weight)
 
 
-def project_back_kernel(low_ref, high_ref, w_ref, out_ref):
+def project_back_kernel(
+    low_ref, high_ref, w_ref, x_ref, scale_ref, carry_ref, out_ref, shift_sum_ref, scale_sum_ref, total
+):
     step = pl.program_id(0)
 
     @pl.when(step == 0)
     def _():
-        out_ref[...] = dot_nt(low_ref[0], w_ref[...])
+        total[...] = dot_nt(low_ref[0], w_ref[...])
 
     @pl.when((step > 0) & (step % 2 == 0))
     def _():
-        out_ref[...] += dot_nt(low_ref[0], w_ref[...])
+        total[...] += dot_nt(low_ref[0], w_ref[...])
 
     @pl.when(step % 2 == 1)
     def _():
-        out_ref[...] += dot_nt(high_ref[0], w_ref[...])
-
-
-def project_back(low, high, weight):
+        total[...] += dot_nt(high_ref[0], w_ref[...])
+
+    @pl.when(step == pl.num_programs(0) - 1)
+    def _():
+        gain = 1.0 + scale_ref[...]
+        shift_sum = jnp.zeros(gain.shape, jnp.float32)
+        scale_sum = jnp.zeros(gain.shape, jnp.float32)
+        for start in range(0, x_ref.shape[0], NORM_ROWS):
+            rows = slice(start, start + NORM_ROWS)
+            values = x_ref[rows, :].astype(jnp.float32)
+            centred = values - jnp.mean(values, axis=-1, keepdims=True)
+            variance = jnp.mean(centred * centred, axis=-1, keepdims=True)
+            inverse = lax.rsqrt(variance + EPS_NORM)
+            normal = centred * inverse
+            grad = total[rows, :]
+            shift_sum += jnp.sum(grad, axis=0, keepdims=True)
+            scale_sum += jnp.sum(grad * normal, axis=0, keepdims=True)
+            inner = grad * gain
+            average = jnp.mean(inner, axis=-1, keepdims=True)
+            along = jnp.mean(inner * normal, axis=-1, keepdims=True)
+            out_ref[rows, :] = carry_ref[rows, :] + inverse * (inner - average - normal * along)
+        shift_sum_ref[...] = shift_sum
+        scale_sum_ref[...] = scale_sum
+
+
+def project_back(low, high, weight, x, scale, carry):
     groups, tokens, width = low.shape
     depth = weight.shape[0]
     block = pl.BlockSpec((1, tokens, width), lambda i: (i // 2, 0, 0))
+    whole = pl.BlockSpec((tokens, depth), lambda i: (0, 0))
+    line = pl.BlockSpec((1, depth), lambda i: (0, 0))
+    row = jax.ShapeDtypeStruct((1, depth), jnp.float32)
     return pl.pallas_call(
         project_back_kernel,
         grid=(2 * groups,),
-        in_specs=[block, block, pl.BlockSpec((depth, width), lambda i: (0, i))],
-        out_specs=pl.BlockSpec((tokens, depth), lambda i: (0, 0)),
-        out_shape=jax.ShapeDtypeStruct((tokens, depth), jnp.float32),
-        compiler_params=kernel_params(40),
+        in_specs=[
+            block,
+            block,
+            pl.BlockSpec((depth, width), lambda i: (0, i)),
+            whole,
+            line,
+            whole,
+        ],
+        out_specs=[whole, line, line],
+        out_shape=[jax.ShapeDtypeStruct((tokens, depth), jnp.float32), row, row],
+        scratch_shapes=[pltpu.VMEM((tokens, depth), jnp.float32)],
+        compiler_params=kernel_params(48),
         cost_estimate=cost(groups * tokens * depth * width, tokens * width),
         name="project_back",
-    )(low, high, weight)
+    )(low, high, weight, x, scale, carry)
 
 
 def store_rows(total, own_core, own_slot, pieces, keep_ref, send_ref):
@@ -237,6 +273,50 @@
         cost_estimate=cost(groups * tokens * depth * columns, tokens * columns),
         name=name,
     )(own, x, dy)
+
+
+def grad_pair_kernel(pieces, first, own_ref, x_ref, dx_ref, y_ref, dy_ref, keep_ref, send_ref):
+    step = pl.program_id(0)
+
+    @pl.when(step < first)
+    def _():
+        total = dot_tn(x_ref[...], dx_ref[...])
+        store_rows(total, own_ref[0], own_ref[1], pieces, keep_ref, send_ref)
+
+    @pl.when(step >= first)
+    def _():
+        total = dot_tn(y_ref[...], dy_ref[0])
+        store_rows(total, own_ref[0], own_ref[1], pieces, keep_ref, send_ref)
+
+
+def grad_pair(own, x, dx, y, dy, pieces, name):
+    tokens, depth = x.shape
+    first = dx.shape[1] // COL_BLOCK
+    groups = dy.shape[0]
+    columns = dx.shape[1] + groups * COL_BLOCK
+    whole = pl.BlockSpec((tokens, depth), lambda i, own: (0, 0))
+    block = pl.BlockSpec((depth // 2, COL_BLOCK), lambda i, own: (0, i))
+    half = jax.ShapeDtypeStruct((depth // 2, columns), jnp.bfloat16)
+    return pl.pallas_call(
+        partial(grad_pair_kernel, pieces, first),
+        grid_spec=pltpu.PrefetchScalarGridSpec(
+            num_scalar_prefetch=1,
+            grid=(first + groups,),
+            in_specs=[
+                whole,
+                pl.BlockSpec((tokens, COL_BLOCK), lambda i, own: (0, jnp.minimum(i, first - 1))),
+                whole,
+                pl.BlockSpec(
+                    (1, tokens, COL_BLOCK), lambda i, own: (jnp.maximum(i - first, 0), 0, 0)
+                ),
+            ],
+            out_specs=[block, block],
+        ),
+        out_shape=[half, half],
+        compiler_params=kernel_params(40),
+        cost_estimate=cost(tokens * depth * columns, tokens * columns),
+        name=name,
+    )(own, x, dx, y, dy)
 
 
 def feed_forward_kernel(
@@ -505,7 +585,7 @@
 
 
 MASKS = {"core": (1, 0), "y": (2, 0), "x": (0, 1), "z1": (0, 2), "z2": (0, 4)}
-GATHER_ORDERS = (("z1", "z2", "x", "y"), ("z1", "z2", "y", "x"))
+GATHER_ORDERS = (("z2", "z1", "x", "y"), ("z2", "z1", "y", "x"))
 
 
 def exchange(value, rep_mask, fsdp_mask):
@@ -743,11 +823,14 @@
     branch_m, d_norm_m, keep_e, send_e, keep_s, send_s, g_expandbias = feed_forward(
         own, norm_m, d_branch_m, w_expand, b_expand, w_shrink, depth_pieces, unit_pieces
     )
-    sum_e = depth_sum((keep_e, send_e), ("y", "x", "z2", "z1"))
-    sum_s = unit_sum((keep_s, send_s), ("x", "y", "z2", "z1"))
+    sum_e = depth_sum((keep_e, send_e), ("y", "x", "z1", "z2"))
+    sum_s = unit_sum((keep_s, send_s), ("x", "y", "z1", "z2"))
     branch_m = (branch_m + b_shrink).reshape(seqs_dev, seq_len, feature)
     layer_out = middle + gate_m[:, None, :] * branch_m
     d_gate_m = jnp.sum(grad_out * branch_m, axis=1)
+    d_norm_m, layer_out, d_gate_m = hold((d_norm_m, layer_out, d_gate_m), sum_e, sum_s)
+    sum_e.step()
+    sum_s.step()
     _, norm_pull_m = jax.vjp(modulate, middle, shift_m, scale_m)
     d_mid_norm, d_shift_m, d_scale_m = norm_pull_m(d_norm_m.reshape(seqs_dev, seq_len, feature))
     d_middle = grad_out + d_mid_norm
@@ -755,43 +838,47 @@
     d_gate_a = jnp.sum(d_middle * branch_a, axis=1)
     g_outbiases = jnp.sum(d_branch_a, axis=0, dtype=jnp.float32)
     d_attended = backward_dot(d_branch_a, *out_at, jnp.bfloat16, "attention_out_back")
-    d_attended = hold(d_attended, sum_e, sum_s)
-    sum_e.step()
-    sum_s.step()
     half_pairs = HEADS // 4
     d_low, q_low, v_low = attention_backward(
         projected, d_attended, attended_t, log_totals, 0, half_pairs, "attention_backward_low"
     )
-    sum_low = depth_sum(
-        grad_dot(own, norm_a, d_low, depth_pieces, "projector_grad_low"), ("y", "x", "z2", "z1")
-    )
-    sum_out = depth_sum(
-        grad_dot(own, attended, d_branch_a[None], depth_pieces, "outweight_grad"),
-        ("x", "y", "z2", "z1"),
-    )
-    d_attended = hold(d_attended, sum_e, sum_s, sum_low, sum_out)
-    for total in (sum_e, sum_s, sum_low, sum_out):
+    halves_low = grad_pair(
+        own, attended, d_branch_a, norm_a, d_low, depth_pieces, "weight_grad_low"
+    )
+    d_attended, halves_low = hold((d_attended, halves_low), sum_e, sum_s)
+    sum_low = depth_sum(halves_low, ("y", "x", "z1", "z2"))
+    for total in (sum_e, sum_s):
         total.step()
     d_high, q_high, v_high = attention_backward(
         projected, d_attended, attended_t, log_totals, half_pairs, half_pairs, "attention_backward_high"
     )
-    d_high = hold(d_high, sum_e, sum_s, sum_low, sum_out)
-    for total in (sum_e, sum_s, sum_low, sum_out):
+    d_high = hold(d_high, sum_e, sum_s, sum_low)
+    for total in (sum_e, sum_s, sum_low):
         total.step()
     sum_high = depth_sum(
-        grad_dot(own, norm_a, d_high, depth_pieces, "projector_grad_high"), ("x", "y", "z2", "z1")
-    )
-    d_norm_a = project_back(d_low, d_high, w_proj)
-    d_norm_a = hold(d_norm_a, sum_high)
+        grad_dot(own, norm_a, d_high, depth_pieces, "weight_grad_high"), ("x", "y", "z1", "z2")
+    )
+    d_high = hold(d_high, sum_high)
     sum_high.step()
+    latents_grad, d_shift_a, d_scale_a = project_back(
+        d_low,
+        d_high,
+        w_proj,
+        latents.reshape(token_count, feature),
+        scale_a,
+        d_middle.reshape(token_count, feature),
+    )
+    latents_grad = latents_grad.reshape(seqs_dev, seq_len, feature)
+    latents_grad, d_shift_a, d_scale_a = hold(
+        (latents_grad, d_shift_a, d_scale_a), sum_e, sum_s, sum_low, sum_high
+    )
+    for total in (sum_e, sum_s, sum_low, sum_high):
+        total.step()
     g_querybias = jnp.concatenate([q_low, q_high], axis=1)
     g_valuebias = jnp.concatenate([v_low, v_high], axis=1)
-    _, norm_pull_a = jax.vjp(modulate, resid_in, shift_a, scale_a)
-    d_in_norm, d_shift_a, d_scale_a = norm_pull_a(d_norm_a.reshape(seqs_dev, seq_len, feature))
-    latents_grad = d_middle + d_in_norm
     small = jnp.concatenate(
         [
-            part.astype(jnp.bfloat16).reshape(-1)
+            part.astype(jnp.float32).reshape(-1, 128)
             for part in (
                 d_shift_a,
                 d_scale_a,
@@ -807,15 +894,15 @@
                 g_shrinkbias,
             )
         ]
-    )
+    ).astype(jnp.bfloat16)
     devices = reps * shards
     size = seqs_dev * feature
-    gathered = gather_relative(small.reshape(-1, 128)).reshape(devices, -1)
+    gathered = gather_relative(small).reshape(devices, -1)
     g_expander, g_shrinker = sum_e.finish(), sum_s.finish()
-    g_outweight = sum_out.finish()
     low, high = sum_low.finish(), sum_high.finish()
+    g_outweight = low[:, :feature]
     g_projector = jnp.stack(
-        [low.reshape(own_rows, 3, feature // 2), high.reshape(own_rows, 3, feature // 2)], axis=2
+        [low[:, feature:].reshape(own_rows, 3, -1), high.reshape(own_rows, 3, -1)], axis=2
     ).reshape(own_rows, 3 * feature)
 
     cond_all = gathered[:, 6 * size : 7 * size].reshape(devices * seqs_dev, feature)

time: 632 us -> 590 us (0.934)
  waiting for transfers between devices: 216 us -> 105 us
  local copies, waits for them, and re-layouts: 59 us -> 101 us
  other arithmetic: 86.3 us -> 107 us
  Pallas kernels: 197 us -> 208 us
    ppermute x50 -> x43, waiting for transfers between devices: 202 us -> 87.3 us  [exchange(): return lax.ppermute(value, ('rep', 'fsdp'), pairs)]
    convert_element_type x25 -> x20, other arithmetic: 19.5 us -> 45.3 us  [half(): (stay.astype(jnp.float32) + arrived.astype(jnp.float32)).astype(jnp.bfloa...]
    unnamed x170 -> x166, local copies, waits for them, and re-layouts: 25.3 us -> 48.8 us
    pallas_call x0 -> x1, Pallas kernels: none -> 10 us  [grad_pair(): pl.pallas_call(partial(grad_pair_kernel, pieces, first), grid_spec=pltpu....]
    reduce_sum x4 -> x2, other arithmetic: 13.3 us -> 4.11 us  [modulate(): return normalize(values) * (1.0 + scales[:, None, :]) + shifts[:, None, :]]
    convert_element_type x0 -> x4, local copies, waits for them, and re-layouts: none -> 8.06 us  [the longest x3 7.84 us: half(): (stay.astype(jnp.float32) + arrived.astype(jnp.float32)).astype(jnp.bfloa...]
    pallas_call x3 -> x1, Pallas kernels: 13.5 us -> 5.6 us  [grad_dot(): pl.pallas_call(partial(grad_dot_kernel, pieces), grid_spec=pltpu.Prefetch...]
    pallas_call x1, Pallas kernels: 9.18 us -> 16.5 us  [project_back(): pl.pallas_call(project_back_kernel, grid=(2 * groups,), in_specs=[block,...]
  transfers between devices with their start and end apart: 52 -> 45, of which waited for: 24 -> 13; matrix products, arithmetic and copies ran while one was open for 19% -> 29% of each run, Pallas kernels for 15% -> 21%
where the time goes in v5:
time: 590 us; the launch traced here: 585 us
  Pallas kernels  208 us (35%)
  other arithmetic  107 us (18%)
  waiting for transfers between devices  105 us (18%)
  local copies, waits for them, and re-layouts  101 us (17%)
  starting transfers between devices  46.4 us (8%)
  between operations  15.6 us (3%)
    ppermute x43, waiting for transfers between devices, exchange(): return lax.ppermute(value, ('rep', 'fsdp'), pairs)  87.3 us
    pallas_call x1, Pallas kernels, feed_forward(): pl.pallas_call(partial(feed_forward_kernel, depth_pieces, unit_pieces), g...  74.3 us
    pallas_call x2, Pallas kernels, attention_backward(): pl.pallas_call(attention_backward_kernel, grid=(count,), in_specs=[pl.Blo...  49.6 us
    unnamed x166, local copies, waits for them, and re-layouts  48.8 us
    convert_element_type x20, other arithmetic, half(): (stay.astype(jnp.float32) + arrived.astype(jnp.float32)).astype(jnp.bfloa...  45.3 us
    ppermute x43, starting transfers between devices, exchange(): return lax.ppermute(value, ('rep', 'fsdp'), pairs)  40 us
    pallas_call x1, Pallas kernels, attention_forward(): pl.pallas_call(attention_forward_kernel, grid=(pairs,), in_specs=[pl.Bloc...  30.1 us
    all_gather x1, waiting for transfers between devices, gather_packed(): full = lax.all_gather(packed, ('fsdp', 'rep'), axis=0, tiled=True)  17.8 us
  transfers between devices with their start and end apart: 45, of which 13 were waited for; matrix products, arithmetic and copies ran while one was open for 29% of the time, Pallas kernels for 21%

profile of v5, /device:TPU:0, one launch (start us, length us, event | category | flops | bytes accessed | tf_op | source)
XLA Modules:
  0.0 585.4 jit_solution(15295591492657612824)
XLA Ops:
  13.0 4.0 collective-permute-start.5
  19.8 6.3 %all-to-all-start = ((f32[8,1,7936]{2,1,0:T(1,128)}), f32[8,1,7936]{2,1,0:T(1,128)S(1)}, u32[]{:S(2)}, u32[]{:S(2)}) async-start(f32[8,1,7936]{2,1,0:T(1,128)} %copy.97), calls=%async_computation | async-start | bytes 507904 | tf_op jit(solution)/shard_map/all_to_all | solution.py:794
  33.2 14.3 %collective-permute-done.6 = bf16[2,32,1536]{2,1,0:T(8,128)(2,1)S(1)} collective-permute-done((bf16[2,32,1536]{2,1,0:T(8,128)(2,1)S(1)}, bf16[2,32,1536]{2,1,0:T(8,128)(2,1)S(1)}, u32[]{:S(2)}, u32[]{:S(2)}) %collective-permute-start.6) | collective-permute-done | bytes 196640 | tf_op jit(solution)/shard_map/ppermute | solution.py:598
  55.1 7.8 %collective-permute-done.7 = bf16[4,32,1536]{2,1,0:T(8,128)(2,1)S(1)} collective-permute-done((bf16[4,32,1536]{2,1,0:T(8,128)(2,1)}, bf16[4,32,1536]{2,1,0:T(8,128)(2,1)S(1)}, u32[]{:S(2)}, u32[]{:S(2)}) %collective-permute-start.7) | collective-permute-done | bytes 393248 | tf_op jit(solution)/shard_map/ppermute | solution.py:598
  64.3 7.6 %collective-permute-done.2 = bf16[4,32,1536]{2,1,0:T(8,128)(2,1)S(1)} collective-permute-done((bf16[4,32,1536]{2,1,0:T(8,128)(2,1)}, bf16[4,32,1536]{2,1,0:T(8,128)(2,1)S(1)}, u32[]{:S(2)}, u32[]{:S(2)}) %collective-permute-start.2) | collective-permute-done | bytes 393248 | tf_op jit(solution)/shard_map/ppermute | solution.py:598
  75.1 21.7 %collective-permute-done.8 = bf16[8,32,1536]{2,1,0:T(8,128)(2,1)S(1)} collective-permute-done((bf16[8,32,1536]{2,1,0:T(8,128)(2,1)S(1)}, bf16[8,32,1536]{2,1,0:T(8,128)(2,1)S(1)}, u32[]{:S(2)}, u32[]{:S(2)}) %collective-permute-start.8) | collective-permute-done | bytes 786464 | tf_op jit(solution)/shard_map/ppermute | solution.py:598
  104.4 12.7 %project.1 = (bf16[1024,3072]{1,0:T(8,128)(2,1)}, bf16[1024,3072]{1,0:T(8,128)(2,1)}) custom-call(s32[1]{0:T(128)} %bitcast.6.own_ref, bf16[1024,1024]{1,0:T(8,128)(2,1)S(1)} %fusion.19.x_ref.y_ref, f32[1,3072]{1,0:T(1,128)S(1)} %pad_maximum_fusion.17.b_ref, bf16[16,32,1536]{2,1,0:T(8,128)(2,1)} %constant_dynamic-update-slice_fusion.refs_0_, ...), custom_call_target="tpu_custom_call" | custom-call | flops 3221225472 | bytes 3145728 | tf_op jit(solution)/shard_map/project/pallas_call | solution.py:106
  117.1 30.1 %attention_forward.1 = (bf16[1024,1024]{1,0:T(8,128)(2,1)S(1)}, f32[1024,1024]{1,0:T(8,128)}, f32[8,2,1024]{2,1,0:T(2,128)S(1)}) custom-call(bf16[1024,3072]{1,0:T(8,128)(2,1)} %get-tuple-element.62.q_ref.k_ref.v_ref, bf16[1024,3072]{1,0:T(8,128)(2,1)} %get-tuple-element.62.q_ref.k_ref.v_ref, bf16[1024,3072]{1,0:T(8,128)(2,1)} %get-tuple-element.62.q_ref.k_ref.v_ref), custom_call_target="tpu_custom_call" | custom-call | flops 4294967296 | bytes 8388608 | tf_op jit(solution)/shard_map/attention_forward/pallas_call | solution.py:476
  148.5 17.8 %all-gather.2.cloned.1.call-done = bf16[9216,1024]{1,0:T(8,128)(2,1)} async-done(((bf16[288,1024]{1,0:T(8,128)(2,1)}), bf16[9216,1024]{1,0:T(8,128)(2,1)}) %all-gather.2.cloned.1.call-update) | async-done | bytes 18874384 | tf_op jit(solution)/shard_map/all_gather | solution.py:710
  167.9 4.2 attention_out.1
  176.8 74.3 %feed_forward.1 = (f32[1024,1024]{1,0:T(8,128)}, f32[1024,1024]{1,0:T(8,128)}, bf16[512,4096]{1,0:T(8,128)(2,1)}, bf16[512,4096]{1,0:T(8,128)(2,1)}, bf16[2048,1...) custom-call(s32[4]{0:T(128)} %pad_add_fusion.own_ref, bf16[1024,1024]{1,0:T(8,128)(2,1)} %fusion.14.norm_ref, ...), custom_call_target="tpu_custom_call" | custom-call | flops 25769803776 | bytes 16777216 | tf_op jit(solution)/shard_map/feed_forward/pallas_call | solution.py:408
  251.7 4.3 fusion.85
  256.1 6.0 %fusion.8 = (f32[1024]{0:T(1024)S(1)}, f32[1,1024,1024]{2,1,0:T(8,128)}) fusion(bf16[1,1024,1024]{2,1,0:T(8,128)(2,1)S(1)} %copy-done.24, f32[1024,1024]{1,0:T(8,128)} %get-tuple-element.65, f32[1024]{0:T(1024)S(1)} %get-tuple-element.235, f32[1,1024,1024]{2,1,0:T(8,128)S(1)} %copy-done.21, f32[1024]{0:T(1024)S(1)} %bitcast.391), kind=kLoop, calls=%fused_computation.18 | loop fusion | flops 6290432 | bytes 14692352 | tf_op jit(solution)/shard_map/reduce_sum | solution.py:830
  264.7 4.0 fusion.86
  283.8 4.7 attention_out_back.1.g_ref
  288.5 25.4 %attention_backward_low.1 = (bf16[3,1024,512]{2,1,0:T(8,128)(2,1)S(1)}, f32[1,512]{1,0:T(1,128)S(1)}, f32[1,512]{1,0:T(1,128)S(1)}) custom-call(bf16[1024,3072]{1,0:T(8,128)(2,1)} %get-tuple-element.62.q_ref.k_ref.v_ref, bf16[1024,3072]{1,0:T(8,128)(2,1)} %get-tuple-element.62.q_ref.k_ref.v_ref, bf16[1024,3072]{1,0:T(8,128)(2,1)} %get-tuple-element.62.q_ref.k_ref.v_ref, ...), custom_call_target="tpu_custom_call" | custom-call | flops 2147483648 | bytes 8388608 | tf_op jit(solution)/shard_map/attention_backward_low/pallas_call | solution.py:553
  315.7 10.0 %weight_grad_low.1 = (bf16[512,2560]{1,0:T(8,128)(2,1)S(1)}, bf16[512,2560]{1,0:T(8,128)(2,1)}) custom-call(s32[4]{0:T(128)S(1)} %copy-done.19, bf16[1024,1024]{1,0:T(8,128)(2,1)S(1)} %copy-done.18, bf16[1024,1024]{1,0:T(8,128)(2,1)S(1)} %get-tuple-element.181.dy_ref.dx_ref, bf16[1024,1024]{1,0:T(8,128)(2,1)S(1)} %copy-done.14, bf16[3,1024,512]{2,1,0:T(8,128)(2,1)} %copy-done.7), custom_call_target="tpu_custom_call" | custom-call | flops 2684354560 | bytes 2621440 | tf_op jit(solution)/shard_map/weight_grad_low/pallas_call | solution.py:300
  329.9 3.8 fusion.30
  342.0 4.0 fusion.20
  346.1 4.1 copy.162
  351.8 24.1 %attention_backward_high.1 = (bf16[3,1024,512]{2,1,0:T(8,128)(2,1)S(1)}, f32[1,512]{1,0:T(1,128)S(1)}, f32[1,512]{1,0:T(1,128)S(1)}) custom-call(bf16[1024,3072]{1,0:T(8,128)(2,1)} %get-tuple-element.62.q_ref.k_ref.v_ref, bf16[1024,3072]{1,0:T(8,128)(2,1)} %get-tuple-element.62.q_ref.k_ref.v_ref, bf16[1024,3072]{1,0:T(8,128)(2,1)} %get-tuple-element.62.q_ref.k_ref.v_ref, ...), custom_call_target="tpu_custom_call" | custom-call | flops 2147483648 | bytes 8388608 | tf_op jit(solution)/shard_map/attention_backward_high/pallas_call | solution.py:553
  376.0 5.6 weight_grad_high.1
  395.1 5.2 copy.163
  405.1 6.3 %fusion = bf16[2,2,2,32,2560]{3,4,1,0,2:T(8,128)(2,1)} fusion(bf16[2,2,2,1,32,2560]{4,5,1,0,2,3:T(8,128)(2,1)S(1)} %copy-done.25, bf16[2,2,2,1,32,2560]{4,5,1,0,2,3:T(8,128)(2,1)} %copy.162), kind=kLoop, calls=%fused_computation.8 | loop fusion | flops 2621440 | bytes 3932160 | tf_op jit(solution)/shard_map/convert_element_type | solution.py:648
  411.5 16.5 %project_back.1 = (f32[1024,1024]{1,0:T(8,128)}, f32[1,1024]{1,0:T(1,128)S(1)}, f32[1,1024]{1,0:T(1,128)S(1)}) custom-call(bf16[3,1024,512]{2,1,0:T(8,128)(2,1)S(1)} %copy-done.8, bf16[3,1024,512]{2,1,0:T(8,128)(2,1)} %copy-done.9, bf16[1024,3072]{1,0:T(8,128)(2,1)} %get-tuple-element.87.w_ref, bf16[1024,1024]{1,0:T(8,128)(2,1)S(1)} %bitcast.342, ...), custom_call_target="tpu_custom_call" | custom-call | flops 1610612736 | bytes 524288 | tf_op jit(solution)/shard_map/project_back/pallas_call | solution.py:218
  443.4 5.5 copy.119
  448.9 8.5 %collective-permute-done.22 = bf16[1,120,128]{2,1,0:T(8,128)(2,1)S(1)} collective-permute-done((bf16[1,120,128]{2,1,0:T(8,128)(2,1)S(1)}, bf16[1,120,128]{2,1,0:T(8,128)(2,1)S(1)}, u32[]{:S(2)}, u32[]{:S(2)}) %collective-permute-start.22) | collective-permute-done | bytes 30752 | tf_op jit(solution)/shard_map/ppermute | solution.py:598
  458.8 6.2 %fusion.12 = (bf16[2,2,32,2560]{2,3,1,0:T(8,128)(2,1)}, bf16[2,2,32,2560]{2,3,1,0:T(8,128)(2,1)}) fusion(bf16[2,2,2,32,2560]{3,4,1,0,2:T(8,128)(2,1)} %copy.119, bf16[2,2,2,32,2560]{3,4,1,0,2:T(8,128)(2,1)} %fusion), kind=kLoop, calls=%fused_computation.33 | loop fusion | flops 2621440 | bytes 3932160 | tf_op jit(solution)/shard_map/convert_element_type | solution.py:648
  465.1 3.7 copy.121
  474.2 14.0 %collective-permute-done.24 = bf16[4,120,128]{2,1,0:T(8,128)(2,1)S(1)} collective-permute-done((bf16[4,120,128]{2,1,0:T(8,128)(2,1)S(1)}, bf16[4,120,128]{2,1,0:T(8,128)(2,1)S(1)}, u32[]{:S(2)}, u32[]{:S(2)}) %collective-permute-start.24) | collective-permute-done | bytes 122912 | tf_op jit(solution)/shard_map/ppermute | solution.py:598
  507.2 4.2 add_convert_fusion.9
  561.2 6.4 %collective-permute-done.31 = bf16[2,32,2560]{2,1,0:T(8,128)(2,1)S(1)} collective-permute-done((bf16[2,32,2560]{2,1,0:T(8,128)(2,1)}, bf16[2,32,2560]{2,1,0:T(8,128)(2,1)S(1)}, u32[]{:S(2)}, u32[]{:S(2)}) %collective-permute-start.31) | collective-permute-done | bytes 327712 | tf_op jit(solution)/shard_map/ppermute | solution.py:598
  (382 shorter events, 196.5 us)
Async XLA Ops:
  7.2 159.1 %all-gather.2.cloned.1.call-start = ((), (), s32[]{:S(2)}) async-start(), calls=%async_computation.1 | async-start | bytes 19464192 | tf_op jit(solution)/shard_map/all_gather | solution.py:710
  13.0 16.6 %collective-permute-start.5 = (bf16[1,32,1536]{2,1,0:T(8,128)(2,1)S(1)}, bf16[1,32,1536]{2,1,0:T(8,128)(2,1)S(1)}, u32[]{:S(2)}, u32[]{:S(2)}) collective-permute-start(bf16[1,32,1536]{2,1,0:T(8,128)(2,1)S(1)} %get-tuple-element.175), channel_id=1, source_target_pairs={{0,4},{1,5},{2,6},{3,7},{4,0},{5,1},{6,2},{7,3},{8,12},{9,13},{10,... | collective-permute-start | bytes 294920 | tf_op jit(solution)/shard_map/ppermute | solution.py:598
  17.1 14.7 %collective-permute-start = (bf16[1,32,1536]{2,1,0:T(8,128)(2,1)S(1)}, bf16[1,32,1536]{2,1,0:T(8,128)(2,1)S(1)}, u32[]{:S(2)}, u32[]{:S(2)}) collective-permute-start(bf16[1,32,1536]{2,1,0:T(8,128)(2,1)S(1)} %get-tuple-element.224), channel_id=1, source_target_pairs={{0,4},{1,5},{2,6},{3,7},{4,0},{5,1},{6,2},{7,3},{8,12},{9,13},{10,... | collective-permute-start | bytes 294920 | tf_op jit(solution)/shard_map/ppermute | solution.py:598
  19.8 35.3 %all-to-all-start = ((f32[8,1,7936]{2,1,0:T(1,128)}), f32[8,1,7936]{2,1,0:T(1,128)S(1)}, u32[]{:S(2)}, u32[]{:S(2)}) async-start(f32[8,1,7936]{2,1,0:T(1,128)} %copy.97), calls=%async_computation | async-start | bytes 507904 | tf_op jit(solution)/shard_map/all_to_all | solution.py:794
  29.7 17.8 %collective-permute-start.6 = (bf16[2,32,1536]{2,1,0:T(8,128)(2,1)S(1)}, bf16[2,32,1536]{2,1,0:T(8,128)(2,1)S(1)}, u32[]{:S(2)}, u32[]{:S(2)}) collective-permute-start(bf16[2,32,1536]{2,1,0:T(8,128)(2,1)S(1)} %pad_maximum_fusion.13), channel_id=1, source_target_pairs={{0,2},{1,3},{2,0},{3,1},{4,6},{5,7},{6,4},{7,5},{8,10},{9,11},{10,... | collective-permute-start | bytes 589832 | tf_op jit(solution)/shard_map/ppermute | solution.py:598
  31.8 19.5 %collective-permute-start.1 = (bf16[2,32,1536]{2,1,0:T(8,128)(2,1)S(1)}, bf16[2,32,1536]{2,1,0:T(8,128)(2,1)S(1)}, u32[]{:S(2)}, u32[]{:S(2)}) collective-permute-start(bf16[2,32,1536]{2,1,0:T(8,128)(2,1)S(1)} %pad_maximum_fusion.12), channel_id=1, source_target_pairs={{0,2},{1,3},{2,0},{3,1},{4,6},{5,7},{6,4},{7,5},{8,10},{9,11},{10,... | collective-permute-start | bytes 589832 | tf_op jit(solution)/shard_map/ppermute | solution.py:598
  48.3 14.5 %collective-permute-start.7 = (bf16[4,32,1536]{2,1,0:T(8,128)(2,1)}, bf16[4,32,1536]{2,1,0:T(8,128)(2,1)S(1)}, u32[]{:S(2)}, u32[]{:S(2)}) collective-permute-start(bf16[4,32,1536]{2,1,0:T(8,128)(2,1)} %pad_maximum_fusion.9), channel_id=1, source_target_pairs={{0,16},{1,17},{2,18},{3,19},{4,20},{5,21},{6,22},{7,23},{8,24},{9,... | collective-permute-start | bytes 1179656 | tf_op jit(solution)/shard_map/ppermute | solution.py:598
  52.1 19.7 %collective-permute-start.2 = (bf16[4,32,1536]{2,1,0:T(8,128)(2,1)}, bf16[4,32,1536]{2,1,0:T(8,128)(2,1)S(1)}, u32[]{:S(2)}, u32[]{:S(2)}) collective-permute-start(bf16[4,32,1536]{2,1,0:T(8,128)(2,1)} %pad_maximum_fusion.8), channel_id=1, source_target_pairs={{0,1},{1,0},{2,3},{3,2},{4,5},{5,4},{6,7},{7,6},{8,9},{9,8},{10,11... | collective-permute-start | bytes 1179656 | tf_op jit(solution)/shard_map/ppermute | solution.py:598
  62.9 33.8 %collective-permute-start.8 = (bf16[8,32,1536]{2,1,0:T(8,128)(2,1)S(1)}, bf16[8,32,1536]{2,1,0:T(8,128)(2,1)S(1)}, u32[]{:S(2)}, u32[]{:S(2)}) collective-permute-start(bf16[8,32,1536]{2,1,0:T(8,128)(2,1)S(1)} %pad_maximum_fusion.3), channel_id=1, source_target_pairs={{0,1},{1,0},{2,3},{3,2},{4,5},{5,4},{6,7},{7,6},{8,9},{9,8},{10,11... | collective-permute-start | bytes 2359304 | tf_op jit(solution)/shard_map/ppermute | solution.py:598
  71.9 25.8 %collective-permute-start.3 = (bf16[8,32,1536]{2,1,0:T(8,128)(2,1)S(1)}, bf16[8,32,1536]{2,1,0:T(8,128)(2,1)S(1)}, u32[]{:S(2)}, u32[]{:S(2)}) collective-permute-start(bf16[8,32,1536]{2,1,0:T(8,128)(2,1)S(1)} %pad_maximum_fusion.2), channel_id=1, source_target_pairs={{0,16},{1,17},{2,18},{3,19},{4,20},{5,21},{6,22},{7,23},{8,24},{9,... | collective-permute-start | bytes 2359304 | tf_op jit(solution)/shard_map/ppermute | solution.py:598
  251.4 13.2 %collective-permute-start.11 = (bf16[2048,1024]{1,0:T(8,128)(2,1)}, bf16[2048,1024]{1,0:T(8,128)(2,1)}, u32[]{:S(2)}, u32[]{:S(2)}) collective-permute-start(bf16[2048,1024]{1,0:T(8,128)(2,1)} %get-tuple-element.67), channel_id=1, source_target_pairs={{0,8},{1,9},{2,10},{3,11},{4,12},{5,13},{6,14},{7,15},{8,0},{9,1},... | collective-permute-start | bytes 12582920 | tf_op jit(solution)/shard_map/ppermute | solution.py:598
  271.0 56.2 %collective-permute-start.13 = (bf16[2,2,2,128,1024]{4,3,1,0,2:T(8,128)(2,1)}, bf16[2,2,2,128,1024]{4,3,1,0,2:T(8,128)(2,1)}, u32[]{:S(2)}, u32[]{:S(2)}) collective-permute-start(bf16[2,2,2,128,1024]{4,3,1,0,2:T(8,128)(2,1)} %fusion.16), channel_id=1, source_target_pairs={{0,1},{1,0},{2,3},{3,2},{4,5},{5,4},{6,7},{7,6},{8,9},{9,8},{10,11... | collective-permute-start | bytes 6291464 | tf_op jit(solution)/shard_map/ppermute | solution.py:598
  276.3 50.9 %collective-permute-start.12 = (bf16[2,2,2,32,4096]{4,3,1,0,2:T(8,128)(2,1)}, bf16[2,2,2,32,4096]{4,3,1,0,2:T(8,128)(2,1)}, u32[]{:S(2)}, u32[]{:S(2)}) collective-permute-start(bf16[2,2,2,32,4096]{4,3,1,0,2:T(8,128)(2,1)} %fusion.15), channel_id=1, source_target_pairs={{0,16},{1,17},{2,18},{3,19},{4,20},{5,21},{6,22},{7,23},{8,24},{9,... | collective-permute-start | bytes 6291464 | tf_op jit(solution)/shard_map/ppermute | solution.py:598
  327.2 48.7 %collective-permute-start.16 = (bf16[512,2560]{1,0:T(8,128)(2,1)}, bf16[512,2560]{1,0:T(8,128)(2,1)}, u32[]{:S(2)}, u32[]{:S(2)}) collective-permute-start(bf16[512,2560]{1,0:T(8,128)(2,1)} %get-tuple-element.83), channel_id=1, source_target_pairs={{0,8},{1,9},{2,10},{3,11},{4,12},{5,13},{6,14},{7,15},{8,0},{9,1},... | collective-permute-start | bytes 7864328 | tf_op jit(solution)/shard_map/ppermute | solution.py:598
  333.7 42.2 %collective-permute-start.15 = (bf16[2,2,128,1024]{3,2,1,0:T(8,128)(2,1)}, bf16[2,2,128,1024]{3,2,1,0:T(8,128)(2,1)}, u32[]{:S(2)}, u32[]{:S(2)}) collective-permute-start(bf16[2,2,128,1024]{3,2,1,0:T(8,128)(2,1)} %get-tuple-element.186), channel_id=1, source_target_pairs={{0,16},{1,17},{2,18},{3,19},{4,20},{5,21},{6,22},{7,23},{8,24},{9,... | collective-permute-start | bytes 3145736 | tf_op jit(solution)/shard_map/ppermute | solution.py:598
  338.5 37.4 %collective-permute-start.14 = (bf16[2,2,32,4096]{3,2,1,0:T(8,128)(2,1)}, bf16[2,2,32,4096]{3,2,1,0:T(8,128)(2,1)}, u32[]{:S(2)}, u32[]{:S(2)}) collective-permute-start(bf16[2,2,32,4096]{3,2,1,0:T(8,128)(2,1)} %get-tuple-element.188), channel_id=1, source_target_pairs={{0,1},{1,0},{2,3},{3,2},{4,5},{5,4},{6,7},{7,6},{8,9},{9,8},{10,11... | collective-permute-start | bytes 3145736 | tf_op jit(solution)/shard_map/ppermute | solution.py:598
  381.6 18.8 %collective-permute-start.17 = (bf16[512,1536]{1,0:T(8,128)(2,1)}, bf16[512,1536]{1,0:T(8,128)(2,1)}, u32[]{:S(2)}, u32[]{:S(2)}) collective-permute-start(bf16[512,1536]{1,0:T(8,128)(2,1)} %get-tuple-element.85), channel_id=1, source_target_pairs={{0,8},{1,9},{2,10},{3,11},{4,12},{5,13},{6,14},{7,15},{8,0},{9,1},... | collective-permute-start | bytes 4718600 | tf_op jit(solution)/shard_map/ppermute | solution.py:598
  386.9 41.4 %collective-permute-start.20 = (bf16[2,2,2,32,2560]{4,3,2,1,0:T(8,128)(2,1)}, bf16[2,2,2,32,2560]{4,3,2,1,0:T(8,128)(2,1)}, u32[]{:S(2)}, u32[]{:S(2)}) collective-permute-start(bf16[2,2,2,32,2560]{4,3,2,1,0:T(8,128)(2,1)} %fusion.22), channel_id=1, source_target_pairs={{0,16},{1,17},{2,18},{3,19},{4,20},{5,21},{6,22},{7,23},{8,24},{9,... | collective-permute-start | bytes 3932168 | tf_op jit(solution)/shard_map/ppermute | solution.py:598
  390.6 37.6 %collective-permute-start.19 = (bf16[2,128,1024]{2,1,0:T(8,128)(2,1)}, bf16[2,128,1024]{2,1,0:T(8,128)(2,1)}, u32[]{:S(2)}, u32[]{:S(2)}) collective-permute-start(bf16[2,128,1024]{2,1,0:T(8,128)(2,1)} %get-tuple-element.204), channel_id=1, source_target_pairs={{0,2},{1,3},{2,0},{3,1},{4,6},{5,7},{6,4},{7,5},{8,10},{9,11},{10,... | collective-permute-start | bytes 1572872 | tf_op jit(solution)/shard_map/ppermute | solution.py:598
  393.2 35.0 %collective-permute-start.18 = (bf16[2,32,4096]{2,1,0:T(8,128)(2,1)}, bf16[2,32,4096]{2,1,0:T(8,128)(2,1)}, u32[]{:S(2)}, u32[]{:S(2)}) collective-permute-start(bf16[2,32,4096]{2,1,0:T(8,128)(2,1)} %get-tuple-element.206), channel_id=1, source_target_pairs={{0,2},{1,3},{2,0},{3,1},{4,6},{5,7},{6,4},{7,5},{8,10},{9,11},{10,... | collective-permute-start | bytes 1572872 | tf_op jit(solution)/shard_map/ppermute | solution.py:598
  404.4 23.9 %collective-permute-start.21 = (bf16[2,2,2,32,1536]{4,3,1,0,2:T(8,128)(2,1)}, bf16[2,2,2,32,1536]{4,3,1,0,2:T(8,128)(2,1)}, u32[]{:S(2)}, u32[]{:S(2)}) collective-permute-start(bf16[2,2,2,32,1536]{4,3,1,0,2:T(8,128)(2,1)} %fusion.33), channel_id=1, source_target_pairs={{0,1},{1,0},{2,3},{3,2},{4,5},{5,4},{6,7},{7,6},{8,9},{9,8},{10,11... | collective-permute-start | bytes 2359304 | tf_op jit(solution)/shard_map/ppermute | solution.py:598
  430.8 58.8 %collective-permute-start.40 = (bf16[128,1024]{1,0:T(8,128)(2,1)}, bf16[128,1024]{1,0:T(8,128)(2,1)}, u32[]{:S(2)}, u32[]{:S(2)}) collective-permute-start(bf16[128,1024]{1,0:T(8,128)(2,1)} %fusion.50), channel_id=1, source_target_pairs={{0,4},{1,5},{2,6},{3,7},{4,0},{5,1},{6,2},{7,3},{8,12},{9,13},{10,... | collective-permute-start | bytes 786440 | tf_op jit(solution)/shard_map/ppermute | solution.py:598
  434.0 56.8 %collective-permute-start.37 = (bf16[32,4096]{1,0:T(8,128)(2,1)}, bf16[32,4096]{1,0:T(8,128)(2,1)}, u32[]{:S(2)}, u32[]{:S(2)}) collective-permute-start(bf16[32,4096]{1,0:T(8,128)(2,1)} %fusion.48), channel_id=1, source_target_pairs={{0,4},{1,5},{2,6},{3,7},{4,0},{5,1},{6,2},{7,3},{8,12},{9,13},{10,... | collective-permute-start | bytes 786440 | tf_op jit(solution)/shard_map/ppermute | solution.py:598
  441.3 16.0 %collective-permute-start.22 = (bf16[1,120,128]{2,1,0:T(8,128)(2,1)S(1)}, bf16[1,120,128]{2,1,0:T(8,128)(2,1)S(1)}, u32[]{:S(2)}, u32[]{:S(2)}) collective-permute-start(bf16[1,120,128]{2,1,0:T(8,128)(2,1)S(1)} %constant_dynamic-update-slice_fusion.22), channel_id=1, source_target_pairs={{0,4},{1,5},{2,6},{3,7},{4,0},{5,1},{6,2},{7,3},{8,12},{9,13},{10,... | collective-permute-start | bytes 92168 | tf_op jit(solution)/shard_map/ppermute | solution.py:598
  468.7 31.9 %collective-permute-start.27 = (bf16[2,2,32,2560]{3,2,1,0:T(8,128)(2,1)}, bf16[2,2,32,2560]{3,2,1,0:T(8,128)(2,1)S(1)}, u32[]{:S(2)}, u32[]{:S(2)}) collective-permute-start(bf16[2,2,32,2560]{3,2,1,0:T(8,128)(2,1)} %copy.121), channel_id=1, source_target_pairs={{0,1},{1,0},{2,3},{3,2},{4,5},{5,4},{6,7},{7,6},{8,9},{9,8},{10,11... | collective-permute-start | bytes 1966088 | tf_op jit(solution)/shard_map/ppermute | solution.py:598
  470.8 17.4 %collective-permute-start.24 = (bf16[4,120,128]{2,1,0:T(8,128)(2,1)S(1)}, bf16[4,120,128]{2,1,0:T(8,128)(2,1)S(1)}, u32[]{:S(2)}, u32[]{:S(2)}) collective-permute-start(bf16[4,120,128]{2,1,0:T(8,128)(2,1)S(1)} %bitcast.383), channel_id=1, source_target_pairs={{0,1},{1,0},{2,3},{3,2},{4,5},{5,4},{6,7},{7,6},{8,9},{9,8},{10,11... | collective-permute-start | bytes 368648 | tf_op jit(solution)/shard_map/ppermute | solution.py:598
  473.0 19.5 %collective-permute-start.32 = (bf16[2,2,32,1536]{3,2,1,0:T(8,128)(2,1)S(1)}, bf16[2,2,32,1536]{3,2,1,0:T(8,128)(2,1)S(1)}, u32[]{:S(2)}, u32[]{:S(2)}) collective-permute-start(bf16[2,2,32,1536]{3,2,1,0:T(8,128)(2,1)S(1)} %get-tuple-element.208), channel_id=1, source_target_pairs={{0,16},{1,17},{2,18},{3,19},{4,20},{5,21},{6,22},{7,23},{8,24},{9,... | collective-permute-start | bytes 1179656 | tf_op jit(solution)/shard_map/ppermute | solution.py:598
  495.5 21.0 %collective-permute-start.26 = (bf16[16,120,128]{2,1,0:T(8,128)(2,1)S(1)}, bf16[16,120,128]{2,1,0:T(8,128)(2,1)}, u32[]{:S(2)}, u32[]{:S(2)}) collective-permute-start(bf16[16,120,128]{2,1,0:T(8,128)(2,1)S(1)} %bitcast.365), channel_id=1, source_target_pairs={{0,8},{1,9},{2,10},{3,11},{4,12},{5,13},{6,14},{7,15},{8,0},{9,1},... | collective-permute-start | bytes 1474568 | tf_op jit(solution)/shard_map/ppermute | solution.py:598
  496.5 61.7 %collective-permute-start.42 = (bf16[2,128,1024]{2,1,0:T(8,128)(2,1)}, bf16[2,128,1024]{2,1,0:T(8,128)(2,1)}, u32[]{:S(2)}, u32[]{:S(2)}) collective-permute-start(bf16[2,128,1024]{2,1,0:T(8,128)(2,1)} %pad_maximum_fusion.6), channel_id=1, source_target_pairs={{0,16},{1,17},{2,18},{3,19},{4,20},{5,21},{6,22},{7,23},{8,24},{9,... | collective-permute-start | bytes 1572872 | tf_op jit(solution)/shard_map/ppermute | solution.py:598
  498.5 49.1 %collective-permute-start.39 = (bf16[2,32,4096]{2,1,0:T(8,128)(2,1)}, bf16[2,32,4096]{2,1,0:T(8,128)(2,1)}, u32[]{:S(2)}, u32[]{:S(2)}) collective-permute-start(bf16[2,32,4096]{2,1,0:T(8,128)(2,1)} %pad_maximum_fusion.5), channel_id=1, source_target_pairs={{0,16},{1,17},{2,18},{3,19},{4,20},{5,21},{6,22},{7,23},{8,24},{9,... | collective-permute-start | bytes 1572872 | tf_op jit(solution)/shard_map/ppermute | solution.py:598
  515.3 21.2 %collective-permute-start.36 = (bf16[2,32,1536]{2,1,0:T(8,128)(2,1)}, bf16[2,32,1536]{2,1,0:T(8,128)(2,1)}, u32[]{:S(2)}, u32[]{:S(2)}) collective-permute-start(bf16[2,32,1536]{2,1,0:T(8,128)(2,1)} %pad_maximum_fusion.14), channel_id=1, source_target_pairs={{0,16},{1,17},{2,18},{3,19},{4,20},{5,21},{6,22},{7,23},{8,24},{9,... | collective-permute-start | bytes 589832 | tf_op jit(solution)/shard_map/ppermute | solution.py:598
  532.8 16.9 %collective-permute-start.29 = (bf16[32,2560]{1,0:T(8,128)(2,1)}, bf16[32,2560]{1,0:T(8,128)(2,1)}, u32[]{:S(2)}, u32[]{:S(2)}) collective-permute-start(bf16[32,2560]{1,0:T(8,128)(2,1)} %copy.127), channel_id=1, source_target_pairs={{0,4},{1,5},{2,6},{3,7},{4,0},{5,1},{6,2},{7,3},{8,12},{9,13},{10,... | collective-permute-start | bytes 491528 | tf_op jit(solution)/shard_map/ppermute | solution.py:598
  (72 other events, 848.3 us)
Sparse Core Ops, SparseCore 0:
  11.5 154.7 all-gather.1

commit v6 on v5

--- a/solution.py
+++ b/solution.py
@@ -235,93 +235,116 @@
     )(low, high, weight, x, scale, carry)
 
 
-def store_rows(total, own_core, own_slot, pieces, keep_ref, send_ref):
-    rows = total.shape[0] // pieces
+def store_pieces(total, own_core, place_of, keep_ref, send_ref):
+    rows = keep_ref.shape[-2]
+    pieces = total.shape[0] // rows
     low = total.astype(jnp.bfloat16).reshape(pieces // 2, 2, rows, total.shape[1])
     here = own_core == 0
     for slot in range(pieces // 2):
         first, second = low[slot, 0], low[slot, 1]
-        place = pl.ds(pl.multiple_of((own_slot ^ slot) * rows, rows), rows)
-        keep_ref[place, :] = jnp.where(here, first, second)
-        send_ref[place, :] = jnp.where(here, second, first)
-
-
-def grad_dot_kernel(pieces, own_ref, x_ref, dy_ref, keep_ref, send_ref):
-    total = dot_tn(x_ref[...], dy_ref[0])
-    store_rows(total, own_ref[0], own_ref[1], pieces, keep_ref, send_ref)
-
-
-def grad_dot(own, x, dy, pieces, name):
-    tokens, depth = x.shape
-    groups, _, columns = dy.shape
-    per = columns // COL_BLOCK
-    half = jax.ShapeDtypeStruct((depth // 2, groups * columns), jnp.bfloat16)
-    block = pl.BlockSpec((depth // 2, COL_BLOCK), lambda i, own: (0, i))
+        keep_ref[place_of(slot)] = jnp.where(here, first, second)
+        send_ref[place_of(slot)] = jnp.where(here, second, first)
+
+
+def weight_grad_kernel(table, first, own_ref, x_ref, dx_ref, y_ref, dy_ref, keep_ref, send_ref, left):
+    step = pl.program_id(0)
+
+    def place_of(slot):
+        return own_ref[1] ^ table[slot], 0
+
+    if first:
+
+        @pl.when(step == 0)
+        def _():
+            left[...] = x_ref[...].T
+
+    @pl.when(step == first)
+    def _():
+        left[...] = y_ref[...].T
+
+    right = jnp.where(step < first, dx_ref[...], dy_ref[0]) if first else dy_ref[0]
+    store_pieces(dot_nn(left[...], right), own_ref[0], place_of, keep_ref, send_ref)
+
+
+def weight_grad(own, x, dx, y, dy, table, rows, name):
+    tokens, depth = y.shape
+    first = 0 if dx is None else dx.shape[1] // COL_BLOCK
+    groups = dy.shape[0]
+    blocks = first + groups
+    whole = pl.BlockSpec((tokens, depth), lambda i, own: (0, 0))
+    block = pl.BlockSpec((len(table), 1, rows, COL_BLOCK), lambda i, own: (0, i, 0, 0))
+    half = jax.ShapeDtypeStruct((len(table), blocks, rows, COL_BLOCK), jnp.bfloat16)
+    if dx is None:
+        x, dx = y, y
     return pl.pallas_call(
-        partial(grad_dot_kernel, pieces),
+        partial(weight_grad_kernel, table, first),
         grid_spec=pltpu.PrefetchScalarGridSpec(
             num_scalar_prefetch=1,
-            grid=(groups * per,),
-            in_specs=[
-                pl.BlockSpec((tokens, depth), lambda i, own: (0, 0)),
-                pl.BlockSpec((1, tokens, COL_BLOCK), lambda i, own: (i // per, 0, i % per)),
-            ],
-            out_specs=[block, block],
-        ),
-        out_shape=[half, half],
-        compiler_params=kernel_params(40),
-        cost_estimate=cost(groups * tokens * depth * columns, tokens * columns),
-        name=name,
-    )(own, x, dy)
-
-
-def grad_pair_kernel(pieces, first, own_ref, x_ref, dx_ref, y_ref, dy_ref, keep_ref, send_ref):
-    step = pl.program_id(0)
-
-    @pl.when(step < first)
-    def _():
-        total = dot_tn(x_ref[...], dx_ref[...])
-        store_rows(total, own_ref[0], own_ref[1], pieces, keep_ref, send_ref)
-
-    @pl.when(step >= first)
-    def _():
-        total = dot_tn(y_ref[...], dy_ref[0])
-        store_rows(total, own_ref[0], own_ref[1], pieces, keep_ref, send_ref)
-
-
-def grad_pair(own, x, dx, y, dy, pieces, name):
-    tokens, depth = x.shape
-    first = dx.shape[1] // COL_BLOCK
-    groups = dy.shape[0]
-    columns = dx.shape[1] + groups * COL_BLOCK
-    whole = pl.BlockSpec((tokens, depth), lambda i, own: (0, 0))
-    block = pl.BlockSpec((depth // 2, COL_BLOCK), lambda i, own: (0, i))
-    half = jax.ShapeDtypeStruct((depth // 2, columns), jnp.bfloat16)
-    return pl.pallas_call(
-        partial(grad_pair_kernel, pieces, first),
-        grid_spec=pltpu.PrefetchScalarGridSpec(
-            num_scalar_prefetch=1,
-            grid=(first + groups,),
+            grid=(blocks,),
             in_specs=[
                 whole,
-                pl.BlockSpec((tokens, COL_BLOCK), lambda i, own: (0, jnp.minimum(i, first - 1))),
+                pl.BlockSpec(
+                    (tokens, COL_BLOCK), lambda i, own: (0, jnp.clip(i, 0, max(first - 1, 0)))
+                ),
                 whole,
                 pl.BlockSpec(
                     (1, tokens, COL_BLOCK), lambda i, own: (jnp.maximum(i - first, 0), 0, 0)
                 ),
             ],
             out_specs=[block, block],
+            scratch_shapes=[pltpu.VMEM((depth, tokens), jnp.bfloat16)],
         ),
         out_shape=[half, half],
         compiler_params=kernel_params(40),
-        cost_estimate=cost(tokens * depth * columns, tokens * columns),
+        cost_estimate=cost(tokens * depth * blocks * COL_BLOCK, tokens * blocks * COL_BLOCK),
         name=name,
     )(own, x, dx, y, dy)
 
 
+def place_units_kernel(own_ref, *refs):
+    sources, (expand_ref, shrink_ref) = refs[:4], refs[4:]
+    for flip, source in enumerate(sources):
+        at = own_ref[0] ^ flip
+        rows = expand_ref.shape[0] // 4
+        place = pl.ds(pl.multiple_of(at * rows, rows), rows)
+        width = source.shape[2]
+        for block in range(expand_ref.shape[1] // width):
+            piece = source[0, block * rows : (block + 1) * rows, :]
+            expand_ref[place, block * width : (block + 1) * width] = piece.astype(jnp.float32)
+        rows = source.shape[1]
+        place = pl.ds(pl.multiple_of(at * rows, rows), rows)
+        shrink_ref[place, :] = source[1].astype(jnp.float32)
+
+
+def place_attention_kernel(own_ref, *refs):
+    sources, (out_ref, proj_ref) = refs[:4], refs[4:]
+    for flip, source in enumerate(sources):
+        blocks, rows, width = source.shape
+        place = pl.ds(pl.multiple_of((own_ref[0] ^ flip) * rows, rows), rows)
+        for block in range(blocks):
+            piece = source[block].astype(jnp.float32)
+            if block < 2:
+                out_ref[place, block * width : (block + 1) * width] = piece
+            else:
+                group, half = (block - 2) % 3, (block - 2) // 3
+                start = (2 * group + half) * width
+                proj_ref[place, start : start + width] = piece
+
+
+def place_reps(kernel, rep_id, own, shapes, name):
+    parts = [own] + [exchange(own, mask, 0) for mask in (1, 2, 3)]
+    return pl.pallas_call(
+        kernel,
+        grid_spec=pltpu.PrefetchScalarGridSpec(num_scalar_prefetch=1, grid=()),
+        out_shape=[jax.ShapeDtypeStruct(shape, jnp.float32) for shape in shapes],
+        compiler_params=kernel_params(32),
+        cost_estimate=cost(2**20, 2**20),
+        name=name,
+    )(rep_id.astype(jnp.int32)[None], *parts)
+
+
 def feed_forward_kernel(
-    depth_pieces,
-    unit_pieces,
+    table,
     own_ref,
     norm_ref,
     grad_ref,
@@ -379,34 +402,54 @@
         branch_ref[rows, :] += dot_nn(unit, shrink)
         d_norm_ref[rows, :] += dot_nt(d_low, expand)
     d_bias_ref[...] = bias_sum
-    store_rows(
-        dot_tn(hidden[...], grad_ref[...]), own_ref[0], own_ref[3], unit_pieces, keep_s_ref, send_s_ref
-    )
-    store_rows(
-        dot_nn(norm_t[...], d_pre[...]), own_ref[0], own_ref[1], depth_pieces, keep_e_ref, send_e_ref
-    )
-
-
-def feed_forward(own, norm, grad, expand, bias, shrink, depth_pieces, unit_pieces):
+    store_pieces(
+        dot_tn(hidden[...], grad_ref[...]),
+        own_ref[0],
+        lambda slot: (0, own_ref[3] ^ slot, 0),
+        keep_s_ref,
+        send_s_ref,
+    )
+    store_pieces(
+        dot_nn(norm_t[...], d_pre[...]),
+        own_ref[0],
+        lambda slot: (own_ref[1] ^ table[slot], 0),
+        keep_e_ref,
+        send_e_ref,
+    )
+
+
+def feed_forward(own, norm, grad, expand, bias, shrink, table):
     tokens, depth = norm.shape
     total = bias.shape[1]
     steps = total // FF_BLOCK
+    slots = len(table)
+    rows_e = depth // (2 * slots)
+    per = depth // FF_BLOCK
     whole = pl.BlockSpec((tokens, depth), lambda i, own: (0, 0))
-    half_e = pl.BlockSpec((depth // 2, FF_BLOCK), lambda i, own: (0, i))
-    half_s = pl.BlockSpec((FF_BLOCK // 2, depth), lambda i, own: (i ^ own[2], 0))
-    line = pl.BlockSpec((1, FF_BLOCK), lambda i, own: (0, i))
-    if shrink.ndim == 2:
+    half_e = pl.BlockSpec(
+        (slots, 1, rows_e, FF_BLOCK), lambda i, own: (0, i // per, 0, i % per)
+    )
+    if slots > 1:
+        spec_e = weight_spec(expand, 4, FF_BLOCK, lambda i, own: i)
+        spec_s = pl.BlockSpec(
+            (shrink.shape[0] // steps, 4) + shrink.shape[2:], lambda i, own: (i, 0, 0, 0)
+        )
+        shape_s = (2, 2, steps // 2, FF_BLOCK // 4, depth)
+        half_s = pl.BlockSpec(
+            (1, 2, 1, FF_BLOCK // 4, depth),
+            lambda i, own: ((i & 1) ^ own[2], 0, ((i & 2) | (i >> 2)) ^ own[4], 0, 0),
+        )
+    else:
         spec_e = weight_spec(expand, 0, FF_BLOCK, lambda i, own: i)
         spec_s = pl.BlockSpec((FF_BLOCK, depth), lambda i, own: (i, 0))
-    else:
-        devices, blocks, rows, columns = shrink.shape
-        spec_e = weight_spec(expand, 4, FF_BLOCK, lambda i, own: i)
-        spec_s = pl.BlockSpec((devices // steps, 4, rows, columns), lambda i, own: (i, 0, 0, 0))
+        shape_s = (1, 1, steps, FF_BLOCK // 2, depth)
+        half_s = pl.BlockSpec((1, 1, 1, FF_BLOCK // 2, depth), lambda i, own: (0, 0, i, 0, 0))
+    line = pl.BlockSpec((1, FF_BLOCK), lambda i, own: (0, i))
     wide = jax.ShapeDtypeStruct((tokens, depth), jnp.float32)
-    out_e = jax.ShapeDtypeStruct((depth // 2, total), jnp.bfloat16)
-    out_s = jax.ShapeDtypeStruct((total // 2, depth), jnp.bfloat16)
+    out_e = jax.ShapeDtypeStruct((slots, total // depth, rows_e, depth), jnp.bfloat16)
+    out_s = jax.ShapeDtypeStruct(shape_s, jnp.bfloat16)
     return pl.pallas_call(
-        partial(feed_forward_kernel, depth_pieces, unit_pieces),
+        partial(feed_forward_kernel, table),
         grid_spec=pltpu.PrefetchScalarGridSpec(
             num_scalar_prefetch=1,
             grid=(steps,),
@@ -604,7 +647,7 @@
     masks += [(1 << bit, 0) for bit in reversed(range(reps.bit_length() - 1))]
     rows = row[None]
     for pair in masks:
-        rows = jnp.stack([rows, exchange(rows, *pair)], axis=1).reshape(-1, *row.shape)
+        rows = jnp.concatenate([rows, exchange(rows, *pair)], axis=0)
     return rows
 
 
@@ -633,37 +676,38 @@
     return parts
 
 
+ORDERS = (("y", "x", "z1", "z2"), ("x", "y", "z1", "z2"))
+
+
+def place_in(order, shard, y):
+    bits = {"z2": (shard >> 2) & 1, "z1": (shard >> 1) & 1, "x": shard & 1, "y": y}
+    place = 0
+    for name in order:
+        place = place * 2 + bits[name]
+    return place
+
+
 class HalvingSum:
-    def __init__(self, keep, send, order):
-        rows, columns = keep.shape[0] // 16, keep.shape[1]
-        self.shape = (2, 2, 2, 2, rows, columns)
-        self.axes = ["z2", "z1", "x", "y"]
-        self.order = list(order)
-        self.stay = keep.reshape(self.shape)
+    def __init__(self, halves, order):
+        keep, send = halves
+        self.masks = [MASKS[name] for name in order]
+        self.stay = keep
         self.arrived = exchange(send, *MASKS["core"])
 
-    def half(self, axis, side):
-        stay = lax.index_in_dim(self.stay, side, axis, keepdims=False)
-        arrived = lax.index_in_dim(self.arrived.reshape(self.stay.shape), side, axis, keepdims=False)
+    def added(self, start, stop):
+        stay, arrived = self.stay[start:stop], self.arrived[start:stop]
         return (stay.astype(jnp.float32) + arrived.astype(jnp.float32)).astype(jnp.bfloat16)
 
     def step(self):
-        name = self.order.pop(0)
-        axis = self.axes.index(name)
-        self.axes.pop(axis)
-        away, stay = self.half(axis, 1), self.half(axis, 0)
-        self.stay, self.arrived = stay, exchange(away, *MASKS[name])
+        count = self.stay.shape[0]
+        away = self.added(count // 2, count)
+        self.stay = self.added(0, count // 2)
+        self.arrived = exchange(away, *self.masks.pop(0))
 
     def finish(self):
-        while self.order:
+        while self.masks:
             self.step()
-        own = self.stay.astype(jnp.float32) + self.arrived.reshape(self.stay.shape).astype(jnp.float32)
-        own = own.astype(jnp.bfloat16)
-        pair = [own, exchange(own, *MASKS["core"])]
-        both = jnp.stack(pair)
-        other = exchange(both, *MASKS["y"])
-        parts = to_absolute([*pair, other[0], other[1]], lax.axis_index("rep"))
-        return jnp.concatenate(parts, axis=0).astype(jnp.float32)
+        return self.added(0, 1)[0]
 
 
 class PlainSum:
@@ -754,24 +798,40 @@
         )
         out_at = (packed, 8)
         w_expand, w_shrink = packed, packed
-        depth_pieces, unit_pieces = shards * reps, reps
-        own = jnp.stack(
-            [rep_id & 1, shard_id * 2 + (rep_id >> 1), shard_id, rep_id >> 1]
-        ).astype(jnp.int32)
+        y_id = rep_id >> 1
+        own, own_high = [
+            jnp.stack(
+                [
+                    rep_id & 1,
+                    place_in(order, shard_id, y_id),
+                    shard_id & 1,
+                    y_id,
+                    (shard_id & 2) | (shard_id >> 2),
+                ]
+            ).astype(jnp.int32)
+            for order in ORDERS
+        ]
+        tables = [
+            tuple(place_in(order, slot >> 1, slot & 1) for slot in range(2 * shards))
+            for order in ORDERS
+        ]
+        piece = quarter
     else:
         w_proj, out_at = gather_rows(projector), (gather_rows(outweight), 0)
         w_expand, w_shrink = gather_rows(expander), gather_rows(shrinker)
-        depth_pieces, unit_pieces = 2, 2
-        own = jnp.zeros((4,), jnp.int32)
+        own = own_high = jnp.zeros((5,), jnp.int32)
+        tables = [(0,), (0,)]
+        piece = feature // 2
 
     def depth_sum(halves, order):
         if halving:
-            return HalvingSum(*halves, order)
-        return PlainSum(jnp.concatenate(halves, axis=0))
+            return HalvingSum(halves, order)
+        columns = [half[0].transpose(1, 0, 2).reshape(feature // 2, -1) for half in halves]
+        return PlainSum(jnp.concatenate(columns, axis=0))
 
     def unit_sum(halves, order):
         if halving:
-            return HalvingSum(*halves, order)
+            return HalvingSum([half.reshape(16, -1, feature) for half in halves], order)
         blocks = [half.reshape(-1, 1, FF_BLOCK // 2, feature) for half in halves]
         return PlainSum(jnp.concatenate(blocks, axis=1).reshape(-1, feature))
 
@@ -821,10 +881,10 @@
     d_branch_m = (gate_m[:, None, :] * grad_out).astype(jnp.bfloat16).reshape(token_count, feature)
     g_shrinkbias = jnp.sum(d_branch_m, axis=0, dtype=jnp.float32)
     branch_m, d_norm_m, keep_e, send_e, keep_s, send_s, g_expandbias = feed_forward(
-        own, norm_m, d_branch_m, w_expand, b_expand, w_shrink, depth_pieces, unit_pieces
-    )
-    sum_e = depth_sum((keep_e, send_e), ("y", "x", "z1", "z2"))
-    sum_s = unit_sum((keep_s, send_s), ("x", "y", "z1", "z2"))
+        own, norm_m, d_branch_m, w_expand, b_expand, w_shrink, tables[0]
+    )
+    sum_e = depth_sum((keep_e, send_e), ORDERS[0])
+    sum_s = unit_sum((keep_s, send_s), ORDERS[1])
     branch_m = (branch_m + b_shrink).reshape(seqs_dev, seq_len, feature)
     layer_out = middle + gate_m[:, None, :] * branch_m
     d_gate_m = jnp.sum(grad_out * branch_m, axis=1)
@@ -842,11 +902,11 @@
     d_low, q_low, v_low = attention_backward(
         projected, d_attended, attended_t, log_totals, 0, half_pairs, "attention_backward_low"
     )
-    halves_low = grad_pair(
-        own, attended, d_branch_a, norm_a, d_low, depth_pieces, "weight_grad_low"
+    halves_low = weight_grad(
+        own, attended, d_branch_a, norm_a, d_low, tables[0], piece, "weight_grad_low"
     )
     d_attended, halves_low = hold((d_attended, halves_low), sum_e, sum_s)
-    sum_low = depth_sum(halves_low, ("y", "x", "z1", "z2"))
+    sum_low = depth_sum(halves_low, ORDERS[0])
     for total in (sum_e, sum_s):
         total.step()
     d_high, q_high, v_high = attention_backward(
@@ -855,9 +915,10 @@
     d_high = hold(d_high, sum_e, sum_s, sum_low)
     for total in (sum_e, sum_s, sum_low):
         total.step()
-    sum_high = depth_sum(
-        grad_dot(own, norm_a, d_high, depth_pieces, "weight_grad_high"), ("x", "y", "z1", "z2")
-    )
+    halves_high = weight_grad(
+        own_high, None, None, norm_a, d_high, tables[1], piece, "weight_grad_high"
+    )
+    sum_high = depth_sum(halves_high, ORDERS[1])
     d_high = hold(d_high, sum_high)
     sum_high.step()
     latents_grad, d_shift_a, d_scale_a = project_back(
@@ -892,38 +953,52 @@
                 g_outbiases,
                 g_expandbias,
                 g_shrinkbias,
+                jnp.zeros((feature,)),
             )
         ]
     ).astype(jnp.bfloat16)
     devices = reps * shards
     size = seqs_dev * feature
-    gathered = gather_relative(small).reshape(devices, -1)
-    g_expander, g_shrinker = sum_e.finish(), sum_s.finish()
-    low, high = sum_low.finish(), sum_high.finish()
-    g_outweight = low[:, :feature]
-    g_projector = jnp.stack(
-        [low[:, feature:].reshape(own_rows, 3, -1), high.reshape(own_rows, 3, -1)], axis=2
-    ).reshape(own_rows, 3 * feature)
-
-    cond_all = gathered[:, 6 * size : 7 * size].reshape(devices * seqs_dev, feature)
+    gathered = gather_relative(small)
+    if halving:
+        done = jnp.stack([total.finish().reshape(-1, feature) for total in (sum_e, sum_s)])
+        g_expander, g_shrinker = place_reps(
+            place_units_kernel, rep_id, done, (expander.shape, shrinker.shape), "place_units"
+        )
+        done = jnp.concatenate([sum_low.finish(), sum_high.finish()], axis=0)
+        g_outweight, g_projector = place_reps(
+            place_attention_kernel, rep_id, done, (outweight.shape, projector.shape), "place_attention"
+        )
+    else:
+        g_expander, g_shrinker = sum_e.finish(), sum_s.finish()
+        low, high = sum_low.finish(), sum_high.finish()
+        g_outweight = low[:, :feature]
+        g_projector = jnp.stack(
+            [low[:, feature:].reshape(own_rows, 3, -1), high.reshape(own_rows, 3, -1)], axis=2
+        ).reshape(own_rows, 3 * feature)
+
+    lines = size // 128
+    cond_all = gathered[:, 6 * lines : 7 * lines].reshape(devices * seqs_dev, feature)
     cond_all = lax.dynamic_slice_in_dim(cond_all, shard_id * own_rows, own_rows, 1)
-    d_mod = gathered[:, : 6 * size]
-    d_mod = d_mod.reshape(devices, 6, seqs_dev, feature).transpose(0, 2, 1, 3)
+    d_mod = gathered[:, : 6 * lines].reshape(devices, 6, seqs_dev, feature).transpose(0, 2, 1, 3)
     d_mod = d_mod.reshape(devices * seqs_dev, 6 * feature)
+    bias_sums = jnp.sum(gathered[:, 7 * lines :], axis=0, dtype=jnp.float32).reshape(-1)
     bias_grads = []
-    start = 7 * size
+    start = 0
     for total in (feature, feature, feature, expandbias.shape[0] * shards, feature):
         part = total // shards
-        own_part = lax.dynamic_slice_in_dim(gathered, start + shard_id * part, part, 1)
-        bias_grads.append(jnp.sum(own_part, axis=0, dtype=jnp.float32))
+        bias_grads.append(lax.dynamic_slice_in_dim(bias_sums, start + shard_id * part, part, 0))
         start += total
     g_modbias = jnp.sum(
         lax.dynamic_slice_in_dim(d_mod, shard_id * own_bias, own_bias, 1), axis=0, dtype=jnp.float32
     )
     g_modulator = jnp.einsum("sr,sc->rc", cond_all, d_mod, preferred_element_type=jnp.float32)
-    own_mod = d_mod.reshape(shards, reps, seqs_dev, 6 * feature)[:, 0].reshape(-1, 6 * feature)
+    own_mod = d_mod[: shards * seqs_dev]
     d_cond_act = jnp.einsum("sc,rc->sr", own_mod, modulator, preferred_element_type=jnp.float32)
-    d_cond_act = jnp.stack(to_absolute(d_cond_act.reshape(shards, seqs_dev, own_rows), shard_id))
+    d_cond_act = d_cond_act.reshape(shards, seqs_dev, own_rows)
+    bits = shards.bit_length() - 1
+    turned = [sum(((i >> bit) & 1) << (bits - 1 - bit) for bit in range(bits)) for i in range(shards)]
+    d_cond_act = jnp.stack(to_absolute([d_cond_act[i] for i in turned], shard_id))
     d_cond_act = d_cond_act.reshape(shards * seqs_dev, own_rows)
     _, silu_pull = jax.vjp(jax.nn.silu, cond_slice)
     conditions_grad = silu_pull(d_cond_act)[0]

time: 590 us -> 516 us (0.87)
  local copies, waits for them, and re-layouts: 101 us -> 31.3 us
  other arithmetic: 107 us -> 67 us
  waiting for transfers between devices: 105 us -> 139 us
    ppermute x43 -> x41, waiting for transfers between devices: 87.3 us -> 122 us  [exchange(): return lax.ppermute(value, ('rep', 'fsdp'), pairs)]
    unnamed x166 -> x121, local copies, waits for them, and re-layouts: 48.8 us -> 19.9 us
    convert_element_type x28 -> x18, other arithmetic: 57 us -> 35.7 us  [added(): (stay.astype(jnp.float32) + arrived.astype(jnp.float32)).astype(jnp.bfloa...]
    slice x14 -> x3, local copies, waits for them, and re-layouts: 21.4 us -> 3.02 us  [the longest x1 2.97 us: added(): stay, arrived = (self.stay[start:stop], self.arrived[start:stop])]
    convert_element_type x4 -> x0, local copies, waits for them, and re-layouts: 8.06 us -> none  [the longest x3 7.84 us: half(): (stay.astype(jnp.float32) + arrived.astype(jnp.float32)).astype(jnp.bfloa...]
    another operation x17 -> x9, other arithmetic: 7.78 us -> 0.19 us  [the longest x4 4.1 us: finish(): both = jnp.stack(pair)]
    concatenate x4 -> x2, local copies, waits for them, and re-layouts: 6.61 us -> 0.2 us  [gather_relative(): rows = jnp.concatenate([rows, exchange(rows, *pair)], axis=0)]
    select_n x4 -> x0, other arithmetic: 6.34 us -> none  [to_absolute(): jnp.where(flipped, parts[i ^ bit], parts[i])]
  transfers between devices with their start and end apart: 45 -> 43, of which waited for: 13 -> 20; matrix products, arithmetic and copies ran while one was open for 29% -> 15% of each run, Pallas kernels for 21% -> 25%
where the time goes in v6:
time: 516 us; the launch traced here: 512 us
  Pallas kernels  213 us (41%)
  waiting for transfers between devices  139 us (27%)
  other arithmetic  67 us (13%)
  starting transfers between devices  43.3 us (8%)
  local copies, waits for them, and re-layouts  31.3 us (6%)
  between operations  15.3 us (3%)
    ppermute x41, waiting for transfers between devices, exchange(): return lax.ppermute(value, ('rep', 'fsdp'), pairs)  122 us
    pallas_call x1, Pallas kernels, feed_forward(): pl.pallas_call(partial(feed_forward_kernel, table), grid_spec=pltpu.Prefe...  74.9 us
    pallas_call x2, Pallas kernels, attention_backward(): pl.pallas_call(attention_backward_kernel, grid=(count,), in_specs=[pl.Blo...  49.3 us
    ppermute x41, starting transfers between devices, exchange(): return lax.ppermute(value, ('rep', 'fsdp'), pairs)  36.9 us
    convert_element_type x18, other arithmetic, added(): (stay.astype(jnp.float32) + arrived.astype(jnp.float32)).astype(jnp.bfloa...  35.7 us
    pallas_call x1, Pallas kernels, attention_forward(): pl.pallas_call(attention_forward_kernel, grid=(pairs,), in_specs=[pl.Bloc...  30.1 us
    unnamed x121, local copies, waits for them, and re-layouts  19.9 us
    all_gather x1, waiting for transfers between devices, gather_packed(): full = lax.all_gather(packed, ('fsdp', 'rep'), axis=0, tiled=True)  17.8 us
  transfers between devices with their start and end apart: 43, of which 20 were waited for; matrix products, arithmetic and copies ran while one was open for 15% of the time, Pallas kernels for 25%

profile of v6, /device:TPU:0, one launch (start us, length us, event | category | flops | bytes accessed | tf_op | source)
XLA Modules:
  0.0 512.1 jit_solution(8980561008725901723)
XLA Ops:
  13.0 4.0 collective-permute-start.5
  19.8 6.3 %all-to-all-start = ((f32[8,1,7936]{2,1,0:T(1,128)}), f32[8,1,7936]{2,1,0:T(1,128)S(1)}, u32[]{:S(2)}, u32[]{:S(2)}) async-start(f32[8,1,7936]{2,1,0:T(1,128)} %copy.29), calls=%async_computation | async-start | bytes 507904 | tf_op jit(solution)/shard_map/all_to_all | solution.py:854
  33.2 14.3 %collective-permute-done.6 = bf16[2,32,1536]{2,1,0:T(8,128)(2,1)S(1)} collective-permute-done((bf16[2,32,1536]{2,1,0:T(8,128)(2,1)S(1)}, bf16[2,32,1536]{2,1,0:T(8,128)(2,1)S(1)}, u32[]{:S(2)}, u32[]{:S(2)}) %collective-permute-start.6) | collective-permute-done | bytes 196640 | tf_op jit(solution)/shard_map/ppermute | solution.py:641
  55.1 7.8 %collective-permute-done.7 = bf16[4,32,1536]{2,1,0:T(8,128)(2,1)S(1)} collective-permute-done((bf16[4,32,1536]{2,1,0:T(8,128)(2,1)}, bf16[4,32,1536]{2,1,0:T(8,128)(2,1)S(1)}, u32[]{:S(2)}, u32[]{:S(2)}) %collective-permute-start.7) | collective-permute-done | bytes 393248 | tf_op jit(solution)/shard_map/ppermute | solution.py:641
  64.2 7.6 %collective-permute-done.2 = bf16[4,32,1536]{2,1,0:T(8,128)(2,1)S(1)} collective-permute-done((bf16[4,32,1536]{2,1,0:T(8,128)(2,1)}, bf16[4,32,1536]{2,1,0:T(8,128)(2,1)S(1)}, u32[]{:S(2)}, u32[]{:S(2)}) %collective-permute-start.2) | collective-permute-done | bytes 393248 | tf_op jit(solution)/shard_map/ppermute | solution.py:641
  75.0 21.7 %collective-permute-done.8 = bf16[8,32,1536]{2,1,0:T(8,128)(2,1)S(1)} collective-permute-done((bf16[8,32,1536]{2,1,0:T(8,128)(2,1)S(1)}, bf16[8,32,1536]{2,1,0:T(8,128)(2,1)S(1)}, u32[]{:S(2)}, u32[]{:S(2)}) %collective-permute-start.8) | collective-permute-done | bytes 786464 | tf_op jit(solution)/shard_map/ppermute | solution.py:641
  99.9 3.6 fusion.16.grad_ref
  104.4 12.7 %project.1 = (bf16[1024,3072]{1,0:T(8,128)(2,1)}, bf16[1024,3072]{1,0:T(8,128)(2,1)}) custom-call(s32[1]{0:T(128)} %bitcast.7.own_ref, bf16[1024,1024]{1,0:T(8,128)(2,1)S(1)} %fusion.14.x_ref.y_ref.dx_ref, f32[1,3072]{1,0:T(1,128)S(1)} %pad_maximum_fusion.12.b_ref, bf16[16,32,1536]{2,1,0:T(8,128)(2,1)} %constant_dynamic-update-slice_fusion.refs_0_, ...), custom_call_target="tpu_custom_call" | custom-call | flops 3221225472 | bytes 3145728 | tf_op jit(solution)/shard_map/project/pallas_call | solution.py:106
  117.1 30.1 %attention_forward.1 = (bf16[1024,1024]{1,0:T(8,128)(2,1)S(1)}, f32[1024,1024]{1,0:T(8,128)}, f32[8,2,1024]{2,1,0:T(2,128)S(1)}) custom-call(bf16[1024,3072]{1,0:T(8,128)(2,1)} %get-tuple-element.66.q_ref.k_ref.v_ref, bf16[1024,3072]{1,0:T(8,128)(2,1)} %get-tuple-element.66.q_ref.k_ref.v_ref, bf16[1024,3072]{1,0:T(8,128)(2,1)} %get-tuple-element.66.q_ref.k_ref.v_ref), custom_call_target="tpu_custom_call" | custom-call | flops 4294967296 | bytes 8388608 | tf_op jit(solution)/shard_map/attention_forward/pallas_call | solution.py:519
  148.5 17.8 %all-gather.2.cloned.1.call-done = bf16[9216,1024]{1,0:T(8,128)(2,1)} async-done(((bf16[288,1024]{1,0:T(8,128)(2,1)}), bf16[9216,1024]{1,0:T(8,128)(2,1)}) %all-gather.2.cloned.1.call-update) | async-done | bytes 18874384 | tf_op jit(solution)/shard_map/all_gather | solution.py:754
  167.8 4.2 attention_out.1
  176.7 74.9 %feed_forward.1 = (f32[1024,1024]{1,0:T(8,128)}, f32[1024,1024]{1,0:T(8,128)}, bf16[16,4,32,1024]{3,2,1,0:T(8,128)(2,1)}, bf16[16,4,32,1024]{3,2,1,0:T(8,128)(2,...) custom-call(s32[5]{0:T(128)} %stack.63.own_ref, ...), custom_call_target="tpu_custom_call" | custom-call | flops 25769803776 | bytes 16777216 | tf_op jit(solution)/shard_map/feed_forward/pallas_call | solution.py:451
  256.3 5.8 %fusion.7 = (f32[1024]{0:T(1024)S(1)}, f32[1,1024,1024]{2,1,0:T(8,128)}) fusion(bf16[1,1024,1024]{2,1,0:T(8,128)(2,1)S(1)} %copy-done.23, f32[1024,1024]{1,0:T(8,128)} %get-tuple-element.69, f32[1024]{0:T(1024)S(1)} %get-tuple-element.175, f32[1,1024,1024]{2,1,0:T(8,128)S(1)} %copy-done.19, f32[1024]{0:T(1024)S(1)} %bitcast.207), kind=kLoop, calls=%fused_computation.14 | loop fusion | flops 6290432 | bytes 14692352 | tf_op jit(solution)/shard_map/reduce_sum | solution.py:890
  267.0 6.7 %fusion.8 = (bf16[8,128,1024]{2,1,0:T(8,128)(2,1)}, bf16[8,128,1024]{2,1,0:T(8,128)(2,1)}) fusion(bf16[1,2,4,128,1024]{4,3,2,1,0:T(8,128)(2,1)S(1)} %get-tuple-element.155, bf16[16,128,1024]{2,1,0:T(8,128)(2,1)} %copy-done.28, bf16[1,2,4,128,1024]{4,3,2,1,0:T(8,128)(2,1)S(1)} %get-tuple-element.156), kind=kLoop, calls=%fused_computation.16 | loop fusion | flops 8388608 | bytes 12582912 | tf_op jit(solution)/shard_map/convert_element_type | solution.py:699
  275.2 3.5 add_convert_fusion
  286.3 4.7 attention_out_back.1.g_ref
  291.0 25.0 %attention_backward_low.1 = (bf16[3,1024,512]{2,1,0:T(8,128)(2,1)S(1)}, f32[1,512]{1,0:T(1,128)S(1)}, f32[1,512]{1,0:T(1,128)S(1)}) custom-call(bf16[1024,3072]{1,0:T(8,128)(2,1)} %get-tuple-element.66.q_ref.k_ref.v_ref, bf16[1024,3072]{1,0:T(8,128)(2,1)} %get-tuple-element.66.q_ref.k_ref.v_ref, bf16[1024,3072]{1,0:T(8,128)(2,1)} %get-tuple-element.66.q_ref.k_ref.v_ref, ...), custom_call_target="tpu_custom_call" | custom-call | flops 2147483648 | bytes 8388608 | tf_op jit(solution)/shard_map/attention_backward_low/pallas_call | solution.py:596
  317.7 10.6 %weight_grad_low.1 = (bf16[16,5,32,512]{3,2,1,0:T(8,128)(2,1)S(1)}, bf16[16,5,32,512]{3,2,1,0:T(8,128)(2,1)}) custom-call(s32[5]{0:T(128)S(1)} %copy-done.17, bf16[1024,1024]{1,0:T(8,128)(2,1)S(1)} %copy-done.16, bf16[1024,1024]{1,0:T(8,128)(2,1)S(1)} %get-tuple-element.143.dy_ref.dx_ref, bf16[1024,1024]{1,0:T(8,128)(2,1)S(1)} %copy-done.6, ...), custom_call_target="tpu_custom_call" | custom-call | flops 2684354560 | bytes 2621440 | tf_op jit(solution)/shard_map/weight_grad_low/pallas_call | solution.py:279
  328.5 4.8 add_convert_fusion.5
  334.7 3.9 add_convert_fusion.6
  340.9 24.3 %attention_backward_high.1 = (bf16[3,1024,512]{2,1,0:T(8,128)(2,1)S(1)}, f32[1,512]{1,0:T(1,128)S(1)}, f32[1,512]{1,0:T(1,128)S(1)}) custom-call(bf16[1024,3072]{1,0:T(8,128)(2,1)} %get-tuple-element.66.q_ref.k_ref.v_ref, bf16[1024,3072]{1,0:T(8,128)(2,1)} %get-tuple-element.66.q_ref.k_ref.v_ref, bf16[1024,3072]{1,0:T(8,128)(2,1)} %get-tuple-element.66.q_ref.k_ref.v_ref, ...), custom_call_target="tpu_custom_call" | custom-call | flops 2147483648 | bytes 8388608 | tf_op jit(solution)/shard_map/attention_backward_high/pallas_call | solution.py:596
  366.3 5.9 %weight_grad_high.1 = (bf16[16,3,32,512]{3,2,1,0:T(8,128)(2,1)S(1)}, bf16[16,3,32,512]{3,2,1,0:T(8,128)(2,1)}) custom-call(s32[5]{0:T(128)S(1)} %stack.65.own_ref, bf16[1024,1024]{1,0:T(8,128)(2,1)S(1)} %copy-done.7, bf16[1024,1024]{1,0:T(8,128)(2,1)S(1)} %copy-done.7, bf16[1024,1024]{1,0:T(8,128)(2,1)S(1)} %copy-done.7, ...), custom_call_target="tpu_custom_call" | custom-call | flops 1610612736 | bytes 1572864 | tf_op jit(solution)/shard_map/weight_grad_high/pallas_call | solution.py:279
  374.8 4.7 add_convert_fusion.3
  392.0 16.7 %project_back.1 = (f32[1024,1024]{1,0:T(8,128)}, f32[1,1024]{1,0:T(1,128)S(1)}, f32[1,1024]{1,0:T(1,128)S(1)}) custom-call(bf16[3,1024,512]{2,1,0:T(8,128)(2,1)S(1)} %copy-done.12, bf16[3,1024,512]{2,1,0:T(8,128)(2,1)} %copy-done.10, bf16[1024,3072]{1,0:T(8,128)(2,1)} %get-tuple-element.91.w_ref, bf16[1024,1024]{1,0:T(8,128)(2,1)S(1)} %bitcast.185, ...), custom_call_target="tpu_custom_call" | custom-call | flops 1610612736 | bytes 524288 | tf_op jit(solution)/shard_map/project_back/pallas_call | solution.py:218
  421.3 16.7 %collective-permute-done.22 = bf16[1,128,128]{2,1,0:T(8,128)(2,1)S(1)} collective-permute-done((bf16[1,128,128]{2,1,0:T(8,128)(2,1)S(1)}, bf16[1,128,128]{2,1,0:T(8,128)(2,1)S(1)}, u32[]{:S(2)}, u32[]{:S(2)}) %collective-permute-start.22) | collective-permute-done | bytes 32800 | tf_op jit(solution)/shard_map/ppermute | solution.py:641
  438.0 4.2 collective-permute-done.23
  443.9 3.5 collective-permute-done.24
  457.4 7.2 %collective-permute-done.32 = bf16[1,3,32,512]{3,2,1,0:T(8,128)(2,1)S(1)} collective-permute-done((bf16[1,3,32,512]{3,2,1,0:T(8,128)(2,1)S(1)}, bf16[1,3,32,512]{3,2,1,0:T(8,128)(2,1)S(1)}, u32[]{:S(2)}, u32[]{:S(2)}) %collective-permute-start.32) | collective-permute-done | bytes 98336 | tf_op jit(solution)/shard_map/ppermute | solution.py:641
  466.0 10.3 %collective-permute-done.40.refs_3_ = bf16[2,128,1024]{2,1,0:T(8,128)(2,1)S(1)} collective-permute-done((bf16[2,128,1024]{2,1,0:T(8,128)(2,1)S(1)}, bf16[2,128,1024]{2,1,0:T(8,128)(2,1)S(1)}, u32[]{:S(2)}, u32[]{:S(2)}) %collective-permute-start.40) | collective-permute-done | bytes 524320 | tf_op jit(solution)/shard_map/ppermute | solution.py:641
  483.3 6.2 %collective-permute-done.29 = bf16[1,5,32,512]{3,2,1,0:T(8,128)(2,1)S(1)} collective-permute-done((bf16[1,5,32,512]{3,2,1,0:T(8,128)(2,1)S(1)}, bf16[1,5,32,512]{3,2,1,0:T(8,128)(2,1)S(1)}, u32[]{:S(2)}, u32[]{:S(2)}) %collective-permute-start.29) | collective-permute-done | bytes 163872 | tf_op jit(solution)/shard_map/ppermute | solution.py:641
  493.8 5.0 collective-permute-done.34.refs_2_
  498.9 4.7 collective-permute-done.35.refs_3_
  (296 shorter events, 117.3 us)
Async XLA Ops:
  7.2 159.0 %all-gather.2.cloned.1.call-start = ((), (), s32[]{:S(2)}) async-start(), calls=%async_computation.1 | async-start | bytes 19464192 | tf_op jit(solution)/shard_map/all_gather | solution.py:754
  13.0 16.6 %collective-permute-start.5 = (bf16[1,32,1536]{2,1,0:T(8,128)(2,1)S(1)}, bf16[1,32,1536]{2,1,0:T(8,128)(2,1)S(1)}, u32[]{:S(2)}, u32[]{:S(2)}) collective-permute-start(bf16[1,32,1536]{2,1,0:T(8,128)(2,1)S(1)} %get-tuple-element.137), channel_id=1, source_target_pairs={{0,4},{1,5},{2,6},{3,7},{4,0},{5,1},{6,2},{7,3},{8,12},{9,13},{10,... | collective-permute-start | bytes 294920 | tf_op jit(solution)/shard_map/ppermute | solution.py:641
  17.1 14.7 %collective-permute-start = (bf16[1,32,1536]{2,1,0:T(8,128)(2,1)S(1)}, bf16[1,32,1536]{2,1,0:T(8,128)(2,1)S(1)}, u32[]{:S(2)}, u32[]{:S(2)}) collective-permute-start(bf16[1,32,1536]{2,1,0:T(8,128)(2,1)S(1)} %get-tuple-element.172), channel_id=1, source_target_pairs={{0,4},{1,5},{2,6},{3,7},{4,0},{5,1},{6,2},{7,3},{8,12},{9,13},{10,... | collective-permute-start | bytes 294920 | tf_op jit(solution)/shard_map/ppermute | solution.py:641
  19.8 35.3 %all-to-all-start = ((f32[8,1,7936]{2,1,0:T(1,128)}), f32[8,1,7936]{2,1,0:T(1,128)S(1)}, u32[]{:S(2)}, u32[]{:S(2)}) async-start(f32[8,1,7936]{2,1,0:T(1,128)} %copy.29), calls=%async_computation | async-start | bytes 507904 | tf_op jit(solution)/shard_map/all_to_all | solution.py:854
  29.7 17.8 %collective-permute-start.6 = (bf16[2,32,1536]{2,1,0:T(8,128)(2,1)S(1)}, bf16[2,32,1536]{2,1,0:T(8,128)(2,1)S(1)}, u32[]{:S(2)}, u32[]{:S(2)}) collective-permute-start(bf16[2,32,1536]{2,1,0:T(8,128)(2,1)S(1)} %pad_maximum_fusion.9), channel_id=1, source_target_pairs={{0,2},{1,3},{2,0},{3,1},{4,6},{5,7},{6,4},{7,5},{8,10},{9,11},{10,... | collective-permute-start | bytes 589832 | tf_op jit(solution)/shard_map/ppermute | solution.py:641
  31.8 19.5 %collective-permute-start.1 = (bf16[2,32,1536]{2,1,0:T(8,128)(2,1)S(1)}, bf16[2,32,1536]{2,1,0:T(8,128)(2,1)S(1)}, u32[]{:S(2)}, u32[]{:S(2)}) collective-permute-start(bf16[2,32,1536]{2,1,0:T(8,128)(2,1)S(1)} %pad_maximum_fusion.8), channel_id=1, source_target_pairs={{0,2},{1,3},{2,0},{3,1},{4,6},{5,7},{6,4},{7,5},{8,10},{9,11},{10,... | collective-permute-start | bytes 589832 | tf_op jit(solution)/shard_map/ppermute | solution.py:641
  48.3 14.5 %collective-permute-start.7 = (bf16[4,32,1536]{2,1,0:T(8,128)(2,1)}, bf16[4,32,1536]{2,1,0:T(8,128)(2,1)S(1)}, u32[]{:S(2)}, u32[]{:S(2)}) collective-permute-start(bf16[4,32,1536]{2,1,0:T(8,128)(2,1)} %pad_maximum_fusion.5), channel_id=1, source_target_pairs={{0,16},{1,17},{2,18},{3,19},{4,20},{5,21},{6,22},{7,23},{8,24},{9,... | collective-permute-start | bytes 1179656 | tf_op jit(solution)/shard_map/ppermute | solution.py:641
  52.1 19.7 %collective-permute-start.2 = (bf16[4,32,1536]{2,1,0:T(8,128)(2,1)}, bf16[4,32,1536]{2,1,0:T(8,128)(2,1)S(1)}, u32[]{:S(2)}, u32[]{:S(2)}) collective-permute-start(bf16[4,32,1536]{2,1,0:T(8,128)(2,1)} %pad_maximum_fusion.4), channel_id=1, source_target_pairs={{0,1},{1,0},{2,3},{3,2},{4,5},{5,4},{6,7},{7,6},{8,9},{9,8},{10,11... | collective-permute-start | bytes 1179656 | tf_op jit(solution)/shard_map/ppermute | solution.py:641
  62.9 33.8 %collective-permute-start.8 = (bf16[8,32,1536]{2,1,0:T(8,128)(2,1)S(1)}, bf16[8,32,1536]{2,1,0:T(8,128)(2,1)S(1)}, u32[]{:S(2)}, u32[]{:S(2)}) collective-permute-start(bf16[8,32,1536]{2,1,0:T(8,128)(2,1)S(1)} %pad_maximum_fusion.1), channel_id=1, source_target_pairs={{0,1},{1,0},{2,3},{3,2},{4,5},{5,4},{6,7},{7,6},{8,9},{9,8},{10,11... | collective-permute-start | bytes 2359304 | tf_op jit(solution)/shard_map/ppermute | solution.py:641
  71.9 25.8 %collective-permute-start.3 = (bf16[8,32,1536]{2,1,0:T(8,128)(2,1)S(1)}, bf16[8,32,1536]{2,1,0:T(8,128)(2,1)S(1)}, u32[]{:S(2)}, u32[]{:S(2)}) collective-permute-start(bf16[8,32,1536]{2,1,0:T(8,128)(2,1)S(1)} %pad_maximum_fusion), channel_id=1, source_target_pairs={{0,16},{1,17},{2,18},{3,19},{4,20},{5,21},{6,22},{7,23},{8,24},{9,... | collective-permute-start | bytes 2359304 | tf_op jit(solution)/shard_map/ppermute | solution.py:641
  251.9 13.1 %collective-permute-start.11 = (bf16[16,128,1024]{2,1,0:T(8,128)(2,1)}, bf16[16,128,1024]{2,1,0:T(8,128)(2,1)S(1)}, u32[]{:S(2)}, u32[]{:S(2)}) collective-permute-start(bf16[16,128,1024]{2,1,0:T(8,128)(2,1)} %bitcast.224), channel_id=1, source_target_pairs={{0,8},{1,9},{2,10},{3,11},{4,12},{5,13},{6,14},{7,15},{8,0},{9,1},... | collective-permute-start | bytes 12582920 | tf_op jit(solution)/shard_map/ppermute | solution.py:641
  273.7 54.6 %collective-permute-start.13 = (bf16[8,128,1024]{2,1,0:T(8,128)(2,1)}, bf16[8,128,1024]{2,1,0:T(8,128)(2,1)}, u32[]{:S(2)}, u32[]{:S(2)}) collective-permute-start(bf16[8,128,1024]{2,1,0:T(8,128)(2,1)} %get-tuple-element.154), channel_id=1, source_target_pairs={{0,1},{1,0},{2,3},{3,2},{4,5},{5,4},{6,7},{7,6},{8,9},{9,8},{10,11... | collective-permute-start | bytes 6291464 | tf_op jit(solution)/shard_map/ppermute | solution.py:641
  278.7 49.7 %collective-permute-start.12 = (bf16[8,4,32,1024]{3,2,1,0:T(8,128)(2,1)}, bf16[8,4,32,1024]{3,2,1,0:T(8,128)(2,1)}, u32[]{:S(2)}, u32[]{:S(2)}) collective-permute-start(bf16[8,4,32,1024]{3,2,1,0:T(8,128)(2,1)} %get-tuple-element.141), channel_id=1, source_target_pairs={{0,16},{1,17},{2,18},{3,19},{4,20},{5,21},{6,22},{7,23},{8,24},{9,... | collective-permute-start | bytes 6291464 | tf_op jit(solution)/shard_map/ppermute | solution.py:641
  328.4 36.9 %collective-permute-start.16 = (bf16[16,5,32,512]{3,2,1,0:T(8,128)(2,1)}, bf16[16,5,32,512]{3,2,1,0:T(8,128)(2,1)}, u32[]{:S(2)}, u32[]{:S(2)}) collective-permute-start(bf16[16,5,32,512]{3,2,1,0:T(8,128)(2,1)} %get-tuple-element.87), channel_id=1, source_target_pairs={{0,8},{1,9},{2,10},{3,11},{4,12},{5,13},{6,14},{7,15},{8,0},{9,1},... | collective-permute-start | bytes 7864328 | tf_op jit(solution)/shard_map/ppermute | solution.py:641
  333.3 31.9 %collective-permute-start.15 = (bf16[4,128,1024]{2,1,0:T(8,128)(2,1)}, bf16[4,128,1024]{2,1,0:T(8,128)(2,1)}, u32[]{:S(2)}, u32[]{:S(2)}) collective-permute-start(bf16[4,128,1024]{2,1,0:T(8,128)(2,1)} %get-tuple-element.150), channel_id=1, source_target_pairs={{0,16},{1,17},{2,18},{3,19},{4,20},{5,21},{6,22},{7,23},{8,24},{9,... | collective-permute-start | bytes 3145736 | tf_op jit(solution)/shard_map/ppermute | solution.py:641
  338.7 26.6 %collective-permute-start.14 = (bf16[4,4,32,1024]{3,2,1,0:T(8,128)(2,1)}, bf16[4,4,32,1024]{3,2,1,0:T(8,128)(2,1)S(1)}, u32[]{:S(2)}, u32[]{:S(2)}) collective-permute-start(bf16[4,4,32,1024]{3,2,1,0:T(8,128)(2,1)} %get-tuple-element.152), channel_id=1, source_target_pairs={{0,1},{1,0},{2,3},{3,2},{4,5},{5,4},{6,7},{7,6},{8,9},{9,8},{10,11... | collective-permute-start | bytes 3145736 | tf_op jit(solution)/shard_map/ppermute | solution.py:641
  372.2 11.8 %collective-permute-start.17 = (bf16[16,3,32,512]{3,2,1,0:T(8,128)(2,1)}, bf16[16,3,32,512]{3,2,1,0:T(8,128)(2,1)}, u32[]{:S(2)}, u32[]{:S(2)}) collective-permute-start(bf16[16,3,32,512]{3,2,1,0:T(8,128)(2,1)} %get-tuple-element.89), channel_id=1, source_target_pairs={{0,8},{1,9},{2,10},{3,11},{4,12},{5,13},{6,14},{7,15},{8,0},{9,1},... | collective-permute-start | bytes 4718600 | tf_op jit(solution)/shard_map/ppermute | solution.py:641
  379.5 31.5 %collective-permute-start.20 = (bf16[8,5,32,512]{3,2,1,0:T(8,128)(2,1)}, bf16[8,5,32,512]{3,2,1,0:T(8,128)(2,1)}, u32[]{:S(2)}, u32[]{:S(2)}) collective-permute-start(bf16[8,5,32,512]{3,2,1,0:T(8,128)(2,1)} %get-tuple-element.146), channel_id=1, source_target_pairs={{0,16},{1,17},{2,18},{3,19},{4,20},{5,21},{6,22},{7,23},{8,24},{9,... | collective-permute-start | bytes 3932168 | tf_op jit(solution)/shard_map/ppermute | solution.py:641
  383.7 24.9 %collective-permute-start.19 = (bf16[2,128,1024]{2,1,0:T(8,128)(2,1)}, bf16[2,128,1024]{2,1,0:T(8,128)(2,1)}, u32[]{:S(2)}, u32[]{:S(2)}) collective-permute-start(bf16[2,128,1024]{2,1,0:T(8,128)(2,1)} %get-tuple-element.164), channel_id=1, source_target_pairs={{0,2},{1,3},{2,0},{3,1},{4,6},{5,7},{6,4},{7,5},{8,10},{9,11},{10,... | collective-permute-start | bytes 1572872 | tf_op jit(solution)/shard_map/ppermute | solution.py:641
  387.3 23.7 %collective-permute-start.21 = (bf16[8,3,32,512]{3,2,1,0:T(8,128)(2,1)}, bf16[8,3,32,512]{3,2,1,0:T(8,128)(2,1)S(1)}, u32[]{:S(2)}, u32[]{:S(2)}) collective-permute-start(bf16[8,3,32,512]{3,2,1,0:T(8,128)(2,1)} %get-tuple-element.158), channel_id=1, source_target_pairs={{0,1},{1,0},{2,3},{3,2},{4,5},{5,4},{6,7},{7,6},{8,9},{9,8},{10,11... | collective-permute-start | bytes 2359304 | tf_op jit(solution)/shard_map/ppermute | solution.py:641
  389.0 20.2 %collective-permute-start.18 = (bf16[2,4,32,1024]{3,2,1,0:T(8,128)(2,1)}, bf16[2,4,32,1024]{3,2,1,0:T(8,128)(2,1)S(1)}, u32[]{:S(2)}, u32[]{:S(2)}) collective-permute-start(bf16[2,4,32,1024]{3,2,1,0:T(8,128)(2,1)} %get-tuple-element.162), channel_id=1, source_target_pairs={{0,2},{1,3},{2,0},{3,1},{4,6},{5,7},{6,4},{7,5},{8,10},{9,11},{10,... | collective-permute-start | bytes 1572872 | tf_op jit(solution)/shard_map/ppermute | solution.py:641
  411.1 38.5 %collective-permute-start.36 = (bf16[1,4,32,1024]{3,2,1,0:T(8,128)(2,1)S(1)}, bf16[1,4,32,1024]{3,2,1,0:T(8,128)(2,1)S(1)}, u32[]{:S(2)}, u32[]{:S(2)}) collective-permute-start(bf16[1,4,32,1024]{3,2,1,0:T(8,128)(2,1)S(1)} %add_convert_fusion.25), channel_id=1, source_target_pairs={{0,4},{1,5},{2,6},{3,7},{4,0},{5,1},{6,2},{7,3},{8,12},{9,13},{10,... | collective-permute-start | bytes 786440 | tf_op jit(solution)/shard_map/ppermute | solution.py:641
  413.7 36.1 %collective-permute-start.37 = (bf16[1,128,1024]{2,1,0:T(8,128)(2,1)S(1)}, bf16[1,128,1024]{2,1,0:T(8,128)(2,1)S(1)}, u32[]{:S(2)}, u32[]{:S(2)}) collective-permute-start(bf16[1,128,1024]{2,1,0:T(8,128)(2,1)S(1)} %add_convert_fusion.22), channel_id=1, source_target_pairs={{0,4},{1,5},{2,6},{3,7},{4,0},{5,1},{6,2},{7,3},{8,12},{9,13},{10,... | collective-permute-start | bytes 786440 | tf_op jit(solution)/shard_map/ppermute | solution.py:641
  417.0 39.8 %collective-permute-start.27 = (bf16[4,5,32,512]{3,2,1,0:T(8,128)(2,1)S(1)}, bf16[4,5,32,512]{3,2,1,0:T(8,128)(2,1)S(1)}, u32[]{:S(2)}, u32[]{:S(2)}) collective-permute-start(bf16[4,5,32,512]{3,2,1,0:T(8,128)(2,1)S(1)} %get-tuple-element.160), channel_id=1, source_target_pairs={{0,1},{1,0},{2,3},{3,2},{4,5},{5,4},{6,7},{7,6},{8,9},{9,8},{10,11... | collective-permute-start | bytes 1966088 | tf_op jit(solution)/shard_map/ppermute | solution.py:641
  418.8 32.1 %collective-permute-start.30 = (bf16[4,3,32,512]{3,2,1,0:T(8,128)(2,1)S(1)}, bf16[4,3,32,512]{3,2,1,0:T(8,128)(2,1)S(1)}, u32[]{:S(2)}, u32[]{:S(2)}) collective-permute-start(bf16[4,3,32,512]{3,2,1,0:T(8,128)(2,1)S(1)} %get-tuple-element.166), channel_id=1, source_target_pairs={{0,16},{1,17},{2,18},{3,19},{4,20},{5,21},{6,22},{7,23},{8,24},{9,... | collective-permute-start | bytes 1179656 | tf_op jit(solution)/shard_map/ppermute | solution.py:641
  419.7 18.3 %collective-permute-start.22 = (bf16[1,128,128]{2,1,0:T(8,128)(2,1)S(1)}, bf16[1,128,128]{2,1,0:T(8,128)(2,1)S(1)}, u32[]{:S(2)}, u32[]{:S(2)}) collective-permute-start(bf16[1,128,128]{2,1,0:T(8,128)(2,1)S(1)} %constant_dynamic-update-slice_fusion.10), channel_id=1, source_target_pairs={{0,4},{1,5},{2,6},{3,7},{4,0},{5,1},{6,2},{7,3},{8,12},{9,13},{10,... | collective-permute-start | bytes 98312 | tf_op jit(solution)/shard_map/ppermute | solution.py:641
  451.2 14.0 %collective-permute-start.38 = (bf16[2,128,1024]{2,1,0:T(8,128)(2,1)S(1)}, bf16[2,128,1024]{2,1,0:T(8,128)(2,1)S(1)}, u32[]{:S(2)}, u32[]{:S(2)}) collective-permute-start(bf16[2,128,1024]{2,1,0:T(8,128)(2,1)S(1)} %pad_maximum_fusion.3.refs_0_), channel_id=1, source_target_pairs={{0,8},{1,9},{2,10},{3,11},{4,12},{5,13},{6,14},{7,15},{8,0},{9,1},... | collective-permute-start | bytes 1572872 | tf_op jit(solution)/shard_map/ppermute | solution.py:641
  451.2 14.8 %collective-permute-start.39 = (bf16[2,128,1024]{2,1,0:T(8,128)(2,1)S(1)}, bf16[2,128,1024]{2,1,0:T(8,128)(2,1)S(1)}, u32[]{:S(2)}, u32[]{:S(2)}) collective-permute-start(bf16[2,128,1024]{2,1,0:T(8,128)(2,1)S(1)} %pad_maximum_fusion.3.refs_0_), channel_id=1, source_target_pairs={{0,16},{1,17},{2,18},{3,19},{4,20},{5,21},{6,22},{7,23},{8,24},{9,... | collective-permute-start | bytes 1572872 | tf_op jit(solution)/shard_map/ppermute | solution.py:641
  453.8 22.6 %collective-permute-start.40 = (bf16[2,128,1024]{2,1,0:T(8,128)(2,1)S(1)}, bf16[2,128,1024]{2,1,0:T(8,128)(2,1)S(1)}, u32[]{:S(2)}, u32[]{:S(2)}) collective-permute-start(bf16[2,128,1024]{2,1,0:T(8,128)(2,1)S(1)} %pad_maximum_fusion.3.refs_0_), channel_id=1, source_target_pairs={{0,24},{1,25},{2,26},{3,27},{4,28},{5,29},{6,30},{7,31},{8,16},{9,... | collective-permute-start | bytes 1572872 | tf_op jit(solution)/shard_map/ppermute | solution.py:641
  456.7 24.3 %collective-permute-start.26 = (bf16[16,128,128]{2,1,0:T(8,128)(2,1)S(1)}, bf16[16,128,128]{2,1,0:T(8,128)(2,1)S(1)}, u32[]{:S(2)}, u32[]{:S(2)}) collective-permute-start(bf16[16,128,128]{2,1,0:T(8,128)(2,1)S(1)} %get-tuple-element.173), channel_id=1, source_target_pairs={{0,8},{1,9},{2,10},{3,11},{4,12},{5,13},{6,14},{7,15},{8,0},{9,1},... | collective-permute-start | bytes 1572872 | tf_op jit(solution)/shard_map/ppermute | solution.py:641
  464.5 14.1 %collective-permute-start.28 = (bf16[2,5,32,512]{3,2,1,0:T(8,128)(2,1)S(1)}, bf16[2,5,32,512]{3,2,1,0:T(8,128)(2,1)S(1)}, u32[]{:S(2)}, u32[]{:S(2)}) collective-permute-start(bf16[2,5,32,512]{3,2,1,0:T(8,128)(2,1)S(1)} %get-tuple-element.168), channel_id=1, source_target_pairs={{0,2},{1,3},{2,0},{3,1},{4,6},{5,7},{6,4},{7,5},{8,10},{9,11},{10,... | collective-permute-start | bytes 983048 | tf_op jit(solution)/shard_map/ppermute | solution.py:641
  490.7 12.9 %collective-permute-start.35 = (bf16[8,32,512]{2,1,0:T(8,128)(2,1)S(1)}, bf16[8,32,512]{2,1,0:T(8,128)(2,1)S(1)}, u32[]{:S(2)}, u32[]{:S(2)}) collective-permute-start(bf16[8,32,512]{2,1,0:T(8,128)(2,1)S(1)} %pad_maximum_fusion.7.refs_0_), channel_id=1, source_target_pairs={{0,24},{1,25},{2,26},{3,27},{4,28},{5,29},{6,30},{7,31},{8,16},{9,... | collective-permute-start | bytes 786440 | tf_op jit(solution)/shard_map/ppermute | solution.py:641
  (54 other events, 436.6 us)
Sparse Core Ops, SparseCore 0:
  11.5 154.6 all-gather.1

commit v7 on v6

--- a/solution.py
+++ b/solution.py
@@ -332,7 +332,8 @@
 
 
 def place_reps(kernel, rep_id, own, shapes, name):
-    parts = [own] + [exchange(own, mask, 0) for mask in (1, 2, 3)]
+    across = exchange(own, *MASKS["y"])
+    parts = [own, exchange(own, *MASKS["core"]), across, exchange(across, *MASKS["core"])]
     return pl.pallas_call(
         kernel,
         grid_spec=pltpu.PrefetchScalarGridSpec(num_scalar_prefetch=1, grid=()),
@@ -540,9 +541,8 @@
     )(projected, projected, projected)
 
 
-def attention_backward_kernel(
-    q_ref, k_ref, v_ref, g_ref, o_ref, lse_ref, out_ref, qb_ref, vb_ref, probs, d_scores
-):
+def attention_backward_kernel(q_ref, k_ref, v_ref, g_ref, o_ref, lse_ref, *refs):
+    out_ref, qb_ref, vb_ref, probs, d_scores = refs[-5:]
     length = q_ref.shape[0]
     root = HEAD_DIM ** (-0.5)
     scaled = q_ref[...] * jnp.bfloat16(root)
@@ -587,25 +587,33 @@
     vb_ref[...] = jnp.sum(d_value.astype(jnp.float32), axis=0, keepdims=True)
 
 
-def attention_backward(projected, d_attended, attended_t, lse, first, count, name):
+def attention_backward(operands, first, count, total, at, into, name):
+    projected, d_attended, attended_t, lse = operands
     length = projected.shape[0]
-    width = count * PAIR
     pairs = HEADS // 2
     row = pl.BlockSpec((1, PAIR), lambda i: (0, i))
-    line = jax.ShapeDtypeStruct((1, width), jnp.float32)
+    line = jax.ShapeDtypeStruct((1, count * PAIR), jnp.float32)
+    in_specs = [
+        pl.BlockSpec((length, PAIR), lambda i: (0, first + i)),
+        pl.BlockSpec((length, PAIR), lambda i: (0, pairs + first + i)),
+        pl.BlockSpec((length, PAIR), lambda i: (0, 2 * pairs + first + i)),
+        pl.BlockSpec((length, PAIR), lambda i: (0, first + i)),
+        pl.BlockSpec((PAIR, length), lambda i: (first + i, 0)),
+        pl.BlockSpec((1, 2, length), lambda i: (first + i, 0, 0)),
+    ]
+    arrays = [projected, projected, projected, d_attended, attended_t, lse]
+    aliases = {}
+    if into is not None:
+        in_specs.append(pl.BlockSpec(memory_space=pl.ANY))
+        aliases = {len(arrays): 0}
+        arrays.append(into)
     return pl.pallas_call(
         attention_backward_kernel,
         grid=(count,),
-        in_specs=[
-            pl.BlockSpec((length, PAIR), lambda i: (0, first + i)),
-            pl.BlockSpec((length, PAIR), lambda i: (0, pairs + first + i)),
-            pl.BlockSpec((length, PAIR), lambda i: (0, 2 * pairs + first + i)),
-            pl.BlockSpec((length, PAIR), lambda i: (0, first + i)),
-            pl.BlockSpec((PAIR, length), lambda i: (first + i, 0)),
-            pl.BlockSpec((1, 2, length), lambda i: (first + i, 0, 0)),
-        ],
-        out_specs=[pl.BlockSpec((3, length, PAIR), lambda i: (0, 0, i)), row, row],
-        out_shape=[jax.ShapeDtypeStruct((3, length, width), jnp.bfloat16), line, line],
+        in_specs=in_specs,
+        out_specs=[pl.BlockSpec((3, length, PAIR), lambda i: (0, 0, at + i)), row, row],
+        out_shape=[jax.ShapeDtypeStruct((3, length, total * PAIR), jnp.bfloat16), line, line],
+        input_output_aliases=aliases,
         scratch_shapes=[
             pltpu.VMEM((2, length, CHUNK), jnp.bfloat16),
             pltpu.VMEM((2, length, CHUNK), jnp.bfloat16),
@@ -613,7 +621,7 @@
         compiler_params=kernel_params(48),
         cost_estimate=cost(count * 2**29, count * 2 * 2**20, count * 2**21),
         name=name,
-    )(projected, projected, projected, d_attended, attended_t, lse)
+    )(*arrays)
 
 
 def normalize(values):
@@ -641,13 +649,15 @@
     return lax.ppermute(value, ("rep", "fsdp"), pairs)
 
 
-def gather_relative(row):
+def gather_relative(row, after_first):
     reps, shards = lax.axis_size("rep"), lax.axis_size("fsdp")
     masks = [(0, 1 << bit) for bit in reversed(range(shards.bit_length() - 1))]
     masks += [(1 << bit, 0) for bit in reversed(range(reps.bit_length() - 1))]
     rows = row[None]
-    for pair in masks:
+    for number, pair in enumerate(masks):
         rows = jnp.concatenate([rows, exchange(rows, *pair)], axis=0)
+        if number == 0:
+            rows = after_first(rows)
     return rows
 
 
@@ -799,28 +809,22 @@
         out_at = (packed, 8)
         w_expand, w_shrink = packed, packed
         y_id = rep_id >> 1
-        own, own_high = [
-            jnp.stack(
-                [
-                    rep_id & 1,
-                    place_in(order, shard_id, y_id),
-                    shard_id & 1,
-                    y_id,
-                    (shard_id & 2) | (shard_id >> 2),
-                ]
-            ).astype(jnp.int32)
-            for order in ORDERS
-        ]
-        tables = [
-            tuple(place_in(order, slot >> 1, slot & 1) for slot in range(2 * shards))
-            for order in ORDERS
-        ]
+        own = jnp.stack(
+            [
+                rep_id & 1,
+                place_in(ORDERS[0], shard_id, y_id),
+                shard_id & 1,
+                y_id,
+                (shard_id & 2) | (shard_id >> 2),
+            ]
+        ).astype(jnp.int32)
+        table = tuple(place_in(ORDERS[0], slot >> 1, slot & 1) for slot in range(2 * shards))
         piece = quarter
     else:
         w_proj, out_at = gather_rows(projector), (gather_rows(outweight), 0)
         w_expand, w_shrink = gather_rows(expander), gather_rows(shrinker)
-        own = own_high = jnp.zeros((5,), jnp.int32)
-        tables = [(0,), (0,)]
+        own = jnp.zeros((5,), jnp.int32)
+        table = (0,)
         piece = feature // 2
 
     def depth_sum(halves, order):
@@ -881,7 +885,7 @@
     d_branch_m = (gate_m[:, None, :] * grad_out).astype(jnp.bfloat16).reshape(token_count, feature)
     g_shrinkbias = jnp.sum(d_branch_m, axis=0, dtype=jnp.float32)
     branch_m, d_norm_m, keep_e, send_e, keep_s, send_s, g_expandbias = feed_forward(
-        own, norm_m, d_branch_m, w_expand, b_expand, w_shrink, tables[0]
+        own, norm_m, d_branch_m, w_expand, b_expand, w_shrink, table
     )
     sum_e = depth_sum((keep_e, send_e), ORDERS[0])
     sum_s = unit_sum((keep_s, send_s), ORDERS[1])
@@ -899,26 +903,52 @@
     g_outbiases = jnp.sum(d_branch_a, axis=0, dtype=jnp.float32)
     d_attended = backward_dot(d_branch_a, *out_at, jnp.bfloat16, "attention_out_back")
     half_pairs = HEADS // 4
+    part_pairs = half_pairs // 2
     d_low, q_low, v_low = attention_backward(
-        projected, d_attended, attended_t, log_totals, 0, half_pairs, "attention_backward_low"
+        (projected, d_attended, attended_t, log_totals),
+        0,
+        half_pairs,
+        half_pairs,
+        0,
+        None,
+        "attention_backward_low",
     )
     halves_low = weight_grad(
-        own, attended, d_branch_a, norm_a, d_low, tables[0], piece, "weight_grad_low"
+        own, attended, d_branch_a, norm_a, d_low, table, piece, "weight_grad_low"
     )
     d_attended, halves_low = hold((d_attended, halves_low), sum_e, sum_s)
     sum_low = depth_sum(halves_low, ORDERS[0])
     for total in (sum_e, sum_s):
         total.step()
-    d_high, q_high, v_high = attention_backward(
-        projected, d_attended, attended_t, log_totals, half_pairs, half_pairs, "attention_backward_high"
+    d_high, *sums_mid = attention_backward(
+        (projected, d_attended, attended_t, log_totals),
+        half_pairs,
+        part_pairs,
+        half_pairs,
+        0,
+        None,
+        "attention_backward_mid",
     )
     d_high = hold(d_high, sum_e, sum_s, sum_low)
     for total in (sum_e, sum_s, sum_low):
         total.step()
+    d_high, *sums_high = attention_backward(
+        (projected, d_attended, attended_t, log_totals),
+        half_pairs + part_pairs,
+        part_pairs,
+        half_pairs,
+        part_pairs,
+        d_high,
+        "attention_backward_high",
+    )
+    q_high, v_high = [jnp.concatenate(parts, axis=1) for parts in zip(sums_mid, sums_high)]
     halves_high = weight_grad(
-        own_high, None, None, norm_a, d_high, tables[1], piece, "weight_grad_high"
-    )
-    sum_high = depth_sum(halves_high, ORDERS[1])
+        own, None, None, norm_a, d_high, table, piece, "weight_grad_high"
+    )
+    d_high, halves_high = hold((d_high, halves_high), sum_e, sum_s, sum_low)
+    sum_high = depth_sum(halves_high, ORDERS[0])
+    for total in (sum_e, sum_s, sum_low):
+        total.step()
     d_high = hold(d_high, sum_high)
     sum_high.step()
     latents_grad, d_shift_a, d_scale_a = project_back(
@@ -930,11 +960,6 @@
         d_middle.reshape(token_count, feature),
     )
     latents_grad = latents_grad.reshape(seqs_dev, seq_len, feature)
-    latents_grad, d_shift_a, d_scale_a = hold(
-        (latents_grad, d_shift_a, d_scale_a), sum_e, sum_s, sum_low, sum_high
-    )
-    for total in (sum_e, sum_s, sum_low, sum_high):
-        total.step()
     g_querybias = jnp.concatenate([q_low, q_high], axis=1)
     g_valuebias = jnp.concatenate([v_low, v_high], axis=1)
     small = jnp.concatenate(
@@ -959,7 +984,14 @@
     ).astype(jnp.bfloat16)
     devices = reps * shards
     size = seqs_dev * feature
-    gathered = gather_relative(small)
+
+    def advance(rows):
+        rows = hold(rows, sum_e, sum_s, sum_low, sum_high)
+        for total in (sum_low, sum_high):
+            total.step()
+        return rows
+
+    gathered = gather_relative(small, advance)
     if halving:
         done = jnp.stack([total.finish().reshape(-1, feature) for total in (sum_e, sum_s)])
         g_expander, g_shrinker = place_reps(

time: 516 us -> 506 us (0.981)
  waiting for transfers between devices: 139 us -> 109 us
  other arithmetic: 67 us -> 80.6 us
    ppermute x41, waiting for transfers between devices: 122 us -> 93.4 us  [exchange(): return lax.ppermute(value, ('rep', 'fsdp'), pairs)]
    unnamed x121 -> x128, local copies, waits for them, and re-layouts: 19.9 us -> 24.3 us
    pallas_call x2 -> x3, Pallas kernels: 49.3 us -> 50.1 us  [attention_backward(): pl.pallas_call(attention_backward_kernel, grid=(count,), in_specs=in_spec...]
  transfers between devices with their start and end apart: 43 -> 43, of which waited for: 20 -> 19; matrix products, arithmetic and copies ran while one was open for 15% -> 17% of each run, Pallas kernels for 25% -> 26%
where the time goes in v7:
time: 506 us; the launch traced here: 502 us
  Pallas kernels  213 us (42%)
  waiting for transfers between devices  109 us (22%)
  other arithmetic  80.6 us (16%)
  starting transfers between devices  45.3 us (9%)
  local copies, waits for them, and re-layouts  35.2 us (7%)
  between operations  15.2 us (3%)
    ppermute x41, waiting for transfers between devices, exchange(): return lax.ppermute(value, ('rep', 'fsdp'), pairs)  93.4 us
    pallas_call x1, Pallas kernels, feed_forward(): pl.pallas_call(partial(feed_forward_kernel, table), grid_spec=pltpu.Prefe...  74.7 us
    pallas_call x3, Pallas kernels, attention_backward(): pl.pallas_call(attention_backward_kernel, grid=(count,), in_specs=in_spec...  50.1 us
    convert_element_type x18, other arithmetic, added(): (stay.astype(jnp.float32) + arrived.astype(jnp.float32)).astype(jnp.bfloa...  38.9 us
    ppermute x41, starting transfers between devices, exchange(): return lax.ppermute(value, ('rep', 'fsdp'), pairs)  38.6 us
    pallas_call x1, Pallas kernels, attention_forward(): pl.pallas_call(attention_forward_kernel, grid=(pairs,), in_specs=[pl.Bloc...  30.1 us
    unnamed x128, local copies, waits for them, and re-layouts  24.3 us
    pallas_call x1, Pallas kernels, project_back(): pl.pallas_call(project_back_kernel, grid=(2 * groups,), in_specs=[block,...  16.6 us
  transfers between devices with their start and end apart: 43, of which 19 were waited for; matrix products, arithmetic and copies ran while one was open for 17% of the time, Pallas kernels for 26%

profile of v7, /device:TPU:0, one launch (start us, length us, event | category | flops | bytes accessed | tf_op | source)
XLA Modules:
  0.0 502.1 jit_solution(15690172042529931687)
XLA Ops:
  13.0 4.0 collective-permute-start.5
  23.5 6.7 %all-to-all-start = ((f32[8,1,7936]{2,1,0:T(1,128)}), f32[8,1,7936]{2,1,0:T(1,128)}, u32[]{:S(2)}, u32[]{:S(2)}) async-start(f32[8,1,7936]{2,1,0:T(1,128)} %copy.30), calls=%async_computation | async-start | bytes 507904 | tf_op jit(solution)/shard_map/all_to_all | solution.py:858
  40.3 7.4 %collective-permute-done.6 = bf16[2,32,1536]{2,1,0:T(8,128)(2,1)S(1)} collective-permute-done((bf16[2,32,1536]{2,1,0:T(8,128)(2,1)S(1)}, bf16[2,32,1536]{2,1,0:T(8,128)(2,1)S(1)}, u32[]{:S(2)}, u32[]{:S(2)}) %collective-permute-start.6) | collective-permute-done | bytes 196640 | tf_op jit(solution)/shard_map/ppermute | solution.py:649
  57.1 10.3 %collective-permute-done.7 = bf16[4,32,1536]{2,1,0:T(8,128)(2,1)} collective-permute-done((bf16[4,32,1536]{2,1,0:T(8,128)(2,1)}, bf16[4,32,1536]{2,1,0:T(8,128)(2,1)}, u32[]{:S(2)}, u32[]{:S(2)}) %collective-permute-start.7) | collective-permute-done | bytes 393248 | tf_op jit(solution)/shard_map/ppermute | solution.py:649
  69.9 4.1 collective-permute-done.2
  79.4 17.4 %collective-permute-done.8 = bf16[8,32,1536]{2,1,0:T(8,128)(2,1)S(1)} collective-permute-done((bf16[8,32,1536]{2,1,0:T(8,128)(2,1)S(1)}, bf16[8,32,1536]{2,1,0:T(8,128)(2,1)S(1)}, u32[]{:S(2)}, u32[]{:S(2)}) %collective-permute-start.8) | collective-permute-done | bytes 786464 | tf_op jit(solution)/shard_map/ppermute | solution.py:649
  99.2 3.6 fusion.16.grad_ref
  103.7 12.3 %project.1 = (bf16[1024,3072]{1,0:T(8,128)(2,1)}, bf16[1024,3072]{1,0:T(8,128)(2,1)}) custom-call(s32[1]{0:T(128)} %bitcast.7.own_ref, bf16[1024,1024]{1,0:T(8,128)(2,1)S(1)} %fusion.14.x_ref.y_ref.dx_ref, f32[1,3072]{1,0:T(1,128)S(1)} %pad_maximum_fusion.12.b_ref, bf16[16,32,1536]{2,1,0:T(8,128)(2,1)S(1)} %constant_dynamic-update-slice_fusion.refs_0_, ...), custom_call_target="tpu_custom_call" | custom-call | flops 3221225472 | bytes 3145728 | tf_op jit(solution)/shard_map/project/pallas_call | solution.py:106
  116.0 30.1 %attention_forward.1 = (bf16[1024,1024]{1,0:T(8,128)(2,1)S(1)}, f32[1024,1024]{1,0:T(8,128)}, f32[8,2,1024]{2,1,0:T(2,128)S(1)}) custom-call(bf16[1024,3072]{1,0:T(8,128)(2,1)} %get-tuple-element.73.q_ref.k_ref.v_ref, bf16[1024,3072]{1,0:T(8,128)(2,1)} %get-tuple-element.73.q_ref.k_ref.v_ref, bf16[1024,3072]{1,0:T(8,128)(2,1)} %get-tuple-element.73.q_ref.k_ref.v_ref), custom_call_target="tpu_custom_call" | custom-call | flops 4294967296 | bytes 8388608 | tf_op jit(solution)/shard_map/attention_forward/pallas_call | solution.py:520
  147.5 15.7 %all-gather.2.cloned.1.call-done = bf16[9216,1024]{1,0:T(8,128)(2,1)} async-done(((bf16[288,1024]{1,0:T(8,128)(2,1)}), bf16[9216,1024]{1,0:T(8,128)(2,1)}) %all-gather.2.cloned.1.call-update) | async-done | bytes 18874384 | tf_op jit(solution)/shard_map/all_gather | solution.py:764
  164.7 4.2 attention_out.1
  173.6 74.7 %feed_forward.1 = (f32[1024,1024]{1,0:T(8,128)}, f32[1024,1024]{1,0:T(8,128)}, bf16[16,4,32,1024]{3,2,1,0:T(8,128)(2,1)}, bf16[16,4,32,1024]{3,2,1,0:T(8,128)(2,...) custom-call(s32[5]{0:T(128)} %stack.53.own_ref, ...), custom_call_target="tpu_custom_call" | custom-call | flops 25769803776 | bytes 16777216 | tf_op jit(solution)/shard_map/feed_forward/pallas_call | solution.py:452
  253.1 5.8 %fusion.7 = (f32[1024]{0:T(1024)S(1)}, f32[1,1024,1024]{2,1,0:T(8,128)}) fusion(bf16[1,1024,1024]{2,1,0:T(8,128)(2,1)S(1)} %copy-done.18, f32[1024,1024]{1,0:T(8,128)} %get-tuple-element.76, f32[1024]{0:T(1024)S(1)} %get-tuple-element.187, f32[1,1024,1024]{2,1,0:T(8,128)S(1)} %copy-done.15, f32[1024]{0:T(1024)S(1)} %bitcast.182), kind=kLoop, calls=%fused_computation.14 | loop fusion | flops 6290432 | bytes 14692352 | tf_op jit(solution)/shard_map/reduce_sum | solution.py:894
  261.9 6.7 %fusion.8 = (bf16[8,128,1024]{2,1,0:T(8,128)(2,1)}, bf16[8,128,1024]{2,1,0:T(8,128)(2,1)}) fusion(bf16[1,2,4,128,1024]{4,3,2,1,0:T(8,128)(2,1)S(1)} %get-tuple-element.169, bf16[16,128,1024]{2,1,0:T(8,128)(2,1)} %collective-permute-done.11, bf16[1,2,4,128,1024]{4,3,2,1,0:T(8,128)(2,1)S(1)} %get-tuple-element.170), kind=kLoop, calls=%fused_computation.16 | loop fusion | flops 8388608 | bytes 12582912 | tf_op jit(solution)/shard_map/convert_element_type | solution.py:709
  270.1 5.0 add_convert_fusion
  282.7 4.7 attention_out_back.1.g_ref
  287.4 24.3 %attention_backward_low.1 = (bf16[3,1024,512]{2,1,0:T(8,128)(2,1)S(1)}, f32[1,512]{1,0:T(1,128)S(1)}, f32[1,512]{1,0:T(1,128)S(1)}) custom-call(bf16[1024,3072]{1,0:T(8,128)(2,1)} %get-tuple-element.73.q_ref.k_ref.v_ref, bf16[1024,3072]{1,0:T(8,128)(2,1)} %get-tuple-element.73.q_ref.k_ref.v_ref, bf16[1024,3072]{1,0:T(8,128)(2,1)} %get-tuple-element.73.q_ref.k_ref.v_ref, ...), custom_call_target="tpu_custom_call" | custom-call | flops 2147483648 | bytes 8388608 | tf_op jit(solution)/shard_map/attention_backward_low/pallas_call | solution.py:610
  315.0 10.6 %weight_grad_low.1 = (bf16[16,5,32,512]{3,2,1,0:T(8,128)(2,1)S(1)}, bf16[16,5,32,512]{3,2,1,0:T(8,128)(2,1)}) custom-call(s32[5]{0:T(128)S(1)} %copy-done.13, bf16[1024,1024]{1,0:T(8,128)(2,1)S(1)} %copy-done.12, bf16[1024,1024]{1,0:T(8,128)(2,1)S(1)} %get-tuple-element.157.dy_ref.dx_ref, bf16[1024,1024]{1,0:T(8,128)(2,1)S(1)} %copy-done.6, ...), custom_call_target="tpu_custom_call" | custom-call | flops 2684354560 | bytes 2621440 | tf_op jit(solution)/shard_map/weight_grad_low/pallas_call | solution.py:279
  325.7 3.6 add_convert_fusion.5
  330.8 3.5 add_convert_fusion.6
  334.9 13.0 %attention_backward_mid.1 = (bf16[3,1024,512]{2,1,0:T(8,128)(2,1)S(1)}, f32[1,256]{1,0:T(1,128)S(1)}, f32[1,256]{1,0:T(1,128)S(1)}) custom-call(bf16[1024,3072]{1,0:T(8,128)(2,1)} %get-tuple-element.73.q_ref.k_ref.v_ref, bf16[1024,3072]{1,0:T(8,128)(2,1)} %get-tuple-element.73.q_ref.k_ref.v_ref, bf16[1024,3072]{1,0:T(8,128)(2,1)} %get-tuple-element.73.q_ref.k_ref.v_ref, ...), custom_call_target="tpu_custom_call" | custom-call | flops 1073741824 | bytes 4194304 | tf_op jit(solution)/shard_map/attention_backward_mid/pallas_call | solution.py:610
  347.9 7.3 %collective-permute-done.15 = bf16[4,128,1024]{2,1,0:T(8,128)(2,1)} collective-permute-done((bf16[4,128,1024]{2,1,0:T(8,128)(2,1)}, bf16[4,128,1024]{2,1,0:T(8,128)(2,1)}, u32[]{:S(2)}, u32[]{:S(2)}) %collective-permute-start.15) | collective-permute-done | bytes 1048608 | tf_op jit(solution)/shard_map/ppermute | solution.py:649
  355.2 4.5 collective-permute-done.14
  359.8 4.3 add_convert_fusion.3
  370.2 12.7 %attention_backward_high.1 = (bf16[3,1024,512]{2,1,0:T(8,128)(2,1)S(1)}, f32[1,256]{1,0:T(1,128)S(1)}, f32[1,256]{1,0:T(1,128)S(1)}) custom-call(bf16[1024,3072]{1,0:T(8,128)(2,1)} %get-tuple-element.73.q_ref.k_ref.v_ref, bf16[1024,3072]{1,0:T(8,128)(2,1)} %get-tuple-element.73.q_ref.k_ref.v_ref, ...), custom_call_target="tpu_custom_call", output_to_operand_aliasing={{0}: (6, {})} | custom-call | flops 1073741824 | bytes 4194304 | tf_op jit(solution)/shard_map/attention_backward_high/pallas_call | solution.py:610
  383.0 5.9 %weight_grad_high.1 = (bf16[16,3,32,512]{3,2,1,0:T(8,128)(2,1)S(1)}, bf16[16,3,32,512]{3,2,1,0:T(8,128)(2,1)}) custom-call(s32[5]{0:T(128)S(1)} %copy-done.13, bf16[1024,1024]{1,0:T(8,128)(2,1)S(1)} %copy-done.6, bf16[1024,1024]{1,0:T(8,128)(2,1)S(1)} %copy-done.6, bf16[1024,1024]{1,0:T(8,128)(2,1)S(1)} %copy-done.6, ...), custom_call_target="tpu_custom_call" | custom-call | flops 1610612736 | bytes 1572864 | tf_op jit(solution)/shard_map/weight_grad_high/pallas_call | solution.py:279
  397.8 3.9 fusion.15
  413.9 16.6 %project_back.1 = (f32[1024,1024]{1,0:T(8,128)}, f32[1,1024]{1,0:T(1,128)S(1)}, f32[1,1024]{1,0:T(1,128)S(1)}) custom-call(bf16[3,1024,512]{2,1,0:T(8,128)(2,1)S(1)} %copy-done.9, bf16[3,1024,512]{2,1,0:T(8,128)(2,1)} %copy-done.7, bf16[1024,3072]{1,0:T(8,128)(2,1)} %get-tuple-element.106.w_ref, bf16[1024,1024]{1,0:T(8,128)(2,1)S(1)} %bitcast.160, ...), custom_call_target="tpu_custom_call" | custom-call | flops 1610612736 | bytes 524288 | tf_op jit(solution)/shard_map/project_back/pallas_call | solution.py:218
  442.2 9.5 %collective-permute-done.26 = bf16[2,128,128]{2,1,0:T(8,128)(2,1)S(1)} collective-permute-done((bf16[2,128,128]{2,1,0:T(8,128)(2,1)S(1)}, bf16[2,128,128]{2,1,0:T(8,128)(2,1)S(1)}, u32[]{:S(2)}, u32[]{:S(2)}) %collective-permute-start.26) | collective-permute-done | bytes 65568 | tf_op jit(solution)/shard_map/ppermute | solution.py:649
  460.3 5.1 %collective-permute-done.32 = bf16[4,3,32,512]{3,2,1,0:T(8,128)(2,1)S(1)} collective-permute-done((bf16[4,3,32,512]{3,2,1,0:T(8,128)(2,1)S(1)}, bf16[4,3,32,512]{3,2,1,0:T(8,128)(2,1)S(1)}, u32[]{:S(2)}, u32[]{:S(2)}) %collective-permute-start.32) | collective-permute-done | bytes 393248 | tf_op jit(solution)/shard_map/ppermute | solution.py:649
  467.8 6.8 %collective-permute-done.33 = bf16[2,3,32,512]{3,2,1,0:T(8,128)(2,1)S(1)} collective-permute-done((bf16[2,3,32,512]{3,2,1,0:T(8,128)(2,1)S(1)}, bf16[2,3,32,512]{3,2,1,0:T(8,128)(2,1)S(1)}, u32[]{:S(2)}, u32[]{:S(2)}) %collective-permute-start.33) | collective-permute-done | bytes 196640 | tf_op jit(solution)/shard_map/ppermute | solution.py:649
  474.8 5.5 %collective-permute-done.34 = bf16[1,3,32,512]{3,2,1,0:T(8,128)(2,1)S(1)} collective-permute-done((bf16[1,3,32,512]{3,2,1,0:T(8,128)(2,1)S(1)}, bf16[1,3,32,512]{3,2,1,0:T(8,128)(2,1)S(1)}, u32[]{:S(2)}, u32[]{:S(2)}) %collective-permute-start.34) | collective-permute-done | bytes 98336 | tf_op jit(solution)/shard_map/ppermute | solution.py:649
  (304 shorter events, 137.0 us)
Async XLA Ops:
  7.2 155.9 %all-gather.2.cloned.1.call-start = ((), (), s32[]{:S(2)}) async-start(), calls=%async_computation.1 | async-start | bytes 19464192 | tf_op jit(solution)/shard_map/all_gather | solution.py:764
  13.0 21.4 %collective-permute-start.5 = (bf16[1,32,1536]{2,1,0:T(8,128)(2,1)S(1)}, bf16[1,32,1536]{2,1,0:T(8,128)(2,1)S(1)}, u32[]{:S(2)}, u32[]{:S(2)}) collective-permute-start(bf16[1,32,1536]{2,1,0:T(8,128)(2,1)S(1)} %get-tuple-element.151), channel_id=1, source_target_pairs={{0,4},{1,5},{2,6},{3,7},{4,0},{5,1},{6,2},{7,3},{8,12},{9,13},{10,... | collective-permute-start | bytes 294920 | tf_op jit(solution)/shard_map/ppermute | solution.py:649
  17.0 20.1 %collective-permute-start = (bf16[1,32,1536]{2,1,0:T(8,128)(2,1)S(1)}, bf16[1,32,1536]{2,1,0:T(8,128)(2,1)S(1)}, u32[]{:S(2)}, u32[]{:S(2)}) collective-permute-start(bf16[1,32,1536]{2,1,0:T(8,128)(2,1)S(1)} %get-tuple-element.186), channel_id=1, source_target_pairs={{0,4},{1,5},{2,6},{3,7},{4,0},{5,1},{6,2},{7,3},{8,12},{9,13},{10,... | collective-permute-start | bytes 294920 | tf_op jit(solution)/shard_map/ppermute | solution.py:649
  23.5 32.0 %all-to-all-start = ((f32[8,1,7936]{2,1,0:T(1,128)}), f32[8,1,7936]{2,1,0:T(1,128)}, u32[]{:S(2)}, u32[]{:S(2)}) async-start(f32[8,1,7936]{2,1,0:T(1,128)} %copy.30), calls=%async_computation | async-start | bytes 507904 | tf_op jit(solution)/shard_map/all_to_all | solution.py:858
  35.0 12.7 %collective-permute-start.6 = (bf16[2,32,1536]{2,1,0:T(8,128)(2,1)S(1)}, bf16[2,32,1536]{2,1,0:T(8,128)(2,1)S(1)}, u32[]{:S(2)}, u32[]{:S(2)}) collective-permute-start(bf16[2,32,1536]{2,1,0:T(8,128)(2,1)S(1)} %pad_maximum_fusion.9), channel_id=1, source_target_pairs={{0,2},{1,3},{2,0},{3,1},{4,6},{5,7},{6,4},{7,5},{8,10},{9,11},{10,... | collective-permute-start | bytes 589832 | tf_op jit(solution)/shard_map/ppermute | solution.py:649
  37.7 13.8 %collective-permute-start.1 = (bf16[2,32,1536]{2,1,0:T(8,128)(2,1)S(1)}, bf16[2,32,1536]{2,1,0:T(8,128)(2,1)S(1)}, u32[]{:S(2)}, u32[]{:S(2)}) collective-permute-start(bf16[2,32,1536]{2,1,0:T(8,128)(2,1)S(1)} %pad_maximum_fusion.8), channel_id=1, source_target_pairs={{0,2},{1,3},{2,0},{3,1},{4,6},{5,7},{6,4},{7,5},{8,10},{9,11},{10,... | collective-permute-start | bytes 589832 | tf_op jit(solution)/shard_map/ppermute | solution.py:649
  49.4 18.0 %collective-permute-start.7 = (bf16[4,32,1536]{2,1,0:T(8,128)(2,1)}, bf16[4,32,1536]{2,1,0:T(8,128)(2,1)}, u32[]{:S(2)}, u32[]{:S(2)}) collective-permute-start(bf16[4,32,1536]{2,1,0:T(8,128)(2,1)} %pad_maximum_fusion.6), channel_id=1, source_target_pairs={{0,16},{1,17},{2,18},{3,19},{4,20},{5,21},{6,22},{7,23},{8,24},{9,... | collective-permute-start | bytes 1179656 | tf_op jit(solution)/shard_map/ppermute | solution.py:649
  53.3 20.7 %collective-permute-start.2 = (bf16[4,32,1536]{2,1,0:T(8,128)(2,1)}, bf16[4,32,1536]{2,1,0:T(8,128)(2,1)}, u32[]{:S(2)}, u32[]{:S(2)}) collective-permute-start(bf16[4,32,1536]{2,1,0:T(8,128)(2,1)} %pad_maximum_fusion.5), channel_id=1, source_target_pairs={{0,1},{1,0},{2,3},{3,2},{4,5},{5,4},{6,7},{7,6},{8,9},{9,8},{10,11... | collective-permute-start | bytes 1179656 | tf_op jit(solution)/shard_map/ppermute | solution.py:649
  68.5 28.3 %collective-permute-start.8 = (bf16[8,32,1536]{2,1,0:T(8,128)(2,1)S(1)}, bf16[8,32,1536]{2,1,0:T(8,128)(2,1)S(1)}, u32[]{:S(2)}, u32[]{:S(2)}) collective-permute-start(bf16[8,32,1536]{2,1,0:T(8,128)(2,1)S(1)} %pad_maximum_fusion.1), channel_id=1, source_target_pairs={{0,1},{1,0},{2,3},{3,2},{4,5},{5,4},{6,7},{7,6},{8,9},{9,8},{10,11... | collective-permute-start | bytes 2359304 | tf_op jit(solution)/shard_map/ppermute | solution.py:649
  75.0 22.7 %collective-permute-start.3 = (bf16[8,32,1536]{2,1,0:T(8,128)(2,1)S(1)}, bf16[8,32,1536]{2,1,0:T(8,128)(2,1)S(1)}, u32[]{:S(2)}, u32[]{:S(2)}) collective-permute-start(bf16[8,32,1536]{2,1,0:T(8,128)(2,1)S(1)} %pad_maximum_fusion), channel_id=1, source_target_pairs={{0,16},{1,17},{2,18},{3,19},{4,20},{5,21},{6,22},{7,23},{8,24},{9,... | collective-permute-start | bytes 2359304 | tf_op jit(solution)/shard_map/ppermute | solution.py:649
  248.3 10.9 %collective-permute-start.10 = (bf16[16,4,32,1024]{3,2,1,0:T(8,128)(2,1)}, bf16[16,4,32,1024]{3,2,1,0:T(8,128)(2,1)S(1)}, u32[]{:S(2)}, u32[]{:S(2)}) collective-permute-start(bf16[16,4,32,1024]{3,2,1,0:T(8,128)(2,1)} %get-tuple-element.77), channel_id=1, source_target_pairs={{0,8},{1,9},{2,10},{3,11},{4,12},{5,13},{6,14},{7,15},{8,0},{9,1},... | collective-permute-start | bytes 12582920 | tf_op jit(solution)/shard_map/ppermute | solution.py:649
  248.7 13.3 %collective-permute-start.11 = (bf16[16,128,1024]{2,1,0:T(8,128)(2,1)}, bf16[16,128,1024]{2,1,0:T(8,128)(2,1)}, u32[]{:S(2)}, u32[]{:S(2)}) collective-permute-start(bf16[16,128,1024]{2,1,0:T(8,128)(2,1)} %bitcast.199), channel_id=1, source_target_pairs={{0,8},{1,9},{2,10},{3,11},{4,12},{5,13},{6,14},{7,15},{8,0},{9,1},... | collective-permute-start | bytes 12582920 | tf_op jit(solution)/shard_map/ppermute | solution.py:649
  268.6 57.0 %collective-permute-start.13 = (bf16[8,128,1024]{2,1,0:T(8,128)(2,1)}, bf16[8,128,1024]{2,1,0:T(8,128)(2,1)}, u32[]{:S(2)}, u32[]{:S(2)}) collective-permute-start(bf16[8,128,1024]{2,1,0:T(8,128)(2,1)} %get-tuple-element.168), channel_id=1, source_target_pairs={{0,1},{1,0},{2,3},{3,2},{4,5},{5,4},{6,7},{7,6},{8,9},{9,8},{10,11... | collective-permute-start | bytes 6291464 | tf_op jit(solution)/shard_map/ppermute | solution.py:649
  275.1 50.6 %collective-permute-start.12 = (bf16[8,4,32,1024]{3,2,1,0:T(8,128)(2,1)}, bf16[8,4,32,1024]{3,2,1,0:T(8,128)(2,1)}, u32[]{:S(2)}, u32[]{:S(2)}) collective-permute-start(bf16[8,4,32,1024]{3,2,1,0:T(8,128)(2,1)} %get-tuple-element.155), channel_id=1, source_target_pairs={{0,16},{1,17},{2,18},{3,19},{4,20},{5,21},{6,22},{7,23},{8,24},{9,... | collective-permute-start | bytes 6291464 | tf_op jit(solution)/shard_map/ppermute | solution.py:649
  325.6 34.1 %collective-permute-start.16 = (bf16[16,5,32,512]{3,2,1,0:T(8,128)(2,1)}, bf16[16,5,32,512]{3,2,1,0:T(8,128)(2,1)}, u32[]{:S(2)}, u32[]{:S(2)}) collective-permute-start(bf16[16,5,32,512]{3,2,1,0:T(8,128)(2,1)} %get-tuple-element.94), channel_id=1, source_target_pairs={{0,8},{1,9},{2,10},{3,11},{4,12},{5,13},{6,14},{7,15},{8,0},{9,1},... | collective-permute-start | bytes 7864328 | tf_op jit(solution)/shard_map/ppermute | solution.py:649
  329.4 25.9 %collective-permute-start.15 = (bf16[4,128,1024]{2,1,0:T(8,128)(2,1)}, bf16[4,128,1024]{2,1,0:T(8,128)(2,1)}, u32[]{:S(2)}, u32[]{:S(2)}) collective-permute-start(bf16[4,128,1024]{2,1,0:T(8,128)(2,1)} %get-tuple-element.164), channel_id=1, source_target_pairs={{0,16},{1,17},{2,18},{3,19},{4,20},{5,21},{6,22},{7,23},{8,24},{9,... | collective-permute-start | bytes 3145736 | tf_op jit(solution)/shard_map/ppermute | solution.py:649
  334.3 25.5 %collective-permute-start.14 = (bf16[4,4,32,1024]{3,2,1,0:T(8,128)(2,1)}, bf16[4,4,32,1024]{3,2,1,0:T(8,128)(2,1)S(1)}, u32[]{:S(2)}, u32[]{:S(2)}) collective-permute-start(bf16[4,4,32,1024]{3,2,1,0:T(8,128)(2,1)} %get-tuple-element.166), channel_id=1, source_target_pairs={{0,1},{1,0},{2,3},{3,2},{4,5},{5,4},{6,7},{7,6},{8,9},{9,8},{10,11... | collective-permute-start | bytes 3145736 | tf_op jit(solution)/shard_map/ppermute | solution.py:649
  364.0 30.4 %collective-permute-start.19 = (bf16[8,5,32,512]{3,2,1,0:T(8,128)(2,1)}, bf16[8,5,32,512]{3,2,1,0:T(8,128)(2,1)}, u32[]{:S(2)}, u32[]{:S(2)}) collective-permute-start(bf16[8,5,32,512]{3,2,1,0:T(8,128)(2,1)} %get-tuple-element.160), channel_id=1, source_target_pairs={{0,16},{1,17},{2,18},{3,19},{4,20},{5,21},{6,22},{7,23},{8,24},{9,... | collective-permute-start | bytes 3932168 | tf_op jit(solution)/shard_map/ppermute | solution.py:649
  367.0 21.9 %collective-permute-start.18 = (bf16[2,128,1024]{2,1,0:T(8,128)(2,1)S(1)}, bf16[2,128,1024]{2,1,0:T(8,128)(2,1)S(1)}, u32[]{:S(2)}, u32[]{:S(2)}) collective-permute-start(bf16[2,128,1024]{2,1,0:T(8,128)(2,1)S(1)} %get-tuple-element.176), channel_id=1, source_target_pairs={{0,2},{1,3},{2,0},{3,1},{4,6},{5,7},{6,4},{7,5},{8,10},{9,11},{10,... | collective-permute-start | bytes 1572872 | tf_op jit(solution)/shard_map/ppermute | solution.py:649
  368.4 22.8 %collective-permute-start.17 = (bf16[2,4,32,1024]{3,2,1,0:T(8,128)(2,1)S(1)}, bf16[2,4,32,1024]{3,2,1,0:T(8,128)(2,1)S(1)}, u32[]{:S(2)}, u32[]{:S(2)}) collective-permute-start(bf16[2,4,32,1024]{3,2,1,0:T(8,128)(2,1)S(1)} %get-tuple-element.178), channel_id=1, source_target_pairs={{0,2},{1,3},{2,0},{3,1},{4,6},{5,7},{6,4},{7,5},{8,10},{9,11},{10,... | collective-permute-start | bytes 1572872 | tf_op jit(solution)/shard_map/ppermute | solution.py:649
  394.4 15.0 %collective-permute-start.20 = (bf16[16,3,32,512]{3,2,1,0:T(8,128)(2,1)}, bf16[16,3,32,512]{3,2,1,0:T(8,128)(2,1)}, u32[]{:S(2)}, u32[]{:S(2)}) collective-permute-start(bf16[16,3,32,512]{3,2,1,0:T(8,128)(2,1)} %get-tuple-element.104), channel_id=1, source_target_pairs={{0,8},{1,9},{2,10},{3,11},{4,12},{5,13},{6,14},{7,15},{8,0},{9,1},... | collective-permute-start | bytes 4718600 | tf_op jit(solution)/shard_map/ppermute | solution.py:649
  404.9 30.8 %collective-permute-start.24 = (bf16[4,5,32,512]{3,2,1,0:T(8,128)(2,1)}, bf16[4,5,32,512]{3,2,1,0:T(8,128)(2,1)}, u32[]{:S(2)}, u32[]{:S(2)}) collective-permute-start(bf16[4,5,32,512]{3,2,1,0:T(8,128)(2,1)} %get-tuple-element.174), channel_id=1, source_target_pairs={{0,1},{1,0},{2,3},{3,2},{4,5},{5,4},{6,7},{7,6},{8,9},{9,8},{10,11... | collective-permute-start | bytes 1966088 | tf_op jit(solution)/shard_map/ppermute | solution.py:649
  405.6 30.1 %collective-permute-start.23 = (bf16[1,128,1024]{2,1,0:T(8,128)(2,1)S(1)}, bf16[1,128,1024]{2,1,0:T(8,128)(2,1)}, u32[]{:S(2)}, u32[]{:S(2)}) collective-permute-start(bf16[1,128,1024]{2,1,0:T(8,128)(2,1)S(1)} %add_convert_fusion.25), channel_id=1, source_target_pairs={{0,4},{1,5},{2,6},{3,7},{4,0},{5,1},{6,2},{7,3},{8,12},{9,13},{10,... | collective-permute-start | bytes 786440 | tf_op jit(solution)/shard_map/ppermute | solution.py:649
  407.9 27.7 %collective-permute-start.22 = (bf16[1,4,32,1024]{3,2,1,0:T(8,128)(2,1)}, bf16[1,4,32,1024]{3,2,1,0:T(8,128)(2,1)}, u32[]{:S(2)}, u32[]{:S(2)}) collective-permute-start(bf16[1,4,32,1024]{3,2,1,0:T(8,128)(2,1)} %add_convert_fusion.26), channel_id=1, source_target_pairs={{0,4},{1,5},{2,6},{3,7},{4,0},{5,1},{6,2},{7,3},{8,12},{9,13},{10,... | collective-permute-start | bytes 786440 | tf_op jit(solution)/shard_map/ppermute | solution.py:649
  412.5 23.2 %collective-permute-start.25 = (bf16[8,3,32,512]{3,2,1,0:T(8,128)(2,1)}, bf16[8,3,32,512]{3,2,1,0:T(8,128)(2,1)}, u32[]{:S(2)}, u32[]{:S(2)}) collective-permute-start(bf16[8,3,32,512]{3,2,1,0:T(8,128)(2,1)} %get-tuple-element.172), channel_id=1, source_target_pairs={{0,16},{1,17},{2,18},{3,19},{4,20},{5,21},{6,22},{7,23},{8,24},{9,... | collective-permute-start | bytes 2359304 | tf_op jit(solution)/shard_map/ppermute | solution.py:649
  438.2 45.2 %collective-permute-start.39 = (bf16[2,128,1024]{2,1,0:T(8,128)(2,1)S(1)}, bf16[2,128,1024]{2,1,0:T(8,128)(2,1)S(1)}, u32[]{:S(2)}, u32[]{:S(2)}) collective-permute-start(bf16[2,128,1024]{2,1,0:T(8,128)(2,1)S(1)} %pad_maximum_fusion.4.refs_0_), channel_id=1, source_target_pairs={{0,16},{1,17},{2,18},{3,19},{4,20},{5,21},{6,22},{7,23},{8,24},{9,... | collective-permute-start | bytes 1572872 | tf_op jit(solution)/shard_map/ppermute | solution.py:649
  438.9 52.4 %collective-permute-start.38 = (bf16[2,128,1024]{2,1,0:T(8,128)(2,1)S(1)}, bf16[2,128,1024]{2,1,0:T(8,128)(2,1)S(1)}, u32[]{:S(2)}, u32[]{:S(2)}) collective-permute-start(bf16[2,128,1024]{2,1,0:T(8,128)(2,1)S(1)} %pad_maximum_fusion.4.refs_0_), channel_id=1, source_target_pairs={{0,8},{1,9},{2,10},{3,11},{4,12},{5,13},{6,14},{7,15},{8,0},{9,1},... | collective-permute-start | bytes 1572872 | tf_op jit(solution)/shard_map/ppermute | solution.py:649
  440.1 25.8 %collective-permute-start.30 = (bf16[2,5,32,512]{3,2,1,0:T(8,128)(2,1)S(1)}, bf16[2,5,32,512]{3,2,1,0:T(8,128)(2,1)S(1)}, u32[]{:S(2)}, u32[]{:S(2)}) collective-permute-start(bf16[2,5,32,512]{3,2,1,0:T(8,128)(2,1)S(1)} %get-tuple-element.182), channel_id=1, source_target_pairs={{0,2},{1,3},{2,0},{3,1},{4,6},{5,7},{6,4},{7,5},{8,10},{9,11},{10,... | collective-permute-start | bytes 983048 | tf_op jit(solution)/shard_map/ppermute | solution.py:649
  440.4 11.4 %collective-permute-start.26 = (bf16[2,128,128]{2,1,0:T(8,128)(2,1)S(1)}, bf16[2,128,128]{2,1,0:T(8,128)(2,1)S(1)}, u32[]{:S(2)}, u32[]{:S(2)}) collective-permute-start(bf16[2,128,128]{2,1,0:T(8,128)(2,1)S(1)} %pad_maximum_fusion.11), channel_id=1, source_target_pairs={{0,2},{1,3},{2,0},{3,1},{4,6},{5,7},{6,4},{7,5},{8,10},{9,11},{10,... | collective-permute-start | bytes 196616 | tf_op jit(solution)/shard_map/ppermute | solution.py:649
  454.6 10.8 %collective-permute-start.32 = (bf16[4,3,32,512]{3,2,1,0:T(8,128)(2,1)S(1)}, bf16[4,3,32,512]{3,2,1,0:T(8,128)(2,1)S(1)}, u32[]{:S(2)}, u32[]{:S(2)}) collective-permute-start(bf16[4,3,32,512]{3,2,1,0:T(8,128)(2,1)S(1)} %get-tuple-element.180), channel_id=1, source_target_pairs={{0,1},{1,0},{2,3},{3,2},{4,5},{5,4},{6,7},{7,6},{8,9},{9,8},{10,11... | collective-permute-start | bytes 1179656 | tf_op jit(solution)/shard_map/ppermute | solution.py:649
  457.2 10.5 %collective-permute-start.28 = (bf16[8,128,128]{2,1,0:T(8,128)(2,1)S(1)}, bf16[8,128,128]{2,1,0:T(8,128)(2,1)S(1)}, u32[]{:S(2)}, u32[]{:S(2)}) collective-permute-start(bf16[8,128,128]{2,1,0:T(8,128)(2,1)S(1)} %get-tuple-element.192), channel_id=1, source_target_pairs={{0,16},{1,17},{2,18},{3,19},{4,20},{5,21},{6,22},{7,23},{8,24},{9,... | collective-permute-start | bytes 786440 | tf_op jit(solution)/shard_map/ppermute | solution.py:649
  467.7 19.1 %collective-permute-start.29 = (bf16[16,128,128]{2,1,0:T(8,128)(2,1)S(1)}, bf16[16,128,128]{2,1,0:T(8,128)(2,1)S(1)}, u32[]{:S(2)}, u32[]{:S(2)}) collective-permute-start(bf16[16,128,128]{2,1,0:T(8,128)(2,1)S(1)} %pad_maximum_fusion.3), channel_id=1, source_target_pairs={{0,8},{1,9},{2,10},{3,11},{4,12},{5,13},{6,14},{7,15},{8,0},{9,1},... | collective-permute-start | bytes 1572872 | tf_op jit(solution)/shard_map/ppermute | solution.py:649
  (58 other events, 463.4 us)
Sparse Core Ops, SparseCore 0:
  11.5 151.5 all-gather.1
